TPU v7x, 32 devices: a whole 2x2x4 slice. The times are simulated.
32 devices in a mesh: dp: 4 (over y, core), seq: 8 (over z, x).
Axes of the slice: x: 2, y: 2, z: 4, core: 2. Of those that a mesh axis runs over, the one named last changes fastest.
Arguments:
- queries: bfloat16 [4, 1024, 2048], P('dp', 'seq'), may hold values from -40 to 40, as said below
- keys: bfloat16 [4, 1024, 2048], P('dp', 'seq'), may hold values from -40 to 40, as said below
- values: bfloat16 [4, 1024, 2048], P('dp', 'seq'), may hold values from -40 to 40, as said below
- gain: float32 [2048], replicated, may hold values from 0.1 to 1.9
- cotangent: bfloat16 [4, 1024, 2048], P('dp', 'seq'), may hold values from -240 to 240, as said below
Outputs:
- output: bfloat16 [4, 1024, 2048], P('dp', 'seq')
- grad_query: bfloat16 [4, 1024, 2048], P('dp', 'seq')
- grad_key: bfloat16 [4, 1024, 2048], P('dp', 'seq')
- grad_value: bfloat16 [4, 1024, 2048], P('dp', 'seq')
- gain_grad: float32 [2048], replicated
Inputs may be any that keep to these rules, and one draw needn't show every extreme that they name: queries: independent entries with row and feature scales. keys: independent entries with row and feature scales. values: independent entries with row and feature scales. cotangent: independent entries with row and feature scales.
All inputs are finite; a program needn't handle non-finite values.
Results may differ from a plain program's by a relative error of at most 0.0058.
Values may be sent and summed in bfloat16 or wider, within the bound.
No kernel may reach another device: no remote copies, remote signals or barrier semaphores. Data moves between devices by JAX's collectives and lax.ppermute only.
A program may use at most 64 MiB of HBM per device.

v0:
```python
import functools

import jax
import jax.numpy as jnp
from jax import lax
from jax.experimental import pallas as pl
from jax.experimental.pallas import tpu as pltpu
from jax.sharding import PartitionSpec as P

HEADS = 16

EPSILON = 1e-06

STATE_LIMIT = 63 * 1024 * 1024

F32 = jnp.float32
HALF = jnp.bfloat16


def dot(lhs, rhs, lhs_dim, rhs_dim):
    return lax.dot_general(
        lhs, rhs, (((lhs_dim,), (rhs_dim,)), ((), ())), preferred_element_type=F32
    )


def causal(size):
    rows = lax.broadcasted_iota(jnp.int32, (size, size), 0)
    columns = lax.broadcasted_iota(jnp.int32, (size, size), 1)
    return rows >= columns


def member_of(group):
    return lax.rem(lax.axis_index("seq"), group)


def block_at(index, size):
    return pl.ds(pl.multiple_of(index * size, size), size)


def gathered(member, piece_refs, size, whole_ref):
    for j, ref in enumerate(piece_refs):
        whole_ref[block_at(member ^ j, size), :] = ref[0:size, :]


def scattered(member, whole_ref, size, piece_refs):
    for j, ref in enumerate(piece_refs):
        ref[...] = whole_ref[block_at(member ^ j, size), :]


def state_kernel(head, group, k_ref, v_ref, *refs):
    piece_refs = refs[:group]
    k_chunks, v_chunks, arrived = refs[group:]
    member = member_of(group)
    size = piece_refs[0].shape[0]
    copies = []
    for j in range(group):
        source = block_at(member ^ j, size)
        for i, (ref, chunks) in enumerate(((k_ref, k_chunks), (v_ref, v_chunks))):
            copy = pltpu.make_async_copy(
                ref.at[:, source], chunks.at[j], arrived.at[i, j]
            )
            copy.start()
            copies.append(copy)
    for j in range(group):
        copies[2 * j].wait()
        copies[2 * j + 1].wait()
        for i in range(size // head):
            part = slice(i * head, (i + 1) * head)
            piece_refs[j][part, :] = dot(
                k_chunks[j, :, part], v_chunks[j, :, part], 0, 0
            ).astype(HALF)


def local_kernel(head, q_ref, k_ref, v_ref, scores_ref, intra_ref):
    rows = q_ref.shape[0]
    mask = causal(rows)
    scaling = head ** (-0.5)
    for h in range(HEADS):
        part = slice(h * head, (h + 1) * head)
        scores = dot(q_ref[:, part], k_ref[:, part], 1, 1) * scaling
        scores = jnp.where(mask, scores, 0.0).astype(HALF)
        scores_ref[h * rows : (h + 1) * rows, :] = scores
        intra_ref[:, part] = dot(scores, v_ref[:, part], 1, 0)


def norm_kernel(head, group, replicas, *refs):
    q_ref, intra_ref, gain_ref, cot_ref = refs[:4]
    prefix_refs = refs[4 : 4 + group]
    attended_ref, inverse_ref, grad_ref, gain_grad_ref = refs[4 + group : 8 + group]
    piece_refs = refs[8 + group : 8 + 2 * group]
    whole_ref = refs[8 + 2 * group]
    member = member_of(group)
    rows = q_ref.shape[0]
    scaling = head ** (-0.5)
    features = HEADS * head
    size = features // group
    gathered(member, prefix_refs, size, whole_ref)
    squares = jnp.zeros((rows, head), F32)
    inner = jnp.zeros((rows, head), F32)
    for h in range(HEADS):
        part = slice(h * head, (h + 1) * head)
        attended = intra_ref[:, part] + scaling * dot(
            q_ref[:, part], whole_ref[part, :], 1, 0
        )
        attended_ref[:, part] = attended
        scaled = cot_ref[:, part].astype(F32) * gain_ref[h : h + 1, :]
        squares += attended * attended
        inner += scaled * attended
    inverse = lax.rsqrt(
        jnp.sum(squares, axis=1, keepdims=True) * (1.0 / features) + EPSILON
    )
    inner_mean = jnp.sum(inner, axis=1, keepdims=True) * (1.0 / features) * inverse
    inverse_ref[...] = jnp.broadcast_to(inverse, inverse_ref.shape)
    for h in range(HEADS):
        part = slice(h * head, (h + 1) * head)
        normalized = attended_ref[:, part] * inverse
        upstream = cot_ref[:, part].astype(F32)
        gain = gain_ref[h : h + 1, :]
        gain_grad_ref[h : h + 1, :] = jnp.sum(
            upstream * normalized, axis=0, keepdims=True
        ) * (1.0 / replicas)
        grad = ((upstream * gain - normalized * inner_mean) * inverse).astype(HALF)
        grad_ref[:, part] = grad
        whole_ref[part, :] = (scaling * dot(q_ref[:, part], grad, 0, 0)).astype(HALF)
    scattered(member, whole_ref, size, piece_refs)


def backward_kernel(head, group, *refs):
    q_ref, k_ref, v_ref, scores_ref, grad_ref = refs[:5]
    attended_ref, inverse_ref, gain_ref = refs[5:8]
    prefix_refs = refs[8 : 8 + group]
    out_ref, grad_query_ref, key_part_ref, value_part_ref, token_ref = refs[
        8 + group : 13 + group
    ]
    whole_ref = refs[13 + group]
    rows = q_ref.shape[0]
    mask = causal(rows)
    scaling = head ** (-0.5)
    gathered(member_of(group), prefix_refs, prefix_refs[0].shape[0], whole_ref)
    inverse = inverse_ref[...]
    for h in range(HEADS):
        part = slice(h * head, (h + 1) * head)
        out_ref[:, part] = (
            gain_ref[h : h + 1, :] * (attended_ref[:, part] * inverse)
        ).astype(HALF)
        grad = grad_ref[:, part]
        grad_scores = dot(grad, v_ref[:, part], 1, 1)
        grad_scores = jnp.where(mask, grad_scores, 0.0).astype(HALF)
        grad_query = dot(grad_scores, k_ref[:, part], 1, 0) + dot(
            grad, whole_ref[part, :], 1, 1
        )
        grad_query_ref[:, part] = (scaling * grad_query).astype(HALF)
        key_part_ref[:, part] = scaling * dot(grad_scores, q_ref[:, part], 0, 0)
        value_part_ref[:, part] = dot(
            scores_ref[h * rows : (h + 1) * rows, :], grad, 0, 0
        )
    token_ref[...] = jnp.zeros_like(token_ref)


def final_kernel(head, group, *refs):
    k_ref, v_ref, key_part_ref, value_part_ref = refs[:4]
    suffix_refs = refs[4 : 4 + group]
    grad_key_ref, grad_value_ref, gain_grad_ref = refs[4 + group : 7 + group]
    whole_ref, key_buffer, value_buffer, written = refs[7 + group :]
    size = whole_ref.shape[0] // group
    gathered(member_of(group), suffix_refs, size, whole_ref)
    copies = []
    for chunk in range(group):
        for i in range(size // head):
            start = chunk * size + i * head
            part = slice(start, start + head)
            suffix = whole_ref[part, :]
            key_buffer[:, part] = (
                key_part_ref[:, part] + dot(v_ref[:, part], suffix, 1, 1)
            ).astype(HALF)
            value_buffer[:, part] = (
                value_part_ref[:, part] + dot(k_ref[:, part], suffix, 1, 0)
            ).astype(HALF)
        part = slice(chunk * size, (chunk + 1) * size)
        for i, (buffer, ref) in enumerate(
            ((key_buffer, grad_key_ref), (value_buffer, grad_value_ref))
        ):
            copy = pltpu.make_async_copy(
                buffer.at[:, part], ref.at[:, part], written.at[i, chunk]
            )
            copy.start()
            copies.append(copy)
    terms = []
    for ref in suffix_refs:
        rows = (ref.shape[0] - size) // 2
        high, low = ref[size : size + rows, :], ref[size + rows : size + 2 * rows, :]
        terms.append(high.astype(F32) + low.astype(F32))
    while len(terms) > 1:
        terms = [a + b for a, b in zip(terms[::2], terms[1::2])]
    gain_grad_ref[...] = terms[0]
    for copy in copies:
        copy.wait()


def total_kernel(*refs):
    total = refs[0][...].astype(F32)
    for ref in refs[1:-1]:
        total += ref[...].astype(F32)
    refs[-1][...] = total.astype(HALF)


def group_flag(group, reverse, distance):
    index = lax.axis_index("seq") // group
    last = lax.axis_size("seq") // group - 1
    known = index + distance <= last if reverse else index >= distance
    return jnp.where(known, 1.0, 0.0)


def carry_kernel(group, reverse, distance, first, own_ref, moved_ref, out_ref):
    own = own_ref[...].astype(F32)
    if first:
        own = own * group_flag(group, reverse, 1)
    moved = moved_ref[...].astype(F32) * group_flag(group, reverse, distance)
    out_ref[...] = (own + moved).astype(HALF)


def scan_kernel(group, reverse, masked, sums, *refs):
    member = member_of(group)
    carry = refs[0][...].astype(F32)
    if masked:
        carry = carry * group_flag(group, reverse, 1)
    blocks = [ref[...].astype(F32) for ref in refs[1 : 1 + group]]
    out_refs = refs[-group:]
    size = blocks[0].shape[0]
    for j in range(group):
        total = carry
        for i in range(group):
            if i != j:
                earlier = (member ^ i) < (member ^ j)
                keep = jnp.where(earlier != reverse, 1.0, 0.0)
                total += keep * blocks[i]
        out_refs[j][0:size, :] = total.astype(HALF)
    if sums:
        total = refs[1 + group][...]
        for ref in refs[2 + group : 1 + group + sums]:
            total = total + ref[...]
        high = total.astype(HALF)
        low = (total - high.astype(F32)).astype(HALF)
        rows = total.shape[0]
        for ref in out_refs:
            ref[size : size + rows, :] = high
            ref[size + rows : size + 2 * rows, :] = low


VMEM = pl.BlockSpec(memory_space=pltpu.VMEM)
ANY = pl.BlockSpec(memory_space=pl.ANY)
HBM = pl.BlockSpec(memory_space=pltpu.HBM)


def call(
    kernel,
    outs,
    args,
    matmuls,
    scratch=(),
    in_any=(),
    out_any=(),
    in_hbm=(),
    limit=16 * 1024 * 1024,
):
    size = sum(a.size * a.dtype.itemsize for a in args)
    size += sum(o.size * o.dtype.itemsize for o in outs)
    return pl.pallas_call(
        kernel,
        out_shape=tuple(outs),
        in_specs=[
            HBM if i in in_hbm else ANY if i in in_any else VMEM
            for i in range(len(args))
        ],
        out_specs=tuple(HBM if i in out_any else VMEM for i in range(len(outs))),
        scratch_shapes=list(scratch),
        compiler_params=pltpu.CompilerParams(vmem_limit_bytes=limit),
        cost_estimate=pl.CostEstimate(
            flops=2 * 128 * 128 * 128 * HEADS * matmuls,
            bytes_accessed=size,
            transcendentals=0,
        ),
    )(*args)


def swap(array, axis, offset):
    count = lax.axis_size(axis)
    return lax.ppermute(array, axis, [(i, i ^ offset) for i in range(count)])


def own_and_swapped(pieces):
    order = sorted(range(1, len(pieces)), key=lambda j: -bin(j).count("1"))
    moved = {j: swap(pieces[j], "seq", j) for j in order}
    return [pieces[0]] + [moved[j] for j in range(1, len(pieces))]


def exclusive_scan(pieces, reverse, token, gain_part=None):
    group = len(pieces)
    count = lax.axis_size("seq")
    piece = jax.ShapeDtypeStruct(pieces[0].shape, HALF)
    blocks = own_and_swapped(pieces)

    def shifted(array, distance):
        step = -distance if reverse else distance
        pairs = [(i, (i + step) % count) for i in range(count)]
        return lax.ppermute(array, "seq", pairs)

    (total,) = call(total_kernel, [piece], blocks, 0)
    carry = shifted(total, group)
    distance = 1
    while distance < count // group - 1:
        kernel = functools.partial(
            carry_kernel, group, reverse, distance + (distance == 1), distance == 1
        )
        (carry,) = call(kernel, [piece], [carry, shifted(carry, distance * group)], 0)
        distance *= 2
    gains = gain_terms(gain_part, group) if gain_part is not None else []
    rows = piece.shape[0] + 2 * (gain_part.shape[0] if gains else 0)
    inputs = [carry] + blocks + gains + [token]
    sums = call(
        functools.partial(scan_kernel, group, reverse, distance == 1, len(gains)),
        [jax.ShapeDtypeStruct((rows, piece.shape[1]), HALF)] * group,
        inputs,
        0,
        in_any=(len(inputs) - 1,),
    )
    return own_and_swapped(sums)


def gain_terms(array, group):
    for axis, stride in (("dp", 1), ("seq", group)):
        count = lax.axis_size(axis)
        terms = [array]
        while stride < count:
            array = functools.reduce(jnp.add, terms)
            width = 4 if count // stride % 4 == 0 else 2
            terms = [array] + [swap(array, axis, i * stride) for i in range(1, width)]
            if width == 4:
                terms = [terms[0] + terms[1], terms[2] + terms[3]]
            stride *= width
        array = functools.reduce(jnp.add, terms) if axis == "dp" else array
    return terms


def per_device(queries, keys, values, gain, cotangent):
    q, k, v, cot = queries[0], keys[0], values[0], cotangent[0]
    rows, features = q.shape
    head = features // HEADS
    group = 4
    size = features // group
    part = functools.partial
    wide = jax.ShapeDtypeStruct((rows, features), F32)
    half = jax.ShapeDtypeStruct((rows, features), HALF)
    square = jax.ShapeDtypeStruct((rows, head), F32)
    piece = jax.ShapeDtypeStruct((size, head), HALF)
    scores_shape = jax.ShapeDtypeStruct((HEADS * rows, rows), HALF)
    gain_shape = jax.ShapeDtypeStruct((HEADS, head), F32)
    token_shape = jax.ShapeDtypeStruct((8, head), F32)
    whole = pltpu.VMEM((features, head), HALF)
    gain_rows = gain.reshape(HEADS, head)

    pieces = call(
        part(state_kernel, head, group),
        [piece] * group,
        [k, v],
        1,
        [pltpu.VMEM((group, rows, size), HALF)] * 2
        + [pltpu.SemaphoreType.DMA((2, group))],
        in_hbm=(0, 1),
        limit=STATE_LIMIT,
    )
    scores, intra = call(part(local_kernel, head), [scores_shape, wide], [q, k, v], 2)
    prefix = exclusive_scan(pieces, False, intra)
    attended, inverse, grad, gain_part, *pieces = call(
        part(norm_kernel, head, group, lax.axis_size("dp")),
        [wide, square, half, gain_shape] + [piece] * group,
        [q, intra, gain_rows, cot] + prefix,
        2,
        [whole],
    )
    output, grad_query, key_part, value_part, token = call(
        part(backward_kernel, head, group),
        [half, half, wide, wide, token_shape],
        [q, k, v, scores, grad, attended, inverse, gain_rows] + prefix,
        5,
        [whole],
    )
    suffix = exclusive_scan(pieces, True, token, gain_part)
    grad_key, grad_value, gain_grad = call(
        part(final_kernel, head, group),
        [half, half, gain_shape],
        [k, v, key_part, value_part] + suffix,
        2,
        [
            whole,
            pltpu.VMEM((rows, features), HALF),
            pltpu.VMEM((rows, features), HALF),
            pltpu.SemaphoreType.DMA((2, group)),
        ],
        out_any=(0, 1),
    )
    return (
        output[None],
        grad_query[None],
        grad_key[None],
        grad_value[None],
        gain_grad.reshape(features),
    )


def solution(mesh):
    spec = P("dp", "seq", None)
    return jax.shard_map(
        per_device,
        mesh=mesh,
        in_specs=(spec, spec, spec, P(), spec),
        out_specs=(spec, spec, spec, spec, P()),
        check_vma=False,
    )
```

profile of v0, /device:TPU:0, one launch (start us, length us, event | category | flops | bytes accessed | tf_op | source)
XLA Modules:
  0.0 61.0 jit_solution(2871839830170354815)
XLA Ops:
  0.6 2.6 %shard_map.93 = (bf16[512,128]{1,0:T(8,128)(2,1)}, bf16[512,128]{1,0:T(8,128)(2,1)}, bf16[512,128]{1,0:T(8,128)(2,1)}, bf16[512,128]{1,0:T(8,128)(2,1)}) custom-call(bf16[128,2048]{1,0:T(8,128)(2,1)} %bitcast.10, bf16[128,2048]{1,0:T(8,128)(2,1)} %bitcast.14), custom_call_target="tpu_custom_call" | custom-call | flops 67108864 | bytes 1572864 | tf_op jit(solution)/shard_map/pallas_call | solution.py:268
  3.3 3.0 %collective-permute-start = (bf16[512,128]{1,0:T(8,128)(2,1)}, bf16[512,128]{1,0:T(8,128)(2,1)S(1)}, u32[]{:S(2)}, u32[]{:S(2)}) collective-permute-start(bf16[512,128]{1,0:T(8,128)(2,1)} %get-tuple-element.38), channel_id=1, source_target_pairs={{0,1},{1,0},{2,3},{3,2},{4,5},{5,4},{6,7},{7,6},{8,9},{9,8},{10,11... | collective-permute-start | bytes 393224 | tf_op jit(solution)/shard_map/ppermute | solution.py:288
  6.3 1.6 %collective-permute-start.1 = (bf16[512,128]{1,0:T(8,128)(2,1)}, bf16[512,128]{1,0:T(8,128)(2,1)S(1)}, u32[]{:S(2)}, u32[]{:S(2)}) collective-permute-start(bf16[512,128]{1,0:T(8,128)(2,1)} %get-tuple-element.39), channel_id=1, source_target_pairs={{0,2},{1,3},{2,0},{3,1},{4,6},{5,7},{6,4},{7,5},{8,10},{9,11},{10,... | collective-permute-start | bytes 393224 | tf_op jit(solution)/shard_map/ppermute | solution.py:288
  7.9 2.1 %collective-permute-done.refs_1_.refs_2_ = bf16[512,128]{1,0:T(8,128)(2,1)S(1)} collective-permute-done((bf16[512,128]{1,0:T(8,128)(2,1)}, bf16[512,128]{1,0:T(8,128)(2,1)S(1)}, u32[]{:S(2)}, u32[]{:S(2)}) %collective-permute-start) | collective-permute-done | bytes 131104 | tf_op jit(solution)/shard_map/ppermute | solution.py:288
  10.0 2.9 %collective-permute-done.1.refs_2_.refs_3_ = bf16[512,128]{1,0:T(8,128)(2,1)S(1)} collective-permute-done((bf16[512,128]{1,0:T(8,128)(2,1)}, bf16[512,128]{1,0:T(8,128)(2,1)S(1)}, u32[]{:S(2)}, u32[]{:S(2)}) %collective-permute-start.1) | collective-permute-done | bytes 131104 | tf_op jit(solution)/shard_map/ppermute | solution.py:288
  12.9 1.2 %collective-permute-done.2.refs_3_.refs_4_ = bf16[512,128]{1,0:T(8,128)(2,1)S(1)} collective-permute-done((bf16[512,128]{1,0:T(8,128)(2,1)}, bf16[512,128]{1,0:T(8,128)(2,1)S(1)}, u32[]{:S(2)}, u32[]{:S(2)}) %collective-permute-start.2) | collective-permute-done | bytes 131104 | tf_op jit(solution)/shard_map/ppermute | solution.py:288
  14.1 0.9 %copy-done.5 = bf16[512,128]{1,0:T(8,128)(2,1)S(1)} copy-done((bf16[512,128]{1,0:T(8,128)(2,1)S(1)}, bf16[512,128]{1,0:T(8,128)(2,1)}, u32[]{:S(2)}) %copy-start.5) | copy-done | bytes 131096
  15.0 2.8 %collective-permute-start.3 = (bf16[512,128]{1,0:T(8,128)(2,1)S(1)}, bf16[512,128]{1,0:T(8,128)(2,1)S(1)}, u32[]{:S(2)}, u32[]{:S(2)}) collective-permute-start(bf16[512,128]{1,0:T(8,128)(2,1)S(1)} %shard_map.94), channel_id=1, source_target_pairs={{0,4},{1,5},{2,6},{3,7},{4,0},{5,1},{6,2},{7,3},{8,12},{9,13},{10,... | collective-permute-start | bytes 393224 | tf_op jit(solution)/shard_map/ppermute | solution.py:306
  17.9 1.0 %copy-done.2 = bf16[1,128,2048]{2,1,0:T(8,128)(2,1)S(1)} copy-done((bf16[1,128,2048]{2,1,0:T(8,128)(2,1)S(1)}, bf16[1,128,2048]{2,1,0:T(8,128)(2,1)}, u32[]{:S(2)}) %copy-start.2) | copy-done | bytes 524312
  18.9 2.6 %shard_map.92 = (bf16[2048,128]{1,0:T(8,128)(2,1)S(1)}, f32[128,2048]{1,0:T(8,128)S(1)}) custom-call(bf16[128,2048]{1,0:T(8,128)(2,1)S(1)} %bitcast.18, bf16[128,2048]{1,0:T(8,128)(2,1)S(1)} %bitcast.11, bf16[128,2048]{1,0:T(8,128)(2,1)S(1)} %bitcast.15), custom_call_target="tpu_custom_call" | custom-call | flops 134217728 | bytes 3145728 | tf_op jit(solution)/shard_map/pallas_call | solution.py:268
  21.5 1.8 %collective-permute-done.3.refs_0_ = bf16[512,128]{1,0:T(8,128)(2,1)S(1)} collective-permute-done((bf16[512,128]{1,0:T(8,128)(2,1)S(1)}, bf16[512,128]{1,0:T(8,128)(2,1)S(1)}, u32[]{:S(2)}, u32[]{:S(2)}) %collective-permute-start.3) | collective-permute-done | bytes 131104 | tf_op jit(solution)/shard_map/ppermute | solution.py:306
  23.6 1.0 %collective-permute-start.4 = (bf16[512,128]{1,0:T(8,128)(2,1)S(1)}, bf16[512,128]{1,0:T(8,128)(2,1)S(1)}, u32[]{:S(2)}, u32[]{:S(2)}) collective-permute-start(bf16[512,128]{1,0:T(8,128)(2,1)S(1)} %get-tuple-element.42), channel_id=1, source_target_pairs={{0,1},{1,0},{2,3},{3,2},{4,5},{5,4},{6,7},{7,6},{8,9},{9,8},{10,11... | collective-permute-start | bytes 393224 | tf_op jit(solution)/shard_map/ppermute | solution.py:288
  24.6 0.7 %collective-permute-start.5 = (bf16[512,128]{1,0:T(8,128)(2,1)S(1)}, bf16[512,128]{1,0:T(8,128)(2,1)S(1)}, u32[]{:S(2)}, u32[]{:S(2)}) collective-permute-start(bf16[512,128]{1,0:T(8,128)(2,1)S(1)} %get-tuple-element.43), channel_id=1, source_target_pairs={{0,2},{1,3},{2,0},{3,1},{4,6},{5,7},{6,4},{7,5},{8,10},{9,11},{10,... | collective-permute-start | bytes 393224 | tf_op jit(solution)/shard_map/ppermute | solution.py:288
  25.3 1.9 %collective-permute-start.6 = (bf16[512,128]{1,0:T(8,128)(2,1)S(1)}, bf16[512,128]{1,0:T(8,128)(2,1)S(1)}, u32[]{:S(2)}, u32[]{:S(2)}) collective-permute-start(bf16[512,128]{1,0:T(8,128)(2,1)S(1)} %get-tuple-element.44), channel_id=1, source_target_pairs={{0,3},{1,2},{2,1},{3,0},{4,7},{5,6},{6,5},{7,4},{8,11},{9,10},{10,... | collective-permute-start | bytes 393224 | tf_op jit(solution)/shard_map/ppermute | solution.py:288
  27.2 2.2 %collective-permute-done.4.refs_5_.refs_9_ = bf16[512,128]{1,0:T(8,128)(2,1)S(1)} collective-permute-done((bf16[512,128]{1,0:T(8,128)(2,1)S(1)}, bf16[512,128]{1,0:T(8,128)(2,1)S(1)}, u32[]{:S(2)}, u32[]{:S(2)}) %collective-permute-start.4) | collective-permute-done | bytes 131104 | tf_op jit(solution)/shard_map/ppermute | solution.py:288
  29.4 0.7 %collective-permute-done.5.refs_6_.refs_10_ = bf16[512,128]{1,0:T(8,128)(2,1)S(1)} collective-permute-done((bf16[512,128]{1,0:T(8,128)(2,1)S(1)}, bf16[512,128]{1,0:T(8,128)(2,1)S(1)}, u32[]{:S(2)}, u32[]{:S(2)}) %collective-permute-start.5) | collective-permute-done | bytes 131104 | tf_op jit(solution)/shard_map/ppermute | solution.py:288
  30.1 2.5 %collective-permute-done.6.refs_7_.refs_11_ = bf16[512,128]{1,0:T(8,128)(2,1)S(1)} collective-permute-done((bf16[512,128]{1,0:T(8,128)(2,1)S(1)}, bf16[512,128]{1,0:T(8,128)(2,1)S(1)}, u32[]{:S(2)}, u32[]{:S(2)}) %collective-permute-start.6) | collective-permute-done | bytes 131104 | tf_op jit(solution)/shard_map/ppermute | solution.py:288
  32.6 1.2 %shard_map.96 = (f32[128,2048]{1,0:T(8,128)S(1)}, f32[128,128]{1,0:T(8,128)S(1)}, bf16[128,2048]{1,0:T(8,128)(2,1)S(1)}, f32[16,128]{1,0:T(8,128)S(1)}, bf16[512...) custom-call(bf16[128,2048]{1,0:T(8,128)(2,1)S(1)} %bitcast.19, ...), custom_call_target="tpu_custom_call" | custom-call | flops 134217728 | bytes 4800512 | tf_op jit(solution)/shard_map/pallas_call | solution.py:268
  34.2 1.4 %collective-permute-start.8 = (bf16[512,128]{1,0:T(8,128)(2,1)S(1)}, bf16[512,128]{1,0:T(8,128)(2,1)S(1)}, u32[]{:S(2)}, u32[]{:S(2)}) collective-permute-start(bf16[512,128]{1,0:T(8,128)(2,1)S(1)} %get-tuple-element.54), channel_id=1, source_target_pairs={{0,2},{1,3},{2,0},{3,1},{4,6},{5,7},{6,4},{7,5},{8,10},{9,11},{10,... | collective-permute-start | bytes 393224 | tf_op jit(solution)/shard_map/ppermute | solution.py:288
  35.6 1.7 %collective-permute-start.9 = (bf16[512,128]{1,0:T(8,128)(2,1)S(1)}, bf16[512,128]{1,0:T(8,128)(2,1)S(1)}, u32[]{:S(2)}, u32[]{:S(2)}) collective-permute-start(bf16[512,128]{1,0:T(8,128)(2,1)S(1)} %get-tuple-element.55), channel_id=1, source_target_pairs={{0,3},{1,2},{2,1},{3,0},{4,7},{5,6},{6,5},{7,4},{8,11},{9,10},{10,... | collective-permute-start | bytes 393224 | tf_op jit(solution)/shard_map/ppermute | solution.py:288
  37.3 1.5 %collective-permute-start.12 = (f32[16,128]{1,0:T(8,128)S(1)}, f32[16,128]{1,0:T(8,128)S(1)}, u32[]{:S(2)}, u32[]{:S(2)}) collective-permute-start(f32[16,128]{1,0:T(8,128)S(1)} %get-tuple-element.56), channel_id=1, source_target_pairs={{0,16},{8,24},{16,0},{24,8},{1,17},{9,25},{17,1},{25,9},{2,18},{10... | collective-permute-start | bytes 24584 | tf_op jit(solution)/shard_map/ppermute | solution.py:288
  38.8 1.0 %collective-permute-done.7.refs_1_.refs_2_ = bf16[512,128]{1,0:T(8,128)(2,1)S(1)} collective-permute-done((bf16[512,128]{1,0:T(8,128)(2,1)S(1)}, bf16[512,128]{1,0:T(8,128)(2,1)S(1)}, u32[]{:S(2)}, u32[]{:S(2)}) %collective-permute-start.7) | collective-permute-done | bytes 131104 | tf_op jit(solution)/shard_map/ppermute | solution.py:288
  39.8 1.8 %collective-permute-done.9.refs_3_.refs_4_ = bf16[512,128]{1,0:T(8,128)(2,1)S(1)} collective-permute-done((bf16[512,128]{1,0:T(8,128)(2,1)S(1)}, bf16[512,128]{1,0:T(8,128)(2,1)S(1)}, u32[]{:S(2)}, u32[]{:S(2)}) %collective-permute-start.9) | collective-permute-done | bytes 131104 | tf_op jit(solution)/shard_map/ppermute | solution.py:288
  41.7 2.4 %collective-permute-start.10 = (bf16[512,128]{1,0:T(8,128)(2,1)S(1)}, bf16[512,128]{1,0:T(8,128)(2,1)S(1)}, u32[]{:S(2)}, u32[]{:S(2)}) collective-permute-start(bf16[512,128]{1,0:T(8,128)(2,1)S(1)} %shard_map.98), channel_id=1, source_target_pairs={{0,4},{1,5},{2,6},{3,7},{4,0},{5,1},{6,2},{7,3},{8,12},{9,13},{10,... | collective-permute-start | bytes 393224 | tf_op jit(solution)/shard_map/ppermute | solution.py:306
  44.1 0.7 %collective-permute-start.14 = (f32[16,128]{1,0:T(8,128)S(1)}, f32[16,128]{1,0:T(8,128)S(1)}, u32[]{:S(2)}, u32[]{:S(2)}) collective-permute-start(f32[16,128]{1,0:T(8,128)S(1)} %add_add_fusion.refs_5_), channel_id=1, source_target_pairs={{0,4},{1,5},{2,6},{3,7},{4,0},{5,1},{6,2},{7,3},{8,12},{9,13},{10,... | collective-permute-start | bytes 24584 | tf_op jit(solution)/shard_map/ppermute | solution.py:288
  44.8 3.6 %shard_map.97 = (bf16[128,2048]{1,0:T(8,128)(2,1)}, bf16[128,2048]{1,0:T(8,128)(2,1)}, f32[128,2048]{1,0:T(8,128)S(1)}, f32[128,2048]{1,0:T(8,128)S(1)}, f32[8,128]{1,0:T(8,128)S(1)}) custom-call(bf16[128,2048]{1,0:T(8,128)(2,1)S(1)} %bitcast.20, bf16[128,2048]{1,0:T(8,128)(2,1)S(1)} %bitcast.12, bf16[128,2048]{1,0:T(8,128)(2,1)S(1)} %bitcast.16, ...), custom_call_target="tpu_custom_call" | custom-call | flops 335544320 | bytes 7417856 | tf_op jit(solution)/shard_map/pallas_call | solution.py:268
  48.3 1.4 %collective-permute-done.14.refs_6_ = f32[16,128]{1,0:T(8,128)S(1)} collective-permute-done((f32[16,128]{1,0:T(8,128)S(1)}, f32[16,128]{1,0:T(8,128)S(1)}, u32[]{:S(2)}, u32[]{:S(2)}) %collective-permute-start.14) | collective-permute-done | bytes 8224 | tf_op jit(solution)/shard_map/ppermute | solution.py:288
  50.1 0.6 collective-permute-start.15
  51.2 2.4 %collective-permute-start.17 = (bf16[544,128]{1,0:T(8,128)(2,1)S(1)}, bf16[544,128]{1,0:T(8,128)(2,1)S(1)}, u32[]{:S(2)}, u32[]{:S(2)}) collective-permute-start(bf16[544,128]{1,0:T(8,128)(2,1)S(1)} %get-tuple-element.61), channel_id=1, source_target_pairs={{0,3},{1,2},{2,1},{3,0},{4,7},{5,6},{6,5},{7,4},{8,11},{9,10},{10,... | collective-permute-start | bytes 417800 | tf_op jit(solution)/shard_map/ppermute | solution.py:288
  53.6 3.0 %collective-permute-done.15.refs_5_ = bf16[544,128]{1,0:T(8,128)(2,1)S(1)} collective-permute-done((bf16[544,128]{1,0:T(8,128)(2,1)S(1)}, bf16[544,128]{1,0:T(8,128)(2,1)S(1)}, u32[]{:S(2)}, u32[]{:S(2)}) %collective-permute-start.15) | collective-permute-done | bytes 139296 | tf_op jit(solution)/shard_map/ppermute | solution.py:288
  56.6 2.4 %collective-permute-done.17.refs_7_ = bf16[544,128]{1,0:T(8,128)(2,1)S(1)} collective-permute-done((bf16[544,128]{1,0:T(8,128)(2,1)S(1)}, bf16[544,128]{1,0:T(8,128)(2,1)S(1)}, u32[]{:S(2)}, u32[]{:S(2)}) %collective-permute-start.17) | collective-permute-done | bytes 139296 | tf_op jit(solution)/shard_map/ppermute | solution.py:288
  59.0 2.0 %shard_map.100 = (bf16[128,2048]{1,0:T(8,128)(2,1)}, bf16[128,2048]{1,0:T(8,128)(2,1)}, f32[16,128]{1,0:T(8,128)}) custom-call(bf16[128,2048]{1,0:T(8,128)(2,1)S(1)} %bitcast.13, bf16[128,2048]{1,0:T(8,128)(2,1)S(1)} %bitcast.17, f32[128,2048]{1,0:T(8,128)S(1)} %get-tuple-element.50.refs_2_, f32[128,2048]{1,0:T(8,128)S(1)} %get-tuple-element.51.refs_3_, ...), custom_call_target="tpu_custom_call" | custom-call | flops 134217728 | bytes 4759552 | tf_op jit(solution)/shard_map/pallas_call | solution.py:268
  (30 shorter events, 1.8 us)
Async XLA Ops:
  0.6 17.3 %copy-start.1 = (bf16[1,128,2048]{2,1,0:T(8,128)(2,1)S(1)}, bf16[1,128,2048]{2,1,0:T(8,128)(2,1)}, u32[]{:S(2)}) copy-start(bf16[1,128,2048]{2,1,0:T(8,128)(2,1)} %param.7) | copy-start | bytes 1572868
  3.3 14.6 %copy-start = (bf16[1,128,2048]{2,1,0:T(8,128)(2,1)S(1)}, bf16[1,128,2048]{2,1,0:T(8,128)(2,1)}, u32[]{:S(2)}) copy-start(bf16[1,128,2048]{2,1,0:T(8,128)(2,1)} %param.6) | copy-start | bytes 1572868
  3.3 6.7 %collective-permute-start = (bf16[512,128]{1,0:T(8,128)(2,1)}, bf16[512,128]{1,0:T(8,128)(2,1)S(1)}, u32[]{:S(2)}, u32[]{:S(2)}) collective-permute-start(bf16[512,128]{1,0:T(8,128)(2,1)} %get-tuple-element.38), channel_id=1, source_target_pairs={{0,1},{1,0},{2,3},{3,2},{4,5},{5,4},{6,7},{7,6},{8,9},{9,8},{10,11... | collective-permute-start | bytes 393224 | tf_op jit(solution)/shard_map/ppermute | solution.py:288
  6.3 6.6 %collective-permute-start.1 = (bf16[512,128]{1,0:T(8,128)(2,1)}, bf16[512,128]{1,0:T(8,128)(2,1)S(1)}, u32[]{:S(2)}, u32[]{:S(2)}) collective-permute-start(bf16[512,128]{1,0:T(8,128)(2,1)} %get-tuple-element.39), channel_id=1, source_target_pairs={{0,2},{1,3},{2,0},{3,1},{4,6},{5,7},{6,4},{7,5},{8,10},{9,11},{10,... | collective-permute-start | bytes 393224 | tf_op jit(solution)/shard_map/ppermute | solution.py:288
  7.9 6.2 %collective-permute-start.2 = (bf16[512,128]{1,0:T(8,128)(2,1)}, bf16[512,128]{1,0:T(8,128)(2,1)S(1)}, u32[]{:S(2)}, u32[]{:S(2)}) collective-permute-start(bf16[512,128]{1,0:T(8,128)(2,1)} %get-tuple-element.40), channel_id=1, source_target_pairs={{0,3},{1,2},{2,1},{3,0},{4,7},{5,6},{6,5},{7,4},{8,11},{9,10},{10,... | collective-permute-start | bytes 393224 | tf_op jit(solution)/shard_map/ppermute | solution.py:288
  14.1 0.9 %copy-start.5 = (bf16[512,128]{1,0:T(8,128)(2,1)S(1)}, bf16[512,128]{1,0:T(8,128)(2,1)}, u32[]{:S(2)}) copy-start(bf16[512,128]{1,0:T(8,128)(2,1)} %get-tuple-element.37.refs_0_.refs_1_) | copy-start | bytes 393220
  15.0 8.2 %collective-permute-start.3 = (bf16[512,128]{1,0:T(8,128)(2,1)S(1)}, bf16[512,128]{1,0:T(8,128)(2,1)S(1)}, u32[]{:S(2)}, u32[]{:S(2)}) collective-permute-start(bf16[512,128]{1,0:T(8,128)(2,1)S(1)} %shard_map.94), channel_id=1, source_target_pairs={{0,4},{1,5},{2,6},{3,7},{4,0},{5,1},{6,2},{7,3},{8,12},{9,13},{10,... | collective-permute-start | bytes 393224 | tf_op jit(solution)/shard_map/ppermute | solution.py:306
  17.9 1.0 %copy-start.2 = (bf16[1,128,2048]{2,1,0:T(8,128)(2,1)S(1)}, bf16[1,128,2048]{2,1,0:T(8,128)(2,1)}, u32[]{:S(2)}) copy-start(bf16[1,128,2048]{2,1,0:T(8,128)(2,1)} %param.5) | copy-start | bytes 1572868
  18.9 4.4 %copy-start.6 = (bf16[512,128]{1,0:T(8,128)(2,1)S(1)}, bf16[512,128]{1,0:T(8,128)(2,1)}, u32[]{:S(2)}) copy-start(bf16[512,128]{1,0:T(8,128)(2,1)} %get-tuple-element.37.refs_0_.refs_1_) | copy-start | bytes 393220
  23.3 9.3 %copy-start.3 = (bf16[1,128,2048]{2,1,0:T(8,128)(2,1)S(1)}, bf16[1,128,2048]{2,1,0:T(8,128)(2,1)}, u32[]{:S(2)}) copy-start(bf16[1,128,2048]{2,1,0:T(8,128)(2,1)} %param.5) | copy-start | bytes 1572868
  23.3 9.3 %copy-start.4 = (bf16[1,128,2048]{2,1,0:T(8,128)(2,1)S(1)}, bf16[1,128,2048]{2,1,0:T(8,128)(2,1)}, u32[]{:S(2)}) copy-start(bf16[1,128,2048]{2,1,0:T(8,128)(2,1)} %param.9) | copy-start | bytes 1572868
  23.6 9.0 %copy-start.7 = (f32[2048]{0:T(1024)S(1)}, f32[2048]{0:T(1024)}, u32[]{:S(2)}) copy-start(f32[2048]{0:T(1024)} %param.8) | copy-start | bytes 24580
  23.6 5.7 %collective-permute-start.4 = (bf16[512,128]{1,0:T(8,128)(2,1)S(1)}, bf16[512,128]{1,0:T(8,128)(2,1)S(1)}, u32[]{:S(2)}, u32[]{:S(2)}) collective-permute-start(bf16[512,128]{1,0:T(8,128)(2,1)S(1)} %get-tuple-element.42), channel_id=1, source_target_pairs={{0,1},{1,0},{2,3},{3,2},{4,5},{5,4},{6,7},{7,6},{8,9},{9,8},{10,11... | collective-permute-start | bytes 393224 | tf_op jit(solution)/shard_map/ppermute | solution.py:288
  24.6 5.5 %collective-permute-start.5 = (bf16[512,128]{1,0:T(8,128)(2,1)S(1)}, bf16[512,128]{1,0:T(8,128)(2,1)S(1)}, u32[]{:S(2)}, u32[]{:S(2)}) collective-permute-start(bf16[512,128]{1,0:T(8,128)(2,1)S(1)} %get-tuple-element.43), channel_id=1, source_target_pairs={{0,2},{1,3},{2,0},{3,1},{4,6},{5,7},{6,4},{7,5},{8,10},{9,11},{10,... | collective-permute-start | bytes 393224 | tf_op jit(solution)/shard_map/ppermute | solution.py:288
  25.3 7.3 %collective-permute-start.6 = (bf16[512,128]{1,0:T(8,128)(2,1)S(1)}, bf16[512,128]{1,0:T(8,128)(2,1)S(1)}, u32[]{:S(2)}, u32[]{:S(2)}) collective-permute-start(bf16[512,128]{1,0:T(8,128)(2,1)S(1)} %get-tuple-element.44), channel_id=1, source_target_pairs={{0,3},{1,2},{2,1},{3,0},{4,7},{5,6},{6,5},{7,4},{8,11},{9,10},{10,... | collective-permute-start | bytes 393224 | tf_op jit(solution)/shard_map/ppermute | solution.py:288
  33.7 6.0 %collective-permute-start.7 = (bf16[512,128]{1,0:T(8,128)(2,1)S(1)}, bf16[512,128]{1,0:T(8,128)(2,1)S(1)}, u32[]{:S(2)}, u32[]{:S(2)}) collective-permute-start(bf16[512,128]{1,0:T(8,128)(2,1)S(1)} %get-tuple-element.53), channel_id=1, source_target_pairs={{0,1},{1,0},{2,3},{3,2},{4,5},{5,4},{6,7},{7,6},{8,9},{9,8},{10,11... | collective-permute-start | bytes 393224 | tf_op jit(solution)/shard_map/ppermute | solution.py:288
  34.2 5.6 %collective-permute-start.8 = (bf16[512,128]{1,0:T(8,128)(2,1)S(1)}, bf16[512,128]{1,0:T(8,128)(2,1)S(1)}, u32[]{:S(2)}, u32[]{:S(2)}) collective-permute-start(bf16[512,128]{1,0:T(8,128)(2,1)S(1)} %get-tuple-element.54), channel_id=1, source_target_pairs={{0,2},{1,3},{2,0},{3,1},{4,6},{5,7},{6,4},{7,5},{8,10},{9,11},{10,... | collective-permute-start | bytes 393224 | tf_op jit(solution)/shard_map/ppermute | solution.py:288
  35.6 6.0 %collective-permute-start.9 = (bf16[512,128]{1,0:T(8,128)(2,1)S(1)}, bf16[512,128]{1,0:T(8,128)(2,1)S(1)}, u32[]{:S(2)}, u32[]{:S(2)}) collective-permute-start(bf16[512,128]{1,0:T(8,128)(2,1)S(1)} %get-tuple-element.55), channel_id=1, source_target_pairs={{0,3},{1,2},{2,1},{3,0},{4,7},{5,6},{6,5},{7,4},{8,11},{9,10},{10,... | collective-permute-start | bytes 393224 | tf_op jit(solution)/shard_map/ppermute | solution.py:288
  37.3 6.8 %collective-permute-start.12 = (f32[16,128]{1,0:T(8,128)S(1)}, f32[16,128]{1,0:T(8,128)S(1)}, u32[]{:S(2)}, u32[]{:S(2)}) collective-permute-start(f32[16,128]{1,0:T(8,128)S(1)} %get-tuple-element.56), channel_id=1, source_target_pairs={{0,16},{8,24},{16,0},{24,8},{1,17},{9,25},{17,1},{25,9},{2,18},{10... | collective-permute-start | bytes 24584 | tf_op jit(solution)/shard_map/ppermute | solution.py:288
  38.8 5.3 %collective-permute-start.13 = (f32[16,128]{1,0:T(8,128)S(1)}, f32[16,128]{1,0:T(8,128)S(1)}, u32[]{:S(2)}, u32[]{:S(2)}) collective-permute-start(f32[16,128]{1,0:T(8,128)S(1)} %get-tuple-element.56), channel_id=1, source_target_pairs={{0,24},{8,16},{16,8},{24,0},{1,25},{9,17},{17,9},{25,1},{2,26},{10... | collective-permute-start | bytes 24584 | tf_op jit(solution)/shard_map/ppermute | solution.py:288
  39.8 4.3 %collective-permute-start.11 = (f32[16,128]{1,0:T(8,128)S(1)}, f32[16,128]{1,0:T(8,128)S(1)}, u32[]{:S(2)}, u32[]{:S(2)}) collective-permute-start(f32[16,128]{1,0:T(8,128)S(1)} %get-tuple-element.56), channel_id=1, source_target_pairs={{0,8},{8,0},{16,24},{24,16},{1,9},{9,1},{17,25},{25,17},{2,10},{10... | collective-permute-start | bytes 24584 | tf_op jit(solution)/shard_map/ppermute | solution.py:288
  41.7 8.0 %collective-permute-start.10 = (bf16[512,128]{1,0:T(8,128)(2,1)S(1)}, bf16[512,128]{1,0:T(8,128)(2,1)S(1)}, u32[]{:S(2)}, u32[]{:S(2)}) collective-permute-start(bf16[512,128]{1,0:T(8,128)(2,1)S(1)} %shard_map.98), channel_id=1, source_target_pairs={{0,4},{1,5},{2,6},{3,7},{4,0},{5,1},{6,2},{7,3},{8,12},{9,13},{10,... | collective-permute-start | bytes 393224 | tf_op jit(solution)/shard_map/ppermute | solution.py:306
  44.1 5.6 %collective-permute-start.14 = (f32[16,128]{1,0:T(8,128)S(1)}, f32[16,128]{1,0:T(8,128)S(1)}, u32[]{:S(2)}, u32[]{:S(2)}) collective-permute-start(f32[16,128]{1,0:T(8,128)S(1)} %add_add_fusion.refs_5_), channel_id=1, source_target_pairs={{0,4},{1,5},{2,6},{3,7},{4,0},{5,1},{6,2},{7,3},{8,12},{9,13},{10,... | collective-permute-start | bytes 24584 | tf_op jit(solution)/shard_map/ppermute | solution.py:288
  50.1 6.5 %collective-permute-start.15 = (bf16[544,128]{1,0:T(8,128)(2,1)S(1)}, bf16[544,128]{1,0:T(8,128)(2,1)S(1)}, u32[]{:S(2)}, u32[]{:S(2)}) collective-permute-start(bf16[544,128]{1,0:T(8,128)(2,1)S(1)} %get-tuple-element.59), channel_id=1, source_target_pairs={{0,1},{1,0},{2,3},{3,2},{4,5},{5,4},{6,7},{7,6},{8,9},{9,8},{10,11... | collective-permute-start | bytes 417800 | tf_op jit(solution)/shard_map/ppermute | solution.py:288
  50.6 6.0 %collective-permute-start.16 = (bf16[544,128]{1,0:T(8,128)(2,1)S(1)}, bf16[544,128]{1,0:T(8,128)(2,1)S(1)}, u32[]{:S(2)}, u32[]{:S(2)}) collective-permute-start(bf16[544,128]{1,0:T(8,128)(2,1)S(1)} %get-tuple-element.60), channel_id=1, source_target_pairs={{0,2},{1,3},{2,0},{3,1},{4,6},{5,7},{6,4},{7,5},{8,10},{9,11},{10,... | collective-permute-start | bytes 417800 | tf_op jit(solution)/shard_map/ppermute | solution.py:288
  51.2 7.8 %collective-permute-start.17 = (bf16[544,128]{1,0:T(8,128)(2,1)S(1)}, bf16[544,128]{1,0:T(8,128)(2,1)S(1)}, u32[]{:S(2)}, u32[]{:S(2)}) collective-permute-start(bf16[544,128]{1,0:T(8,128)(2,1)S(1)} %get-tuple-element.61), channel_id=1, source_target_pairs={{0,3},{1,2},{2,1},{3,0},{4,7},{5,6},{6,5},{7,4},{8,11},{9,10},{10,... | collective-permute-start | bytes 417800 | tf_op jit(solution)/shard_map/ppermute | solution.py:288
where the time goes:
time: 61.2 us; the launch traced here: 61 us
  waiting for transfers between devices  23 us (38%)
  starting transfers between devices  22.6 us (37%)
  Pallas kernels  12.7 us (21%)
  local copies, waits for them, and re-layouts  1.97 us (3%)
  between operations  0.72 us (1%)
    ppermute x16, waiting for transfers between devices, swap(): return lax.ppermute(array, axis, [(i, i ^ offset) for i in range(count)])  21.2 us
    ppermute x16, starting transfers between devices, swap(): return lax.ppermute(array, axis, [(i, i ^ offset) for i in range(count)])  17.4 us
    pallas_call x9, Pallas kernels, call(): pl.pallas_call(kernel, out_shape=tuple(outs), in_specs=[HBM if i in in_hb...  12.7 us
    ppermute x2, starting transfers between devices, shifted(): return lax.ppermute(array, 'seq', pairs)  5.22 us
    unnamed x16, local copies, waits for them, and re-layouts  1.97 us
    ppermute x2, waiting for transfers between devices, shifted(): return lax.ppermute(array, 'seq', pairs)  1.77 us
  transfers between devices with their start and end apart: 18, of which 12 were waited for; matrix products, arithmetic and copies ran while one was open for 0% of the time, Pallas kernels for 10%

commit v1 on v0

v1 whole, which is shorter than its diff:
```python
import functools

import jax
import jax.numpy as jnp
from jax import lax
from jax.experimental import pallas as pl
from jax.experimental.pallas import tpu as pltpu
from jax.sharding import PartitionSpec as P

HEADS = 16

EPSILON = 1e-06

F32 = jnp.float32
HALF = jnp.bfloat16


def dot(lhs, rhs, lhs_dim, rhs_dim):
    return lax.dot_general(
        lhs, rhs, (((lhs_dim,), (rhs_dim,)), ((), ())), preferred_element_type=F32
    )


def causal(size):
    rows = lax.broadcasted_iota(jnp.int32, (size, size), 0)
    columns = lax.broadcasted_iota(jnp.int32, (size, size), 1)
    return rows >= columns


def member_of(group):
    return lax.rem(lax.axis_index("seq"), group)


def block_at(index, size):
    return pl.ds(pl.multiple_of(index * size, size), size)


def gathered(member, piece_refs, size, whole_ref):
    for j, ref in enumerate(piece_refs):
        whole_ref[block_at(member ^ j, size), :] = ref[0:size, :]


def scattered(member, whole_ref, size, piece_refs):
    for j, ref in enumerate(piece_refs):
        ref[...] = whole_ref[block_at(member ^ j, size), :]


def columns(first, count):
    return slice(first, first + count)


def state_kernel(head, group, k_ref, v_ref, *refs):
    piece_refs = refs[:group]
    whole_ref, k_buffer, v_buffer, arrived = refs[group:]
    copies = [
        pltpu.make_async_copy(k_ref, k_buffer, arrived.at[0]),
        pltpu.make_async_copy(v_ref, v_buffer, arrived.at[1]),
    ]
    for copy in copies:
        copy.start()
    for copy in copies:
        copy.wait()
    for h in range(HEADS):
        part = columns(h * head, head)
        whole_ref[part, :] = dot(k_buffer[:, part], v_buffer[:, part], 0, 0).astype(HALF)
    scattered(member_of(group), whole_ref, piece_refs[0].shape[0], piece_refs)


def local_kernel(head, q_ref, k_ref, v_ref, scores_ref, intra_ref):
    rows = q_ref.shape[0]
    mask = causal(rows)
    scaling = head ** (-0.5)
    for h in range(HEADS):
        part = columns(h * head, head)
        scores = dot(q_ref[:, part], k_ref[:, part], 1, 1) * scaling
        scores = jnp.where(mask, scores, 0.0).astype(HALF)
        scores_ref[columns(h * rows, rows), :] = scores
        intra_ref[:, part] = dot(scores, v_ref[:, part], 1, 0)


def norm_kernel(head, group, replicas, *refs):
    q_ref, intra_ref, gain_ref, cot_ref = refs[:4]
    prefix_refs = refs[4 : 4 + group]
    attended_ref, inverse_ref, grad_ref, gain_grad_ref = refs[4 + group : 8 + group]
    piece_refs = refs[8 + group : 8 + 2 * group]
    whole_ref = refs[8 + 2 * group]
    member = member_of(group)
    rows = q_ref.shape[0]
    scaling = head ** (-0.5)
    features = HEADS * head
    size = features // group
    gathered(member, prefix_refs, size, whole_ref)
    squares = jnp.zeros((rows, head), F32)
    inner = jnp.zeros((rows, head), F32)
    for h in range(HEADS):
        part = columns(h * head, head)
        attended = intra_ref[:, part] + scaling * dot(
            q_ref[:, part], whole_ref[part, :], 1, 0
        )
        attended_ref[:, part] = attended
        scaled = cot_ref[:, part].astype(F32) * gain_ref[h : h + 1, :]
        squares += attended * attended
        inner += scaled * attended
    inverse = lax.rsqrt(
        jnp.sum(squares, axis=1, keepdims=True) * (1.0 / features) + EPSILON
    )
    inner_mean = jnp.sum(inner, axis=1, keepdims=True) * (1.0 / features) * inverse
    inverse_ref[...] = jnp.broadcast_to(inverse, inverse_ref.shape)
    for h in range(HEADS):
        part = columns(h * head, head)
        normalized = attended_ref[:, part] * inverse
        upstream = cot_ref[:, part].astype(F32)
        gain = gain_ref[h : h + 1, :]
        gain_grad_ref[h : h + 1, :] = jnp.sum(
            upstream * normalized, axis=0, keepdims=True
        ) * (1.0 / replicas)
        grad = ((upstream * gain - normalized * inner_mean) * inverse).astype(HALF)
        grad_ref[:, part] = grad
        whole_ref[part, :] = (scaling * dot(q_ref[:, part], grad, 0, 0)).astype(HALF)
    scattered(member, whole_ref, size, piece_refs)


def backward_kernel(head, group, *refs):
    q_ref, k_ref, v_ref, scores_ref, grad_ref = refs[:5]
    attended_ref, inverse_ref, gain_ref = refs[5:8]
    prefix_refs = refs[8 : 8 + group]
    out_ref, grad_query_ref, key_part_ref, value_part_ref, token_ref = refs[
        8 + group : 13 + group
    ]
    whole_ref = refs[13 + group]
    rows = q_ref.shape[0]
    mask = causal(rows)
    scaling = head ** (-0.5)
    gathered(member_of(group), prefix_refs, prefix_refs[0].shape[0], whole_ref)
    inverse = inverse_ref[...]
    for h in range(HEADS):
        part = columns(h * head, head)
        out_ref[:, part] = (
            gain_ref[h : h + 1, :] * (attended_ref[:, part] * inverse)
        ).astype(HALF)
        grad = grad_ref[:, part]
        grad_scores = dot(grad, v_ref[:, part], 1, 1)
        grad_scores = jnp.where(mask, grad_scores, 0.0).astype(HALF)
        grad_query = dot(grad_scores, k_ref[:, part], 1, 0) + dot(
            grad, whole_ref[part, :], 1, 1
        )
        grad_query_ref[:, part] = (scaling * grad_query).astype(HALF)
        key_part_ref[:, part] = scaling * dot(grad_scores, q_ref[:, part], 0, 0)
        value_part_ref[:, part] = dot(
            scores_ref[columns(h * rows, rows), :], grad, 0, 0
        )
    token_ref[...] = jnp.zeros_like(token_ref)


def final_kernel(head, group, chunks, last, *refs):
    k_ref, v_ref, key_part_ref, value_part_ref = refs[:4]
    suffix_refs = refs[4 : 4 + (group if last else len(chunks))]
    refs = refs[4 + len(suffix_refs) + (2 if last else 0) :]
    out_refs, refs = refs[:2], refs[2:]
    if last:
        gain_grad_ref, refs = refs[0], refs[1:]
    key_buffer, value_buffer, written = refs
    member = member_of(group)
    width = key_buffer.shape[2]
    copies = []
    for n, chunk in enumerate(chunks):
        suffix_ref = suffix_refs[chunk if last else n]
        start = (member ^ chunk) * width
        for i in range(width // head):
            part = pl.ds(pl.multiple_of(start + i * head, head), head)
            local = columns(i * head, head)
            suffix = suffix_ref[local, :]
            key_buffer[n, :, local] = (
                key_part_ref[:, part] + dot(v_ref[:, part], suffix, 1, 1)
            ).astype(HALF)
            value_buffer[n, :, local] = (
                value_part_ref[:, part] + dot(k_ref[:, part], suffix, 1, 0)
            ).astype(HALF)
        for i, buffer in enumerate((key_buffer, value_buffer)):
            copy = pltpu.make_async_copy(
                buffer.at[n],
                out_refs[i].at[:, block_at(member ^ chunk, width)],
                written.at[i, n],
            )
            copy.start()
            copies.append(copy)
    if last:
        terms = [wide_rows(ref, width) for ref in suffix_refs]
        while len(terms) > 1:
            terms = [a + b for a, b in zip(terms[::2], terms[1::2])]
        gain_grad_ref[...] = terms[0]
    for copy in copies:
        copy.wait()


def wide_rows(ref, start):
    rows = (ref.shape[0] - start) // 2
    high = ref[columns(start, rows), :].astype(F32)
    return high + ref[columns(start + rows, rows), :].astype(F32)


def put_wide_rows(ref, start, value):
    rows = value.shape[0]
    high = value.astype(HALF)
    ref[columns(start, rows), :] = high
    ref[columns(start + rows, rows), :] = (value - high.astype(F32)).astype(HALF)


def total_kernel(group, *refs):
    total = refs[0][...].astype(F32)
    for ref in refs[1:group]:
        total += ref[...].astype(F32)
    out_ref = refs[-1]
    size = total.shape[0]
    out_ref[0:size, :] = total.astype(HALF)
    gains = [ref[...] for ref in refs[group:-1]]
    if gains:
        put_wide_rows(out_ref, size, functools.reduce(jnp.add, gains))


def group_flag(group, reverse, distance):
    index = lax.axis_index("seq") // group
    last = lax.axis_size("seq") // group - 1
    known = index + distance <= last if reverse else index >= distance
    return jnp.where(known, 1.0, 0.0)


def carry_kernel(group, reverse, distance, first, own_ref, moved_ref, out_ref):
    own = own_ref[...].astype(F32)
    if first:
        own = own * group_flag(group, reverse, 1)
    moved = moved_ref[...].astype(F32) * group_flag(group, reverse, distance)
    out_ref[...] = (own + moved).astype(HALF)


def scan_kernel(group, reverse, masked, extra, *refs):
    member = member_of(group)
    size = refs[1].shape[0]
    carry = refs[0][0:size, :].astype(F32)
    if masked:
        carry = carry * group_flag(group, reverse, 1)
    blocks = [ref[...].astype(F32) for ref in refs[1 : 1 + group]]
    out_refs = refs[-group:]
    for j in range(group):
        total = carry
        for i in range(group):
            if i != j:
                earlier = (member ^ i) < (member ^ j)
                keep = jnp.where(earlier != reverse, 1.0, 0.0)
                total += keep * blocks[i]
        out_refs[j][0:size, :] = total.astype(HALF)
    if extra == "message":
        total = wide_rows(refs[0], size) + wide_rows(refs[1 + group], size)
    elif extra:
        total = functools.reduce(
            jnp.add, [ref[...] for ref in refs[1 + group : 1 + group + extra]]
        )
    if extra:
        for ref in out_refs:
            put_wide_rows(ref, size, total)


VMEM = pl.BlockSpec(memory_space=pltpu.VMEM)
ANY = pl.BlockSpec(memory_space=pl.ANY)
HBM = pl.BlockSpec(memory_space=pltpu.HBM)


def call(kernel, outs, args, matmuls, scratch=(), ins=None, out_specs=None, aliases=None):
    size = sum(a.size * a.dtype.itemsize for a in args)
    size += sum(o.size * o.dtype.itemsize for o in outs)
    ins = ins or {}
    out_specs = out_specs or {}
    return pl.pallas_call(
        kernel,
        out_shape=tuple(outs),
        in_specs=[ins.get(i, VMEM) for i in range(len(args))],
        out_specs=tuple(out_specs.get(i, VMEM) for i in range(len(outs))),
        scratch_shapes=list(scratch),
        input_output_aliases=aliases or {},
        compiler_params=pltpu.CompilerParams(vmem_limit_bytes=16 * 1024 * 1024),
        cost_estimate=pl.CostEstimate(
            flops=2 * 128 * 128 * 128 * HEADS * matmuls,
            bytes_accessed=size,
            transcendentals=0,
        ),
    )(*args)


def swap(array, axis, offset):
    count = lax.axis_size(axis)
    return lax.ppermute(array, axis, [(i, i ^ offset) for i in range(count)])


def own_and_swapped(pieces):
    order = sorted(range(1, len(pieces)), key=lambda j: -bin(j).count("1"))
    moved = {j: swap(pieces[j], "seq", j) for j in order}
    return [pieces[0]] + [moved[j] for j in range(1, len(pieces))]


def exclusive_scan(pieces, reverse, token, gain_part=None):
    group = len(pieces)
    count = lax.axis_size("seq")
    groups = count // group
    part = functools.partial

    def shaped(more=0):
        return jax.ShapeDtypeStruct((pieces[0].shape[0] + more, pieces[0].shape[1]), HALF)

    def shifted(array, distance):
        step = -distance if reverse else distance
        pairs = [(i, (i + step) % count) for i in range(count)]
        return lax.ppermute(array, "seq", pairs)

    received = own_and_swapped(pieces)
    gains, rows = [], 0
    if gain_part is not None:
        gains = summed_over("dp", 1, gain_part)
        rows = 2 * gain_part.shape[0]
        if groups != 2:
            gains = summed_over("seq", group, functools.reduce(jnp.add, gains))
    riding = gains if groups == 2 else []
    (total,) = call(
        part(total_kernel, group), [shaped(rows if riding else 0)], received + riding, 0
    )
    carry = shifted(total, group)
    distance = 1
    while distance < groups - 1:
        moved = shifted(carry, distance * group)
        kernel = part(
            carry_kernel, group, reverse, distance + (distance == 1), distance == 1
        )
        (carry,) = call(kernel, [shaped()], [carry, moved], 0)
        distance *= 2
    more, extra = [], 0
    if gains:
        more, extra = ([total], "message") if riding else (gains, len(gains))
    inputs = [carry] + received + more + [token]
    sums = call(
        part(scan_kernel, group, reverse, groups <= 2, extra),
        [shaped(rows)] * group,
        inputs,
        0,
        ins={len(inputs) - 1: ANY},
    )
    return own_and_swapped(sums)


def summed_over(axis, stride, array):
    count = lax.axis_size(axis)
    terms = [array]
    while stride < count:
        array = functools.reduce(jnp.add, terms)
        width = 4 if count // stride % 4 == 0 else 2
        terms = [array] + [swap(array, axis, i * stride) for i in range(1, width)]
        if width == 4:
            terms = [terms[0] + terms[1], terms[2] + terms[3]]
        stride *= width
    return terms


def per_device(queries, keys, values, gain, cotangent):
    q, k, v, cot = queries[0], keys[0], values[0], cotangent[0]
    rows, features = q.shape
    head = features // HEADS
    group = 4
    width = features // group
    part = functools.partial
    wide = jax.ShapeDtypeStruct((rows, features), F32)
    half = jax.ShapeDtypeStruct((rows, features), HALF)
    square = jax.ShapeDtypeStruct((rows, head), F32)
    piece = jax.ShapeDtypeStruct((width, head), HALF)
    scores_shape = jax.ShapeDtypeStruct((HEADS * rows, rows), HALF)
    gain_shape = jax.ShapeDtypeStruct((HEADS, head), F32)
    token_shape = jax.ShapeDtypeStruct((8, head), F32)
    whole = pltpu.VMEM((features, head), HALF)
    gain_rows = gain.reshape(HEADS, head)

    pieces = call(
        part(state_kernel, head, group),
        [piece] * group,
        [pltpu.with_memory_space_constraint(a, pltpu.HBM) for a in (k, v)],
        1,
        [whole]
        + [pltpu.VMEM((rows, features), HALF)] * 2
        + [pltpu.SemaphoreType.DMA((2,))],
        ins={0: HBM, 1: HBM},
    )
    scores, intra = call(part(local_kernel, head), [scores_shape, wide], [q, k, v], 2)
    prefix = exclusive_scan(pieces, False, intra)
    attended, inverse, grad, gain_part, *pieces = call(
        part(norm_kernel, head, group, lax.axis_size("dp")),
        [wide, square, half, gain_shape] + [piece] * group,
        [q, intra, gain_rows, cot] + prefix,
        2,
        [whole],
    )
    output, grad_query, key_part, value_part, token = call(
        part(backward_kernel, head, group),
        [half, half, wide, wide, token_shape],
        [q, k, v, scores, grad, attended, inverse, gain_rows] + prefix,
        5,
        [whole],
    )
    suffix = exclusive_scan(pieces, True, token, gain_part)
    inputs = [k, v, key_part, value_part]
    early, late = [0, 3, 1], [2]

    def buffers(count):
        return [pltpu.VMEM((count, rows, width), HALF)] * 2 + [
            pltpu.SemaphoreType.DMA((2, count))
        ]

    first = call(
        part(final_kernel, head, group, early, False),
        [half, half],
        inputs + [suffix[j] for j in early],
        1,
        buffers(len(early)),
        out_specs={0: HBM, 1: HBM},
    )
    at = len(inputs) + group
    grad_key, grad_value, gain_grad = call(
        part(final_kernel, head, group, late, True),
        [half, half, gain_shape],
        inputs + suffix + list(first),
        1,
        buffers(len(late)),
        ins={at: HBM, at + 1: HBM},
        out_specs={0: HBM, 1: HBM},
        aliases={at: 0, at + 1: 1},
    )
    return (
        output[None],
        grad_query[None],
        grad_key[None],
        grad_value[None],
        gain_grad.reshape(features),
    )


def solution(mesh):
    spec = P("dp", "seq", None)
    return jax.shard_map(
        per_device,
        mesh=mesh,
        in_specs=(spec, spec, spec, P(), spec),
        out_specs=(spec, spec, spec, spec, P()),
        check_vma=False,
    )
```

time: 61.2 us -> 61.5 us (level)
  waiting for transfers between devices: 23 us -> 25.3 us
  local copies, waits for them, and re-layouts: 1.97 us -> 0.02 us
    ppermute x2, waiting for transfers between devices: 1.77 us -> 6.67 us  [shifted(): return lax.ppermute(array, 'seq', pairs)]
    ppermute x16 -> x15, waiting for transfers between devices: 21.2 us -> 18.6 us  [swap(): return lax.ppermute(array, axis, [(i, i ^ offset) for i in range(count)])]
    unnamed x16 -> x10, local copies, waits for them, and re-layouts: 1.97 us -> 0.02 us
    ppermute x16 -> x15, starting transfers between devices: 17.4 us -> 17.7 us  [swap(): return lax.ppermute(array, axis, [(i, i ^ offset) for i in range(count)])]
    pallas_call x9 -> x10, Pallas kernels: 12.7 us -> 12.6 us  [call(): pl.pallas_call(kernel, out_shape=tuple(outs), in_specs=[ins.get(i, VMEM)...]
  transfers between devices with their start and end apart: 18 -> 17, of which waited for: 12 -> 11; matrix products, arithmetic and copies ran while one was open for 0% -> 0% of each run, Pallas kernels for 10% -> 12%
where the time goes in v1:
time: 61.5 us; the launch traced here: 61.3 us
  waiting for transfers between devices  25.3 us (41%)
  starting transfers between devices  22.7 us (37%)
  Pallas kernels  12.6 us (20%)
  between operations  0.74 us (1%)
    ppermute x15, waiting for transfers between devices, swap(): return lax.ppermute(array, axis, [(i, i ^ offset) for i in range(count)])  18.6 us
    ppermute x15, starting transfers between devices, swap(): return lax.ppermute(array, axis, [(i, i ^ offset) for i in range(count)])  17.7 us
    pallas_call x10, Pallas kernels, call(): pl.pallas_call(kernel, out_shape=tuple(outs), in_specs=[ins.get(i, VMEM)...  12.6 us
    ppermute x2, waiting for transfers between devices, shifted(): return lax.ppermute(array, 'seq', pairs)  6.67 us
    ppermute x2, starting transfers between devices, shifted(): return lax.ppermute(array, 'seq', pairs)  4.98 us
  transfers between devices with their start and end apart: 17, of which 11 were waited for; matrix products, arithmetic and copies ran while one was open for 0% of the time, Pallas kernels for 12%

profile of v1, /device:TPU:0, one launch (start us, length us, event | category | flops | bytes accessed | tf_op | source)
XLA Modules:
  0.0 61.3 jit_solution(3087915742029635677)
XLA Ops:
  0.7 1.7 %shard_map.93 = (bf16[512,128]{1,0:T(8,128)(2,1)S(1)}, bf16[512,128]{1,0:T(8,128)(2,1)S(1)}, bf16[512,128]{1,0:T(8,128)(2,1)S(1)}, bf16[512,128]{1,0:T(8,128)(2,1)S(1)}) custom-call(bf16[128,2048]{1,0:T(8,128)(2,1)} %bitcast.10, bf16[128,2048]{1,0:T(8,128)(2,1)} %bitcast.15), custom_call_target="tpu_custom_call" | custom-call | flops 67108864 | bytes 1572864 | tf_op jit(solution)/shard_map/pallas_call | solution.py:273
  2.4 3.0 %collective-permute-start = (bf16[512,128]{1,0:T(8,128)(2,1)S(1)}, bf16[512,128]{1,0:T(8,128)(2,1)S(1)}, u32[]{:S(2)}, u32[]{:S(2)}) collective-permute-start(bf16[512,128]{1,0:T(8,128)(2,1)S(1)} %get-tuple-element.40), channel_id=1, source_target_pairs={{0,1},{1,0},{2,3},{3,2},{4,5},{5,4},{6,7},{7,6},{8,9},{9,8},{10,11... | collective-permute-start | bytes 393224 | tf_op jit(solution)/shard_map/ppermute | solution.py:291
  5.4 1.6 %collective-permute-start.1 = (bf16[512,128]{1,0:T(8,128)(2,1)S(1)}, bf16[512,128]{1,0:T(8,128)(2,1)S(1)}, u32[]{:S(2)}, u32[]{:S(2)}) collective-permute-start(bf16[512,128]{1,0:T(8,128)(2,1)S(1)} %get-tuple-element.41), channel_id=1, source_target_pairs={{0,2},{1,3},{2,0},{3,1},{4,6},{5,7},{6,4},{7,5},{8,10},{9,11},{10,... | collective-permute-start | bytes 393224 | tf_op jit(solution)/shard_map/ppermute | solution.py:291
  7.0 1.9 %collective-permute-done.refs_1_.refs_2_ = bf16[512,128]{1,0:T(8,128)(2,1)S(1)} collective-permute-done((bf16[512,128]{1,0:T(8,128)(2,1)S(1)}, bf16[512,128]{1,0:T(8,128)(2,1)S(1)}, u32[]{:S(2)}, u32[]{:S(2)}) %collective-permute-start) | collective-permute-done | bytes 131104 | tf_op jit(solution)/shard_map/ppermute | solution.py:291
  8.9 2.9 %collective-permute-done.1.refs_2_.refs_3_ = bf16[512,128]{1,0:T(8,128)(2,1)S(1)} collective-permute-done((bf16[512,128]{1,0:T(8,128)(2,1)S(1)}, bf16[512,128]{1,0:T(8,128)(2,1)S(1)}, u32[]{:S(2)}, u32[]{:S(2)}) %collective-permute-start.1) | collective-permute-done | bytes 131104 | tf_op jit(solution)/shard_map/ppermute | solution.py:291
  11.7 1.2 %collective-permute-done.2.refs_3_.refs_4_ = bf16[512,128]{1,0:T(8,128)(2,1)S(1)} collective-permute-done((bf16[512,128]{1,0:T(8,128)(2,1)S(1)}, bf16[512,128]{1,0:T(8,128)(2,1)S(1)}, u32[]{:S(2)}, u32[]{:S(2)}) %collective-permute-start.2) | collective-permute-done | bytes 131104 | tf_op jit(solution)/shard_map/ppermute | solution.py:291
  13.0 2.8 %collective-permute-start.3 = (bf16[512,128]{1,0:T(8,128)(2,1)S(1)}, bf16[512,128]{1,0:T(8,128)(2,1)S(1)}, u32[]{:S(2)}, u32[]{:S(2)}) collective-permute-start(bf16[512,128]{1,0:T(8,128)(2,1)S(1)} %shard_map.94), channel_id=1, source_target_pairs={{0,4},{1,5},{2,6},{3,7},{4,0},{5,1},{6,2},{7,3},{8,12},{9,13},{10,... | collective-permute-start | bytes 393224 | tf_op jit(solution)/shard_map/ppermute | solution.py:312
  15.8 2.6 %shard_map.92 = (bf16[2048,128]{1,0:T(8,128)(2,1)S(1)}, f32[128,2048]{1,0:T(8,128)S(1)}) custom-call(bf16[128,2048]{1,0:T(8,128)(2,1)S(1)} %bitcast.20, bf16[128,2048]{1,0:T(8,128)(2,1)S(1)} %bitcast.11, bf16[128,2048]{1,0:T(8,128)(2,1)S(1)} %bitcast.16), custom_call_target="tpu_custom_call" | custom-call | flops 134217728 | bytes 3145728 | tf_op jit(solution)/shard_map/pallas_call | solution.py:273
  18.4 2.8 %collective-permute-done.3.refs_0_ = bf16[512,128]{1,0:T(8,128)(2,1)S(1)} collective-permute-done((bf16[512,128]{1,0:T(8,128)(2,1)S(1)}, bf16[512,128]{1,0:T(8,128)(2,1)S(1)}, u32[]{:S(2)}, u32[]{:S(2)}) %collective-permute-start.3) | collective-permute-done | bytes 131104 | tf_op jit(solution)/shard_map/ppermute | solution.py:312
  21.5 1.0 %collective-permute-start.4 = (bf16[512,128]{1,0:T(8,128)(2,1)S(1)}, bf16[512,128]{1,0:T(8,128)(2,1)S(1)}, u32[]{:S(2)}, u32[]{:S(2)}) collective-permute-start(bf16[512,128]{1,0:T(8,128)(2,1)S(1)} %get-tuple-element.44), channel_id=1, source_target_pairs={{0,1},{1,0},{2,3},{3,2},{4,5},{5,4},{6,7},{7,6},{8,9},{9,8},{10,11... | collective-permute-start | bytes 393224 | tf_op jit(solution)/shard_map/ppermute | solution.py:291
  22.6 0.7 %collective-permute-start.5 = (bf16[512,128]{1,0:T(8,128)(2,1)S(1)}, bf16[512,128]{1,0:T(8,128)(2,1)S(1)}, u32[]{:S(2)}, u32[]{:S(2)}) collective-permute-start(bf16[512,128]{1,0:T(8,128)(2,1)S(1)} %get-tuple-element.45), channel_id=1, source_target_pairs={{0,2},{1,3},{2,0},{3,1},{4,6},{5,7},{6,4},{7,5},{8,10},{9,11},{10,... | collective-permute-start | bytes 393224 | tf_op jit(solution)/shard_map/ppermute | solution.py:291
  23.2 1.8 %collective-permute-start.6 = (bf16[512,128]{1,0:T(8,128)(2,1)S(1)}, bf16[512,128]{1,0:T(8,128)(2,1)S(1)}, u32[]{:S(2)}, u32[]{:S(2)}) collective-permute-start(bf16[512,128]{1,0:T(8,128)(2,1)S(1)} %get-tuple-element.46), channel_id=1, source_target_pairs={{0,3},{1,2},{2,1},{3,0},{4,7},{5,6},{6,5},{7,4},{8,11},{9,10},{10,... | collective-permute-start | bytes 393224 | tf_op jit(solution)/shard_map/ppermute | solution.py:291
  25.1 2.2 %collective-permute-done.4.refs_5_.refs_9_ = bf16[512,128]{1,0:T(8,128)(2,1)S(1)} collective-permute-done((bf16[512,128]{1,0:T(8,128)(2,1)S(1)}, bf16[512,128]{1,0:T(8,128)(2,1)S(1)}, u32[]{:S(2)}, u32[]{:S(2)}) %collective-permute-start.4) | collective-permute-done | bytes 131104 | tf_op jit(solution)/shard_map/ppermute | solution.py:291
  27.3 0.7 %collective-permute-done.5.refs_6_.refs_10_ = bf16[512,128]{1,0:T(8,128)(2,1)S(1)} collective-permute-done((bf16[512,128]{1,0:T(8,128)(2,1)S(1)}, bf16[512,128]{1,0:T(8,128)(2,1)S(1)}, u32[]{:S(2)}, u32[]{:S(2)}) %collective-permute-start.5) | collective-permute-done | bytes 131104 | tf_op jit(solution)/shard_map/ppermute | solution.py:291
  28.0 2.5 %collective-permute-done.6.refs_7_.refs_11_ = bf16[512,128]{1,0:T(8,128)(2,1)S(1)} collective-permute-done((bf16[512,128]{1,0:T(8,128)(2,1)S(1)}, bf16[512,128]{1,0:T(8,128)(2,1)S(1)}, u32[]{:S(2)}, u32[]{:S(2)}) %collective-permute-start.6) | collective-permute-done | bytes 131104 | tf_op jit(solution)/shard_map/ppermute | solution.py:291
  30.5 1.2 %shard_map.96 = (f32[128,2048]{1,0:T(8,128)S(1)}, f32[128,128]{1,0:T(8,128)S(1)}, bf16[128,2048]{1,0:T(8,128)(2,1)S(1)}, f32[16,128]{1,0:T(8,128)S(1)}, bf16[512...) custom-call(bf16[128,2048]{1,0:T(8,128)(2,1)S(1)} %bitcast.21, ...), custom_call_target="tpu_custom_call" | custom-call | flops 134217728 | bytes 4800512 | tf_op jit(solution)/shard_map/pallas_call | solution.py:273
  31.6 0.5 collective-permute-start.7
  32.1 1.4 %collective-permute-start.8 = (bf16[512,128]{1,0:T(8,128)(2,1)S(1)}, bf16[512,128]{1,0:T(8,128)(2,1)S(1)}, u32[]{:S(2)}, u32[]{:S(2)}) collective-permute-start(bf16[512,128]{1,0:T(8,128)(2,1)S(1)} %get-tuple-element.56), channel_id=1, source_target_pairs={{0,2},{1,3},{2,0},{3,1},{4,6},{5,7},{6,4},{7,5},{8,10},{9,11},{10,... | collective-permute-start | bytes 393224 | tf_op jit(solution)/shard_map/ppermute | solution.py:291
  33.5 1.7 %collective-permute-start.9 = (bf16[512,128]{1,0:T(8,128)(2,1)S(1)}, bf16[512,128]{1,0:T(8,128)(2,1)S(1)}, u32[]{:S(2)}, u32[]{:S(2)}) collective-permute-start(bf16[512,128]{1,0:T(8,128)(2,1)S(1)} %get-tuple-element.57), channel_id=1, source_target_pairs={{0,3},{1,2},{2,1},{3,0},{4,7},{5,6},{6,5},{7,4},{8,11},{9,10},{10,... | collective-permute-start | bytes 393224 | tf_op jit(solution)/shard_map/ppermute | solution.py:291
  35.2 1.5 %collective-permute-start.11 = (f32[16,128]{1,0:T(8,128)S(1)}, f32[16,128]{1,0:T(8,128)S(1)}, u32[]{:S(2)}, u32[]{:S(2)}) collective-permute-start(f32[16,128]{1,0:T(8,128)S(1)} %get-tuple-element.58), channel_id=1, source_target_pairs={{0,16},{8,24},{16,0},{24,8},{1,17},{9,25},{17,1},{25,9},{2,18},{10... | collective-permute-start | bytes 24584 | tf_op jit(solution)/shard_map/ppermute | solution.py:291
  36.7 0.9 %collective-permute-start.12 = (f32[16,128]{1,0:T(8,128)S(1)}, f32[16,128]{1,0:T(8,128)S(1)}, u32[]{:S(2)}, u32[]{:S(2)}) collective-permute-start(f32[16,128]{1,0:T(8,128)S(1)} %get-tuple-element.58), channel_id=1, source_target_pairs={{0,24},{8,16},{16,8},{24,0},{1,25},{9,17},{17,9},{25,1},{2,26},{10... | collective-permute-start | bytes 24584 | tf_op jit(solution)/shard_map/ppermute | solution.py:291
  37.7 1.2 %collective-permute-done.11 = f32[16,128]{1,0:T(8,128)S(1)} collective-permute-done((f32[16,128]{1,0:T(8,128)S(1)}, f32[16,128]{1,0:T(8,128)S(1)}, u32[]{:S(2)}, u32[]{:S(2)}) %collective-permute-start.11) | collective-permute-done | bytes 8224 | tf_op jit(solution)/shard_map/ppermute | solution.py:291
  38.8 1.0 %collective-permute-done.12 = f32[16,128]{1,0:T(8,128)S(1)} collective-permute-done((f32[16,128]{1,0:T(8,128)S(1)}, f32[16,128]{1,0:T(8,128)S(1)}, u32[]{:S(2)}, u32[]{:S(2)}) %collective-permute-start.12) | collective-permute-done | bytes 8224 | tf_op jit(solution)/shard_map/ppermute | solution.py:291
  39.9 2.2 %collective-permute-start.13 = (bf16[544,128]{1,0:T(8,128)(2,1)S(1)}, bf16[544,128]{1,0:T(8,128)(2,1)S(1)}, u32[]{:S(2)}, u32[]{:S(2)}) collective-permute-start(bf16[544,128]{1,0:T(8,128)(2,1)S(1)} %shard_map.98.refs_5_), channel_id=1, source_target_pairs={{0,4},{1,5},{2,6},{3,7},{4,0},{5,1},{6,2},{7,3},{8,12},{9,13},{10,... | collective-permute-start | bytes 417800 | tf_op jit(solution)/shard_map/ppermute | solution.py:312
  42.0 3.6 %shard_map.97 = (bf16[128,2048]{1,0:T(8,128)(2,1)}, bf16[128,2048]{1,0:T(8,128)(2,1)}, f32[128,2048]{1,0:T(8,128)S(1)}, f32[128,2048]{1,0:T(8,128)S(1)}, f32[8,128]{1,0:T(8,128)S(1)}) custom-call(bf16[128,2048]{1,0:T(8,128)(2,1)S(1)} %bitcast.22, bf16[128,2048]{1,0:T(8,128)(2,1)S(1)} %bitcast.12, bf16[128,2048]{1,0:T(8,128)(2,1)S(1)} %bitcast.17, ...), custom_call_target="tpu_custom_call" | custom-call | flops 335544320 | bytes 7417856 | tf_op jit(solution)/shard_map/pallas_call | solution.py:273
  45.6 3.9 %collective-permute-done.13.refs_0_ = bf16[544,128]{1,0:T(8,128)(2,1)S(1)} collective-permute-done((bf16[544,128]{1,0:T(8,128)(2,1)S(1)}, bf16[544,128]{1,0:T(8,128)(2,1)S(1)}, u32[]{:S(2)}, u32[]{:S(2)}) %collective-permute-start.13) | collective-permute-done | bytes 139296 | tf_op jit(solution)/shard_map/ppermute | solution.py:312
  49.8 0.6 %collective-permute-start.14 = (bf16[544,128]{1,0:T(8,128)(2,1)S(1)}, bf16[544,128]{1,0:T(8,128)(2,1)S(1)}, u32[]{:S(2)}, u32[]{:S(2)}) collective-permute-start(bf16[544,128]{1,0:T(8,128)(2,1)S(1)} %get-tuple-element.61), channel_id=1, source_target_pairs={{0,1},{1,0},{2,3},{3,2},{4,5},{5,4},{6,7},{7,6},{8,9},{9,8},{10,11... | collective-permute-start | bytes 417800 | tf_op jit(solution)/shard_map/ppermute | solution.py:291
  50.4 0.7 %collective-permute-start.16 = (bf16[544,128]{1,0:T(8,128)(2,1)S(1)}, bf16[544,128]{1,0:T(8,128)(2,1)S(1)}, u32[]{:S(2)}, u32[]{:S(2)}) collective-permute-start(bf16[544,128]{1,0:T(8,128)(2,1)S(1)} %get-tuple-element.63), channel_id=1, source_target_pairs={{0,3},{1,2},{2,1},{3,0},{4,7},{5,6},{6,5},{7,4},{8,11},{9,10},{10,... | collective-permute-start | bytes 417800 | tf_op jit(solution)/shard_map/ppermute | solution.py:291
  51.1 2.2 %collective-permute-start.15 = (bf16[544,128]{1,0:T(8,128)(2,1)S(1)}, bf16[544,128]{1,0:T(8,128)(2,1)S(1)}, u32[]{:S(2)}, u32[]{:S(2)}) collective-permute-start(bf16[544,128]{1,0:T(8,128)(2,1)S(1)} %get-tuple-element.62), channel_id=1, source_target_pairs={{0,2},{1,3},{2,0},{3,1},{4,6},{5,7},{6,4},{7,5},{8,10},{9,11},{10,... | collective-permute-start | bytes 417800 | tf_op jit(solution)/shard_map/ppermute | solution.py:291
  53.4 5.1 %collective-permute-done.14.refs_6_.refs_5_ = bf16[544,128]{1,0:T(8,128)(2,1)S(1)} collective-permute-done((bf16[544,128]{1,0:T(8,128)(2,1)S(1)}, bf16[544,128]{1,0:T(8,128)(2,1)S(1)}, u32[]{:S(2)}, u32[]{:S(2)}) %collective-permute-start.14) | collective-permute-done | bytes 139296 | tf_op jit(solution)/shard_map/ppermute | solution.py:291
  58.5 1.3 %shard_map.100 = (bf16[128,2048]{1,0:T(8,128)(2,1)}, bf16[128,2048]{1,0:T(8,128)(2,1)}) custom-call(bf16[128,2048]{1,0:T(8,128)(2,1)S(1)} %bitcast.13, bf16[128,2048]{1,0:T(8,128)(2,1)S(1)} %bitcast.18, f32[128,2048]{1,0:T(8,128)S(1)} %get-tuple-element.52.refs_2_, f32[128,2048]{1,0:T(8,128)S(1)} %get-tuple-element.53.refs_3_, ...), custom_call_target="tpu_custom_call" | custom-call | flops 67108864 | bytes 4612096 | tf_op jit(solution)/shard_map/pallas_call | solution.py:273
  59.8 1.6 %shard_map.101 = (bf16[128,2048]{1,0:T(8,128)(2,1)}, bf16[128,2048]{1,0:T(8,128)(2,1)}, f32[16,128]{1,0:T(8,128)}) custom-call(bf16[128,2048]{1,0:T(8,128)(2,1)S(1)} %bitcast.14, bf16[128,2048]{1,0:T(8,128)(2,1)S(1)} %bitcast.19, f32[128,2048]{1,0:T(8,128)S(1)} %get-tuple-element.52.refs_2_, ...), custom_call_target="tpu_custom_call", output_to_operand_aliasing={{0}: (8, {}), {1}: (9, {})} | custom-call | flops 67108864 | bytes 5808128 | tf_op jit(solution)/shard_map/pallas_call | solution.py:273
  (24 shorter events, 0.8 us)
Async XLA Ops:
  0.6 15.2 %copy-start.1 = (bf16[1,128,2048]{2,1,0:T(8,128)(2,1)S(1)}, bf16[1,128,2048]{2,1,0:T(8,128)(2,1)}, u32[]{:S(2)}) copy-start(bf16[1,128,2048]{2,1,0:T(8,128)(2,1)} %param.7) | copy-start | bytes 1572868
  0.6 15.2 %copy-start.2 = (bf16[1,128,2048]{2,1,0:T(8,128)(2,1)S(1)}, bf16[1,128,2048]{2,1,0:T(8,128)(2,1)}, u32[]{:S(2)}) copy-start(bf16[1,128,2048]{2,1,0:T(8,128)(2,1)} %param.5) | copy-start | bytes 1572868
  2.3 13.5 %copy-start = (bf16[1,128,2048]{2,1,0:T(8,128)(2,1)S(1)}, bf16[1,128,2048]{2,1,0:T(8,128)(2,1)}, u32[]{:S(2)}) copy-start(bf16[1,128,2048]{2,1,0:T(8,128)(2,1)} %param.6) | copy-start | bytes 1572868
  2.4 6.5 %collective-permute-start = (bf16[512,128]{1,0:T(8,128)(2,1)S(1)}, bf16[512,128]{1,0:T(8,128)(2,1)S(1)}, u32[]{:S(2)}, u32[]{:S(2)}) collective-permute-start(bf16[512,128]{1,0:T(8,128)(2,1)S(1)} %get-tuple-element.40), channel_id=1, source_target_pairs={{0,1},{1,0},{2,3},{3,2},{4,5},{5,4},{6,7},{7,6},{8,9},{9,8},{10,11... | collective-permute-start | bytes 393224 | tf_op jit(solution)/shard_map/ppermute | solution.py:291
  5.4 6.4 %collective-permute-start.1 = (bf16[512,128]{1,0:T(8,128)(2,1)S(1)}, bf16[512,128]{1,0:T(8,128)(2,1)S(1)}, u32[]{:S(2)}, u32[]{:S(2)}) collective-permute-start(bf16[512,128]{1,0:T(8,128)(2,1)S(1)} %get-tuple-element.41), channel_id=1, source_target_pairs={{0,2},{1,3},{2,0},{3,1},{4,6},{5,7},{6,4},{7,5},{8,10},{9,11},{10,... | collective-permute-start | bytes 393224 | tf_op jit(solution)/shard_map/ppermute | solution.py:291
  7.0 6.0 %collective-permute-start.2 = (bf16[512,128]{1,0:T(8,128)(2,1)S(1)}, bf16[512,128]{1,0:T(8,128)(2,1)S(1)}, u32[]{:S(2)}, u32[]{:S(2)}) collective-permute-start(bf16[512,128]{1,0:T(8,128)(2,1)S(1)} %get-tuple-element.42), channel_id=1, source_target_pairs={{0,3},{1,2},{2,1},{3,0},{4,7},{5,6},{6,5},{7,4},{8,11},{9,10},{10,... | collective-permute-start | bytes 393224 | tf_op jit(solution)/shard_map/ppermute | solution.py:291
  13.0 8.2 %collective-permute-start.3 = (bf16[512,128]{1,0:T(8,128)(2,1)S(1)}, bf16[512,128]{1,0:T(8,128)(2,1)S(1)}, u32[]{:S(2)}, u32[]{:S(2)}) collective-permute-start(bf16[512,128]{1,0:T(8,128)(2,1)S(1)} %shard_map.94), channel_id=1, source_target_pairs={{0,4},{1,5},{2,6},{3,7},{4,0},{5,1},{6,2},{7,3},{8,12},{9,13},{10,... | collective-permute-start | bytes 393224 | tf_op jit(solution)/shard_map/ppermute | solution.py:312
  21.2 9.2 %copy-start.3 = (bf16[1,128,2048]{2,1,0:T(8,128)(2,1)S(1)}, bf16[1,128,2048]{2,1,0:T(8,128)(2,1)}, u32[]{:S(2)}) copy-start(bf16[1,128,2048]{2,1,0:T(8,128)(2,1)} %param.9) | copy-start | bytes 1572868
  21.5 8.9 %copy-start.4 = (f32[2048]{0:T(1024)S(1)}, f32[2048]{0:T(1024)}, u32[]{:S(2)}) copy-start(f32[2048]{0:T(1024)} %param.8) | copy-start | bytes 24580
  21.5 5.8 %collective-permute-start.4 = (bf16[512,128]{1,0:T(8,128)(2,1)S(1)}, bf16[512,128]{1,0:T(8,128)(2,1)S(1)}, u32[]{:S(2)}, u32[]{:S(2)}) collective-permute-start(bf16[512,128]{1,0:T(8,128)(2,1)S(1)} %get-tuple-element.44), channel_id=1, source_target_pairs={{0,1},{1,0},{2,3},{3,2},{4,5},{5,4},{6,7},{7,6},{8,9},{9,8},{10,11... | collective-permute-start | bytes 393224 | tf_op jit(solution)/shard_map/ppermute | solution.py:291
  22.6 5.4 %collective-permute-start.5 = (bf16[512,128]{1,0:T(8,128)(2,1)S(1)}, bf16[512,128]{1,0:T(8,128)(2,1)S(1)}, u32[]{:S(2)}, u32[]{:S(2)}) collective-permute-start(bf16[512,128]{1,0:T(8,128)(2,1)S(1)} %get-tuple-element.45), channel_id=1, source_target_pairs={{0,2},{1,3},{2,0},{3,1},{4,6},{5,7},{6,4},{7,5},{8,10},{9,11},{10,... | collective-permute-start | bytes 393224 | tf_op jit(solution)/shard_map/ppermute | solution.py:291
  23.2 7.2 %collective-permute-start.6 = (bf16[512,128]{1,0:T(8,128)(2,1)S(1)}, bf16[512,128]{1,0:T(8,128)(2,1)S(1)}, u32[]{:S(2)}, u32[]{:S(2)}) collective-permute-start(bf16[512,128]{1,0:T(8,128)(2,1)S(1)} %get-tuple-element.46), channel_id=1, source_target_pairs={{0,3},{1,2},{2,1},{3,0},{4,7},{5,6},{6,5},{7,4},{8,11},{9,10},{10,... | collective-permute-start | bytes 393224 | tf_op jit(solution)/shard_map/ppermute | solution.py:291
  31.6 8.2 %collective-permute-start.7 = (bf16[512,128]{1,0:T(8,128)(2,1)S(1)}, bf16[512,128]{1,0:T(8,128)(2,1)S(1)}, u32[]{:S(2)}, u32[]{:S(2)}) collective-permute-start(bf16[512,128]{1,0:T(8,128)(2,1)S(1)} %get-tuple-element.55), channel_id=1, source_target_pairs={{0,1},{1,0},{2,3},{3,2},{4,5},{5,4},{6,7},{7,6},{8,9},{9,8},{10,11... | collective-permute-start | bytes 393224 | tf_op jit(solution)/shard_map/ppermute | solution.py:291
  32.1 7.7 %collective-permute-start.8 = (bf16[512,128]{1,0:T(8,128)(2,1)S(1)}, bf16[512,128]{1,0:T(8,128)(2,1)S(1)}, u32[]{:S(2)}, u32[]{:S(2)}) collective-permute-start(bf16[512,128]{1,0:T(8,128)(2,1)S(1)} %get-tuple-element.56), channel_id=1, source_target_pairs={{0,2},{1,3},{2,0},{3,1},{4,6},{5,7},{6,4},{7,5},{8,10},{9,11},{10,... | collective-permute-start | bytes 393224 | tf_op jit(solution)/shard_map/ppermute | solution.py:291
  33.5 6.3 %collective-permute-start.9 = (bf16[512,128]{1,0:T(8,128)(2,1)S(1)}, bf16[512,128]{1,0:T(8,128)(2,1)S(1)}, u32[]{:S(2)}, u32[]{:S(2)}) collective-permute-start(bf16[512,128]{1,0:T(8,128)(2,1)S(1)} %get-tuple-element.57), channel_id=1, source_target_pairs={{0,3},{1,2},{2,1},{3,0},{4,7},{5,6},{6,5},{7,4},{8,11},{9,10},{10,... | collective-permute-start | bytes 393224 | tf_op jit(solution)/shard_map/ppermute | solution.py:291
  35.2 1.5 %collective-permute-start.10 = (f32[16,128]{1,0:T(8,128)S(1)}, f32[16,128]{1,0:T(8,128)S(1)}, u32[]{:S(2)}, u32[]{:S(2)}) collective-permute-start(f32[16,128]{1,0:T(8,128)S(1)} %get-tuple-element.58), channel_id=1, source_target_pairs={{0,8},{8,0},{16,24},{24,16},{1,9},{9,1},{17,25},{25,17},{2,10},{10... | collective-permute-start | bytes 24584 | tf_op jit(solution)/shard_map/ppermute | solution.py:291
  35.2 3.7 %collective-permute-start.11 = (f32[16,128]{1,0:T(8,128)S(1)}, f32[16,128]{1,0:T(8,128)S(1)}, u32[]{:S(2)}, u32[]{:S(2)}) collective-permute-start(f32[16,128]{1,0:T(8,128)S(1)} %get-tuple-element.58), channel_id=1, source_target_pairs={{0,16},{8,24},{16,0},{24,8},{1,17},{9,25},{17,1},{25,9},{2,18},{10... | collective-permute-start | bytes 24584 | tf_op jit(solution)/shard_map/ppermute | solution.py:291
  36.7 3.1 %collective-permute-start.12 = (f32[16,128]{1,0:T(8,128)S(1)}, f32[16,128]{1,0:T(8,128)S(1)}, u32[]{:S(2)}, u32[]{:S(2)}) collective-permute-start(f32[16,128]{1,0:T(8,128)S(1)} %get-tuple-element.58), channel_id=1, source_target_pairs={{0,24},{8,16},{16,8},{24,0},{1,25},{9,17},{17,9},{25,1},{2,26},{10... | collective-permute-start | bytes 24584 | tf_op jit(solution)/shard_map/ppermute | solution.py:291
  39.9 9.6 %collective-permute-start.13 = (bf16[544,128]{1,0:T(8,128)(2,1)S(1)}, bf16[544,128]{1,0:T(8,128)(2,1)S(1)}, u32[]{:S(2)}, u32[]{:S(2)}) collective-permute-start(bf16[544,128]{1,0:T(8,128)(2,1)S(1)} %shard_map.98.refs_5_), channel_id=1, source_target_pairs={{0,4},{1,5},{2,6},{3,7},{4,0},{5,1},{6,2},{7,3},{8,12},{9,13},{10,... | collective-permute-start | bytes 417800 | tf_op jit(solution)/shard_map/ppermute | solution.py:312
  49.8 8.7 %collective-permute-start.14 = (bf16[544,128]{1,0:T(8,128)(2,1)S(1)}, bf16[544,128]{1,0:T(8,128)(2,1)S(1)}, u32[]{:S(2)}, u32[]{:S(2)}) collective-permute-start(bf16[544,128]{1,0:T(8,128)(2,1)S(1)} %get-tuple-element.61), channel_id=1, source_target_pairs={{0,1},{1,0},{2,3},{3,2},{4,5},{5,4},{6,7},{7,6},{8,9},{9,8},{10,11... | collective-permute-start | bytes 417800 | tf_op jit(solution)/shard_map/ppermute | solution.py:291
  50.4 8.1 %collective-permute-start.16 = (bf16[544,128]{1,0:T(8,128)(2,1)S(1)}, bf16[544,128]{1,0:T(8,128)(2,1)S(1)}, u32[]{:S(2)}, u32[]{:S(2)}) collective-permute-start(bf16[544,128]{1,0:T(8,128)(2,1)S(1)} %get-tuple-element.63), channel_id=1, source_target_pairs={{0,3},{1,2},{2,1},{3,0},{4,7},{5,6},{6,5},{7,4},{8,11},{9,10},{10,... | collective-permute-start | bytes 417800 | tf_op jit(solution)/shard_map/ppermute | solution.py:291
  51.1 8.6 %collective-permute-start.15 = (bf16[544,128]{1,0:T(8,128)(2,1)S(1)}, bf16[544,128]{1,0:T(8,128)(2,1)S(1)}, u32[]{:S(2)}, u32[]{:S(2)}) collective-permute-start(bf16[544,128]{1,0:T(8,128)(2,1)S(1)} %get-tuple-element.62), channel_id=1, source_target_pairs={{0,2},{1,3},{2,0},{3,1},{4,6},{5,7},{6,4},{7,5},{8,10},{9,11},{10,... | collective-permute-start | bytes 417800 | tf_op jit(solution)/shard_map/ppermute | solution.py:291

commit v2 on v1

--- a/solution.py
+++ b/solution.py
@@ -42,7 +42,7 @@
 
 def scattered(member, whole_ref, size, piece_refs):
     for j, ref in enumerate(piece_refs):
-        ref[...] = whole_ref[block_at(member ^ j, size), :]
+        ref[0:size, :] = whole_ref[block_at(member ^ j, size), :]
 
 
 def columns(first, count):
@@ -81,9 +81,9 @@
 def norm_kernel(head, group, replicas, *refs):
     q_ref, intra_ref, gain_ref, cot_ref = refs[:4]
     prefix_refs = refs[4 : 4 + group]
-    attended_ref, inverse_ref, grad_ref, gain_grad_ref = refs[4 + group : 8 + group]
-    piece_refs = refs[8 + group : 8 + 2 * group]
-    whole_ref = refs[8 + 2 * group]
+    attended_ref, inverse_ref, grad_ref = refs[4 + group : 7 + group]
+    piece_refs = refs[7 + group : 7 + 2 * group]
+    whole_ref, gain_grad_ref = refs[7 + 2 * group :]
     member = member_of(group)
     rows = q_ref.shape[0]
     scaling = head ** (-0.5)
@@ -118,6 +118,8 @@
         grad_ref[:, part] = grad
         whole_ref[part, :] = (scaling * dot(q_ref[:, part], grad, 0, 0)).astype(HALF)
     scattered(member, whole_ref, size, piece_refs)
+    for ref in piece_refs:
+        put_wide_rows(ref, size, gain_grad_ref[...])
 
 
 def backward_kernel(head, group, *refs):
@@ -154,17 +156,22 @@
 
 def final_kernel(head, group, chunks, last, *refs):
     k_ref, v_ref, key_part_ref, value_part_ref = refs[:4]
-    suffix_refs = refs[4 : 4 + (group if last else len(chunks))]
-    refs = refs[4 + len(suffix_refs) + (2 if last else 0) :]
-    out_refs, refs = refs[:2], refs[2:]
+    suffix_refs = refs[4 : 4 + len(chunks)]
+    refs = refs[4 + len(suffix_refs) :]
+    copies = []
     if last:
-        gain_grad_ref, refs = refs[0], refs[1:]
+        gain_grad_ref, total_ref, gain_written = refs[-6], refs[-2], refs[-1]
+        total_ref[...] = tree_sum([ref[...] for ref in refs[2:-8]])
+        copies.append(pltpu.make_async_copy(total_ref, gain_grad_ref, gain_written))
+        copies[0].start()
+        out_refs, refs = refs[-8:-6], refs[-5:-2]
+    else:
+        out_refs, refs = refs[:2], refs[2:]
     key_buffer, value_buffer, written = refs
     member = member_of(group)
     width = key_buffer.shape[2]
-    copies = []
     for n, chunk in enumerate(chunks):
-        suffix_ref = suffix_refs[chunk if last else n]
+        suffix_ref = suffix_refs[n]
         start = (member ^ chunk) * width
         for i in range(width // head):
             part = pl.ds(pl.multiple_of(start + i * head, head), head)
@@ -184,13 +191,14 @@
             )
             copy.start()
             copies.append(copy)
-    if last:
-        terms = [wide_rows(ref, width) for ref in suffix_refs]
-        while len(terms) > 1:
-            terms = [a + b for a, b in zip(terms[::2], terms[1::2])]
-        gain_grad_ref[...] = terms[0]
     for copy in copies:
         copy.wait()
+
+
+def tree_sum(terms):
+    while len(terms) > 1:
+        terms = [a + b for a, b in zip(terms[::2], terms[1::2])]
+    return terms[0]
 
 
 def wide_rows(ref, start):
@@ -206,16 +214,14 @@
     ref[columns(start + rows, rows), :] = (value - high.astype(F32)).astype(HALF)
 
 
-def total_kernel(group, *refs):
-    total = refs[0][...].astype(F32)
-    for ref in refs[1:group]:
-        total += ref[...].astype(F32)
+def total_kernel(size, *refs):
     out_ref = refs[-1]
-    size = total.shape[0]
+    total = refs[0][0:size, :].astype(F32)
+    for ref in refs[1:-1]:
+        total += ref[0:size, :].astype(F32)
     out_ref[0:size, :] = total.astype(HALF)
-    gains = [ref[...] for ref in refs[group:-1]]
-    if gains:
-        put_wide_rows(out_ref, size, functools.reduce(jnp.add, gains))
+    if out_ref.shape[0] > size:
+        put_wide_rows(out_ref, size, tree_sum([wide_rows(ref, size) for ref in refs[:-1]]))
 
 
 def group_flag(group, reverse, distance):
@@ -233,14 +239,13 @@
     out_ref[...] = (own + moved).astype(HALF)
 
 
-def scan_kernel(group, reverse, masked, extra, *refs):
+def scan_kernel(group, reverse, masked, size, riding, *refs):
     member = member_of(group)
-    size = refs[1].shape[0]
     carry = refs[0][0:size, :].astype(F32)
     if masked:
         carry = carry * group_flag(group, reverse, 1)
-    blocks = [ref[...].astype(F32) for ref in refs[1 : 1 + group]]
-    out_refs = refs[-group:]
+    blocks = [ref[0:size, :].astype(F32) for ref in refs[1 : 1 + group]]
+    out_refs = refs[-group - riding :][:group]
     for j in range(group):
         total = carry
         for i in range(group):
@@ -248,16 +253,9 @@
                 earlier = (member ^ i) < (member ^ j)
                 keep = jnp.where(earlier != reverse, 1.0, 0.0)
                 total += keep * blocks[i]
-        out_refs[j][0:size, :] = total.astype(HALF)
-    if extra == "message":
-        total = wide_rows(refs[0], size) + wide_rows(refs[1 + group], size)
-    elif extra:
-        total = functools.reduce(
-            jnp.add, [ref[...] for ref in refs[1 + group : 1 + group + extra]]
-        )
-    if extra:
-        for ref in out_refs:
-            put_wide_rows(ref, size, total)
+        out_refs[j][...] = total.astype(HALF)
+    if riding:
+        refs[-1][...] = wide_rows(refs[0], size) + wide_rows(refs[1 + group], size)
 
 
 VMEM = pl.BlockSpec(memory_space=pltpu.VMEM)
@@ -297,14 +295,15 @@
     return [pieces[0]] + [moved[j] for j in range(1, len(pieces))]
 
 
-def exclusive_scan(pieces, reverse, token, gain_part=None):
+def exclusive_scan(pieces, size, reverse, token):
     group = len(pieces)
     count = lax.axis_size("seq")
     groups = count // group
     part = functools.partial
-
-    def shaped(more=0):
-        return jax.ShapeDtypeStruct((pieces[0].shape[0] + more, pieces[0].shape[1]), HALF)
+    lanes = pieces[0].shape[1]
+    extra = pieces[0].shape[0] - size
+    piece = jax.ShapeDtypeStruct((size, lanes), HALF)
+    gain_shape = jax.ShapeDtypeStruct((extra // 2, lanes), F32)
 
     def shifted(array, distance):
         step = -distance if reverse else distance
@@ -312,16 +311,18 @@
         return lax.ppermute(array, "seq", pairs)
 
     received = own_and_swapped(pieces)
-    gains, rows = [], 0
-    if gain_part is not None:
-        gains = summed_over("dp", 1, gain_part)
-        rows = 2 * gain_part.shape[0]
-        if groups != 2:
-            gains = summed_over("seq", group, functools.reduce(jnp.add, gains))
-    riding = gains if groups == 2 else []
     (total,) = call(
-        part(total_kernel, group), [shaped(rows if riding else 0)], received + riding, 0
-    )
+        part(total_kernel, size),
+        [jax.ShapeDtypeStruct(pieces[0].shape, HALF)],
+        received,
+        0,
+    )
+    riding = int(extra > 0 and groups == 2)
+    gain = None
+    if extra and not riding:
+        gain = total[size : size + extra // 2].astype(F32) + total[size + extra // 2 :]
+        gain = tree_sum(summed_over("seq", group, gain))
+        total = total[:size]
     carry = shifted(total, group)
     distance = 1
     while distance < groups - 1:
@@ -329,31 +330,27 @@
         kernel = part(
             carry_kernel, group, reverse, distance + (distance == 1), distance == 1
         )
-        (carry,) = call(kernel, [shaped()], [carry, moved], 0)
+        (carry,) = call(kernel, [piece], [carry, moved], 0)
         distance *= 2
-    more, extra = [], 0
-    if gains:
-        more, extra = ([total], "message") if riding else (gains, len(gains))
-    inputs = [carry] + received + more + [token]
+    inputs = [carry] + received + ([total] if riding else []) + [token]
     sums = call(
-        part(scan_kernel, group, reverse, groups <= 2, extra),
-        [shaped(rows)] * group,
+        part(scan_kernel, group, reverse, groups <= 2, size, riding),
+        [piece] * group + [gain_shape] * riding,
         inputs,
         0,
         ins={len(inputs) - 1: ANY},
     )
-    return own_and_swapped(sums)
+    results = own_and_swapped(sums[:group])
+    return results, (sums[-1] if riding else gain)
 
 
 def summed_over(axis, stride, array):
     count = lax.axis_size(axis)
     terms = [array]
     while stride < count:
-        array = functools.reduce(jnp.add, terms)
+        array = tree_sum(terms)
         width = 4 if count // stride % 4 == 0 else 2
         terms = [array] + [swap(array, axis, i * stride) for i in range(1, width)]
-        if width == 4:
-            terms = [terms[0] + terms[1], terms[2] + terms[3]]
         stride *= width
     return terms
 
@@ -386,13 +383,14 @@
         ins={0: HBM, 1: HBM},
     )
     scores, intra = call(part(local_kernel, head), [scores_shape, wide], [q, k, v], 2)
-    prefix = exclusive_scan(pieces, False, intra)
-    attended, inverse, grad, gain_part, *pieces = call(
+    prefix, _ = exclusive_scan(pieces, width, False, intra)
+    message = jax.ShapeDtypeStruct((width + 2 * HEADS, head), HALF)
+    attended, inverse, grad, *pieces = call(
         part(norm_kernel, head, group, lax.axis_size("dp")),
-        [wide, square, half, gain_shape] + [piece] * group,
+        [wide, square, half] + [message] * group,
         [q, intra, gain_rows, cot] + prefix,
         2,
-        [whole],
+        [whole, pltpu.VMEM((HEADS, head), F32)],
     )
     output, grad_query, key_part, value_part, token = call(
         part(backward_kernel, head, group),
@@ -401,7 +399,8 @@
         5,
         [whole],
     )
-    suffix = exclusive_scan(pieces, True, token, gain_part)
+    suffix, gain_grad = exclusive_scan(pieces, width, True, token)
+    gains = summed_over("dp", 1, gain_grad)
     inputs = [k, v, key_part, value_part]
     early, late = [0, 3, 1], [2]
 
@@ -418,15 +417,16 @@
         buffers(len(early)),
         out_specs={0: HBM, 1: HBM},
     )
-    at = len(inputs) + group
+    at = len(inputs) + len(late)
     grad_key, grad_value, gain_grad = call(
         part(final_kernel, head, group, late, True),
         [half, half, gain_shape],
-        inputs + suffix + list(first),
+        inputs + [suffix[j] for j in late] + list(first) + gains,
         1,
-        buffers(len(late)),
+        buffers(len(late))
+        + [pltpu.VMEM((HEADS, head), F32), pltpu.SemaphoreType.DMA(())],
         ins={at: HBM, at + 1: HBM},
-        out_specs={0: HBM, 1: HBM},
+        out_specs={0: HBM, 1: HBM, 2: HBM},
         aliases={at: 0, at + 1: 1},
     )
     return (

time: 61.5 us -> 57.8 us (0.940)
  waiting for transfers between devices: 25.3 us -> 22.4 us
    ppermute x2, waiting for transfers between devices: 6.67 us -> 3.77 us  [shifted(): return lax.ppermute(array, 'seq', pairs)]
    ppermute x15, starting transfers between devices: 17.7 us -> 16.8 us  [swap(): return lax.ppermute(array, axis, [(i, i ^ offset) for i in range(count)])]
    ppermute x2, starting transfers between devices: 4.98 us -> 5.71 us  [shifted(): return lax.ppermute(array, 'seq', pairs)]
  transfers between devices with their start and end apart: 17 -> 17, of which waited for: 11 -> 13; matrix products, arithmetic and copies ran while one was open for 0% -> 0% of each run, Pallas kernels for 12% -> 13%
where the time goes in v2:
time: 57.8 us; the launch traced here: 57.6 us
  starting transfers between devices  22.5 us (39%)
  waiting for transfers between devices  22.4 us (39%)
  Pallas kernels  12 us (21%)
  between operations  0.73 us (1%)
    ppermute x15, waiting for transfers between devices, swap(): return lax.ppermute(array, axis, [(i, i ^ offset) for i in range(count)])  18.6 us
    ppermute x15, starting transfers between devices, swap(): return lax.ppermute(array, axis, [(i, i ^ offset) for i in range(count)])  16.8 us
    pallas_call x10, Pallas kernels, call(): pl.pallas_call(kernel, out_shape=tuple(outs), in_specs=[ins.get(i, VMEM)...  12 us
    ppermute x2, starting transfers between devices, shifted(): return lax.ppermute(array, 'seq', pairs)  5.71 us
    ppermute x2, waiting for transfers between devices, shifted(): return lax.ppermute(array, 'seq', pairs)  3.77 us
  transfers between devices with their start and end apart: 17, of which 13 were waited for; matrix products, arithmetic and copies ran while one was open for 0% of the time, Pallas kernels for 13%

profile of v2, /device:TPU:0, one launch (start us, length us, event | category | flops | bytes accessed | tf_op | source)
XLA Modules:
  0.0 57.6 jit_solution(47418446994091839)
XLA Ops:
  0.7 1.7 %shard_map.93 = (bf16[512,128]{1,0:T(8,128)(2,1)S(1)}, bf16[512,128]{1,0:T(8,128)(2,1)S(1)}, bf16[512,128]{1,0:T(8,128)(2,1)S(1)}, bf16[512,128]{1,0:T(8,128)(2,1)S(1)}) custom-call(bf16[128,2048]{1,0:T(8,128)(2,1)} %bitcast.10, bf16[128,2048]{1,0:T(8,128)(2,1)} %bitcast.15), custom_call_target="tpu_custom_call" | custom-call | flops 67108864 | bytes 1572864 | tf_op jit(solution)/shard_map/pallas_call | solution.py:271
  2.4 3.0 %collective-permute-start = (bf16[512,128]{1,0:T(8,128)(2,1)S(1)}, bf16[512,128]{1,0:T(8,128)(2,1)S(1)}, u32[]{:S(2)}, u32[]{:S(2)}) collective-permute-start(bf16[512,128]{1,0:T(8,128)(2,1)S(1)} %get-tuple-element.40), channel_id=1, source_target_pairs={{0,1},{1,0},{2,3},{3,2},{4,5},{5,4},{6,7},{7,6},{8,9},{9,8},{10,11... | collective-permute-start | bytes 393224 | tf_op jit(solution)/shard_map/ppermute | solution.py:289
  5.4 1.6 %collective-permute-start.1 = (bf16[512,128]{1,0:T(8,128)(2,1)S(1)}, bf16[512,128]{1,0:T(8,128)(2,1)S(1)}, u32[]{:S(2)}, u32[]{:S(2)}) collective-permute-start(bf16[512,128]{1,0:T(8,128)(2,1)S(1)} %get-tuple-element.41), channel_id=1, source_target_pairs={{0,2},{1,3},{2,0},{3,1},{4,6},{5,7},{6,4},{7,5},{8,10},{9,11},{10,... | collective-permute-start | bytes 393224 | tf_op jit(solution)/shard_map/ppermute | solution.py:289
  7.0 1.9 %collective-permute-done.refs_1_.refs_2_ = bf16[512,128]{1,0:T(8,128)(2,1)S(1)} collective-permute-done((bf16[512,128]{1,0:T(8,128)(2,1)S(1)}, bf16[512,128]{1,0:T(8,128)(2,1)S(1)}, u32[]{:S(2)}, u32[]{:S(2)}) %collective-permute-start) | collective-permute-done | bytes 131104 | tf_op jit(solution)/shard_map/ppermute | solution.py:289
  8.9 2.9 %collective-permute-done.1.refs_2_.refs_3_ = bf16[512,128]{1,0:T(8,128)(2,1)S(1)} collective-permute-done((bf16[512,128]{1,0:T(8,128)(2,1)S(1)}, bf16[512,128]{1,0:T(8,128)(2,1)S(1)}, u32[]{:S(2)}, u32[]{:S(2)}) %collective-permute-start.1) | collective-permute-done | bytes 131104 | tf_op jit(solution)/shard_map/ppermute | solution.py:289
  11.7 1.2 %collective-permute-done.2.refs_3_.refs_4_ = bf16[512,128]{1,0:T(8,128)(2,1)S(1)} collective-permute-done((bf16[512,128]{1,0:T(8,128)(2,1)S(1)}, bf16[512,128]{1,0:T(8,128)(2,1)S(1)}, u32[]{:S(2)}, u32[]{:S(2)}) %collective-permute-start.2) | collective-permute-done | bytes 131104 | tf_op jit(solution)/shard_map/ppermute | solution.py:289
  13.0 2.8 %collective-permute-start.3 = (bf16[512,128]{1,0:T(8,128)(2,1)S(1)}, bf16[512,128]{1,0:T(8,128)(2,1)S(1)}, u32[]{:S(2)}, u32[]{:S(2)}) collective-permute-start(bf16[512,128]{1,0:T(8,128)(2,1)S(1)} %shard_map.94), channel_id=1, source_target_pairs={{0,4},{1,5},{2,6},{3,7},{4,0},{5,1},{6,2},{7,3},{8,12},{9,13},{10,... | collective-permute-start | bytes 393224 | tf_op jit(solution)/shard_map/ppermute | solution.py:311
  15.8 2.6 %shard_map.92 = (bf16[2048,128]{1,0:T(8,128)(2,1)S(1)}, f32[128,2048]{1,0:T(8,128)S(1)}) custom-call(bf16[128,2048]{1,0:T(8,128)(2,1)S(1)} %bitcast.20, bf16[128,2048]{1,0:T(8,128)(2,1)S(1)} %bitcast.11, bf16[128,2048]{1,0:T(8,128)(2,1)S(1)} %bitcast.16), custom_call_target="tpu_custom_call" | custom-call | flops 134217728 | bytes 3145728 | tf_op jit(solution)/shard_map/pallas_call | solution.py:271
  18.4 2.8 %collective-permute-done.3.refs_0_ = bf16[512,128]{1,0:T(8,128)(2,1)S(1)} collective-permute-done((bf16[512,128]{1,0:T(8,128)(2,1)S(1)}, bf16[512,128]{1,0:T(8,128)(2,1)S(1)}, u32[]{:S(2)}, u32[]{:S(2)}) %collective-permute-start.3) | collective-permute-done | bytes 131104 | tf_op jit(solution)/shard_map/ppermute | solution.py:311
  21.5 1.0 %collective-permute-start.4 = (bf16[512,128]{1,0:T(8,128)(2,1)S(1)}, bf16[512,128]{1,0:T(8,128)(2,1)S(1)}, u32[]{:S(2)}, u32[]{:S(2)}) collective-permute-start(bf16[512,128]{1,0:T(8,128)(2,1)S(1)} %get-tuple-element.44), channel_id=1, source_target_pairs={{0,1},{1,0},{2,3},{3,2},{4,5},{5,4},{6,7},{7,6},{8,9},{9,8},{10,11... | collective-permute-start | bytes 393224 | tf_op jit(solution)/shard_map/ppermute | solution.py:289
  22.6 0.7 %collective-permute-start.5 = (bf16[512,128]{1,0:T(8,128)(2,1)S(1)}, bf16[512,128]{1,0:T(8,128)(2,1)S(1)}, u32[]{:S(2)}, u32[]{:S(2)}) collective-permute-start(bf16[512,128]{1,0:T(8,128)(2,1)S(1)} %get-tuple-element.45), channel_id=1, source_target_pairs={{0,2},{1,3},{2,0},{3,1},{4,6},{5,7},{6,4},{7,5},{8,10},{9,11},{10,... | collective-permute-start | bytes 393224 | tf_op jit(solution)/shard_map/ppermute | solution.py:289
  23.2 1.8 %collective-permute-start.6 = (bf16[512,128]{1,0:T(8,128)(2,1)S(1)}, bf16[512,128]{1,0:T(8,128)(2,1)S(1)}, u32[]{:S(2)}, u32[]{:S(2)}) collective-permute-start(bf16[512,128]{1,0:T(8,128)(2,1)S(1)} %get-tuple-element.46), channel_id=1, source_target_pairs={{0,3},{1,2},{2,1},{3,0},{4,7},{5,6},{6,5},{7,4},{8,11},{9,10},{10,... | collective-permute-start | bytes 393224 | tf_op jit(solution)/shard_map/ppermute | solution.py:289
  25.1 2.2 %collective-permute-done.4.refs_5_.refs_9_ = bf16[512,128]{1,0:T(8,128)(2,1)S(1)} collective-permute-done((bf16[512,128]{1,0:T(8,128)(2,1)S(1)}, bf16[512,128]{1,0:T(8,128)(2,1)S(1)}, u32[]{:S(2)}, u32[]{:S(2)}) %collective-permute-start.4) | collective-permute-done | bytes 131104 | tf_op jit(solution)/shard_map/ppermute | solution.py:289
  27.3 0.7 %collective-permute-done.5.refs_6_.refs_10_ = bf16[512,128]{1,0:T(8,128)(2,1)S(1)} collective-permute-done((bf16[512,128]{1,0:T(8,128)(2,1)S(1)}, bf16[512,128]{1,0:T(8,128)(2,1)S(1)}, u32[]{:S(2)}, u32[]{:S(2)}) %collective-permute-start.5) | collective-permute-done | bytes 131104 | tf_op jit(solution)/shard_map/ppermute | solution.py:289
  28.0 2.5 %collective-permute-done.6.refs_7_.refs_11_ = bf16[512,128]{1,0:T(8,128)(2,1)S(1)} collective-permute-done((bf16[512,128]{1,0:T(8,128)(2,1)S(1)}, bf16[512,128]{1,0:T(8,128)(2,1)S(1)}, u32[]{:S(2)}, u32[]{:S(2)}) %collective-permute-start.6) | collective-permute-done | bytes 131104 | tf_op jit(solution)/shard_map/ppermute | solution.py:289
  30.5 1.2 %shard_map.96 = (f32[128,2048]{1,0:T(8,128)S(1)}, f32[128,128]{1,0:T(8,128)S(1)}, bf16[128,2048]{1,0:T(8,128)(2,1)S(1)}, bf16[544,128]{1,0:T(8,128)(2,1)S(1)}, b...) custom-call(bf16[128,2048]{1,0:T(8,128)(2,1)S(1)} %bitcast.21, ...), custom_call_target="tpu_custom_call" | custom-call | flops 134217728 | bytes 4825088 | tf_op jit(solution)/shard_map/pallas_call | solution.py:271
  31.7 0.5 collective-permute-start.7
  32.1 1.4 %collective-permute-start.8 = (bf16[544,128]{1,0:T(8,128)(2,1)S(1)}, bf16[544,128]{1,0:T(8,128)(2,1)S(1)}, u32[]{:S(2)}, u32[]{:S(2)}) collective-permute-start(bf16[544,128]{1,0:T(8,128)(2,1)S(1)} %get-tuple-element.56), channel_id=1, source_target_pairs={{0,2},{1,3},{2,0},{3,1},{4,6},{5,7},{6,4},{7,5},{8,10},{9,11},{10,... | collective-permute-start | bytes 417800 | tf_op jit(solution)/shard_map/ppermute | solution.py:289
  33.5 1.7 %collective-permute-start.9 = (bf16[544,128]{1,0:T(8,128)(2,1)S(1)}, bf16[544,128]{1,0:T(8,128)(2,1)S(1)}, u32[]{:S(2)}, u32[]{:S(2)}) collective-permute-start(bf16[544,128]{1,0:T(8,128)(2,1)S(1)} %get-tuple-element.57), channel_id=1, source_target_pairs={{0,3},{1,2},{2,1},{3,0},{4,7},{5,6},{6,5},{7,4},{8,11},{9,10},{10,... | collective-permute-start | bytes 417800 | tf_op jit(solution)/shard_map/ppermute | solution.py:289
  35.2 2.7 %collective-permute-done.7.refs_1_.refs_2_ = bf16[544,128]{1,0:T(8,128)(2,1)S(1)} collective-permute-done((bf16[544,128]{1,0:T(8,128)(2,1)S(1)}, bf16[544,128]{1,0:T(8,128)(2,1)S(1)}, u32[]{:S(2)}, u32[]{:S(2)}) %collective-permute-start.7) | collective-permute-done | bytes 139296 | tf_op jit(solution)/shard_map/ppermute | solution.py:289
  37.9 1.8 %collective-permute-done.9.refs_3_.refs_4_ = bf16[544,128]{1,0:T(8,128)(2,1)S(1)} collective-permute-done((bf16[544,128]{1,0:T(8,128)(2,1)S(1)}, bf16[544,128]{1,0:T(8,128)(2,1)S(1)}, u32[]{:S(2)}, u32[]{:S(2)}) %collective-permute-start.9) | collective-permute-done | bytes 139296 | tf_op jit(solution)/shard_map/ppermute | solution.py:289
  39.8 2.9 %collective-permute-start.10 = (bf16[544,128]{1,0:T(8,128)(2,1)S(1)}, bf16[544,128]{1,0:T(8,128)(2,1)S(1)}, u32[]{:S(2)}, u32[]{:S(2)}) collective-permute-start(bf16[544,128]{1,0:T(8,128)(2,1)S(1)} %shard_map.98.refs_5_), channel_id=1, source_target_pairs={{0,4},{1,5},{2,6},{3,7},{4,0},{5,1},{6,2},{7,3},{8,12},{9,13},{10,... | collective-permute-start | bytes 417800 | tf_op jit(solution)/shard_map/ppermute | solution.py:311
  42.7 3.6 %shard_map.97 = (bf16[128,2048]{1,0:T(8,128)(2,1)}, bf16[128,2048]{1,0:T(8,128)(2,1)}, f32[128,2048]{1,0:T(8,128)S(1)}, f32[128,2048]{1,0:T(8,128)S(1)}, f32[8,128]{1,0:T(8,128)S(1)}) custom-call(bf16[128,2048]{1,0:T(8,128)(2,1)S(1)} %bitcast.22, bf16[128,2048]{1,0:T(8,128)(2,1)S(1)} %bitcast.12, bf16[128,2048]{1,0:T(8,128)(2,1)S(1)} %bitcast.17, ...), custom_call_target="tpu_custom_call" | custom-call | flops 335544320 | bytes 7417856 | tf_op jit(solution)/shard_map/pallas_call | solution.py:271
  46.2 1.0 %collective-permute-done.10.refs_0_ = bf16[544,128]{1,0:T(8,128)(2,1)S(1)} collective-permute-done((bf16[544,128]{1,0:T(8,128)(2,1)S(1)}, bf16[544,128]{1,0:T(8,128)(2,1)S(1)}, u32[]{:S(2)}, u32[]{:S(2)}) %collective-permute-start.10) | collective-permute-done | bytes 139296 | tf_op jit(solution)/shard_map/ppermute | solution.py:311
  47.7 1.2 %collective-permute-start.13 = (bf16[512,128]{1,0:T(8,128)(2,1)S(1)}, bf16[512,128]{1,0:T(8,128)(2,1)S(1)}, u32[]{:S(2)}, u32[]{:S(2)}) collective-permute-start(bf16[512,128]{1,0:T(8,128)(2,1)S(1)} %get-tuple-element.62), channel_id=1, source_target_pairs={{0,1},{1,0},{2,3},{3,2},{4,5},{5,4},{6,7},{7,6},{8,9},{9,8},{10,11... | collective-permute-start | bytes 393224 | tf_op jit(solution)/shard_map/ppermute | solution.py:289
  48.9 2.1 %collective-permute-start.11 = (bf16[512,128]{1,0:T(8,128)(2,1)S(1)}, bf16[512,128]{1,0:T(8,128)(2,1)S(1)}, u32[]{:S(2)}, u32[]{:S(2)}) collective-permute-start(bf16[512,128]{1,0:T(8,128)(2,1)S(1)} %get-tuple-element.59), channel_id=1, source_target_pairs={{0,2},{1,3},{2,0},{3,1},{4,6},{5,7},{6,4},{7,5},{8,10},{9,11},{10,... | collective-permute-start | bytes 393224 | tf_op jit(solution)/shard_map/ppermute | solution.py:289
  51.1 1.5 %collective-permute-start.15 = (f32[16,128]{1,0:T(8,128)S(1)}, f32[16,128]{1,0:T(8,128)S(1)}, u32[]{:S(2)}, u32[]{:S(2)}) collective-permute-start(f32[16,128]{1,0:T(8,128)S(1)} %get-tuple-element.65.refs_7_), channel_id=1, source_target_pairs={{0,16},{8,24},{16,0},{24,8},{1,17},{9,25},{17,1},{25,9},{2,18},{10... | collective-permute-start | bytes 24584 | tf_op jit(solution)/shard_map/ppermute | solution.py:289
  52.6 1.0 %collective-permute-done.12.refs_5_ = bf16[512,128]{1,0:T(8,128)(2,1)S(1)} collective-permute-done((bf16[512,128]{1,0:T(8,128)(2,1)S(1)}, bf16[512,128]{1,0:T(8,128)(2,1)S(1)}, u32[]{:S(2)}, u32[]{:S(2)}) %collective-permute-start.12) | collective-permute-done | bytes 131104 | tf_op jit(solution)/shard_map/ppermute | solution.py:289
  53.6 0.5 collective-permute-done.13.refs_6_
  54.1 1.3 %shard_map.100 = (bf16[128,2048]{1,0:T(8,128)(2,1)}, bf16[128,2048]{1,0:T(8,128)(2,1)}) custom-call(bf16[128,2048]{1,0:T(8,128)(2,1)S(1)} %bitcast.13, bf16[128,2048]{1,0:T(8,128)(2,1)S(1)} %bitcast.18, f32[128,2048]{1,0:T(8,128)S(1)} %get-tuple-element.52.refs_2_, f32[128,2048]{1,0:T(8,128)S(1)} %get-tuple-element.53.refs_3_, ...), custom_call_target="tpu_custom_call" | custom-call | flops 67108864 | bytes 4587520 | tf_op jit(solution)/shard_map/pallas_call | solution.py:271
  55.4 1.3 %collective-permute-done.16.refs_10_ = f32[16,128]{1,0:T(8,128)S(1)} collective-permute-done((f32[16,128]{1,0:T(8,128)S(1)}, f32[16,128]{1,0:T(8,128)S(1)}, u32[]{:S(2)}, u32[]{:S(2)}) %collective-permute-start.16) | collective-permute-done | bytes 8224 | tf_op jit(solution)/shard_map/ppermute | solution.py:289
  56.7 1.0 %shard_map.101 = (bf16[128,2048]{1,0:T(8,128)(2,1)}, bf16[128,2048]{1,0:T(8,128)(2,1)}, f32[16,128]{1,0:T(8,128)}) custom-call(bf16[128,2048]{1,0:T(8,128)(2,1)S(1)} %bitcast.14, bf16[128,2048]{1,0:T(8,128)(2,1)S(1)} %bitcast.19, f32[128,2048]{1,0:T(8,128)S(1)} %get-tuple-element.52.refs_2_, ...), custom_call_target="tpu_custom_call", output_to_operand_aliasing={{0}: (5, {}), {1}: (6, {})} | custom-call | flops 67108864 | bytes 5414912 | tf_op jit(solution)/shard_map/pallas_call | solution.py:271
  (22 shorter events, 1.0 us)
Async XLA Ops:
  0.6 15.2 %copy-start.1 = (bf16[1,128,2048]{2,1,0:T(8,128)(2,1)S(1)}, bf16[1,128,2048]{2,1,0:T(8,128)(2,1)}, u32[]{:S(2)}) copy-start(bf16[1,128,2048]{2,1,0:T(8,128)(2,1)} %param.7) | copy-start | bytes 1572868
  0.6 15.2 %copy-start.2 = (bf16[1,128,2048]{2,1,0:T(8,128)(2,1)S(1)}, bf16[1,128,2048]{2,1,0:T(8,128)(2,1)}, u32[]{:S(2)}) copy-start(bf16[1,128,2048]{2,1,0:T(8,128)(2,1)} %param.5) | copy-start | bytes 1572868
  2.3 13.5 %copy-start = (bf16[1,128,2048]{2,1,0:T(8,128)(2,1)S(1)}, bf16[1,128,2048]{2,1,0:T(8,128)(2,1)}, u32[]{:S(2)}) copy-start(bf16[1,128,2048]{2,1,0:T(8,128)(2,1)} %param.6) | copy-start | bytes 1572868
  2.4 6.5 %collective-permute-start = (bf16[512,128]{1,0:T(8,128)(2,1)S(1)}, bf16[512,128]{1,0:T(8,128)(2,1)S(1)}, u32[]{:S(2)}, u32[]{:S(2)}) collective-permute-start(bf16[512,128]{1,0:T(8,128)(2,1)S(1)} %get-tuple-element.40), channel_id=1, source_target_pairs={{0,1},{1,0},{2,3},{3,2},{4,5},{5,4},{6,7},{7,6},{8,9},{9,8},{10,11... | collective-permute-start | bytes 393224 | tf_op jit(solution)/shard_map/ppermute | solution.py:289
  5.4 6.4 %collective-permute-start.1 = (bf16[512,128]{1,0:T(8,128)(2,1)S(1)}, bf16[512,128]{1,0:T(8,128)(2,1)S(1)}, u32[]{:S(2)}, u32[]{:S(2)}) collective-permute-start(bf16[512,128]{1,0:T(8,128)(2,1)S(1)} %get-tuple-element.41), channel_id=1, source_target_pairs={{0,2},{1,3},{2,0},{3,1},{4,6},{5,7},{6,4},{7,5},{8,10},{9,11},{10,... | collective-permute-start | bytes 393224 | tf_op jit(solution)/shard_map/ppermute | solution.py:289
  7.0 6.0 %collective-permute-start.2 = (bf16[512,128]{1,0:T(8,128)(2,1)S(1)}, bf16[512,128]{1,0:T(8,128)(2,1)S(1)}, u32[]{:S(2)}, u32[]{:S(2)}) collective-permute-start(bf16[512,128]{1,0:T(8,128)(2,1)S(1)} %get-tuple-element.42), channel_id=1, source_target_pairs={{0,3},{1,2},{2,1},{3,0},{4,7},{5,6},{6,5},{7,4},{8,11},{9,10},{10,... | collective-permute-start | bytes 393224 | tf_op jit(solution)/shard_map/ppermute | solution.py:289
  13.0 8.2 %collective-permute-start.3 = (bf16[512,128]{1,0:T(8,128)(2,1)S(1)}, bf16[512,128]{1,0:T(8,128)(2,1)S(1)}, u32[]{:S(2)}, u32[]{:S(2)}) collective-permute-start(bf16[512,128]{1,0:T(8,128)(2,1)S(1)} %shard_map.94), channel_id=1, source_target_pairs={{0,4},{1,5},{2,6},{3,7},{4,0},{5,1},{6,2},{7,3},{8,12},{9,13},{10,... | collective-permute-start | bytes 393224 | tf_op jit(solution)/shard_map/ppermute | solution.py:311
  21.2 9.2 %copy-start.3 = (bf16[1,128,2048]{2,1,0:T(8,128)(2,1)S(1)}, bf16[1,128,2048]{2,1,0:T(8,128)(2,1)}, u32[]{:S(2)}) copy-start(bf16[1,128,2048]{2,1,0:T(8,128)(2,1)} %param.9) | copy-start | bytes 1572868
  21.5 8.9 %copy-start.4 = (f32[2048]{0:T(1024)S(1)}, f32[2048]{0:T(1024)}, u32[]{:S(2)}) copy-start(f32[2048]{0:T(1024)} %param.8) | copy-start | bytes 24580
  21.5 5.8 %collective-permute-start.4 = (bf16[512,128]{1,0:T(8,128)(2,1)S(1)}, bf16[512,128]{1,0:T(8,128)(2,1)S(1)}, u32[]{:S(2)}, u32[]{:S(2)}) collective-permute-start(bf16[512,128]{1,0:T(8,128)(2,1)S(1)} %get-tuple-element.44), channel_id=1, source_target_pairs={{0,1},{1,0},{2,3},{3,2},{4,5},{5,4},{6,7},{7,6},{8,9},{9,8},{10,11... | collective-permute-start | bytes 393224 | tf_op jit(solution)/shard_map/ppermute | solution.py:289
  22.6 5.4 %collective-permute-start.5 = (bf16[512,128]{1,0:T(8,128)(2,1)S(1)}, bf16[512,128]{1,0:T(8,128)(2,1)S(1)}, u32[]{:S(2)}, u32[]{:S(2)}) collective-permute-start(bf16[512,128]{1,0:T(8,128)(2,1)S(1)} %get-tuple-element.45), channel_id=1, source_target_pairs={{0,2},{1,3},{2,0},{3,1},{4,6},{5,7},{6,4},{7,5},{8,10},{9,11},{10,... | collective-permute-start | bytes 393224 | tf_op jit(solution)/shard_map/ppermute | solution.py:289
  23.2 7.2 %collective-permute-start.6 = (bf16[512,128]{1,0:T(8,128)(2,1)S(1)}, bf16[512,128]{1,0:T(8,128)(2,1)S(1)}, u32[]{:S(2)}, u32[]{:S(2)}) collective-permute-start(bf16[512,128]{1,0:T(8,128)(2,1)S(1)} %get-tuple-element.46), channel_id=1, source_target_pairs={{0,3},{1,2},{2,1},{3,0},{4,7},{5,6},{6,5},{7,4},{8,11},{9,10},{10,... | collective-permute-start | bytes 393224 | tf_op jit(solution)/shard_map/ppermute | solution.py:289
  31.7 6.3 %collective-permute-start.7 = (bf16[544,128]{1,0:T(8,128)(2,1)S(1)}, bf16[544,128]{1,0:T(8,128)(2,1)S(1)}, u32[]{:S(2)}, u32[]{:S(2)}) collective-permute-start(bf16[544,128]{1,0:T(8,128)(2,1)S(1)} %get-tuple-element.55), channel_id=1, source_target_pairs={{0,1},{1,0},{2,3},{3,2},{4,5},{5,4},{6,7},{7,6},{8,9},{9,8},{10,11... | collective-permute-start | bytes 417800 | tf_op jit(solution)/shard_map/ppermute | solution.py:289
  32.1 5.8 %collective-permute-start.8 = (bf16[544,128]{1,0:T(8,128)(2,1)S(1)}, bf16[544,128]{1,0:T(8,128)(2,1)S(1)}, u32[]{:S(2)}, u32[]{:S(2)}) collective-permute-start(bf16[544,128]{1,0:T(8,128)(2,1)S(1)} %get-tuple-element.56), channel_id=1, source_target_pairs={{0,2},{1,3},{2,0},{3,1},{4,6},{5,7},{6,4},{7,5},{8,10},{9,11},{10,... | collective-permute-start | bytes 417800 | tf_op jit(solution)/shard_map/ppermute | solution.py:289
  33.5 6.2 %collective-permute-start.9 = (bf16[544,128]{1,0:T(8,128)(2,1)S(1)}, bf16[544,128]{1,0:T(8,128)(2,1)S(1)}, u32[]{:S(2)}, u32[]{:S(2)}) collective-permute-start(bf16[544,128]{1,0:T(8,128)(2,1)S(1)} %get-tuple-element.57), channel_id=1, source_target_pairs={{0,3},{1,2},{2,1},{3,0},{4,7},{5,6},{6,5},{7,4},{8,11},{9,10},{10,... | collective-permute-start | bytes 417800 | tf_op jit(solution)/shard_map/ppermute | solution.py:289
  39.8 7.4 %collective-permute-start.10 = (bf16[544,128]{1,0:T(8,128)(2,1)S(1)}, bf16[544,128]{1,0:T(8,128)(2,1)S(1)}, u32[]{:S(2)}, u32[]{:S(2)}) collective-permute-start(bf16[544,128]{1,0:T(8,128)(2,1)S(1)} %shard_map.98.refs_5_), channel_id=1, source_target_pairs={{0,4},{1,5},{2,6},{3,7},{4,0},{5,1},{6,2},{7,3},{8,12},{9,13},{10,... | collective-permute-start | bytes 417800 | tf_op jit(solution)/shard_map/ppermute | solution.py:311
  47.5 6.0 %collective-permute-start.12 = (bf16[512,128]{1,0:T(8,128)(2,1)S(1)}, bf16[512,128]{1,0:T(8,128)(2,1)S(1)}, u32[]{:S(2)}, u32[]{:S(2)}) collective-permute-start(bf16[512,128]{1,0:T(8,128)(2,1)S(1)} %get-tuple-element.61), channel_id=1, source_target_pairs={{0,3},{1,2},{2,1},{3,0},{4,7},{5,6},{6,5},{7,4},{8,11},{9,10},{10,... | collective-permute-start | bytes 393224 | tf_op jit(solution)/shard_map/ppermute | solution.py:289
  47.7 6.4 %collective-permute-start.13 = (bf16[512,128]{1,0:T(8,128)(2,1)S(1)}, bf16[512,128]{1,0:T(8,128)(2,1)S(1)}, u32[]{:S(2)}, u32[]{:S(2)}) collective-permute-start(bf16[512,128]{1,0:T(8,128)(2,1)S(1)} %get-tuple-element.62), channel_id=1, source_target_pairs={{0,1},{1,0},{2,3},{3,2},{4,5},{5,4},{6,7},{7,6},{8,9},{9,8},{10,11... | collective-permute-start | bytes 393224 | tf_op jit(solution)/shard_map/ppermute | solution.py:289
  48.9 7.7 %collective-permute-start.11 = (bf16[512,128]{1,0:T(8,128)(2,1)S(1)}, bf16[512,128]{1,0:T(8,128)(2,1)S(1)}, u32[]{:S(2)}, u32[]{:S(2)}) collective-permute-start(bf16[512,128]{1,0:T(8,128)(2,1)S(1)} %get-tuple-element.59), channel_id=1, source_target_pairs={{0,2},{1,3},{2,0},{3,1},{4,6},{5,7},{6,4},{7,5},{8,10},{9,11},{10,... | collective-permute-start | bytes 393224 | tf_op jit(solution)/shard_map/ppermute | solution.py:289
  51.1 4.3 %collective-permute-start.14 = (f32[16,128]{1,0:T(8,128)S(1)}, f32[16,128]{1,0:T(8,128)S(1)}, u32[]{:S(2)}, u32[]{:S(2)}) collective-permute-start(f32[16,128]{1,0:T(8,128)S(1)} %get-tuple-element.65.refs_7_), channel_id=1, source_target_pairs={{0,8},{8,0},{16,24},{24,16},{1,9},{9,1},{17,25},{25,17},{2,10},{10... | collective-permute-start | bytes 24584 | tf_op jit(solution)/shard_map/ppermute | solution.py:289
  51.1 4.3 %collective-permute-start.15 = (f32[16,128]{1,0:T(8,128)S(1)}, f32[16,128]{1,0:T(8,128)S(1)}, u32[]{:S(2)}, u32[]{:S(2)}) collective-permute-start(f32[16,128]{1,0:T(8,128)S(1)} %get-tuple-element.65.refs_7_), channel_id=1, source_target_pairs={{0,16},{8,24},{16,0},{24,8},{1,17},{9,25},{17,1},{25,9},{2,18},{10... | collective-permute-start | bytes 24584 | tf_op jit(solution)/shard_map/ppermute | solution.py:289
  53.6 3.1 %collective-permute-start.16 = (f32[16,128]{1,0:T(8,128)S(1)}, f32[16,128]{1,0:T(8,128)S(1)}, u32[]{:S(2)}, u32[]{:S(2)}) collective-permute-start(f32[16,128]{1,0:T(8,128)S(1)} %get-tuple-element.65.refs_7_), channel_id=1, source_target_pairs={{0,24},{8,16},{16,8},{24,0},{1,25},{9,17},{17,9},{25,1},{2,26},{10... | collective-permute-start | bytes 24584 | tf_op jit(solution)/shard_map/ppermute | solution.py:289

commit v3 on v2

--- a/solution.py
+++ b/solution.py
@@ -31,18 +31,25 @@
     return lax.rem(lax.axis_index("seq"), group)
 
 
+def partner_of(group, slot):
+    if slot in (1, 2):
+        odd = lax.rem(lax.axis_index("dp"), 2) == 1
+        slot = jnp.where(odd, 3 - slot, slot)
+    return member_of(group) ^ slot
+
+
 def block_at(index, size):
     return pl.ds(pl.multiple_of(index * size, size), size)
 
 
-def gathered(member, piece_refs, size, whole_ref):
+def gathered(piece_refs, size, whole_ref):
     for j, ref in enumerate(piece_refs):
-        whole_ref[block_at(member ^ j, size), :] = ref[0:size, :]
-
-
-def scattered(member, whole_ref, size, piece_refs):
+        whole_ref[block_at(partner_of(len(piece_refs), j), size), :] = ref[0:size, :]
+
+
+def scattered(whole_ref, size, piece_refs):
     for j, ref in enumerate(piece_refs):
-        ref[0:size, :] = whole_ref[block_at(member ^ j, size), :]
+        ref[0:size, :] = whole_ref[block_at(partner_of(len(piece_refs), j), size), :]
 
 
 def columns(first, count):
@@ -63,7 +70,7 @@
     for h in range(HEADS):
         part = columns(h * head, head)
         whole_ref[part, :] = dot(k_buffer[:, part], v_buffer[:, part], 0, 0).astype(HALF)
-    scattered(member_of(group), whole_ref, piece_refs[0].shape[0], piece_refs)
+    scattered(whole_ref, piece_refs[0].shape[0], piece_refs)
 
 
 def local_kernel(head, q_ref, k_ref, v_ref, scores_ref, intra_ref):
@@ -84,12 +91,11 @@
     attended_ref, inverse_ref, grad_ref = refs[4 + group : 7 + group]
     piece_refs = refs[7 + group : 7 + 2 * group]
     whole_ref, gain_grad_ref = refs[7 + 2 * group :]
-    member = member_of(group)
     rows = q_ref.shape[0]
     scaling = head ** (-0.5)
     features = HEADS * head
     size = features // group
-    gathered(member, prefix_refs, size, whole_ref)
+    gathered(prefix_refs, size, whole_ref)
     squares = jnp.zeros((rows, head), F32)
     inner = jnp.zeros((rows, head), F32)
     for h in range(HEADS):
@@ -117,7 +123,7 @@
         grad = ((upstream * gain - normalized * inner_mean) * inverse).astype(HALF)
         grad_ref[:, part] = grad
         whole_ref[part, :] = (scaling * dot(q_ref[:, part], grad, 0, 0)).astype(HALF)
-    scattered(member, whole_ref, size, piece_refs)
+    scattered(whole_ref, size, piece_refs)
     for ref in piece_refs:
         put_wide_rows(ref, size, gain_grad_ref[...])
 
@@ -133,7 +139,7 @@
     rows = q_ref.shape[0]
     mask = causal(rows)
     scaling = head ** (-0.5)
-    gathered(member_of(group), prefix_refs, prefix_refs[0].shape[0], whole_ref)
+    gathered(prefix_refs, prefix_refs[0].shape[0], whole_ref)
     inverse = inverse_ref[...]
     for h in range(HEADS):
         part = columns(h * head, head)
@@ -154,25 +160,18 @@
     token_ref[...] = jnp.zeros_like(token_ref)
 
 
-def final_kernel(head, group, chunks, last, *refs):
+def final_kernel(head, group, chunks, *refs):
     k_ref, v_ref, key_part_ref, value_part_ref = refs[:4]
     suffix_refs = refs[4 : 4 + len(chunks)]
     refs = refs[4 + len(suffix_refs) :]
+    out_refs, token_ref = refs[-6:-4], refs[-4]
+    key_buffer, value_buffer, written = refs[-3:]
+    token_ref[...] = jnp.zeros_like(token_ref)
     copies = []
-    if last:
-        gain_grad_ref, total_ref, gain_written = refs[-6], refs[-2], refs[-1]
-        total_ref[...] = tree_sum([ref[...] for ref in refs[2:-8]])
-        copies.append(pltpu.make_async_copy(total_ref, gain_grad_ref, gain_written))
-        copies[0].start()
-        out_refs, refs = refs[-8:-6], refs[-5:-2]
-    else:
-        out_refs, refs = refs[:2], refs[2:]
-    key_buffer, value_buffer, written = refs
-    member = member_of(group)
     width = key_buffer.shape[2]
     for n, chunk in enumerate(chunks):
         suffix_ref = suffix_refs[n]
-        start = (member ^ chunk) * width
+        start = partner_of(group, chunk) * width
         for i in range(width // head):
             part = pl.ds(pl.multiple_of(start + i * head, head), head)
             local = columns(i * head, head)
@@ -186,13 +185,18 @@
         for i, buffer in enumerate((key_buffer, value_buffer)):
             copy = pltpu.make_async_copy(
                 buffer.at[n],
-                out_refs[i].at[:, block_at(member ^ chunk, width)],
+                out_refs[i].at[:, block_at(partner_of(group, chunk), width)],
                 written.at[i, n],
             )
             copy.start()
             copies.append(copy)
     for copy in copies:
         copy.wait()
+
+
+def gain_kernel(token_ref, *refs):
+    del token_ref
+    refs[-1][...] = tree_sum([ref[...] for ref in refs[:-1]])
 
 
 def tree_sum(terms):
@@ -240,7 +244,7 @@
 
 
 def scan_kernel(group, reverse, masked, size, riding, *refs):
-    member = member_of(group)
+    members = [partner_of(group, j) for j in range(group)]
     carry = refs[0][0:size, :].astype(F32)
     if masked:
         carry = carry * group_flag(group, reverse, 1)
@@ -250,7 +254,7 @@
         total = carry
         for i in range(group):
             if i != j:
-                earlier = (member ^ i) < (member ^ j)
+                earlier = members[i] < members[j]
                 keep = jnp.where(earlier != reverse, 1.0, 0.0)
                 total += keep * blocks[i]
         out_refs[j][...] = total.astype(HALF)
@@ -290,9 +294,15 @@
 
 
 def own_and_swapped(pieces):
-    order = sorted(range(1, len(pieces)), key=lambda j: -bin(j).count("1"))
-    moved = {j: swap(pieces[j], "seq", j) for j in order}
-    return [pieces[0]] + [moved[j] for j in range(1, len(pieces))]
+    count = lax.axis_size("seq")
+    results = [pieces[0]]
+    for slot in range(1, len(pieces)):
+        pairs = []
+        for row in range(lax.axis_size("dp")):
+            offset = 3 - slot if slot in (1, 2) and row % 2 else slot
+            pairs += [(row * count + i, row * count + (i ^ offset)) for i in range(count)]
+        results.append(lax.ppermute(pieces[slot], ("dp", "seq"), pairs))
+    return results
 
 
 def exclusive_scan(pieces, size, reverse, token):
@@ -350,7 +360,9 @@
     while stride < count:
         array = tree_sum(terms)
         width = 4 if count // stride % 4 == 0 else 2
-        terms = [array] + [swap(array, axis, i * stride) for i in range(1, width)]
+        order = sorted(range(1, width), key=lambda i: i % 2)
+        moved = {i: swap(array, axis, i * stride) for i in order}
+        terms = [array] + [moved[i] for i in range(1, width)]
         stride *= width
     return terms
 
@@ -402,33 +414,33 @@
     suffix, gain_grad = exclusive_scan(pieces, width, True, token)
     gains = summed_over("dp", 1, gain_grad)
     inputs = [k, v, key_part, value_part]
-    early, late = [0, 3, 1], [2]
+    early, late = [0, 1, 2], [3]
 
     def buffers(count):
         return [pltpu.VMEM((count, rows, width), HALF)] * 2 + [
             pltpu.SemaphoreType.DMA((2, count))
         ]
 
-    first = call(
-        part(final_kernel, head, group, early, False),
-        [half, half],
+    *first, _ = call(
+        part(final_kernel, head, group, early),
+        [half, half, token_shape],
         inputs + [suffix[j] for j in early],
         1,
         buffers(len(early)),
         out_specs={0: HBM, 1: HBM},
     )
     at = len(inputs) + len(late)
-    grad_key, grad_value, gain_grad = call(
-        part(final_kernel, head, group, late, True),
-        [half, half, gain_shape],
-        inputs + [suffix[j] for j in late] + list(first) + gains,
+    grad_key, grad_value, token = call(
+        part(final_kernel, head, group, late),
+        [half, half, token_shape],
+        inputs + [suffix[j] for j in late] + first,
         1,
-        buffers(len(late))
-        + [pltpu.VMEM((HEADS, head), F32), pltpu.SemaphoreType.DMA(())],
+        buffers(len(late)),
         ins={at: HBM, at + 1: HBM},
-        out_specs={0: HBM, 1: HBM, 2: HBM},
+        out_specs={0: HBM, 1: HBM},
         aliases={at: 0, at + 1: 1},
     )
+    (gain_grad,) = call(gain_kernel, [gain_shape], [token] + gains, 0, ins={0: ANY})
     return (
         output[None],
         grad_query[None],

time: 57.8 us -> 58.4 us (1.010)
  waiting for transfers between devices: 22.4 us -> 19.7 us
  starting transfers between devices: 22.5 us -> 24.4 us
  Pallas kernels: 12 us -> 13.2 us
    ppermute x15 -> x3, waiting for transfers between devices: 18.6 us -> 0.01 us  [swap(): return lax.ppermute(array, axis, [(i, i ^ offset) for i in range(count)])]
    ppermute x0 -> x12, waiting for transfers between devices: none -> 16.3 us  [own_and_swapped(): results.append(lax.ppermute(pieces[slot], ('dp', 'seq'), pairs))]
    ppermute x0 -> x12, starting transfers between devices: none -> 15.3 us  [own_and_swapped(): results.append(lax.ppermute(pieces[slot], ('dp', 'seq'), pairs))]
    ppermute x15 -> x3, starting transfers between devices: 16.8 us -> 1.83 us  [swap(): return lax.ppermute(array, axis, [(i, i ^ offset) for i in range(count)])]
    ppermute x2, starting transfers between devices: 5.71 us -> 7.32 us  [shifted(): return lax.ppermute(array, 'seq', pairs)]
    pallas_call x10 -> x11, Pallas kernels: 12 us -> 13.2 us  [call(): pl.pallas_call(kernel, out_shape=tuple(outs), in_specs=[ins.get(i, VMEM)...]
  transfers between devices with their start and end apart: 17 -> 17, of which waited for: 13 -> 10; matrix products, arithmetic and copies ran while one was open for 0% -> 0% of each run, Pallas kernels for 13% -> 15%
where the time goes in v3:
time: 58.4 us; the launch traced here: 58.1 us
  starting transfers between devices  24.4 us (42%)
  waiting for transfers between devices  19.7 us (34%)
  Pallas kernels  13.2 us (23%)
  between operations  0.76 us (1%)
    ppermute x12, waiting for transfers between devices, own_and_swapped(): results.append(lax.ppermute(pieces[slot], ('dp', 'seq'), pairs))  16.3 us
    ppermute x12, starting transfers between devices, own_and_swapped(): results.append(lax.ppermute(pieces[slot], ('dp', 'seq'), pairs))  15.3 us
    pallas_call x11, Pallas kernels, call(): pl.pallas_call(kernel, out_shape=tuple(outs), in_specs=[ins.get(i, VMEM)...  13.2 us
    ppermute x2, starting transfers between devices, shifted(): return lax.ppermute(array, 'seq', pairs)  7.32 us
    ppermute x2, waiting for transfers between devices, shifted(): return lax.ppermute(array, 'seq', pairs)  3.41 us
    ppermute x3, starting transfers between devices, swap(): return lax.ppermute(array, axis, [(i, i ^ offset) for i in range(count)])  1.83 us
  transfers between devices with their start and end apart: 17, of which 10 were waited for; matrix products, arithmetic and copies ran while one was open for 0% of the time, Pallas kernels for 15%

profile of v3, /device:TPU:0, one launch (start us, length us, event | category | flops | bytes accessed | tf_op | source)
XLA Modules:
  0.0 58.1 jit_solution(10197015622885478827)
XLA Ops:
  0.7 1.7 %shard_map.93 = (bf16[512,128]{1,0:T(8,128)(2,1)S(1)}, bf16[512,128]{1,0:T(8,128)(2,1)S(1)}, bf16[512,128]{1,0:T(8,128)(2,1)S(1)}, bf16[512,128]{1,0:T(8,128)(2,1)S(1)}) custom-call(bf16[128,2048]{1,0:T(8,128)(2,1)} %bitcast.10, bf16[128,2048]{1,0:T(8,128)(2,1)} %bitcast.15), custom_call_target="tpu_custom_call" | custom-call | flops 67108864 | bytes 1572864 | tf_op jit(solution)/shard_map/pallas_call | solution.py:275
  2.4 3.0 %collective-permute-start = (bf16[512,128]{1,0:T(8,128)(2,1)S(1)}, bf16[512,128]{1,0:T(8,128)(2,1)S(1)}, u32[]{:S(2)}, u32[]{:S(2)}) collective-permute-start(bf16[512,128]{1,0:T(8,128)(2,1)S(1)} %get-tuple-element.40), channel_id=1, source_target_pairs={{0,1},{1,0},{2,3},{3,2},{4,5},{5,4},{6,7},{7,6},{8,10},{9,11},{10,... | collective-permute-start | bytes 393224 | tf_op jit(solution)/shard_map/ppermute | solution.py:304
  5.4 1.6 %collective-permute-start.1 = (bf16[512,128]{1,0:T(8,128)(2,1)S(1)}, bf16[512,128]{1,0:T(8,128)(2,1)S(1)}, u32[]{:S(2)}, u32[]{:S(2)}) collective-permute-start(bf16[512,128]{1,0:T(8,128)(2,1)S(1)} %get-tuple-element.41), channel_id=1, source_target_pairs={{0,2},{1,3},{2,0},{3,1},{4,6},{5,7},{6,4},{7,5},{8,9},{9,8},{10,11... | collective-permute-start | bytes 393224 | tf_op jit(solution)/shard_map/ppermute | solution.py:304
  7.0 3.1 %collective-permute-done.refs_1_.refs_2_ = bf16[512,128]{1,0:T(8,128)(2,1)S(1)} collective-permute-done((bf16[512,128]{1,0:T(8,128)(2,1)S(1)}, bf16[512,128]{1,0:T(8,128)(2,1)S(1)}, u32[]{:S(2)}, u32[]{:S(2)}) %collective-permute-start) | collective-permute-done | bytes 131104 | tf_op jit(solution)/shard_map/ppermute | solution.py:304
  10.0 1.6 %collective-permute-done.1.refs_2_.refs_3_ = bf16[512,128]{1,0:T(8,128)(2,1)S(1)} collective-permute-done((bf16[512,128]{1,0:T(8,128)(2,1)S(1)}, bf16[512,128]{1,0:T(8,128)(2,1)S(1)}, u32[]{:S(2)}, u32[]{:S(2)}) %collective-permute-start.1) | collective-permute-done | bytes 131104 | tf_op jit(solution)/shard_map/ppermute | solution.py:304
  11.6 1.3 %collective-permute-done.2.refs_3_.refs_4_ = bf16[512,128]{1,0:T(8,128)(2,1)S(1)} collective-permute-done((bf16[512,128]{1,0:T(8,128)(2,1)S(1)}, bf16[512,128]{1,0:T(8,128)(2,1)S(1)}, u32[]{:S(2)}, u32[]{:S(2)}) %collective-permute-start.2) | collective-permute-done | bytes 131104 | tf_op jit(solution)/shard_map/ppermute | solution.py:304
  12.9 2.9 %collective-permute-start.3 = (bf16[512,128]{1,0:T(8,128)(2,1)S(1)}, bf16[512,128]{1,0:T(8,128)(2,1)S(1)}, u32[]{:S(2)}, u32[]{:S(2)}) collective-permute-start(bf16[512,128]{1,0:T(8,128)(2,1)S(1)} %shard_map.94), channel_id=1, source_target_pairs={{0,4},{1,5},{2,6},{3,7},{4,0},{5,1},{6,2},{7,3},{8,12},{9,13},{10,... | collective-permute-start | bytes 393224 | tf_op jit(solution)/shard_map/ppermute | solution.py:321
  15.8 2.6 %shard_map.92 = (bf16[2048,128]{1,0:T(8,128)(2,1)S(1)}, f32[128,2048]{1,0:T(8,128)S(1)}) custom-call(bf16[128,2048]{1,0:T(8,128)(2,1)S(1)} %bitcast.20, bf16[128,2048]{1,0:T(8,128)(2,1)S(1)} %bitcast.11, bf16[128,2048]{1,0:T(8,128)(2,1)S(1)} %bitcast.16), custom_call_target="tpu_custom_call" | custom-call | flops 134217728 | bytes 3145728 | tf_op jit(solution)/shard_map/pallas_call | solution.py:275
  18.4 2.8 %collective-permute-done.3.refs_0_ = bf16[512,128]{1,0:T(8,128)(2,1)S(1)} collective-permute-done((bf16[512,128]{1,0:T(8,128)(2,1)S(1)}, bf16[512,128]{1,0:T(8,128)(2,1)S(1)}, u32[]{:S(2)}, u32[]{:S(2)}) %collective-permute-start.3) | collective-permute-done | bytes 131104 | tf_op jit(solution)/shard_map/ppermute | solution.py:321
  21.5 1.3 %collective-permute-start.4 = (bf16[512,128]{1,0:T(8,128)(2,1)S(1)}, bf16[512,128]{1,0:T(8,128)(2,1)S(1)}, u32[]{:S(2)}, u32[]{:S(2)}) collective-permute-start(bf16[512,128]{1,0:T(8,128)(2,1)S(1)} %get-tuple-element.44), channel_id=1, source_target_pairs={{0,1},{1,0},{2,3},{3,2},{4,5},{5,4},{6,7},{7,6},{8,10},{9,11},{10,... | collective-permute-start | bytes 393224 | tf_op jit(solution)/shard_map/ppermute | solution.py:304
  22.8 0.7 %collective-permute-start.5 = (bf16[512,128]{1,0:T(8,128)(2,1)S(1)}, bf16[512,128]{1,0:T(8,128)(2,1)S(1)}, u32[]{:S(2)}, u32[]{:S(2)}) collective-permute-start(bf16[512,128]{1,0:T(8,128)(2,1)S(1)} %get-tuple-element.45), channel_id=1, source_target_pairs={{0,2},{1,3},{2,0},{3,1},{4,6},{5,7},{6,4},{7,5},{8,9},{9,8},{10,11... | collective-permute-start | bytes 393224 | tf_op jit(solution)/shard_map/ppermute | solution.py:304
  23.5 1.6 %collective-permute-start.6 = (bf16[512,128]{1,0:T(8,128)(2,1)S(1)}, bf16[512,128]{1,0:T(8,128)(2,1)S(1)}, u32[]{:S(2)}, u32[]{:S(2)}) collective-permute-start(bf16[512,128]{1,0:T(8,128)(2,1)S(1)} %get-tuple-element.46), channel_id=1, source_target_pairs={{0,3},{1,2},{2,1},{3,0},{4,7},{5,6},{6,5},{7,4},{8,11},{9,10},{10,... | collective-permute-start | bytes 393224 | tf_op jit(solution)/shard_map/ppermute | solution.py:304
  25.1 3.0 %collective-permute-done.4.refs_5_.refs_9_ = bf16[512,128]{1,0:T(8,128)(2,1)S(1)} collective-permute-done((bf16[512,128]{1,0:T(8,128)(2,1)S(1)}, bf16[512,128]{1,0:T(8,128)(2,1)S(1)}, u32[]{:S(2)}, u32[]{:S(2)}) %collective-permute-start.4) | collective-permute-done | bytes 131104 | tf_op jit(solution)/shard_map/ppermute | solution.py:304
  28.1 1.6 %collective-permute-done.6.refs_7_.refs_11_ = bf16[512,128]{1,0:T(8,128)(2,1)S(1)} collective-permute-done((bf16[512,128]{1,0:T(8,128)(2,1)S(1)}, bf16[512,128]{1,0:T(8,128)(2,1)S(1)}, u32[]{:S(2)}, u32[]{:S(2)}) %collective-permute-start.6) | collective-permute-done | bytes 131104 | tf_op jit(solution)/shard_map/ppermute | solution.py:304
  29.7 1.2 %shard_map.96 = (f32[128,2048]{1,0:T(8,128)S(1)}, f32[128,128]{1,0:T(8,128)S(1)}, bf16[128,2048]{1,0:T(8,128)(2,1)S(1)}, bf16[544,128]{1,0:T(8,128)(2,1)S(1)}, b...) custom-call(bf16[128,2048]{1,0:T(8,128)(2,1)S(1)} %bitcast.21, ...), custom_call_target="tpu_custom_call" | custom-call | flops 134217728 | bytes 4825088 | tf_op jit(solution)/shard_map/pallas_call | solution.py:275
  30.9 1.3 %collective-permute-start.7 = (bf16[544,128]{1,0:T(8,128)(2,1)S(1)}, bf16[544,128]{1,0:T(8,128)(2,1)S(1)}, u32[]{:S(2)}, u32[]{:S(2)}) collective-permute-start(bf16[544,128]{1,0:T(8,128)(2,1)S(1)} %get-tuple-element.55), channel_id=1, source_target_pairs={{0,1},{1,0},{2,3},{3,2},{4,5},{5,4},{6,7},{7,6},{8,10},{9,11},{10,... | collective-permute-start | bytes 417800 | tf_op jit(solution)/shard_map/ppermute | solution.py:304
  32.2 1.5 %collective-permute-start.8 = (bf16[544,128]{1,0:T(8,128)(2,1)S(1)}, bf16[544,128]{1,0:T(8,128)(2,1)S(1)}, u32[]{:S(2)}, u32[]{:S(2)}) collective-permute-start(bf16[544,128]{1,0:T(8,128)(2,1)S(1)} %get-tuple-element.56), channel_id=1, source_target_pairs={{0,2},{1,3},{2,0},{3,1},{4,6},{5,7},{6,4},{7,5},{8,9},{9,8},{10,11... | collective-permute-start | bytes 417800 | tf_op jit(solution)/shard_map/ppermute | solution.py:304
  33.7 0.8 %collective-permute-start.9 = (bf16[544,128]{1,0:T(8,128)(2,1)S(1)}, bf16[544,128]{1,0:T(8,128)(2,1)S(1)}, u32[]{:S(2)}, u32[]{:S(2)}) collective-permute-start(bf16[544,128]{1,0:T(8,128)(2,1)S(1)} %get-tuple-element.57), channel_id=1, source_target_pairs={{0,3},{1,2},{2,1},{3,0},{4,7},{5,6},{6,5},{7,4},{8,11},{9,10},{10,... | collective-permute-start | bytes 417800 | tf_op jit(solution)/shard_map/ppermute | solution.py:304
  34.5 3.2 %collective-permute-done.7.refs_1_.refs_2_ = bf16[544,128]{1,0:T(8,128)(2,1)S(1)} collective-permute-done((bf16[544,128]{1,0:T(8,128)(2,1)S(1)}, bf16[544,128]{1,0:T(8,128)(2,1)S(1)}, u32[]{:S(2)}, u32[]{:S(2)}) %collective-permute-start.7) | collective-permute-done | bytes 139296 | tf_op jit(solution)/shard_map/ppermute | solution.py:304
  37.7 1.9 %collective-permute-done.9.refs_3_.refs_4_ = bf16[544,128]{1,0:T(8,128)(2,1)S(1)} collective-permute-done((bf16[544,128]{1,0:T(8,128)(2,1)S(1)}, bf16[544,128]{1,0:T(8,128)(2,1)S(1)}, u32[]{:S(2)}, u32[]{:S(2)}) %collective-permute-start.9) | collective-permute-done | bytes 139296 | tf_op jit(solution)/shard_map/ppermute | solution.py:304
  39.7 4.4 %collective-permute-start.10 = (bf16[544,128]{1,0:T(8,128)(2,1)S(1)}, bf16[544,128]{1,0:T(8,128)(2,1)S(1)}, u32[]{:S(2)}, u32[]{:S(2)}) collective-permute-start(bf16[544,128]{1,0:T(8,128)(2,1)S(1)} %shard_map.98.refs_5_), channel_id=1, source_target_pairs={{0,4},{1,5},{2,6},{3,7},{4,0},{5,1},{6,2},{7,3},{8,12},{9,13},{10,... | collective-permute-start | bytes 417800 | tf_op jit(solution)/shard_map/ppermute | solution.py:321
  44.1 3.6 %shard_map.97 = (bf16[128,2048]{1,0:T(8,128)(2,1)}, bf16[128,2048]{1,0:T(8,128)(2,1)}, f32[128,2048]{1,0:T(8,128)S(1)}, f32[128,2048]{1,0:T(8,128)S(1)}, f32[8,128]{1,0:T(8,128)S(1)}) custom-call(bf16[128,2048]{1,0:T(8,128)(2,1)S(1)} %bitcast.22, bf16[128,2048]{1,0:T(8,128)(2,1)S(1)} %bitcast.12, bf16[128,2048]{1,0:T(8,128)(2,1)S(1)} %bitcast.17, ...), custom_call_target="tpu_custom_call" | custom-call | flops 335544320 | bytes 7417856 | tf_op jit(solution)/shard_map/pallas_call | solution.py:275
  47.7 0.6 %collective-permute-done.10.refs_0_ = bf16[544,128]{1,0:T(8,128)(2,1)S(1)} collective-permute-done((bf16[544,128]{1,0:T(8,128)(2,1)S(1)}, bf16[544,128]{1,0:T(8,128)(2,1)S(1)}, u32[]{:S(2)}, u32[]{:S(2)}) %collective-permute-start.10) | collective-permute-done | bytes 139296 | tf_op jit(solution)/shard_map/ppermute | solution.py:321
  48.3 0.3 shard_map.99
  48.7 1.8 %collective-permute-start.13 = (bf16[512,128]{1,0:T(8,128)(2,1)S(1)}, bf16[512,128]{1,0:T(8,128)(2,1)S(1)}, u32[]{:S(2)}, u32[]{:S(2)}) collective-permute-start(bf16[512,128]{1,0:T(8,128)(2,1)S(1)} %get-tuple-element.62), channel_id=1, source_target_pairs={{0,2},{1,3},{2,0},{3,1},{4,6},{5,7},{6,4},{7,5},{8,9},{9,8},{10,11... | collective-permute-start | bytes 393224 | tf_op jit(solution)/shard_map/ppermute | solution.py:304
  50.5 1.7 %collective-permute-start.11 = (bf16[512,128]{1,0:T(8,128)(2,1)S(1)}, bf16[512,128]{1,0:T(8,128)(2,1)S(1)}, u32[]{:S(2)}, u32[]{:S(2)}) collective-permute-start(bf16[512,128]{1,0:T(8,128)(2,1)S(1)} %get-tuple-element.59), channel_id=1, source_target_pairs={{0,3},{1,2},{2,1},{3,0},{4,7},{5,6},{6,5},{7,4},{8,11},{9,10},{10,... | collective-permute-start | bytes 393224 | tf_op jit(solution)/shard_map/ppermute | solution.py:304
  52.2 1.4 %collective-permute-start.15 = (f32[16,128]{1,0:T(8,128)S(1)}, f32[16,128]{1,0:T(8,128)S(1)}, u32[]{:S(2)}, u32[]{:S(2)}) collective-permute-start(f32[16,128]{1,0:T(8,128)S(1)} %get-tuple-element.68.refs_0_), channel_id=1, source_target_pairs={{0,16},{8,24},{16,0},{24,8},{1,17},{9,25},{17,1},{25,9},{2,18},{10... | collective-permute-start | bytes 24584 | tf_op jit(solution)/shard_map/ppermute | solution.py:293
  53.7 0.4 collective-permute-start.16
  54.1 1.9 %shard_map.100 = (bf16[128,2048]{1,0:T(8,128)(2,1)}, bf16[128,2048]{1,0:T(8,128)(2,1)}, f32[8,128]{1,0:T(8,128)}) custom-call(bf16[128,2048]{1,0:T(8,128)(2,1)S(1)} %bitcast.13, bf16[128,2048]{1,0:T(8,128)(2,1)S(1)} %bitcast.18, f32[128,2048]{1,0:T(8,128)S(1)} %get-tuple-element.52.refs_2_, f32[128,2048]{1,0:T(8,128)S(1)} %get-tuple-element.53.refs_3_, ...), custom_call_target="tpu_custom_call" | custom-call | flops 67108864 | bytes 4591616 | tf_op jit(solution)/shard_map/pallas_call | solution.py:275
  55.9 0.6 %collective-permute-done.11.refs_4_ = bf16[512,128]{1,0:T(8,128)(2,1)S(1)} collective-permute-done((bf16[512,128]{1,0:T(8,128)(2,1)S(1)}, bf16[512,128]{1,0:T(8,128)(2,1)S(1)}, u32[]{:S(2)}, u32[]{:S(2)}) %collective-permute-start.11) | collective-permute-done | bytes 131104 | tf_op jit(solution)/shard_map/ppermute | solution.py:304
  56.5 1.0 %shard_map.101 = (bf16[128,2048]{1,0:T(8,128)(2,1)}, bf16[128,2048]{1,0:T(8,128)(2,1)}, f32[8,128]{1,0:T(8,128)S(1)}) custom-call(bf16[128,2048]{1,0:T(8,128)(2,1)S(1)} %bitcast.14, bf16[128,2048]{1,0:T(8,128)(2,1)S(1)} %bitcast.19, f32[128,2048]{1,0:T(8,128)S(1)} %get-tuple-element.52.refs_2_, ...), custom_call_target="tpu_custom_call", output_to_operand_aliasing={{0}: (5, {}), {1}: (6, {})} | custom-call | flops 67108864 | bytes 5378048 | tf_op jit(solution)/shard_map/pallas_call | solution.py:275
  57.5 0.6 %shard_map.102 = f32[16,128]{1,0:T(8,128)} custom-call(f32[8,128]{1,0:T(8,128)S(1)} %get-tuple-element.67.token_ref, f32[16,128]{1,0:T(8,128)S(1)} %get-tuple-element.68.refs_0_, f32[16,128]{1,0:T(8,128)S(1)} %collective-permute-done.14.refs_1_, f32[16,128]{1,0:T(8,128)S(1)} %collective-permute-done.15.refs_2_, f32[16,128]{1,0:T(8,128)S(1)} %collective-permute-done.16.refs_3_), custom_call_target="tpu_custom_call" | custom-call | bytes 45056 | tf_op jit(solution)/shard_map/pallas_call | solution.py:275
  (23 shorter events, 0.6 us)
Async XLA Ops:
  0.6 15.2 %copy-start.1 = (bf16[1,128,2048]{2,1,0:T(8,128)(2,1)S(1)}, bf16[1,128,2048]{2,1,0:T(8,128)(2,1)}, u32[]{:S(2)}) copy-start(bf16[1,128,2048]{2,1,0:T(8,128)(2,1)} %param.7) | copy-start | bytes 1572868
  0.6 15.2 %copy-start.2 = (bf16[1,128,2048]{2,1,0:T(8,128)(2,1)S(1)}, bf16[1,128,2048]{2,1,0:T(8,128)(2,1)}, u32[]{:S(2)}) copy-start(bf16[1,128,2048]{2,1,0:T(8,128)(2,1)} %param.5) | copy-start | bytes 1572868
  2.3 13.5 %copy-start = (bf16[1,128,2048]{2,1,0:T(8,128)(2,1)S(1)}, bf16[1,128,2048]{2,1,0:T(8,128)(2,1)}, u32[]{:S(2)}) copy-start(bf16[1,128,2048]{2,1,0:T(8,128)(2,1)} %param.6) | copy-start | bytes 1572868
  2.4 7.7 %collective-permute-start = (bf16[512,128]{1,0:T(8,128)(2,1)S(1)}, bf16[512,128]{1,0:T(8,128)(2,1)S(1)}, u32[]{:S(2)}, u32[]{:S(2)}) collective-permute-start(bf16[512,128]{1,0:T(8,128)(2,1)S(1)} %get-tuple-element.40), channel_id=1, source_target_pairs={{0,1},{1,0},{2,3},{3,2},{4,5},{5,4},{6,7},{7,6},{8,10},{9,11},{10,... | collective-permute-start | bytes 393224 | tf_op jit(solution)/shard_map/ppermute | solution.py:304
  5.4 6.2 %collective-permute-start.1 = (bf16[512,128]{1,0:T(8,128)(2,1)S(1)}, bf16[512,128]{1,0:T(8,128)(2,1)S(1)}, u32[]{:S(2)}, u32[]{:S(2)}) collective-permute-start(bf16[512,128]{1,0:T(8,128)(2,1)S(1)} %get-tuple-element.41), channel_id=1, source_target_pairs={{0,2},{1,3},{2,0},{3,1},{4,6},{5,7},{6,4},{7,5},{8,9},{9,8},{10,11... | collective-permute-start | bytes 393224 | tf_op jit(solution)/shard_map/ppermute | solution.py:304
  7.0 5.9 %collective-permute-start.2 = (bf16[512,128]{1,0:T(8,128)(2,1)S(1)}, bf16[512,128]{1,0:T(8,128)(2,1)S(1)}, u32[]{:S(2)}, u32[]{:S(2)}) collective-permute-start(bf16[512,128]{1,0:T(8,128)(2,1)S(1)} %get-tuple-element.42), channel_id=1, source_target_pairs={{0,3},{1,2},{2,1},{3,0},{4,7},{5,6},{6,5},{7,4},{8,11},{9,10},{10,... | collective-permute-start | bytes 393224 | tf_op jit(solution)/shard_map/ppermute | solution.py:304
  12.9 8.3 %collective-permute-start.3 = (bf16[512,128]{1,0:T(8,128)(2,1)S(1)}, bf16[512,128]{1,0:T(8,128)(2,1)S(1)}, u32[]{:S(2)}, u32[]{:S(2)}) collective-permute-start(bf16[512,128]{1,0:T(8,128)(2,1)S(1)} %shard_map.94), channel_id=1, source_target_pairs={{0,4},{1,5},{2,6},{3,7},{4,0},{5,1},{6,2},{7,3},{8,12},{9,13},{10,... | collective-permute-start | bytes 393224 | tf_op jit(solution)/shard_map/ppermute | solution.py:321
  21.2 8.5 %copy-start.3 = (bf16[1,128,2048]{2,1,0:T(8,128)(2,1)S(1)}, bf16[1,128,2048]{2,1,0:T(8,128)(2,1)}, u32[]{:S(2)}) copy-start(bf16[1,128,2048]{2,1,0:T(8,128)(2,1)} %param.9) | copy-start | bytes 1572868
  21.5 8.2 %copy-start.4 = (f32[2048]{0:T(1024)S(1)}, f32[2048]{0:T(1024)}, u32[]{:S(2)}) copy-start(f32[2048]{0:T(1024)} %param.8) | copy-start | bytes 24580
  21.5 6.6 %collective-permute-start.4 = (bf16[512,128]{1,0:T(8,128)(2,1)S(1)}, bf16[512,128]{1,0:T(8,128)(2,1)S(1)}, u32[]{:S(2)}, u32[]{:S(2)}) collective-permute-start(bf16[512,128]{1,0:T(8,128)(2,1)S(1)} %get-tuple-element.44), channel_id=1, source_target_pairs={{0,1},{1,0},{2,3},{3,2},{4,5},{5,4},{6,7},{7,6},{8,10},{9,11},{10,... | collective-permute-start | bytes 393224 | tf_op jit(solution)/shard_map/ppermute | solution.py:304
  22.8 5.3 %collective-permute-start.5 = (bf16[512,128]{1,0:T(8,128)(2,1)S(1)}, bf16[512,128]{1,0:T(8,128)(2,1)S(1)}, u32[]{:S(2)}, u32[]{:S(2)}) collective-permute-start(bf16[512,128]{1,0:T(8,128)(2,1)S(1)} %get-tuple-element.45), channel_id=1, source_target_pairs={{0,2},{1,3},{2,0},{3,1},{4,6},{5,7},{6,4},{7,5},{8,9},{9,8},{10,11... | collective-permute-start | bytes 393224 | tf_op jit(solution)/shard_map/ppermute | solution.py:304
  23.5 6.2 %collective-permute-start.6 = (bf16[512,128]{1,0:T(8,128)(2,1)S(1)}, bf16[512,128]{1,0:T(8,128)(2,1)S(1)}, u32[]{:S(2)}, u32[]{:S(2)}) collective-permute-start(bf16[512,128]{1,0:T(8,128)(2,1)S(1)} %get-tuple-element.46), channel_id=1, source_target_pairs={{0,3},{1,2},{2,1},{3,0},{4,7},{5,6},{6,5},{7,4},{8,11},{9,10},{10,... | collective-permute-start | bytes 393224 | tf_op jit(solution)/shard_map/ppermute | solution.py:304
  30.9 6.8 %collective-permute-start.7 = (bf16[544,128]{1,0:T(8,128)(2,1)S(1)}, bf16[544,128]{1,0:T(8,128)(2,1)S(1)}, u32[]{:S(2)}, u32[]{:S(2)}) collective-permute-start(bf16[544,128]{1,0:T(8,128)(2,1)S(1)} %get-tuple-element.55), channel_id=1, source_target_pairs={{0,1},{1,0},{2,3},{3,2},{4,5},{5,4},{6,7},{7,6},{8,10},{9,11},{10,... | collective-permute-start | bytes 417800 | tf_op jit(solution)/shard_map/ppermute | solution.py:304
  32.2 5.5 %collective-permute-start.8 = (bf16[544,128]{1,0:T(8,128)(2,1)S(1)}, bf16[544,128]{1,0:T(8,128)(2,1)S(1)}, u32[]{:S(2)}, u32[]{:S(2)}) collective-permute-start(bf16[544,128]{1,0:T(8,128)(2,1)S(1)} %get-tuple-element.56), channel_id=1, source_target_pairs={{0,2},{1,3},{2,0},{3,1},{4,6},{5,7},{6,4},{7,5},{8,9},{9,8},{10,11... | collective-permute-start | bytes 417800 | tf_op jit(solution)/shard_map/ppermute | solution.py:304
  33.7 6.0 %collective-permute-start.9 = (bf16[544,128]{1,0:T(8,128)(2,1)S(1)}, bf16[544,128]{1,0:T(8,128)(2,1)S(1)}, u32[]{:S(2)}, u32[]{:S(2)}) collective-permute-start(bf16[544,128]{1,0:T(8,128)(2,1)S(1)} %get-tuple-element.57), channel_id=1, source_target_pairs={{0,3},{1,2},{2,1},{3,0},{4,7},{5,6},{6,5},{7,4},{8,11},{9,10},{10,... | collective-permute-start | bytes 417800 | tf_op jit(solution)/shard_map/ppermute | solution.py:304
  39.7 8.6 %collective-permute-start.10 = (bf16[544,128]{1,0:T(8,128)(2,1)S(1)}, bf16[544,128]{1,0:T(8,128)(2,1)S(1)}, u32[]{:S(2)}, u32[]{:S(2)}) collective-permute-start(bf16[544,128]{1,0:T(8,128)(2,1)S(1)} %shard_map.98.refs_5_), channel_id=1, source_target_pairs={{0,4},{1,5},{2,6},{3,7},{4,0},{5,1},{6,2},{7,3},{8,12},{9,13},{10,... | collective-permute-start | bytes 417800 | tf_op jit(solution)/shard_map/ppermute | solution.py:321
  48.6 5.0 %collective-permute-start.12 = (bf16[512,128]{1,0:T(8,128)(2,1)S(1)}, bf16[512,128]{1,0:T(8,128)(2,1)S(1)}, u32[]{:S(2)}, u32[]{:S(2)}) collective-permute-start(bf16[512,128]{1,0:T(8,128)(2,1)S(1)} %get-tuple-element.61), channel_id=1, source_target_pairs={{0,1},{1,0},{2,3},{3,2},{4,5},{5,4},{6,7},{7,6},{8,10},{9,11},{10,... | collective-permute-start | bytes 393224 | tf_op jit(solution)/shard_map/ppermute | solution.py:304
  48.7 5.3 %collective-permute-start.13 = (bf16[512,128]{1,0:T(8,128)(2,1)S(1)}, bf16[512,128]{1,0:T(8,128)(2,1)S(1)}, u32[]{:S(2)}, u32[]{:S(2)}) collective-permute-start(bf16[512,128]{1,0:T(8,128)(2,1)S(1)} %get-tuple-element.62), channel_id=1, source_target_pairs={{0,2},{1,3},{2,0},{3,1},{4,6},{5,7},{6,4},{7,5},{8,9},{9,8},{10,11... | collective-permute-start | bytes 393224 | tf_op jit(solution)/shard_map/ppermute | solution.py:304
  50.5 6.1 %collective-permute-start.11 = (bf16[512,128]{1,0:T(8,128)(2,1)S(1)}, bf16[512,128]{1,0:T(8,128)(2,1)S(1)}, u32[]{:S(2)}, u32[]{:S(2)}) collective-permute-start(bf16[512,128]{1,0:T(8,128)(2,1)S(1)} %get-tuple-element.59), channel_id=1, source_target_pairs={{0,3},{1,2},{2,1},{3,0},{4,7},{5,6},{6,5},{7,4},{8,11},{9,10},{10,... | collective-permute-start | bytes 393224 | tf_op jit(solution)/shard_map/ppermute | solution.py:304
  52.2 5.3 %collective-permute-start.14 = (f32[16,128]{1,0:T(8,128)S(1)}, f32[16,128]{1,0:T(8,128)S(1)}, u32[]{:S(2)}, u32[]{:S(2)}) collective-permute-start(f32[16,128]{1,0:T(8,128)S(1)} %get-tuple-element.68.refs_0_), channel_id=1, source_target_pairs={{0,8},{8,0},{16,24},{24,16},{1,9},{9,1},{17,25},{25,17},{2,10},{10... | collective-permute-start | bytes 24584 | tf_op jit(solution)/shard_map/ppermute | solution.py:293
  52.2 5.3 %collective-permute-start.15 = (f32[16,128]{1,0:T(8,128)S(1)}, f32[16,128]{1,0:T(8,128)S(1)}, u32[]{:S(2)}, u32[]{:S(2)}) collective-permute-start(f32[16,128]{1,0:T(8,128)S(1)} %get-tuple-element.68.refs_0_), channel_id=1, source_target_pairs={{0,16},{8,24},{16,0},{24,8},{1,17},{9,25},{17,1},{25,9},{2,18},{10... | collective-permute-start | bytes 24584 | tf_op jit(solution)/shard_map/ppermute | solution.py:293
  53.7 3.9 %collective-permute-start.16 = (f32[16,128]{1,0:T(8,128)S(1)}, f32[16,128]{1,0:T(8,128)S(1)}, u32[]{:S(2)}, u32[]{:S(2)}) collective-permute-start(f32[16,128]{1,0:T(8,128)S(1)} %get-tuple-element.68.refs_0_), channel_id=1, source_target_pairs={{0,24},{8,16},{16,8},{24,0},{1,25},{9,17},{17,9},{25,1},{2,26},{10... | collective-permute-start | bytes 24584 | tf_op jit(solution)/shard_map/ppermute | solution.py:293

commit v4 on v2

--- a/solution.py
+++ b/solution.py
@@ -31,18 +31,30 @@
     return lax.rem(lax.axis_index("seq"), group)
 
 
+CROSSED = ((0, 1, 2, 3), (0, 2, 1, 3))
+DIAGONAL_FIRST = ((0, 3, 1, 2), (0, 3, 1, 2))
+
+
+def partner_of(order, slot):
+    even, odd = order[0][slot], order[1][slot]
+    offset = even
+    if even != odd:
+        offset = jnp.where(lax.rem(lax.axis_index("dp"), 2) == 1, odd, even)
+    return member_of(len(order[0])) ^ offset
+
+
 def block_at(index, size):
     return pl.ds(pl.multiple_of(index * size, size), size)
 
 
-def gathered(member, piece_refs, size, whole_ref):
+def gathered(order, piece_refs, size, whole_ref):
     for j, ref in enumerate(piece_refs):
-        whole_ref[block_at(member ^ j, size), :] = ref[0:size, :]
-
-
-def scattered(member, whole_ref, size, piece_refs):
+        whole_ref[block_at(partner_of(order, j), size), :] = ref[0:size, :]
+
+
+def scattered(order, whole_ref, size, piece_refs):
     for j, ref in enumerate(piece_refs):
-        ref[0:size, :] = whole_ref[block_at(member ^ j, size), :]
+        ref[0:size, :] = whole_ref[block_at(partner_of(order, j), size), :]
 
 
 def columns(first, count):
@@ -63,7 +75,7 @@
     for h in range(HEADS):
         part = columns(h * head, head)
         whole_ref[part, :] = dot(k_buffer[:, part], v_buffer[:, part], 0, 0).astype(HALF)
-    scattered(member_of(group), whole_ref, piece_refs[0].shape[0], piece_refs)
+    scattered(CROSSED, whole_ref, piece_refs[0].shape[0], piece_refs)
 
 
 def local_kernel(head, q_ref, k_ref, v_ref, scores_ref, intra_ref):
@@ -84,12 +96,11 @@
     attended_ref, inverse_ref, grad_ref = refs[4 + group : 7 + group]
     piece_refs = refs[7 + group : 7 + 2 * group]
     whole_ref, gain_grad_ref = refs[7 + 2 * group :]
-    member = member_of(group)
     rows = q_ref.shape[0]
     scaling = head ** (-0.5)
     features = HEADS * head
     size = features // group
-    gathered(member, prefix_refs, size, whole_ref)
+    gathered(CROSSED, prefix_refs, size, whole_ref)
     squares = jnp.zeros((rows, head), F32)
     inner = jnp.zeros((rows, head), F32)
     for h in range(HEADS):
@@ -117,7 +128,7 @@
         grad = ((upstream * gain - normalized * inner_mean) * inverse).astype(HALF)
         grad_ref[:, part] = grad
         whole_ref[part, :] = (scaling * dot(q_ref[:, part], grad, 0, 0)).astype(HALF)
-    scattered(member, whole_ref, size, piece_refs)
+    scattered(DIAGONAL_FIRST, whole_ref, size, piece_refs)
     for ref in piece_refs:
         put_wide_rows(ref, size, gain_grad_ref[...])
 
@@ -133,7 +144,7 @@
     rows = q_ref.shape[0]
     mask = causal(rows)
     scaling = head ** (-0.5)
-    gathered(member_of(group), prefix_refs, prefix_refs[0].shape[0], whole_ref)
+    gathered(CROSSED, prefix_refs, prefix_refs[0].shape[0], whole_ref)
     inverse = inverse_ref[...]
     for h in range(HEADS):
         part = columns(h * head, head)
@@ -154,7 +165,7 @@
     token_ref[...] = jnp.zeros_like(token_ref)
 
 
-def final_kernel(head, group, chunks, last, *refs):
+def final_kernel(head, chunks, last, *refs):
     k_ref, v_ref, key_part_ref, value_part_ref = refs[:4]
     suffix_refs = refs[4 : 4 + len(chunks)]
     refs = refs[4 + len(suffix_refs) :]
@@ -168,11 +179,10 @@
     else:
         out_refs, refs = refs[:2], refs[2:]
     key_buffer, value_buffer, written = refs
-    member = member_of(group)
     width = key_buffer.shape[2]
     for n, chunk in enumerate(chunks):
         suffix_ref = suffix_refs[n]
-        start = (member ^ chunk) * width
+        start = partner_of(DIAGONAL_FIRST, chunk) * width
         for i in range(width // head):
             part = pl.ds(pl.multiple_of(start + i * head, head), head)
             local = columns(i * head, head)
@@ -186,7 +196,7 @@
         for i, buffer in enumerate((key_buffer, value_buffer)):
             copy = pltpu.make_async_copy(
                 buffer.at[n],
-                out_refs[i].at[:, block_at(member ^ chunk, width)],
+                out_refs[i].at[:, block_at(partner_of(DIAGONAL_FIRST, chunk), width)],
                 written.at[i, n],
             )
             copy.start()
@@ -239,8 +249,8 @@
     out_ref[...] = (own + moved).astype(HALF)
 
 
-def scan_kernel(group, reverse, masked, size, riding, *refs):
-    member = member_of(group)
+def scan_kernel(group, order, reverse, masked, size, riding, *refs):
+    members = [partner_of(order, j) for j in range(group)]
     carry = refs[0][0:size, :].astype(F32)
     if masked:
         carry = carry * group_flag(group, reverse, 1)
@@ -250,7 +260,7 @@
         total = carry
         for i in range(group):
             if i != j:
-                earlier = (member ^ i) < (member ^ j)
+                earlier = members[i] < members[j]
                 keep = jnp.where(earlier != reverse, 1.0, 0.0)
                 total += keep * blocks[i]
         out_refs[j][...] = total.astype(HALF)
@@ -289,13 +299,19 @@
     return lax.ppermute(array, axis, [(i, i ^ offset) for i in range(count)])
 
 
-def own_and_swapped(pieces):
-    order = sorted(range(1, len(pieces)), key=lambda j: -bin(j).count("1"))
-    moved = {j: swap(pieces[j], "seq", j) for j in order}
-    return [pieces[0]] + [moved[j] for j in range(1, len(pieces))]
-
-
-def exclusive_scan(pieces, size, reverse, token):
+def own_and_swapped(pieces, order):
+    count = lax.axis_size("seq")
+    results = [pieces[0]]
+    for slot in range(1, len(pieces)):
+        pairs = []
+        for row in range(lax.axis_size("dp")):
+            offset = order[row % 2][slot]
+            pairs += [(row * count + i, row * count + (i ^ offset)) for i in range(count)]
+        results.append(lax.ppermute(pieces[slot], ("dp", "seq"), pairs))
+    return results
+
+
+def exclusive_scan(pieces, order, size, reverse, token):
     group = len(pieces)
     count = lax.axis_size("seq")
     groups = count // group
@@ -310,7 +326,7 @@
         pairs = [(i, (i + step) % count) for i in range(count)]
         return lax.ppermute(array, "seq", pairs)
 
-    received = own_and_swapped(pieces)
+    received = own_and_swapped(pieces, order)
     (total,) = call(
         part(total_kernel, size),
         [jax.ShapeDtypeStruct(pieces[0].shape, HALF)],
@@ -334,13 +350,13 @@
         distance *= 2
     inputs = [carry] + received + ([total] if riding else []) + [token]
     sums = call(
-        part(scan_kernel, group, reverse, groups <= 2, size, riding),
+        part(scan_kernel, group, order, reverse, groups <= 2, size, riding),
         [piece] * group + [gain_shape] * riding,
         inputs,
         0,
         ins={len(inputs) - 1: ANY},
     )
-    results = own_and_swapped(sums[:group])
+    results = own_and_swapped(sums[:group], order)
     return results, (sums[-1] if riding else gain)
 
 
@@ -350,7 +366,9 @@
     while stride < count:
         array = tree_sum(terms)
         width = 4 if count // stride % 4 == 0 else 2
-        terms = [array] + [swap(array, axis, i * stride) for i in range(1, width)]
+        order = sorted(range(1, width), key=lambda i: i % 2)
+        moved = {i: swap(array, axis, i * stride) for i in order}
+        terms = [array] + [moved[i] for i in range(1, width)]
         stride *= width
     return terms
 
@@ -383,7 +401,7 @@
         ins={0: HBM, 1: HBM},
     )
     scores, intra = call(part(local_kernel, head), [scores_shape, wide], [q, k, v], 2)
-    prefix, _ = exclusive_scan(pieces, width, False, intra)
+    prefix, _ = exclusive_scan(pieces, CROSSED, width, False, intra)
     message = jax.ShapeDtypeStruct((width + 2 * HEADS, head), HALF)
     attended, inverse, grad, *pieces = call(
         part(norm_kernel, head, group, lax.axis_size("dp")),
@@ -399,10 +417,10 @@
         5,
         [whole],
     )
-    suffix, gain_grad = exclusive_scan(pieces, width, True, token)
+    suffix, gain_grad = exclusive_scan(pieces, DIAGONAL_FIRST, width, True, token)
     gains = summed_over("dp", 1, gain_grad)
     inputs = [k, v, key_part, value_part]
-    early, late = [0, 3, 1], [2]
+    early, late = [0, 1, 2], [3]
 
     def buffers(count):
         return [pltpu.VMEM((count, rows, width), HALF)] * 2 + [
@@ -410,7 +428,7 @@
         ]
 
     first = call(
-        part(final_kernel, head, group, early, False),
+        part(final_kernel, head, early, False),
         [half, half],
         inputs + [suffix[j] for j in early],
         1,
@@ -419,7 +437,7 @@
     )
     at = len(inputs) + len(late)
     grad_key, grad_value, gain_grad = call(
-        part(final_kernel, head, group, late, True),
+        part(final_kernel, head, late, True),
         [half, half, gain_shape],
         inputs + [suffix[j] for j in late] + list(first) + gains,
         1,

time: 57.8 us -> 56.7 us (0.981)
  starting transfers between devices: 22.5 us -> 21.8 us
    ppermute x15 -> x3, waiting for transfers between devices: 18.6 us -> 0.49 us  [swap(): return lax.ppermute(array, axis, [(i, i ^ offset) for i in range(count)])]
    ppermute x0 -> x12, waiting for transfers between devices: none -> 17.7 us  [own_and_swapped(): results.append(lax.ppermute(pieces[slot], ('dp', 'seq'), pairs))]
    ppermute x15 -> x3, starting transfers between devices: 16.8 us -> 1.13 us  [swap(): return lax.ppermute(array, axis, [(i, i ^ offset) for i in range(count)])]
    ppermute x0 -> x12, starting transfers between devices: none -> 15.3 us  [own_and_swapped(): results.append(lax.ppermute(pieces[slot], ('dp', 'seq'), pairs))]
  transfers between devices with their start and end apart: 17 -> 17, of which waited for: 13 -> 12; matrix products, arithmetic and copies ran while one was open for 0% -> 0% of each run, Pallas kernels for 13% -> 13%
where the time goes in v4:
time: 56.7 us; the launch traced here: 56.6 us
  waiting for transfers between devices  22 us (39%)
  starting transfers between devices  21.8 us (38%)
  Pallas kernels  12 us (21%)
  between operations  0.74 us (1%)
    ppermute x12, waiting for transfers between devices, own_and_swapped(): results.append(lax.ppermute(pieces[slot], ('dp', 'seq'), pairs))  17.7 us
    ppermute x12, starting transfers between devices, own_and_swapped(): results.append(lax.ppermute(pieces[slot], ('dp', 'seq'), pairs))  15.3 us
    pallas_call x10, Pallas kernels, call(): pl.pallas_call(kernel, out_shape=tuple(outs), in_specs=[ins.get(i, VMEM)...  12 us
    ppermute x2, starting transfers between devices, shifted(): return lax.ppermute(array, 'seq', pairs)  5.42 us
    ppermute x2, waiting for transfers between devices, shifted(): return lax.ppermute(array, 'seq', pairs)  3.78 us
  transfers between devices with their start and end apart: 17, of which 12 were waited for; matrix products, arithmetic and copies ran while one was open for 0% of the time, Pallas kernels for 13%

profile of v4, /device:TPU:0, one launch (start us, length us, event | category | flops | bytes accessed | tf_op | source)
XLA Modules:
  0.0 56.6 jit_solution(11194076598545013086)
XLA Ops:
  0.7 1.7 %shard_map.93 = (bf16[512,128]{1,0:T(8,128)(2,1)S(1)}, bf16[512,128]{1,0:T(8,128)(2,1)S(1)}, bf16[512,128]{1,0:T(8,128)(2,1)S(1)}, bf16[512,128]{1,0:T(8,128)(2,1)S(1)}) custom-call(bf16[128,2048]{1,0:T(8,128)(2,1)} %bitcast.10, bf16[128,2048]{1,0:T(8,128)(2,1)} %bitcast.15), custom_call_target="tpu_custom_call" | custom-call | flops 67108864 | bytes 1572864 | tf_op jit(solution)/shard_map/pallas_call | solution.py:281
  2.4 3.0 %collective-permute-start = (bf16[512,128]{1,0:T(8,128)(2,1)S(1)}, bf16[512,128]{1,0:T(8,128)(2,1)S(1)}, u32[]{:S(2)}, u32[]{:S(2)}) collective-permute-start(bf16[512,128]{1,0:T(8,128)(2,1)S(1)} %get-tuple-element.40), channel_id=1, source_target_pairs={{0,1},{1,0},{2,3},{3,2},{4,5},{5,4},{6,7},{7,6},{8,10},{9,11},{10,... | collective-permute-start | bytes 393224 | tf_op jit(solution)/shard_map/ppermute | solution.py:310
  5.4 1.6 %collective-permute-start.1 = (bf16[512,128]{1,0:T(8,128)(2,1)S(1)}, bf16[512,128]{1,0:T(8,128)(2,1)S(1)}, u32[]{:S(2)}, u32[]{:S(2)}) collective-permute-start(bf16[512,128]{1,0:T(8,128)(2,1)S(1)} %get-tuple-element.41), channel_id=1, source_target_pairs={{0,2},{1,3},{2,0},{3,1},{4,6},{5,7},{6,4},{7,5},{8,9},{9,8},{10,11... | collective-permute-start | bytes 393224 | tf_op jit(solution)/shard_map/ppermute | solution.py:310
  7.0 3.1 %collective-permute-done.refs_1_.refs_2_ = bf16[512,128]{1,0:T(8,128)(2,1)S(1)} collective-permute-done((bf16[512,128]{1,0:T(8,128)(2,1)S(1)}, bf16[512,128]{1,0:T(8,128)(2,1)S(1)}, u32[]{:S(2)}, u32[]{:S(2)}) %collective-permute-start) | collective-permute-done | bytes 131104 | tf_op jit(solution)/shard_map/ppermute | solution.py:310
  10.0 1.6 %collective-permute-done.1.refs_2_.refs_3_ = bf16[512,128]{1,0:T(8,128)(2,1)S(1)} collective-permute-done((bf16[512,128]{1,0:T(8,128)(2,1)S(1)}, bf16[512,128]{1,0:T(8,128)(2,1)S(1)}, u32[]{:S(2)}, u32[]{:S(2)}) %collective-permute-start.1) | collective-permute-done | bytes 131104 | tf_op jit(solution)/shard_map/ppermute | solution.py:310
  11.6 1.3 %collective-permute-done.2.refs_3_.refs_4_ = bf16[512,128]{1,0:T(8,128)(2,1)S(1)} collective-permute-done((bf16[512,128]{1,0:T(8,128)(2,1)S(1)}, bf16[512,128]{1,0:T(8,128)(2,1)S(1)}, u32[]{:S(2)}, u32[]{:S(2)}) %collective-permute-start.2) | collective-permute-done | bytes 131104 | tf_op jit(solution)/shard_map/ppermute | solution.py:310
  12.9 2.9 %collective-permute-start.3 = (bf16[512,128]{1,0:T(8,128)(2,1)S(1)}, bf16[512,128]{1,0:T(8,128)(2,1)S(1)}, u32[]{:S(2)}, u32[]{:S(2)}) collective-permute-start(bf16[512,128]{1,0:T(8,128)(2,1)S(1)} %shard_map.94), channel_id=1, source_target_pairs={{0,4},{1,5},{2,6},{3,7},{4,0},{5,1},{6,2},{7,3},{8,12},{9,13},{10,... | collective-permute-start | bytes 393224 | tf_op jit(solution)/shard_map/ppermute | solution.py:327
  15.8 2.6 %shard_map.92 = (bf16[2048,128]{1,0:T(8,128)(2,1)S(1)}, f32[128,2048]{1,0:T(8,128)S(1)}) custom-call(bf16[128,2048]{1,0:T(8,128)(2,1)S(1)} %bitcast.20, bf16[128,2048]{1,0:T(8,128)(2,1)S(1)} %bitcast.11, bf16[128,2048]{1,0:T(8,128)(2,1)S(1)} %bitcast.16), custom_call_target="tpu_custom_call" | custom-call | flops 134217728 | bytes 3145728 | tf_op jit(solution)/shard_map/pallas_call | solution.py:281
  18.4 2.8 %collective-permute-done.3.refs_0_ = bf16[512,128]{1,0:T(8,128)(2,1)S(1)} collective-permute-done((bf16[512,128]{1,0:T(8,128)(2,1)S(1)}, bf16[512,128]{1,0:T(8,128)(2,1)S(1)}, u32[]{:S(2)}, u32[]{:S(2)}) %collective-permute-start.3) | collective-permute-done | bytes 131104 | tf_op jit(solution)/shard_map/ppermute | solution.py:327
  21.5 1.3 %collective-permute-start.4 = (bf16[512,128]{1,0:T(8,128)(2,1)S(1)}, bf16[512,128]{1,0:T(8,128)(2,1)S(1)}, u32[]{:S(2)}, u32[]{:S(2)}) collective-permute-start(bf16[512,128]{1,0:T(8,128)(2,1)S(1)} %get-tuple-element.44), channel_id=1, source_target_pairs={{0,1},{1,0},{2,3},{3,2},{4,5},{5,4},{6,7},{7,6},{8,10},{9,11},{10,... | collective-permute-start | bytes 393224 | tf_op jit(solution)/shard_map/ppermute | solution.py:310
  22.8 0.7 %collective-permute-start.5 = (bf16[512,128]{1,0:T(8,128)(2,1)S(1)}, bf16[512,128]{1,0:T(8,128)(2,1)S(1)}, u32[]{:S(2)}, u32[]{:S(2)}) collective-permute-start(bf16[512,128]{1,0:T(8,128)(2,1)S(1)} %get-tuple-element.45), channel_id=1, source_target_pairs={{0,2},{1,3},{2,0},{3,1},{4,6},{5,7},{6,4},{7,5},{8,9},{9,8},{10,11... | collective-permute-start | bytes 393224 | tf_op jit(solution)/shard_map/ppermute | solution.py:310
  23.5 1.6 %collective-permute-start.6 = (bf16[512,128]{1,0:T(8,128)(2,1)S(1)}, bf16[512,128]{1,0:T(8,128)(2,1)S(1)}, u32[]{:S(2)}, u32[]{:S(2)}) collective-permute-start(bf16[512,128]{1,0:T(8,128)(2,1)S(1)} %get-tuple-element.46), channel_id=1, source_target_pairs={{0,3},{1,2},{2,1},{3,0},{4,7},{5,6},{6,5},{7,4},{8,11},{9,10},{10,... | collective-permute-start | bytes 393224 | tf_op jit(solution)/shard_map/ppermute | solution.py:310
  25.1 3.0 %collective-permute-done.4.refs_5_.refs_9_ = bf16[512,128]{1,0:T(8,128)(2,1)S(1)} collective-permute-done((bf16[512,128]{1,0:T(8,128)(2,1)S(1)}, bf16[512,128]{1,0:T(8,128)(2,1)S(1)}, u32[]{:S(2)}, u32[]{:S(2)}) %collective-permute-start.4) | collective-permute-done | bytes 131104 | tf_op jit(solution)/shard_map/ppermute | solution.py:310
  28.1 1.6 %collective-permute-done.6.refs_7_.refs_11_ = bf16[512,128]{1,0:T(8,128)(2,1)S(1)} collective-permute-done((bf16[512,128]{1,0:T(8,128)(2,1)S(1)}, bf16[512,128]{1,0:T(8,128)(2,1)S(1)}, u32[]{:S(2)}, u32[]{:S(2)}) %collective-permute-start.6) | collective-permute-done | bytes 131104 | tf_op jit(solution)/shard_map/ppermute | solution.py:310
  29.7 1.2 %shard_map.96 = (f32[128,2048]{1,0:T(8,128)S(1)}, f32[128,128]{1,0:T(8,128)S(1)}, bf16[128,2048]{1,0:T(8,128)(2,1)S(1)}, bf16[544,128]{1,0:T(8,128)(2,1)S(1)}, b...) custom-call(bf16[128,2048]{1,0:T(8,128)(2,1)S(1)} %bitcast.21, ...), custom_call_target="tpu_custom_call" | custom-call | flops 134217728 | bytes 4825088 | tf_op jit(solution)/shard_map/pallas_call | solution.py:281
  30.9 2.2 %collective-permute-start.7 = (bf16[544,128]{1,0:T(8,128)(2,1)S(1)}, bf16[544,128]{1,0:T(8,128)(2,1)S(1)}, u32[]{:S(2)}, u32[]{:S(2)}) collective-permute-start(bf16[544,128]{1,0:T(8,128)(2,1)S(1)} %get-tuple-element.55), channel_id=1, source_target_pairs={{0,3},{1,2},{2,1},{3,0},{4,7},{5,6},{6,5},{7,4},{8,11},{9,10},{10,... | collective-permute-start | bytes 417800 | tf_op jit(solution)/shard_map/ppermute | solution.py:310
  33.1 0.4 collective-permute-start.8
  33.6 0.9 %collective-permute-start.9 = (bf16[544,128]{1,0:T(8,128)(2,1)S(1)}, bf16[544,128]{1,0:T(8,128)(2,1)S(1)}, u32[]{:S(2)}, u32[]{:S(2)}) collective-permute-start(bf16[544,128]{1,0:T(8,128)(2,1)S(1)} %get-tuple-element.57), channel_id=1, source_target_pairs={{0,2},{1,3},{2,0},{3,1},{4,6},{5,7},{6,4},{7,5},{8,10},{9,11},{10,... | collective-permute-start | bytes 417800 | tf_op jit(solution)/shard_map/ppermute | solution.py:310
  34.5 3.4 %collective-permute-done.7.refs_1_.refs_2_ = bf16[544,128]{1,0:T(8,128)(2,1)S(1)} collective-permute-done((bf16[544,128]{1,0:T(8,128)(2,1)S(1)}, bf16[544,128]{1,0:T(8,128)(2,1)S(1)}, u32[]{:S(2)}, u32[]{:S(2)}) %collective-permute-start.7) | collective-permute-done | bytes 139296 | tf_op jit(solution)/shard_map/ppermute | solution.py:310
  37.8 1.2 %collective-permute-done.8.refs_2_.refs_3_ = bf16[544,128]{1,0:T(8,128)(2,1)S(1)} collective-permute-done((bf16[544,128]{1,0:T(8,128)(2,1)S(1)}, bf16[544,128]{1,0:T(8,128)(2,1)S(1)}, u32[]{:S(2)}, u32[]{:S(2)}) %collective-permute-start.8) | collective-permute-done | bytes 139296 | tf_op jit(solution)/shard_map/ppermute | solution.py:310
  39.1 2.5 %collective-permute-start.10 = (bf16[544,128]{1,0:T(8,128)(2,1)S(1)}, bf16[544,128]{1,0:T(8,128)(2,1)S(1)}, u32[]{:S(2)}, u32[]{:S(2)}) collective-permute-start(bf16[544,128]{1,0:T(8,128)(2,1)S(1)} %shard_map.98.refs_5_), channel_id=1, source_target_pairs={{0,4},{1,5},{2,6},{3,7},{4,0},{5,1},{6,2},{7,3},{8,12},{9,13},{10,... | collective-permute-start | bytes 417800 | tf_op jit(solution)/shard_map/ppermute | solution.py:327
  41.6 3.6 %shard_map.97 = (bf16[128,2048]{1,0:T(8,128)(2,1)}, bf16[128,2048]{1,0:T(8,128)(2,1)}, f32[128,2048]{1,0:T(8,128)S(1)}, f32[128,2048]{1,0:T(8,128)S(1)}, f32[8,128]{1,0:T(8,128)S(1)}) custom-call(bf16[128,2048]{1,0:T(8,128)(2,1)S(1)} %bitcast.22, bf16[128,2048]{1,0:T(8,128)(2,1)S(1)} %bitcast.12, bf16[128,2048]{1,0:T(8,128)(2,1)S(1)} %bitcast.17, ...), custom_call_target="tpu_custom_call" | custom-call | flops 335544320 | bytes 7417856 | tf_op jit(solution)/shard_map/pallas_call | solution.py:281
  45.2 1.0 %collective-permute-done.10.refs_0_ = bf16[544,128]{1,0:T(8,128)(2,1)S(1)} collective-permute-done((bf16[544,128]{1,0:T(8,128)(2,1)S(1)}, bf16[544,128]{1,0:T(8,128)(2,1)S(1)}, u32[]{:S(2)}, u32[]{:S(2)}) %collective-permute-start.10) | collective-permute-done | bytes 139296 | tf_op jit(solution)/shard_map/ppermute | solution.py:327
  46.5 1.0 %collective-permute-start.12 = (bf16[512,128]{1,0:T(8,128)(2,1)S(1)}, bf16[512,128]{1,0:T(8,128)(2,1)S(1)}, u32[]{:S(2)}, u32[]{:S(2)}) collective-permute-start(bf16[512,128]{1,0:T(8,128)(2,1)S(1)} %get-tuple-element.61), channel_id=1, source_target_pairs={{0,3},{1,2},{2,1},{3,0},{4,7},{5,6},{6,5},{7,4},{8,11},{9,10},{10,... | collective-permute-start | bytes 393224 | tf_op jit(solution)/shard_map/ppermute | solution.py:310
  47.5 2.0 %collective-permute-start.13 = (bf16[512,128]{1,0:T(8,128)(2,1)S(1)}, bf16[512,128]{1,0:T(8,128)(2,1)S(1)}, u32[]{:S(2)}, u32[]{:S(2)}) collective-permute-start(bf16[512,128]{1,0:T(8,128)(2,1)S(1)} %get-tuple-element.62), channel_id=1, source_target_pairs={{0,1},{1,0},{2,3},{3,2},{4,5},{5,4},{6,7},{7,6},{8,9},{9,8},{10,11... | collective-permute-start | bytes 393224 | tf_op jit(solution)/shard_map/ppermute | solution.py:310
  49.4 0.6 %collective-permute-start.11 = (bf16[512,128]{1,0:T(8,128)(2,1)S(1)}, bf16[512,128]{1,0:T(8,128)(2,1)S(1)}, u32[]{:S(2)}, u32[]{:S(2)}) collective-permute-start(bf16[512,128]{1,0:T(8,128)(2,1)S(1)} %get-tuple-element.59), channel_id=1, source_target_pairs={{0,2},{1,3},{2,0},{3,1},{4,6},{5,7},{6,4},{7,5},{8,10},{9,11},{10,... | collective-permute-start | bytes 393224 | tf_op jit(solution)/shard_map/ppermute | solution.py:310
  50.0 1.1 %collective-permute-start.15 = (f32[16,128]{1,0:T(8,128)S(1)}, f32[16,128]{1,0:T(8,128)S(1)}, u32[]{:S(2)}, u32[]{:S(2)}) collective-permute-start(f32[16,128]{1,0:T(8,128)S(1)} %get-tuple-element.65.refs_7_), channel_id=1, source_target_pairs={{0,16},{8,24},{16,0},{24,8},{1,17},{9,25},{17,1},{25,9},{2,18},{10... | collective-permute-start | bytes 24584 | tf_op jit(solution)/shard_map/ppermute | solution.py:299
  51.2 1.4 %collective-permute-done.12.refs_5_ = bf16[512,128]{1,0:T(8,128)(2,1)S(1)} collective-permute-done((bf16[512,128]{1,0:T(8,128)(2,1)S(1)}, bf16[512,128]{1,0:T(8,128)(2,1)S(1)}, u32[]{:S(2)}, u32[]{:S(2)}) %collective-permute-start.12) | collective-permute-done | bytes 131104 | tf_op jit(solution)/shard_map/ppermute | solution.py:310
  52.5 1.3 %collective-permute-done.13.refs_6_ = bf16[512,128]{1,0:T(8,128)(2,1)S(1)} collective-permute-done((bf16[512,128]{1,0:T(8,128)(2,1)S(1)}, bf16[512,128]{1,0:T(8,128)(2,1)S(1)}, u32[]{:S(2)}, u32[]{:S(2)}) %collective-permute-start.13) | collective-permute-done | bytes 131104 | tf_op jit(solution)/shard_map/ppermute | solution.py:310
  53.8 1.3 %shard_map.100 = (bf16[128,2048]{1,0:T(8,128)(2,1)}, bf16[128,2048]{1,0:T(8,128)(2,1)}) custom-call(bf16[128,2048]{1,0:T(8,128)(2,1)S(1)} %bitcast.13, bf16[128,2048]{1,0:T(8,128)(2,1)S(1)} %bitcast.18, f32[128,2048]{1,0:T(8,128)S(1)} %get-tuple-element.52.refs_2_, f32[128,2048]{1,0:T(8,128)S(1)} %get-tuple-element.53.refs_3_, ...), custom_call_target="tpu_custom_call" | custom-call | flops 67108864 | bytes 4587520 | tf_op jit(solution)/shard_map/pallas_call | solution.py:281
  55.1 0.5 collective-permute-done.16.refs_10_
  55.6 1.0 %shard_map.101 = (bf16[128,2048]{1,0:T(8,128)(2,1)}, bf16[128,2048]{1,0:T(8,128)(2,1)}, f32[16,128]{1,0:T(8,128)}) custom-call(bf16[128,2048]{1,0:T(8,128)(2,1)S(1)} %bitcast.14, bf16[128,2048]{1,0:T(8,128)(2,1)S(1)} %bitcast.19, f32[128,2048]{1,0:T(8,128)S(1)} %get-tuple-element.52.refs_2_, ...), custom_call_target="tpu_custom_call", output_to_operand_aliasing={{0}: (5, {}), {1}: (6, {})} | custom-call | flops 67108864 | bytes 5414912 | tf_op jit(solution)/shard_map/pallas_call | solution.py:281
  (22 shorter events, 0.8 us)
Async XLA Ops:
  0.6 15.2 %copy-start.1 = (bf16[1,128,2048]{2,1,0:T(8,128)(2,1)S(1)}, bf16[1,128,2048]{2,1,0:T(8,128)(2,1)}, u32[]{:S(2)}) copy-start(bf16[1,128,2048]{2,1,0:T(8,128)(2,1)} %param.7) | copy-start | bytes 1572868
  0.6 15.2 %copy-start.2 = (bf16[1,128,2048]{2,1,0:T(8,128)(2,1)S(1)}, bf16[1,128,2048]{2,1,0:T(8,128)(2,1)}, u32[]{:S(2)}) copy-start(bf16[1,128,2048]{2,1,0:T(8,128)(2,1)} %param.5) | copy-start | bytes 1572868
  2.3 13.5 %copy-start = (bf16[1,128,2048]{2,1,0:T(8,128)(2,1)S(1)}, bf16[1,128,2048]{2,1,0:T(8,128)(2,1)}, u32[]{:S(2)}) copy-start(bf16[1,128,2048]{2,1,0:T(8,128)(2,1)} %param.6) | copy-start | bytes 1572868
  2.4 7.7 %collective-permute-start = (bf16[512,128]{1,0:T(8,128)(2,1)S(1)}, bf16[512,128]{1,0:T(8,128)(2,1)S(1)}, u32[]{:S(2)}, u32[]{:S(2)}) collective-permute-start(bf16[512,128]{1,0:T(8,128)(2,1)S(1)} %get-tuple-element.40), channel_id=1, source_target_pairs={{0,1},{1,0},{2,3},{3,2},{4,5},{5,4},{6,7},{7,6},{8,10},{9,11},{10,... | collective-permute-start | bytes 393224 | tf_op jit(solution)/shard_map/ppermute | solution.py:310
  5.4 6.2 %collective-permute-start.1 = (bf16[512,128]{1,0:T(8,128)(2,1)S(1)}, bf16[512,128]{1,0:T(8,128)(2,1)S(1)}, u32[]{:S(2)}, u32[]{:S(2)}) collective-permute-start(bf16[512,128]{1,0:T(8,128)(2,1)S(1)} %get-tuple-element.41), channel_id=1, source_target_pairs={{0,2},{1,3},{2,0},{3,1},{4,6},{5,7},{6,4},{7,5},{8,9},{9,8},{10,11... | collective-permute-start | bytes 393224 | tf_op jit(solution)/shard_map/ppermute | solution.py:310
  7.0 5.9 %collective-permute-start.2 = (bf16[512,128]{1,0:T(8,128)(2,1)S(1)}, bf16[512,128]{1,0:T(8,128)(2,1)S(1)}, u32[]{:S(2)}, u32[]{:S(2)}) collective-permute-start(bf16[512,128]{1,0:T(8,128)(2,1)S(1)} %get-tuple-element.42), channel_id=1, source_target_pairs={{0,3},{1,2},{2,1},{3,0},{4,7},{5,6},{6,5},{7,4},{8,11},{9,10},{10,... | collective-permute-start | bytes 393224 | tf_op jit(solution)/shard_map/ppermute | solution.py:310
  12.9 8.3 %collective-permute-start.3 = (bf16[512,128]{1,0:T(8,128)(2,1)S(1)}, bf16[512,128]{1,0:T(8,128)(2,1)S(1)}, u32[]{:S(2)}, u32[]{:S(2)}) collective-permute-start(bf16[512,128]{1,0:T(8,128)(2,1)S(1)} %shard_map.94), channel_id=1, source_target_pairs={{0,4},{1,5},{2,6},{3,7},{4,0},{5,1},{6,2},{7,3},{8,12},{9,13},{10,... | collective-permute-start | bytes 393224 | tf_op jit(solution)/shard_map/ppermute | solution.py:327
  21.2 8.5 %copy-start.3 = (bf16[1,128,2048]{2,1,0:T(8,128)(2,1)S(1)}, bf16[1,128,2048]{2,1,0:T(8,128)(2,1)}, u32[]{:S(2)}) copy-start(bf16[1,128,2048]{2,1,0:T(8,128)(2,1)} %param.9) | copy-start | bytes 1572868
  21.5 8.2 %copy-start.4 = (f32[2048]{0:T(1024)S(1)}, f32[2048]{0:T(1024)}, u32[]{:S(2)}) copy-start(f32[2048]{0:T(1024)} %param.8) | copy-start | bytes 24580
  21.5 6.6 %collective-permute-start.4 = (bf16[512,128]{1,0:T(8,128)(2,1)S(1)}, bf16[512,128]{1,0:T(8,128)(2,1)S(1)}, u32[]{:S(2)}, u32[]{:S(2)}) collective-permute-start(bf16[512,128]{1,0:T(8,128)(2,1)S(1)} %get-tuple-element.44), channel_id=1, source_target_pairs={{0,1},{1,0},{2,3},{3,2},{4,5},{5,4},{6,7},{7,6},{8,10},{9,11},{10,... | collective-permute-start | bytes 393224 | tf_op jit(solution)/shard_map/ppermute | solution.py:310
  22.8 5.3 %collective-permute-start.5 = (bf16[512,128]{1,0:T(8,128)(2,1)S(1)}, bf16[512,128]{1,0:T(8,128)(2,1)S(1)}, u32[]{:S(2)}, u32[]{:S(2)}) collective-permute-start(bf16[512,128]{1,0:T(8,128)(2,1)S(1)} %get-tuple-element.45), channel_id=1, source_target_pairs={{0,2},{1,3},{2,0},{3,1},{4,6},{5,7},{6,4},{7,5},{8,9},{9,8},{10,11... | collective-permute-start | bytes 393224 | tf_op jit(solution)/shard_map/ppermute | solution.py:310
  23.5 6.2 %collective-permute-start.6 = (bf16[512,128]{1,0:T(8,128)(2,1)S(1)}, bf16[512,128]{1,0:T(8,128)(2,1)S(1)}, u32[]{:S(2)}, u32[]{:S(2)}) collective-permute-start(bf16[512,128]{1,0:T(8,128)(2,1)S(1)} %get-tuple-element.46), channel_id=1, source_target_pairs={{0,3},{1,2},{2,1},{3,0},{4,7},{5,6},{6,5},{7,4},{8,11},{9,10},{10,... | collective-permute-start | bytes 393224 | tf_op jit(solution)/shard_map/ppermute | solution.py:310
  30.9 6.9 %collective-permute-start.7 = (bf16[544,128]{1,0:T(8,128)(2,1)S(1)}, bf16[544,128]{1,0:T(8,128)(2,1)S(1)}, u32[]{:S(2)}, u32[]{:S(2)}) collective-permute-start(bf16[544,128]{1,0:T(8,128)(2,1)S(1)} %get-tuple-element.55), channel_id=1, source_target_pairs={{0,3},{1,2},{2,1},{3,0},{4,7},{5,6},{6,5},{7,4},{8,11},{9,10},{10,... | collective-permute-start | bytes 417800 | tf_op jit(solution)/shard_map/ppermute | solution.py:310
  33.1 5.9 %collective-permute-start.8 = (bf16[544,128]{1,0:T(8,128)(2,1)S(1)}, bf16[544,128]{1,0:T(8,128)(2,1)S(1)}, u32[]{:S(2)}, u32[]{:S(2)}) collective-permute-start(bf16[544,128]{1,0:T(8,128)(2,1)S(1)} %get-tuple-element.56), channel_id=1, source_target_pairs={{0,1},{1,0},{2,3},{3,2},{4,5},{5,4},{6,7},{7,6},{8,9},{9,8},{10,11... | collective-permute-start | bytes 417800 | tf_op jit(solution)/shard_map/ppermute | solution.py:310
  33.6 5.5 %collective-permute-start.9 = (bf16[544,128]{1,0:T(8,128)(2,1)S(1)}, bf16[544,128]{1,0:T(8,128)(2,1)S(1)}, u32[]{:S(2)}, u32[]{:S(2)}) collective-permute-start(bf16[544,128]{1,0:T(8,128)(2,1)S(1)} %get-tuple-element.57), channel_id=1, source_target_pairs={{0,2},{1,3},{2,0},{3,1},{4,6},{5,7},{6,4},{7,5},{8,10},{9,11},{10,... | collective-permute-start | bytes 417800 | tf_op jit(solution)/shard_map/ppermute | solution.py:310
  39.1 7.1 %collective-permute-start.10 = (bf16[544,128]{1,0:T(8,128)(2,1)S(1)}, bf16[544,128]{1,0:T(8,128)(2,1)S(1)}, u32[]{:S(2)}, u32[]{:S(2)}) collective-permute-start(bf16[544,128]{1,0:T(8,128)(2,1)S(1)} %shard_map.98.refs_5_), channel_id=1, source_target_pairs={{0,4},{1,5},{2,6},{3,7},{4,0},{5,1},{6,2},{7,3},{8,12},{9,13},{10,... | collective-permute-start | bytes 417800 | tf_op jit(solution)/shard_map/ppermute | solution.py:327
  46.5 6.0 %collective-permute-start.12 = (bf16[512,128]{1,0:T(8,128)(2,1)S(1)}, bf16[512,128]{1,0:T(8,128)(2,1)S(1)}, u32[]{:S(2)}, u32[]{:S(2)}) collective-permute-start(bf16[512,128]{1,0:T(8,128)(2,1)S(1)} %get-tuple-element.61), channel_id=1, source_target_pairs={{0,3},{1,2},{2,1},{3,0},{4,7},{5,6},{6,5},{7,4},{8,11},{9,10},{10,... | collective-permute-start | bytes 393224 | tf_op jit(solution)/shard_map/ppermute | solution.py:310
  47.5 6.4 %collective-permute-start.13 = (bf16[512,128]{1,0:T(8,128)(2,1)S(1)}, bf16[512,128]{1,0:T(8,128)(2,1)S(1)}, u32[]{:S(2)}, u32[]{:S(2)}) collective-permute-start(bf16[512,128]{1,0:T(8,128)(2,1)S(1)} %get-tuple-element.62), channel_id=1, source_target_pairs={{0,1},{1,0},{2,3},{3,2},{4,5},{5,4},{6,7},{7,6},{8,9},{9,8},{10,11... | collective-permute-start | bytes 393224 | tf_op jit(solution)/shard_map/ppermute | solution.py:310
  49.4 6.2 %collective-permute-start.11 = (bf16[512,128]{1,0:T(8,128)(2,1)S(1)}, bf16[512,128]{1,0:T(8,128)(2,1)S(1)}, u32[]{:S(2)}, u32[]{:S(2)}) collective-permute-start(bf16[512,128]{1,0:T(8,128)(2,1)S(1)} %get-tuple-element.59), channel_id=1, source_target_pairs={{0,2},{1,3},{2,0},{3,1},{4,6},{5,7},{6,4},{7,5},{8,10},{9,11},{10,... | collective-permute-start | bytes 393224 | tf_op jit(solution)/shard_map/ppermute | solution.py:310
  50.0 5.1 %collective-permute-start.14 = (f32[16,128]{1,0:T(8,128)S(1)}, f32[16,128]{1,0:T(8,128)S(1)}, u32[]{:S(2)}, u32[]{:S(2)}) collective-permute-start(f32[16,128]{1,0:T(8,128)S(1)} %get-tuple-element.65.refs_7_), channel_id=1, source_target_pairs={{0,8},{8,0},{16,24},{24,16},{1,9},{9,1},{17,25},{25,17},{2,10},{10... | collective-permute-start | bytes 24584 | tf_op jit(solution)/shard_map/ppermute | solution.py:299
  50.0 5.1 %collective-permute-start.15 = (f32[16,128]{1,0:T(8,128)S(1)}, f32[16,128]{1,0:T(8,128)S(1)}, u32[]{:S(2)}, u32[]{:S(2)}) collective-permute-start(f32[16,128]{1,0:T(8,128)S(1)} %get-tuple-element.65.refs_7_), channel_id=1, source_target_pairs={{0,16},{8,24},{16,0},{24,8},{1,17},{9,25},{17,1},{25,9},{2,18},{10... | collective-permute-start | bytes 24584 | tf_op jit(solution)/shard_map/ppermute | solution.py:299
  52.5 3.1 %collective-permute-start.16 = (f32[16,128]{1,0:T(8,128)S(1)}, f32[16,128]{1,0:T(8,128)S(1)}, u32[]{:S(2)}, u32[]{:S(2)}) collective-permute-start(f32[16,128]{1,0:T(8,128)S(1)} %get-tuple-element.65.refs_7_), channel_id=1, source_target_pairs={{0,24},{8,16},{16,8},{24,0},{1,25},{9,17},{17,9},{25,1},{2,26},{10... | collective-permute-start | bytes 24584 | tf_op jit(solution)/shard_map/ppermute | solution.py:299

commit v5 on v4

--- a/solution.py
+++ b/solution.py
@@ -224,14 +224,16 @@
     ref[columns(start + rows, rows), :] = (value - high.astype(F32)).astype(HALF)
 
 
-def total_kernel(size, *refs):
-    out_ref = refs[-1]
+def total_kernel(size, count, *refs):
+    refs, out_refs = refs[:count], refs[count + 1 :]
     total = refs[0][0:size, :].astype(F32)
-    for ref in refs[1:-1]:
+    for ref in refs[1:]:
         total += ref[0:size, :].astype(F32)
-    out_ref[0:size, :] = total.astype(HALF)
-    if out_ref.shape[0] > size:
-        put_wide_rows(out_ref, size, tree_sum([wide_rows(ref, size) for ref in refs[:-1]]))
+    out_refs[0][0:size, :] = total.astype(HALF)
+    if len(out_refs) > 1:
+        gain = tree_sum([wide_rows(ref, size) for ref in refs])
+        put_wide_rows(out_refs[0], size, gain)
+        out_refs[1][...] = wide_rows(out_refs[0], size)
 
 
 def group_flag(group, reverse, distance):
@@ -265,7 +267,9 @@
                 total += keep * blocks[i]
         out_refs[j][...] = total.astype(HALF)
     if riding:
-        refs[-1][...] = wide_rows(refs[0], size) + wide_rows(refs[1 + group], size)
+        terms = [refs[1 + group][...], wide_rows(refs[0], size)]
+        terms += [ref[...] for ref in refs[2 + group : -group - 1]]
+        refs[-1][...] = tree_sum(terms)
 
 
 VMEM = pl.BlockSpec(memory_space=pltpu.VMEM)
@@ -313,7 +317,7 @@
 
 def exclusive_scan(pieces, order, size, reverse, token):
     group = len(pieces)
-    count = lax.axis_size("seq")
+    count, rows = lax.axis_size("seq"), lax.axis_size("dp")
     groups = count // group
     part = functools.partial
     lanes = pieces[0].shape[1]
@@ -327,19 +331,27 @@
         return lax.ppermute(array, "seq", pairs)
 
     received = own_and_swapped(pieces, order)
-    (total,) = call(
-        part(total_kernel, size),
-        [jax.ShapeDtypeStruct(pieces[0].shape, HALF)],
-        received,
+    totals = call(
+        part(total_kernel, size, group),
+        [jax.ShapeDtypeStruct(pieces[0].shape, HALF)] + [gain_shape] * (extra > 0),
+        received + [token],
         0,
-    )
-    riding = int(extra > 0 and groups == 2)
-    gain = None
-    if extra and not riding:
-        gain = total[size : size + extra // 2].astype(F32) + total[size + extra // 2 :]
-        gain = tree_sum(summed_over("seq", group, gain))
-        total = total[:size]
-    carry = shifted(total, group)
+        ins={group: ANY},
+    )
+    total, gains = totals[0], list(totals[1:])
+    riding = int(extra > 0 and groups == 2 and rows == 4)
+    carry = shifted(total if riding else total[:size], group)
+    if riding:
+        for offset in (0, group):
+            pairs = [
+                (row * count + i, (row ^ 2) * count + (i ^ offset))
+                for row in range(rows)
+                for i in range(count)
+            ]
+            gains.append(lax.ppermute(gains[0], ("dp", "seq"), pairs))
+    elif extra:
+        gains = [tree_sum(summed_over("seq", group, gains[0]))]
+        gains = [tree_sum(summed_over("dp", 2, gains[0]))]
     distance = 1
     while distance < groups - 1:
         moved = shifted(carry, distance * group)
@@ -348,16 +360,14 @@
         )
         (carry,) = call(kernel, [piece], [carry, moved], 0)
         distance *= 2
-    inputs = [carry] + received + ([total] if riding else []) + [token]
     sums = call(
         part(scan_kernel, group, order, reverse, groups <= 2, size, riding),
         [piece] * group + [gain_shape] * riding,
-        inputs,
+        [carry] + received + (gains if riding else []),
         0,
-        ins={len(inputs) - 1: ANY},
     )
     results = own_and_swapped(sums[:group], order)
-    return results, (sums[-1] if riding else gain)
+    return results, (sums[-1] if riding else gains[0] if gains else None)
 
 
 def summed_over(axis, stride, array):
@@ -366,9 +376,7 @@
     while stride < count:
         array = tree_sum(terms)
         width = 4 if count // stride % 4 == 0 else 2
-        order = sorted(range(1, width), key=lambda i: i % 2)
-        moved = {i: swap(array, axis, i * stride) for i in order}
-        terms = [array] + [moved[i] for i in range(1, width)]
+        terms = [array] + [swap(array, axis, i * stride) for i in range(1, width)]
         stride *= width
     return terms
 
@@ -418,7 +426,7 @@
         [whole],
     )
     suffix, gain_grad = exclusive_scan(pieces, DIAGONAL_FIRST, width, True, token)
-    gains = summed_over("dp", 1, gain_grad)
+    gains = [gain_grad, swap(gain_grad, "dp", 1)]
     inputs = [k, v, key_part, value_part]
     early, late = [0, 1, 2], [3]
 

time: 56.7 us -> 57.6 us (1.016)
  waiting for transfers between devices: 22 us -> 20.5 us
  starting transfers between devices: 21.8 us -> 23 us
  local copies, waits for them, and re-layouts: 0.02 us -> 1.06 us
    ppermute x12, waiting for transfers between devices: 17.7 us -> 11.5 us  [own_and_swapped(): results.append(lax.ppermute(pieces[slot], ('dp', 'seq'), pairs))]
    ppermute x0 -> x2, waiting for transfers between devices: none -> 3.58 us  [exclusive_scan(): gains.append(lax.ppermute(gains[0], ('dp', 'seq'), pairs))]
    ppermute x0 -> x2, starting transfers between devices: none -> 1.96 us  [exclusive_scan(): gains.append(lax.ppermute(gains[0], ('dp', 'seq'), pairs))]
    ppermute x2, waiting for transfers between devices: 3.78 us -> 5.4 us  [shifted(): return lax.ppermute(array, 'seq', pairs)]
    ppermute x3 -> x1, starting transfers between devices: 1.13 us -> 0.01 us  [swap(): return lax.ppermute(array, axis, [(i, i ^ offset) for i in range(count)])]
    unnamed x10 -> x12, local copies, waits for them, and re-layouts: 0.02 us -> 1.06 us
  transfers between devices with their start and end apart: 17 -> 17, of which waited for: 12 -> 10; matrix products, arithmetic and copies ran while one was open for 0% -> 0% of each run, Pallas kernels for 13% -> 13%
where the time goes in v5:
time: 57.6 us; the launch traced here: 57.4 us
  starting transfers between devices  23 us (40%)
  waiting for transfers between devices  20.5 us (36%)
  Pallas kernels  12.1 us (21%)
  local copies, waits for them, and re-layouts  1.06 us (2%)
  between operations  0.75 us (1%)
    ppermute x12, starting transfers between devices, own_and_swapped(): results.append(lax.ppermute(pieces[slot], ('dp', 'seq'), pairs))  15.6 us
    pallas_call x10, Pallas kernels, call(): pl.pallas_call(kernel, out_shape=tuple(outs), in_specs=[ins.get(i, VMEM)...  12.1 us
    ppermute x12, waiting for transfers between devices, own_and_swapped(): results.append(lax.ppermute(pieces[slot], ('dp', 'seq'), pairs))  11.5 us
    ppermute x2, starting transfers between devices, shifted(): return lax.ppermute(array, 'seq', pairs)  5.41 us
    ppermute x2, waiting for transfers between devices, shifted(): return lax.ppermute(array, 'seq', pairs)  5.4 us
    ppermute x2, waiting for transfers between devices, exclusive_scan(): gains.append(lax.ppermute(gains[0], ('dp', 'seq'), pairs))  3.58 us
    ppermute x2, starting transfers between devices, exclusive_scan(): gains.append(lax.ppermute(gains[0], ('dp', 'seq'), pairs))  1.96 us
  transfers between devices with their start and end apart: 17, of which 10 were waited for; matrix products, arithmetic and copies ran while one was open for 0% of the time, Pallas kernels for 13%

profile of v5, /device:TPU:0, one launch (start us, length us, event | category | flops | bytes accessed | tf_op | source)
XLA Modules:
  0.0 57.4 jit_solution(13650336272812272810)
XLA Ops:
  0.7 1.7 %shard_map.93 = (bf16[512,128]{1,0:T(8,128)(2,1)S(1)}, bf16[512,128]{1,0:T(8,128)(2,1)S(1)}, bf16[512,128]{1,0:T(8,128)(2,1)S(1)}, bf16[512,128]{1,0:T(8,128)(2,1)S(1)}) custom-call(bf16[128,2048]{1,0:T(8,128)(2,1)} %bitcast.10, bf16[128,2048]{1,0:T(8,128)(2,1)} %bitcast.15), custom_call_target="tpu_custom_call" | custom-call | flops 67108864 | bytes 1572864 | tf_op jit(solution)/shard_map/pallas_call | solution.py:285
  2.3 3.0 %collective-permute-start = (bf16[512,128]{1,0:T(8,128)(2,1)S(1)}, bf16[512,128]{1,0:T(8,128)(2,1)S(1)}, u32[]{:S(2)}, u32[]{:S(2)}) collective-permute-start(bf16[512,128]{1,0:T(8,128)(2,1)S(1)} %get-tuple-element.42), channel_id=1, source_target_pairs={{0,1},{1,0},{2,3},{3,2},{4,5},{5,4},{6,7},{7,6},{8,10},{9,11},{10,... | collective-permute-start | bytes 393224 | tf_op jit(solution)/shard_map/ppermute | solution.py:314
  5.4 1.6 %collective-permute-start.1 = (bf16[512,128]{1,0:T(8,128)(2,1)S(1)}, bf16[512,128]{1,0:T(8,128)(2,1)S(1)}, u32[]{:S(2)}, u32[]{:S(2)}) collective-permute-start(bf16[512,128]{1,0:T(8,128)(2,1)S(1)} %get-tuple-element.43), channel_id=1, source_target_pairs={{0,2},{1,3},{2,0},{3,1},{4,6},{5,7},{6,4},{7,5},{8,9},{9,8},{10,11... | collective-permute-start | bytes 393224 | tf_op jit(solution)/shard_map/ppermute | solution.py:314
  7.0 1.0 %copy-done.2 = bf16[1,128,2048]{2,1,0:T(8,128)(2,1)S(1)} copy-done((bf16[1,128,2048]{2,1,0:T(8,128)(2,1)S(1)}, bf16[1,128,2048]{2,1,0:T(8,128)(2,1)}, u32[]{:S(2)}) %copy-start.2) | copy-done | bytes 524312
  8.0 2.6 %shard_map.92 = (bf16[2048,128]{1,0:T(8,128)(2,1)S(1)}, f32[128,2048]{1,0:T(8,128)S(1)}) custom-call(bf16[128,2048]{1,0:T(8,128)(2,1)S(1)} %bitcast.20, bf16[128,2048]{1,0:T(8,128)(2,1)S(1)} %bitcast.11, bf16[128,2048]{1,0:T(8,128)(2,1)S(1)} %bitcast.16), custom_call_target="tpu_custom_call" | custom-call | flops 134217728 | bytes 3145728 | tf_op jit(solution)/shard_map/pallas_call | solution.py:285
  10.6 1.0 %collective-permute-done.1.refs_2_.refs_3_ = bf16[512,128]{1,0:T(8,128)(2,1)S(1)} collective-permute-done((bf16[512,128]{1,0:T(8,128)(2,1)S(1)}, bf16[512,128]{1,0:T(8,128)(2,1)S(1)}, u32[]{:S(2)}, u32[]{:S(2)}) %collective-permute-start.1) | collective-permute-done | bytes 131104 | tf_op jit(solution)/shard_map/ppermute | solution.py:314
  11.6 1.3 %collective-permute-done.2.refs_3_.refs_4_ = bf16[512,128]{1,0:T(8,128)(2,1)S(1)} collective-permute-done((bf16[512,128]{1,0:T(8,128)(2,1)S(1)}, bf16[512,128]{1,0:T(8,128)(2,1)S(1)}, u32[]{:S(2)}, u32[]{:S(2)}) %collective-permute-start.2) | collective-permute-done | bytes 131104 | tf_op jit(solution)/shard_map/ppermute | solution.py:314
  12.9 2.9 %collective-permute-start.3 = (bf16[512,128]{1,0:T(8,128)(2,1)S(1)}, bf16[512,128]{1,0:T(8,128)(2,1)S(1)}, u32[]{:S(2)}, u32[]{:S(2)}) collective-permute-start(bf16[512,128]{1,0:T(8,128)(2,1)S(1)} %shard_map.94), channel_id=1, source_target_pairs={{0,4},{1,5},{2,6},{3,7},{4,0},{5,1},{6,2},{7,3},{8,12},{9,13},{10,... | collective-permute-start | bytes 393224 | tf_op jit(solution)/shard_map/ppermute | solution.py:331
  15.8 5.4 %collective-permute-done.3.refs_0_ = bf16[512,128]{1,0:T(8,128)(2,1)S(1)} collective-permute-done((bf16[512,128]{1,0:T(8,128)(2,1)S(1)}, bf16[512,128]{1,0:T(8,128)(2,1)S(1)}, u32[]{:S(2)}, u32[]{:S(2)}) %collective-permute-start.3) | collective-permute-done | bytes 131104 | tf_op jit(solution)/shard_map/ppermute | solution.py:331
  21.2 0.3 shard_map.95
  21.5 1.3 %collective-permute-start.4 = (bf16[512,128]{1,0:T(8,128)(2,1)S(1)}, bf16[512,128]{1,0:T(8,128)(2,1)S(1)}, u32[]{:S(2)}, u32[]{:S(2)}) collective-permute-start(bf16[512,128]{1,0:T(8,128)(2,1)S(1)} %get-tuple-element.46), channel_id=1, source_target_pairs={{0,1},{1,0},{2,3},{3,2},{4,5},{5,4},{6,7},{7,6},{8,10},{9,11},{10,... | collective-permute-start | bytes 393224 | tf_op jit(solution)/shard_map/ppermute | solution.py:314
  22.8 0.7 %collective-permute-start.5 = (bf16[512,128]{1,0:T(8,128)(2,1)S(1)}, bf16[512,128]{1,0:T(8,128)(2,1)S(1)}, u32[]{:S(2)}, u32[]{:S(2)}) collective-permute-start(bf16[512,128]{1,0:T(8,128)(2,1)S(1)} %get-tuple-element.47), channel_id=1, source_target_pairs={{0,2},{1,3},{2,0},{3,1},{4,6},{5,7},{6,4},{7,5},{8,9},{9,8},{10,11... | collective-permute-start | bytes 393224 | tf_op jit(solution)/shard_map/ppermute | solution.py:314
  23.5 1.6 %collective-permute-start.6 = (bf16[512,128]{1,0:T(8,128)(2,1)S(1)}, bf16[512,128]{1,0:T(8,128)(2,1)S(1)}, u32[]{:S(2)}, u32[]{:S(2)}) collective-permute-start(bf16[512,128]{1,0:T(8,128)(2,1)S(1)} %get-tuple-element.48), channel_id=1, source_target_pairs={{0,3},{1,2},{2,1},{3,0},{4,7},{5,6},{6,5},{7,4},{8,11},{9,10},{10,... | collective-permute-start | bytes 393224 | tf_op jit(solution)/shard_map/ppermute | solution.py:314
  25.1 3.0 %collective-permute-done.4.refs_5_.refs_9_ = bf16[512,128]{1,0:T(8,128)(2,1)S(1)} collective-permute-done((bf16[512,128]{1,0:T(8,128)(2,1)S(1)}, bf16[512,128]{1,0:T(8,128)(2,1)S(1)}, u32[]{:S(2)}, u32[]{:S(2)}) %collective-permute-start.4) | collective-permute-done | bytes 131104 | tf_op jit(solution)/shard_map/ppermute | solution.py:314
  28.1 1.6 %collective-permute-done.6.refs_7_.refs_11_ = bf16[512,128]{1,0:T(8,128)(2,1)S(1)} collective-permute-done((bf16[512,128]{1,0:T(8,128)(2,1)S(1)}, bf16[512,128]{1,0:T(8,128)(2,1)S(1)}, u32[]{:S(2)}, u32[]{:S(2)}) %collective-permute-start.6) | collective-permute-done | bytes 131104 | tf_op jit(solution)/shard_map/ppermute | solution.py:314
  29.7 1.2 %shard_map.96 = (f32[128,2048]{1,0:T(8,128)S(1)}, f32[128,128]{1,0:T(8,128)S(1)}, bf16[128,2048]{1,0:T(8,128)(2,1)S(1)}, bf16[544,128]{1,0:T(8,128)(2,1)S(1)}, b...) custom-call(bf16[128,2048]{1,0:T(8,128)(2,1)S(1)} %bitcast.21, ...), custom_call_target="tpu_custom_call" | custom-call | flops 134217728 | bytes 4825088 | tf_op jit(solution)/shard_map/pallas_call | solution.py:285
  30.9 2.2 %collective-permute-start.7 = (bf16[544,128]{1,0:T(8,128)(2,1)S(1)}, bf16[544,128]{1,0:T(8,128)(2,1)S(1)}, u32[]{:S(2)}, u32[]{:S(2)}) collective-permute-start(bf16[544,128]{1,0:T(8,128)(2,1)S(1)} %get-tuple-element.57), channel_id=1, source_target_pairs={{0,3},{1,2},{2,1},{3,0},{4,7},{5,6},{6,5},{7,4},{8,11},{9,10},{10,... | collective-permute-start | bytes 417800 | tf_op jit(solution)/shard_map/ppermute | solution.py:314
  33.2 0.4 collective-permute-start.8
  33.6 0.9 %collective-permute-start.9 = (bf16[544,128]{1,0:T(8,128)(2,1)S(1)}, bf16[544,128]{1,0:T(8,128)(2,1)S(1)}, u32[]{:S(2)}, u32[]{:S(2)}) collective-permute-start(bf16[544,128]{1,0:T(8,128)(2,1)S(1)} %get-tuple-element.59), channel_id=1, source_target_pairs={{0,2},{1,3},{2,0},{3,1},{4,6},{5,7},{6,4},{7,5},{8,10},{9,11},{10,... | collective-permute-start | bytes 417800 | tf_op jit(solution)/shard_map/ppermute | solution.py:314
  34.5 3.6 %shard_map.97 = (bf16[128,2048]{1,0:T(8,128)(2,1)}, bf16[128,2048]{1,0:T(8,128)(2,1)}, f32[128,2048]{1,0:T(8,128)S(1)}, f32[128,2048]{1,0:T(8,128)S(1)}, f32[8,128]{1,0:T(8,128)S(1)}) custom-call(bf16[128,2048]{1,0:T(8,128)(2,1)S(1)} %bitcast.22, bf16[128,2048]{1,0:T(8,128)(2,1)S(1)} %bitcast.12, bf16[128,2048]{1,0:T(8,128)(2,1)S(1)} %bitcast.17, ...), custom_call_target="tpu_custom_call" | custom-call | flops 335544320 | bytes 7417856 | tf_op jit(solution)/shard_map/pallas_call | solution.py:285
  38.1 1.0 %collective-permute-done.8.refs_2_.refs_3_ = bf16[544,128]{1,0:T(8,128)(2,1)S(1)} collective-permute-done((bf16[544,128]{1,0:T(8,128)(2,1)S(1)}, bf16[544,128]{1,0:T(8,128)(2,1)S(1)}, u32[]{:S(2)}, u32[]{:S(2)}) %collective-permute-start.8) | collective-permute-done | bytes 139296 | tf_op jit(solution)/shard_map/ppermute | solution.py:314
  39.2 2.5 %collective-permute-start.10 = (bf16[544,128]{1,0:T(8,128)(2,1)S(1)}, bf16[544,128]{1,0:T(8,128)(2,1)S(1)}, u32[]{:S(2)}, u32[]{:S(2)}) collective-permute-start(bf16[544,128]{1,0:T(8,128)(2,1)S(1)} %get-tuple-element.61), channel_id=1, source_target_pairs={{0,4},{1,5},{2,6},{3,7},{4,0},{5,1},{6,2},{7,3},{8,12},{9,13},{10,... | collective-permute-start | bytes 417800 | tf_op jit(solution)/shard_map/ppermute | solution.py:331
  41.7 1.3 %collective-permute-start.12 = (f32[16,128]{1,0:T(8,128)S(1)}, f32[16,128]{1,0:T(8,128)S(1)}, u32[]{:S(2)}, u32[]{:S(2)}) collective-permute-start(f32[16,128]{1,0:T(8,128)S(1)} %get-tuple-element.62.refs_5_), channel_id=1, source_target_pairs={{0,20},{1,21},{2,22},{3,23},{4,16},{5,17},{6,18},{7,19},{8,28},{9,... | collective-permute-start | bytes 24584 | tf_op jit(solution)/shard_map/ppermute | solution.py:351
  43.0 0.6 %collective-permute-start.11 = (f32[16,128]{1,0:T(8,128)S(1)}, f32[16,128]{1,0:T(8,128)S(1)}, u32[]{:S(2)}, u32[]{:S(2)}) collective-permute-start(f32[16,128]{1,0:T(8,128)S(1)} %get-tuple-element.62.refs_5_), channel_id=1, source_target_pairs={{0,16},{1,17},{2,18},{3,19},{4,20},{5,21},{6,22},{7,23},{8,24},{9,... | collective-permute-start | bytes 24584 | tf_op jit(solution)/shard_map/ppermute | solution.py:351
  43.6 3.6 %collective-permute-done.12.refs_7_ = f32[16,128]{1,0:T(8,128)S(1)} collective-permute-done((f32[16,128]{1,0:T(8,128)S(1)}, f32[16,128]{1,0:T(8,128)S(1)}, u32[]{:S(2)}, u32[]{:S(2)}) %collective-permute-start.12) | collective-permute-done | bytes 8224 | tf_op jit(solution)/shard_map/ppermute | solution.py:351
  47.2 0.3 shard_map.99
  47.5 2.1 %collective-permute-start.14 = (bf16[512,128]{1,0:T(8,128)(2,1)S(1)}, bf16[512,128]{1,0:T(8,128)(2,1)S(1)}, u32[]{:S(2)}, u32[]{:S(2)}) collective-permute-start(bf16[512,128]{1,0:T(8,128)(2,1)S(1)} %get-tuple-element.65), channel_id=1, source_target_pairs={{0,3},{1,2},{2,1},{3,0},{4,7},{5,6},{6,5},{7,4},{8,11},{9,10},{10,... | collective-permute-start | bytes 393224 | tf_op jit(solution)/shard_map/ppermute | solution.py:314
  49.6 1.8 %collective-permute-start.15 = (bf16[512,128]{1,0:T(8,128)(2,1)S(1)}, bf16[512,128]{1,0:T(8,128)(2,1)S(1)}, u32[]{:S(2)}, u32[]{:S(2)}) collective-permute-start(bf16[512,128]{1,0:T(8,128)(2,1)S(1)} %get-tuple-element.66), channel_id=1, source_target_pairs={{0,1},{1,0},{2,3},{3,2},{4,5},{5,4},{6,7},{7,6},{8,9},{9,8},{10,11... | collective-permute-start | bytes 393224 | tf_op jit(solution)/shard_map/ppermute | solution.py:314
  51.4 2.0 %collective-permute-done.14.refs_5_ = bf16[512,128]{1,0:T(8,128)(2,1)S(1)} collective-permute-done((bf16[512,128]{1,0:T(8,128)(2,1)S(1)}, bf16[512,128]{1,0:T(8,128)(2,1)S(1)}, u32[]{:S(2)}, u32[]{:S(2)}) %collective-permute-start.14) | collective-permute-done | bytes 131104 | tf_op jit(solution)/shard_map/ppermute | solution.py:314
  53.5 1.4 %collective-permute-done.15.refs_6_ = bf16[512,128]{1,0:T(8,128)(2,1)S(1)} collective-permute-done((bf16[512,128]{1,0:T(8,128)(2,1)S(1)}, bf16[512,128]{1,0:T(8,128)(2,1)S(1)}, u32[]{:S(2)}, u32[]{:S(2)}) %collective-permute-start.15) | collective-permute-done | bytes 131104 | tf_op jit(solution)/shard_map/ppermute | solution.py:314
  54.8 1.3 %shard_map.100 = (bf16[128,2048]{1,0:T(8,128)(2,1)}, bf16[128,2048]{1,0:T(8,128)(2,1)}) custom-call(bf16[128,2048]{1,0:T(8,128)(2,1)S(1)} %bitcast.13, bf16[128,2048]{1,0:T(8,128)(2,1)S(1)} %bitcast.18, f32[128,2048]{1,0:T(8,128)S(1)} %get-tuple-element.54.refs_2_, f32[128,2048]{1,0:T(8,128)S(1)} %get-tuple-element.55.refs_3_, ...), custom_call_target="tpu_custom_call" | custom-call | flops 67108864 | bytes 4587520 | tf_op jit(solution)/shard_map/pallas_call | solution.py:285
  56.4 1.0 %shard_map.101 = (bf16[128,2048]{1,0:T(8,128)(2,1)}, bf16[128,2048]{1,0:T(8,128)(2,1)}, f32[16,128]{1,0:T(8,128)}) custom-call(bf16[128,2048]{1,0:T(8,128)(2,1)S(1)} %bitcast.14, bf16[128,2048]{1,0:T(8,128)(2,1)S(1)} %bitcast.19, f32[128,2048]{1,0:T(8,128)S(1)} %get-tuple-element.54.refs_2_, ...), custom_call_target="tpu_custom_call", output_to_operand_aliasing={{0}: (5, {}), {1}: (6, {})} | custom-call | flops 67108864 | bytes 5398528 | tf_op jit(solution)/shard_map/pallas_call | solution.py:285
  (24 shorter events, 0.5 us)
Async XLA Ops:
  0.6 6.3 %copy-start = (bf16[1,128,2048]{2,1,0:T(8,128)(2,1)S(1)}, bf16[1,128,2048]{2,1,0:T(8,128)(2,1)}, u32[]{:S(2)}) copy-start(bf16[1,128,2048]{2,1,0:T(8,128)(2,1)} %param.6) | copy-start | bytes 1572868
  0.6 6.3 %copy-start.1 = (bf16[1,128,2048]{2,1,0:T(8,128)(2,1)S(1)}, bf16[1,128,2048]{2,1,0:T(8,128)(2,1)}, u32[]{:S(2)}) copy-start(bf16[1,128,2048]{2,1,0:T(8,128)(2,1)} %param.7) | copy-start | bytes 1572868
  2.3 8.3 %collective-permute-start = (bf16[512,128]{1,0:T(8,128)(2,1)S(1)}, bf16[512,128]{1,0:T(8,128)(2,1)S(1)}, u32[]{:S(2)}, u32[]{:S(2)}) collective-permute-start(bf16[512,128]{1,0:T(8,128)(2,1)S(1)} %get-tuple-element.42), channel_id=1, source_target_pairs={{0,1},{1,0},{2,3},{3,2},{4,5},{5,4},{6,7},{7,6},{8,10},{9,11},{10,... | collective-permute-start | bytes 393224 | tf_op jit(solution)/shard_map/ppermute | solution.py:314
  5.4 6.2 %collective-permute-start.1 = (bf16[512,128]{1,0:T(8,128)(2,1)S(1)}, bf16[512,128]{1,0:T(8,128)(2,1)S(1)}, u32[]{:S(2)}, u32[]{:S(2)}) collective-permute-start(bf16[512,128]{1,0:T(8,128)(2,1)S(1)} %get-tuple-element.43), channel_id=1, source_target_pairs={{0,2},{1,3},{2,0},{3,1},{4,6},{5,7},{6,4},{7,5},{8,9},{9,8},{10,11... | collective-permute-start | bytes 393224 | tf_op jit(solution)/shard_map/ppermute | solution.py:314
  7.0 5.9 %collective-permute-start.2 = (bf16[512,128]{1,0:T(8,128)(2,1)S(1)}, bf16[512,128]{1,0:T(8,128)(2,1)S(1)}, u32[]{:S(2)}, u32[]{:S(2)}) collective-permute-start(bf16[512,128]{1,0:T(8,128)(2,1)S(1)} %get-tuple-element.44), channel_id=1, source_target_pairs={{0,3},{1,2},{2,1},{3,0},{4,7},{5,6},{6,5},{7,4},{8,11},{9,10},{10,... | collective-permute-start | bytes 393224 | tf_op jit(solution)/shard_map/ppermute | solution.py:314
  7.0 1.0 %copy-start.2 = (bf16[1,128,2048]{2,1,0:T(8,128)(2,1)S(1)}, bf16[1,128,2048]{2,1,0:T(8,128)(2,1)}, u32[]{:S(2)}) copy-start(bf16[1,128,2048]{2,1,0:T(8,128)(2,1)} %param.5) | copy-start | bytes 1572868
  12.8 16.9 %copy-start.4 = (bf16[1,128,2048]{2,1,0:T(8,128)(2,1)S(1)}, bf16[1,128,2048]{2,1,0:T(8,128)(2,1)}, u32[]{:S(2)}) copy-start(bf16[1,128,2048]{2,1,0:T(8,128)(2,1)} %param.9) | copy-start | bytes 1572868
  12.9 16.8 %copy-start.3 = (bf16[1,128,2048]{2,1,0:T(8,128)(2,1)S(1)}, bf16[1,128,2048]{2,1,0:T(8,128)(2,1)}, u32[]{:S(2)}) copy-start(bf16[1,128,2048]{2,1,0:T(8,128)(2,1)} %param.5) | copy-start | bytes 1572868
  12.9 8.3 %collective-permute-start.3 = (bf16[512,128]{1,0:T(8,128)(2,1)S(1)}, bf16[512,128]{1,0:T(8,128)(2,1)S(1)}, u32[]{:S(2)}, u32[]{:S(2)}) collective-permute-start(bf16[512,128]{1,0:T(8,128)(2,1)S(1)} %shard_map.94), channel_id=1, source_target_pairs={{0,4},{1,5},{2,6},{3,7},{4,0},{5,1},{6,2},{7,3},{8,12},{9,13},{10,... | collective-permute-start | bytes 393224 | tf_op jit(solution)/shard_map/ppermute | solution.py:331
  21.5 8.2 %copy-start.5 = (f32[2048]{0:T(1024)S(1)}, f32[2048]{0:T(1024)}, u32[]{:S(2)}) copy-start(f32[2048]{0:T(1024)} %param.8) | copy-start | bytes 24580
  21.5 6.6 %collective-permute-start.4 = (bf16[512,128]{1,0:T(8,128)(2,1)S(1)}, bf16[512,128]{1,0:T(8,128)(2,1)S(1)}, u32[]{:S(2)}, u32[]{:S(2)}) collective-permute-start(bf16[512,128]{1,0:T(8,128)(2,1)S(1)} %get-tuple-element.46), channel_id=1, source_target_pairs={{0,1},{1,0},{2,3},{3,2},{4,5},{5,4},{6,7},{7,6},{8,10},{9,11},{10,... | collective-permute-start | bytes 393224 | tf_op jit(solution)/shard_map/ppermute | solution.py:314
  22.8 5.3 %collective-permute-start.5 = (bf16[512,128]{1,0:T(8,128)(2,1)S(1)}, bf16[512,128]{1,0:T(8,128)(2,1)S(1)}, u32[]{:S(2)}, u32[]{:S(2)}) collective-permute-start(bf16[512,128]{1,0:T(8,128)(2,1)S(1)} %get-tuple-element.47), channel_id=1, source_target_pairs={{0,2},{1,3},{2,0},{3,1},{4,6},{5,7},{6,4},{7,5},{8,9},{9,8},{10,11... | collective-permute-start | bytes 393224 | tf_op jit(solution)/shard_map/ppermute | solution.py:314
  23.5 6.2 %collective-permute-start.6 = (bf16[512,128]{1,0:T(8,128)(2,1)S(1)}, bf16[512,128]{1,0:T(8,128)(2,1)S(1)}, u32[]{:S(2)}, u32[]{:S(2)}) collective-permute-start(bf16[512,128]{1,0:T(8,128)(2,1)S(1)} %get-tuple-element.48), channel_id=1, source_target_pairs={{0,3},{1,2},{2,1},{3,0},{4,7},{5,6},{6,5},{7,4},{8,11},{9,10},{10,... | collective-permute-start | bytes 393224 | tf_op jit(solution)/shard_map/ppermute | solution.py:314
  30.9 7.1 %collective-permute-start.7 = (bf16[544,128]{1,0:T(8,128)(2,1)S(1)}, bf16[544,128]{1,0:T(8,128)(2,1)S(1)}, u32[]{:S(2)}, u32[]{:S(2)}) collective-permute-start(bf16[544,128]{1,0:T(8,128)(2,1)S(1)} %get-tuple-element.57), channel_id=1, source_target_pairs={{0,3},{1,2},{2,1},{3,0},{4,7},{5,6},{6,5},{7,4},{8,11},{9,10},{10,... | collective-permute-start | bytes 417800 | tf_op jit(solution)/shard_map/ppermute | solution.py:314
  33.2 5.9 %collective-permute-start.8 = (bf16[544,128]{1,0:T(8,128)(2,1)S(1)}, bf16[544,128]{1,0:T(8,128)(2,1)S(1)}, u32[]{:S(2)}, u32[]{:S(2)}) collective-permute-start(bf16[544,128]{1,0:T(8,128)(2,1)S(1)} %get-tuple-element.58), channel_id=1, source_target_pairs={{0,1},{1,0},{2,3},{3,2},{4,5},{5,4},{6,7},{7,6},{8,9},{9,8},{10,11... | collective-permute-start | bytes 417800 | tf_op jit(solution)/shard_map/ppermute | solution.py:314
  33.6 5.5 %collective-permute-start.9 = (bf16[544,128]{1,0:T(8,128)(2,1)S(1)}, bf16[544,128]{1,0:T(8,128)(2,1)S(1)}, u32[]{:S(2)}, u32[]{:S(2)}) collective-permute-start(bf16[544,128]{1,0:T(8,128)(2,1)S(1)} %get-tuple-element.59), channel_id=1, source_target_pairs={{0,2},{1,3},{2,0},{3,1},{4,6},{5,7},{6,4},{7,5},{8,10},{9,11},{10,... | collective-permute-start | bytes 417800 | tf_op jit(solution)/shard_map/ppermute | solution.py:314
  39.2 8.0 %collective-permute-start.10 = (bf16[544,128]{1,0:T(8,128)(2,1)S(1)}, bf16[544,128]{1,0:T(8,128)(2,1)S(1)}, u32[]{:S(2)}, u32[]{:S(2)}) collective-permute-start(bf16[544,128]{1,0:T(8,128)(2,1)S(1)} %get-tuple-element.61), channel_id=1, source_target_pairs={{0,4},{1,5},{2,6},{3,7},{4,0},{5,1},{6,2},{7,3},{8,12},{9,13},{10,... | collective-permute-start | bytes 417800 | tf_op jit(solution)/shard_map/ppermute | solution.py:331
  41.7 5.5 %collective-permute-start.12 = (f32[16,128]{1,0:T(8,128)S(1)}, f32[16,128]{1,0:T(8,128)S(1)}, u32[]{:S(2)}, u32[]{:S(2)}) collective-permute-start(f32[16,128]{1,0:T(8,128)S(1)} %get-tuple-element.62.refs_5_), channel_id=1, source_target_pairs={{0,20},{1,21},{2,22},{3,23},{4,16},{5,17},{6,18},{7,19},{8,28},{9,... | collective-permute-start | bytes 24584 | tf_op jit(solution)/shard_map/ppermute | solution.py:351
  43.0 4.2 %collective-permute-start.11 = (f32[16,128]{1,0:T(8,128)S(1)}, f32[16,128]{1,0:T(8,128)S(1)}, u32[]{:S(2)}, u32[]{:S(2)}) collective-permute-start(f32[16,128]{1,0:T(8,128)S(1)} %get-tuple-element.62.refs_5_), channel_id=1, source_target_pairs={{0,16},{1,17},{2,18},{3,19},{4,20},{5,21},{6,22},{7,23},{8,24},{9,... | collective-permute-start | bytes 24584 | tf_op jit(solution)/shard_map/ppermute | solution.py:351
  47.5 6.0 %collective-permute-start.14 = (bf16[512,128]{1,0:T(8,128)(2,1)S(1)}, bf16[512,128]{1,0:T(8,128)(2,1)S(1)}, u32[]{:S(2)}, u32[]{:S(2)}) collective-permute-start(bf16[512,128]{1,0:T(8,128)(2,1)S(1)} %get-tuple-element.65), channel_id=1, source_target_pairs={{0,3},{1,2},{2,1},{3,0},{4,7},{5,6},{6,5},{7,4},{8,11},{9,10},{10,... | collective-permute-start | bytes 393224 | tf_op jit(solution)/shard_map/ppermute | solution.py:314
  49.6 5.2 %collective-permute-start.15 = (bf16[512,128]{1,0:T(8,128)(2,1)S(1)}, bf16[512,128]{1,0:T(8,128)(2,1)S(1)}, u32[]{:S(2)}, u32[]{:S(2)}) collective-permute-start(bf16[512,128]{1,0:T(8,128)(2,1)S(1)} %get-tuple-element.66), channel_id=1, source_target_pairs={{0,1},{1,0},{2,3},{3,2},{4,5},{5,4},{6,7},{7,6},{8,9},{9,8},{10,11... | collective-permute-start | bytes 393224 | tf_op jit(solution)/shard_map/ppermute | solution.py:314
  51.4 5.0 %collective-permute-start.13 = (bf16[512,128]{1,0:T(8,128)(2,1)S(1)}, bf16[512,128]{1,0:T(8,128)(2,1)S(1)}, u32[]{:S(2)}, u32[]{:S(2)}) collective-permute-start(bf16[512,128]{1,0:T(8,128)(2,1)S(1)} %get-tuple-element.63), channel_id=1, source_target_pairs={{0,2},{1,3},{2,0},{3,1},{4,6},{5,7},{6,4},{7,5},{8,10},{9,11},{10,... | collective-permute-start | bytes 393224 | tf_op jit(solution)/shard_map/ppermute | solution.py:314
  51.4 4.7 %collective-permute-start.16 = (f32[16,128]{1,0:T(8,128)S(1)}, f32[16,128]{1,0:T(8,128)S(1)}, u32[]{:S(2)}, u32[]{:S(2)}) collective-permute-start(f32[16,128]{1,0:T(8,128)S(1)} %get-tuple-element.69.refs_7_), channel_id=1, source_target_pairs={{0,8},{8,0},{16,24},{24,16},{1,9},{9,1},{17,25},{25,17},{2,10},{10... | collective-permute-start | bytes 24584 | tf_op jit(solution)/shard_map/ppermute | solution.py:303

commit v6 on v4

--- a/solution.py
+++ b/solution.py
@@ -64,12 +64,16 @@
 def state_kernel(head, group, k_ref, v_ref, *refs):
     piece_refs = refs[:group]
     whole_ref, k_buffer, v_buffer, arrived = refs[group:]
-    copies = [
-        pltpu.make_async_copy(k_ref, k_buffer, arrived.at[0]),
-        pltpu.make_async_copy(v_ref, v_buffer, arrived.at[1]),
-    ]
-    for copy in copies:
-        copy.start()
+    step = k_buffer.shape[0] // arrived.shape[1]
+    copies = []
+    for i in range(arrived.shape[1]):
+        part = columns(i * step, step)
+        for n, (ref, buffer) in enumerate(((k_ref, k_buffer), (v_ref, v_buffer))):
+            copy = pltpu.make_async_copy(
+                ref.at[part, :], buffer.at[part, :], arrived.at[n, i]
+            )
+            copy.start()
+            copies.append(copy)
     for copy in copies:
         copy.wait()
     for h in range(HEADS):
@@ -90,67 +94,113 @@
         intra_ref[:, part] = dot(scores, v_ref[:, part], 1, 0)
 
 
-def norm_kernel(head, group, replicas, *refs):
-    q_ref, intra_ref, gain_ref, cot_ref = refs[:4]
-    prefix_refs = refs[4 : 4 + group]
-    attended_ref, inverse_ref, grad_ref = refs[4 + group : 7 + group]
-    piece_refs = refs[7 + group : 7 + 2 * group]
-    whole_ref, gain_grad_ref = refs[7 + 2 * group :]
-    rows = q_ref.shape[0]
+def features_at(order, slot, i, width, head):
+    start = partner_of(order, slot) * width + i * head
+    return pl.ds(pl.multiple_of(start, head), head)
+
+
+def attend(head, order, slot, refs, prefix_ref, attended_ref, at, squares, inner):
+    q_ref, intra_ref, gain_ref, cot_ref = refs
     scaling = head ** (-0.5)
-    features = HEADS * head
-    size = features // group
-    gathered(CROSSED, prefix_refs, size, whole_ref)
-    squares = jnp.zeros((rows, head), F32)
-    inner = jnp.zeros((rows, head), F32)
-    for h in range(HEADS):
-        part = columns(h * head, head)
-        attended = intra_ref[:, part] + scaling * dot(
-            q_ref[:, part], whole_ref[part, :], 1, 0
-        )
-        attended_ref[:, part] = attended
-        scaled = cot_ref[:, part].astype(F32) * gain_ref[h : h + 1, :]
+    width = prefix_ref.shape[0]
+    for i in range(width // head):
+        part = features_at(order, slot, i, width, head)
+        prefix = prefix_ref[columns(i * head, head), :]
+        attended = intra_ref[:, part] + scaling * dot(q_ref[:, part], prefix, 1, 0)
+        attended_ref[:, part if at is None else columns(i * head, head)] = attended
+        scaled = cot_ref[:, part].astype(F32) * gain_ref[:, part]
         squares += attended * attended
         inner += scaled * attended
+    return squares, inner
+
+
+def early_norm_kernel(head, order, *refs):
+    prefix_refs, (attended_ref, squares_ref, inner_ref) = refs[4:-3], refs[-3:]
+    squares = jnp.zeros(squares_ref.shape, F32)
+    inner = jnp.zeros(squares_ref.shape, F32)
+    for slot, prefix_ref in enumerate(prefix_refs):
+        squares, inner = attend(
+            head, order, slot, refs[:4], prefix_ref, attended_ref, None, squares, inner
+        )
+    squares_ref[...] = squares
+    inner_ref[...] = inner
+
+
+def norm_kernel(head, group, orders, replicas, *refs):
+    q_ref, _, gain_ref, cot_ref = refs[:4]
+    early_ref, squares_ref, inner_ref, prefix_ref = refs[4:8]
+    late_ref, inverse_ref, grad_ref = refs[8:11]
+    piece_refs = refs[11 : 11 + group]
+    gain_grad_ref, gain_rows_ref = refs[11 + group :]
+    features = q_ref.shape[1]
+    width = features // group
+    last = orders[0][0][group - 1]
+    squares, inner = attend(
+        head,
+        orders[0],
+        group - 1,
+        refs[:4],
+        prefix_ref,
+        late_ref,
+        0,
+        squares_ref[...],
+        inner_ref[...],
+    )
     inverse = lax.rsqrt(
         jnp.sum(squares, axis=1, keepdims=True) * (1.0 / features) + EPSILON
     )
     inner_mean = jnp.sum(inner, axis=1, keepdims=True) * (1.0 / features) * inverse
     inverse_ref[...] = jnp.broadcast_to(inverse, inverse_ref.shape)
+    scaling = head ** (-0.5)
+    for slot in range(group):
+        for i in range(width // head):
+            part = features_at(orders[1], slot, i, width, head)
+            local = columns(i * head, head)
+            if orders[1][0][slot] == last:
+                attended = late_ref[:, local]
+            else:
+                attended = early_ref[:, part]
+            normalized = attended * inverse
+            upstream = cot_ref[:, part].astype(F32)
+            gain_grad_ref[:, part] = jnp.sum(
+                upstream * normalized, axis=0, keepdims=True
+            ) * (1.0 / replicas)
+            scaled = upstream * gain_ref[:, part]
+            grad = ((scaled - normalized * inner_mean) * inverse).astype(HALF)
+            grad_ref[:, part] = grad
+            piece_refs[slot][local, :] = (
+                scaling * dot(q_ref[:, part], grad, 0, 0)
+            ).astype(HALF)
     for h in range(HEADS):
-        part = columns(h * head, head)
-        normalized = attended_ref[:, part] * inverse
-        upstream = cot_ref[:, part].astype(F32)
-        gain = gain_ref[h : h + 1, :]
-        gain_grad_ref[h : h + 1, :] = jnp.sum(
-            upstream * normalized, axis=0, keepdims=True
-        ) * (1.0 / replicas)
-        grad = ((upstream * gain - normalized * inner_mean) * inverse).astype(HALF)
-        grad_ref[:, part] = grad
-        whole_ref[part, :] = (scaling * dot(q_ref[:, part], grad, 0, 0)).astype(HALF)
-    scattered(DIAGONAL_FIRST, whole_ref, size, piece_refs)
+        gain_rows_ref[h : h + 1, :] = gain_grad_ref[:, columns(h * head, head)]
     for ref in piece_refs:
-        put_wide_rows(ref, size, gain_grad_ref[...])
+        put_wide_rows(ref, width, gain_rows_ref[...])
 
 
 def backward_kernel(head, group, *refs):
     q_ref, k_ref, v_ref, scores_ref, grad_ref = refs[:5]
-    attended_ref, inverse_ref, gain_ref = refs[5:8]
-    prefix_refs = refs[8 : 8 + group]
+    early_ref, late_ref, inverse_ref, gain_ref = refs[5:9]
+    prefix_refs = refs[9 : 9 + group]
     out_ref, grad_query_ref, key_part_ref, value_part_ref, token_ref = refs[
-        8 + group : 13 + group
+        9 + group : 14 + group
     ]
-    whole_ref = refs[13 + group]
+    whole_ref = refs[14 + group]
     rows = q_ref.shape[0]
     mask = causal(rows)
     scaling = head ** (-0.5)
     gathered(CROSSED, prefix_refs, prefix_refs[0].shape[0], whole_ref)
     inverse = inverse_ref[...]
+    width = late_ref.shape[1]
+    for slot in range(group):
+        for i in range(width // head):
+            part = features_at(CROSSED, slot, i, width, head)
+            if slot == group - 1:
+                attended = late_ref[:, columns(i * head, head)]
+            else:
+                attended = early_ref[:, part]
+            out_ref[:, part] = (gain_ref[:, part] * (attended * inverse)).astype(HALF)
     for h in range(HEADS):
         part = columns(h * head, head)
-        out_ref[:, part] = (
-            gain_ref[h : h + 1, :] * (attended_ref[:, part] * inverse)
-        ).astype(HALF)
         grad = grad_ref[:, part]
         grad_scores = dot(grad, v_ref[:, part], 1, 1)
         grad_scores = jnp.where(mask, grad_scores, 0.0).astype(HALF)
@@ -165,39 +215,36 @@
     token_ref[...] = jnp.zeros_like(token_ref)
 
 
-def final_kernel(head, chunks, last, *refs):
-    k_ref, v_ref, key_part_ref, value_part_ref = refs[:4]
-    suffix_refs = refs[4 : 4 + len(chunks)]
-    refs = refs[4 + len(suffix_refs) :]
+def final_kernel(head, slot, last, *refs):
+    k_ref, v_ref, key_part_ref, value_part_ref, suffix_ref = refs[:5]
     copies = []
     if last:
         gain_grad_ref, total_ref, gain_written = refs[-6], refs[-2], refs[-1]
-        total_ref[...] = tree_sum([ref[...] for ref in refs[2:-8]])
+        total_ref[...] = tree_sum([ref[...] for ref in refs[7:-8]])
         copies.append(pltpu.make_async_copy(total_ref, gain_grad_ref, gain_written))
         copies[0].start()
         out_refs, refs = refs[-8:-6], refs[-5:-2]
     else:
-        out_refs, refs = refs[:2], refs[2:]
-    key_buffer, value_buffer, written = refs
-    width = key_buffer.shape[2]
-    for n, chunk in enumerate(chunks):
-        suffix_ref = suffix_refs[n]
-        start = partner_of(DIAGONAL_FIRST, chunk) * width
-        for i in range(width // head):
-            part = pl.ds(pl.multiple_of(start + i * head, head), head)
-            local = columns(i * head, head)
-            suffix = suffix_ref[local, :]
-            key_buffer[n, :, local] = (
-                key_part_ref[:, part] + dot(v_ref[:, part], suffix, 1, 1)
-            ).astype(HALF)
-            value_buffer[n, :, local] = (
-                value_part_ref[:, part] + dot(k_ref[:, part], suffix, 1, 0)
-            ).astype(HALF)
-        for i, buffer in enumerate((key_buffer, value_buffer)):
+        out_refs, refs = refs[-5:-3], refs[-3:]
+    buffers, written = refs[:2], refs[2]
+    rows, width = buffers[0].shape
+    for i in range(width // head):
+        part = features_at(DIAGONAL_FIRST, slot, i, width, head)
+        local = columns(i * head, head)
+        suffix = suffix_ref[local, :]
+        buffers[0][:, local] = (
+            key_part_ref[:, part] + dot(v_ref[:, part], suffix, 1, 1)
+        ).astype(HALF)
+        buffers[1][:, local] = (
+            value_part_ref[:, part] + dot(k_ref[:, part], suffix, 1, 0)
+        ).astype(HALF)
+    block = block_at(partner_of(DIAGONAL_FIRST, slot), width)
+    step = rows // written.shape[1]
+    for n in range(written.shape[1]):
+        part = columns(n * step, step)
+        for i in range(2):
             copy = pltpu.make_async_copy(
-                buffer.at[n],
-                out_refs[i].at[:, block_at(partner_of(DIAGONAL_FIRST, chunk), width)],
-                written.at[i, n],
+                buffers[i].at[part, :], out_refs[i].at[part, block], written.at[i, n]
             )
             copy.start()
             copies.append(copy)
@@ -388,7 +435,7 @@
     gain_shape = jax.ShapeDtypeStruct((HEADS, head), F32)
     token_shape = jax.ShapeDtypeStruct((8, head), F32)
     whole = pltpu.VMEM((features, head), HALF)
-    gain_rows = gain.reshape(HEADS, head)
+    gain_row = gain.reshape(1, features)
 
     pieces = call(
         part(state_kernel, head, group),
@@ -397,56 +444,54 @@
         1,
         [whole]
         + [pltpu.VMEM((rows, features), HALF)] * 2
-        + [pltpu.SemaphoreType.DMA((2,))],
+        + [pltpu.SemaphoreType.DMA((2, 4))],
         ins={0: HBM, 1: HBM},
     )
     scores, intra = call(part(local_kernel, head), [scores_shape, wide], [q, k, v], 2)
     prefix, _ = exclusive_scan(pieces, CROSSED, width, False, intra)
     message = jax.ShapeDtypeStruct((width + 2 * HEADS, head), HALF)
-    attended, inverse, grad, *pieces = call(
-        part(norm_kernel, head, group, lax.axis_size("dp")),
-        [wide, square, half] + [message] * group,
-        [q, intra, gain_rows, cot] + prefix,
+    sources = [q, intra, gain_row, cot]
+    early, squares, inner = call(
+        part(early_norm_kernel, head, CROSSED),
+        [wide, square, square],
+        sources + prefix[:-1],
+        1,
+    )
+    late, inverse, grad, *pieces = call(
+        part(norm_kernel, head, group, (CROSSED, DIAGONAL_FIRST), lax.axis_size("dp")),
+        [jax.ShapeDtypeStruct((rows, width), F32), square, half] + [message] * group,
+        sources + [early, squares, inner, prefix[-1]],
         2,
-        [whole, pltpu.VMEM((HEADS, head), F32)],
+        [pltpu.VMEM((1, features), F32), pltpu.VMEM((HEADS, head), F32)],
     )
     output, grad_query, key_part, value_part, token = call(
         part(backward_kernel, head, group),
         [half, half, wide, wide, token_shape],
-        [q, k, v, scores, grad, attended, inverse, gain_rows] + prefix,
+        [q, k, v, scores, grad, early, late, inverse, gain_row] + prefix,
         5,
         [whole],
     )
     suffix, gain_grad = exclusive_scan(pieces, DIAGONAL_FIRST, width, True, token)
     gains = summed_over("dp", 1, gain_grad)
     inputs = [k, v, key_part, value_part]
-    early, late = [0, 1, 2], [3]
-
-    def buffers(count):
-        return [pltpu.VMEM((count, rows, width), HALF)] * 2 + [
-            pltpu.SemaphoreType.DMA((2, count))
-        ]
-
-    first = call(
-        part(final_kernel, head, early, False),
-        [half, half],
-        inputs + [suffix[j] for j in early],
-        1,
-        buffers(len(early)),
-        out_specs={0: HBM, 1: HBM},
-    )
-    at = len(inputs) + len(late)
-    grad_key, grad_value, gain_grad = call(
-        part(final_kernel, head, late, True),
-        [half, half, gain_shape],
-        inputs + [suffix[j] for j in late] + list(first) + gains,
-        1,
-        buffers(len(late))
-        + [pltpu.VMEM((HEADS, head), F32), pltpu.SemaphoreType.DMA(())],
-        ins={at: HBM, at + 1: HBM},
-        out_specs={0: HBM, 1: HBM, 2: HBM},
-        aliases={at: 0, at + 1: 1},
-    )
+    outs = []
+    for slot in range(group):
+        last = slot == group - 1
+        args = inputs + [suffix[slot]] + outs + (gains if last else [])
+        at = len(inputs) + 1
+        *outs, gain_grad = call(
+            part(final_kernel, head, slot, last),
+            [half, half] + [gain_shape] * last,
+            args,
+            1,
+            [pltpu.VMEM((rows, width), HALF)] * 2
+            + [pltpu.SemaphoreType.DMA((2, 2))]
+            + [pltpu.VMEM((HEADS, head), F32), pltpu.SemaphoreType.DMA(())] * last,
+            ins={at + i: HBM for i in range(len(outs))},
+            out_specs={0: HBM, 1: HBM, 2: HBM},
+            aliases={at + i: i for i in range(len(outs))},
+        ) + (() if last else (None,))
+    grad_key, grad_value = outs
     return (
         output[None],
         grad_query[None],

time: 56.7 us -> 56.6 us (level)
  waiting for transfers between devices: 22 us -> 19 us
  Pallas kernels: 12 us -> 14 us
  starting transfers between devices: 21.8 us -> 22.7 us
    ppermute x12, waiting for transfers between devices: 17.7 us -> 14.7 us  [own_and_swapped(): results.append(lax.ppermute(pieces[slot], ('dp', 'seq'), pairs))]
    pallas_call x10 -> x13, Pallas kernels: 12 us -> 14 us  [call(): pl.pallas_call(kernel, out_shape=tuple(outs), in_specs=[ins.get(i, VMEM)...]
    ppermute x3, starting transfers between devices: 1.13 us -> 1.89 us  [swap(): return lax.ppermute(array, axis, [(i, i ^ offset) for i in range(count)])]
  transfers between devices with their start and end apart: 17 -> 17, of which waited for: 12 -> 11; matrix products, arithmetic and copies ran while one was open for 0% -> 0% of each run, Pallas kernels for 13% -> 17%
where the time goes in v6:
time: 56.6 us; the launch traced here: 56.5 us
  starting transfers between devices  22.7 us (40%)
  waiting for transfers between devices  19 us (34%)
  Pallas kernels  14 us (25%)
  between operations  0.76 us (1%)
    ppermute x12, starting transfers between devices, own_and_swapped(): results.append(lax.ppermute(pieces[slot], ('dp', 'seq'), pairs))  15.3 us
    ppermute x12, waiting for transfers between devices, own_and_swapped(): results.append(lax.ppermute(pieces[slot], ('dp', 'seq'), pairs))  14.7 us
    pallas_call x13, Pallas kernels, call(): pl.pallas_call(kernel, out_shape=tuple(outs), in_specs=[ins.get(i, VMEM)...  14 us
    ppermute x2, starting transfers between devices, shifted(): return lax.ppermute(array, 'seq', pairs)  5.56 us
    ppermute x2, waiting for transfers between devices, shifted(): return lax.ppermute(array, 'seq', pairs)  3.7 us
    ppermute x3, starting transfers between devices, swap(): return lax.ppermute(array, axis, [(i, i ^ offset) for i in range(count)])  1.89 us
  transfers between devices with their start and end apart: 17, of which 11 were waited for; matrix products, arithmetic and copies ran while one was open for 0% of the time, Pallas kernels for 17%

profile of v6, /device:TPU:0, one launch (start us, length us, event | category | flops | bytes accessed | tf_op | source)
XLA Modules:
  0.0 56.5 jit_solution(3559906468156416130)
XLA Ops:
  0.7 1.8 %shard_map.93 = (bf16[512,128]{1,0:T(8,128)(2,1)S(1)}, bf16[512,128]{1,0:T(8,128)(2,1)S(1)}, bf16[512,128]{1,0:T(8,128)(2,1)S(1)}, bf16[512,128]{1,0:T(8,128)(2,1)S(1)}) custom-call(bf16[128,2048]{1,0:T(8,128)(2,1)} %bitcast.10, bf16[128,2048]{1,0:T(8,128)(2,1)} %bitcast.17), custom_call_target="tpu_custom_call" | custom-call | flops 67108864 | bytes 1572864 | tf_op jit(solution)/shard_map/pallas_call | solution.py:328
  2.5 3.0 %collective-permute-start = (bf16[512,128]{1,0:T(8,128)(2,1)S(1)}, bf16[512,128]{1,0:T(8,128)(2,1)S(1)}, u32[]{:S(2)}, u32[]{:S(2)}) collective-permute-start(bf16[512,128]{1,0:T(8,128)(2,1)S(1)} %get-tuple-element.47), channel_id=1, source_target_pairs={{0,1},{1,0},{2,3},{3,2},{4,5},{5,4},{6,7},{7,6},{8,10},{9,11},{10,... | collective-permute-start | bytes 393224 | tf_op jit(solution)/shard_map/ppermute | solution.py:357
  5.5 1.6 %collective-permute-start.1 = (bf16[512,128]{1,0:T(8,128)(2,1)S(1)}, bf16[512,128]{1,0:T(8,128)(2,1)S(1)}, u32[]{:S(2)}, u32[]{:S(2)}) collective-permute-start(bf16[512,128]{1,0:T(8,128)(2,1)S(1)} %get-tuple-element.48), channel_id=1, source_target_pairs={{0,2},{1,3},{2,0},{3,1},{4,6},{5,7},{6,4},{7,5},{8,9},{9,8},{10,11... | collective-permute-start | bytes 393224 | tf_op jit(solution)/shard_map/ppermute | solution.py:357
  7.1 3.1 %collective-permute-done.refs_1_.refs_2_ = bf16[512,128]{1,0:T(8,128)(2,1)S(1)} collective-permute-done((bf16[512,128]{1,0:T(8,128)(2,1)S(1)}, bf16[512,128]{1,0:T(8,128)(2,1)S(1)}, u32[]{:S(2)}, u32[]{:S(2)}) %collective-permute-start) | collective-permute-done | bytes 131104 | tf_op jit(solution)/shard_map/ppermute | solution.py:357
  10.2 1.6 %collective-permute-done.1.refs_2_.refs_3_ = bf16[512,128]{1,0:T(8,128)(2,1)S(1)} collective-permute-done((bf16[512,128]{1,0:T(8,128)(2,1)S(1)}, bf16[512,128]{1,0:T(8,128)(2,1)S(1)}, u32[]{:S(2)}, u32[]{:S(2)}) %collective-permute-start.1) | collective-permute-done | bytes 131104 | tf_op jit(solution)/shard_map/ppermute | solution.py:357
  11.7 1.3 %collective-permute-done.2.refs_3_.refs_4_ = bf16[512,128]{1,0:T(8,128)(2,1)S(1)} collective-permute-done((bf16[512,128]{1,0:T(8,128)(2,1)S(1)}, bf16[512,128]{1,0:T(8,128)(2,1)S(1)}, u32[]{:S(2)}, u32[]{:S(2)}) %collective-permute-start.2) | collective-permute-done | bytes 131104 | tf_op jit(solution)/shard_map/ppermute | solution.py:357
  13.0 2.9 %collective-permute-start.3 = (bf16[512,128]{1,0:T(8,128)(2,1)S(1)}, bf16[512,128]{1,0:T(8,128)(2,1)S(1)}, u32[]{:S(2)}, u32[]{:S(2)}) collective-permute-start(bf16[512,128]{1,0:T(8,128)(2,1)S(1)} %shard_map.94), channel_id=1, source_target_pairs={{0,4},{1,5},{2,6},{3,7},{4,0},{5,1},{6,2},{7,3},{8,12},{9,13},{10,... | collective-permute-start | bytes 393224 | tf_op jit(solution)/shard_map/ppermute | solution.py:374
  16.0 2.6 %shard_map.92 = (bf16[2048,128]{1,0:T(8,128)(2,1)S(1)}, f32[128,2048]{1,0:T(8,128)S(1)}) custom-call(bf16[128,2048]{1,0:T(8,128)(2,1)S(1)} %bitcast.24, bf16[128,2048]{1,0:T(8,128)(2,1)S(1)} %bitcast.11, bf16[128,2048]{1,0:T(8,128)(2,1)S(1)} %bitcast.18), custom_call_target="tpu_custom_call" | custom-call | flops 134217728 | bytes 3145728 | tf_op jit(solution)/shard_map/pallas_call | solution.py:328
  18.6 2.8 %collective-permute-done.3.refs_0_ = bf16[512,128]{1,0:T(8,128)(2,1)S(1)} collective-permute-done((bf16[512,128]{1,0:T(8,128)(2,1)S(1)}, bf16[512,128]{1,0:T(8,128)(2,1)S(1)}, u32[]{:S(2)}, u32[]{:S(2)}) %collective-permute-start.3) | collective-permute-done | bytes 131104 | tf_op jit(solution)/shard_map/ppermute | solution.py:374
  21.7 1.3 %collective-permute-start.4 = (bf16[512,128]{1,0:T(8,128)(2,1)S(1)}, bf16[512,128]{1,0:T(8,128)(2,1)S(1)}, u32[]{:S(2)}, u32[]{:S(2)}) collective-permute-start(bf16[512,128]{1,0:T(8,128)(2,1)S(1)} %get-tuple-element.51), channel_id=1, source_target_pairs={{0,1},{1,0},{2,3},{3,2},{4,5},{5,4},{6,7},{7,6},{8,10},{9,11},{10,... | collective-permute-start | bytes 393224 | tf_op jit(solution)/shard_map/ppermute | solution.py:357
  22.9 0.7 %collective-permute-start.5 = (bf16[512,128]{1,0:T(8,128)(2,1)S(1)}, bf16[512,128]{1,0:T(8,128)(2,1)S(1)}, u32[]{:S(2)}, u32[]{:S(2)}) collective-permute-start(bf16[512,128]{1,0:T(8,128)(2,1)S(1)} %get-tuple-element.52), channel_id=1, source_target_pairs={{0,2},{1,3},{2,0},{3,1},{4,6},{5,7},{6,4},{7,5},{8,9},{9,8},{10,11... | collective-permute-start | bytes 393224 | tf_op jit(solution)/shard_map/ppermute | solution.py:357
  23.6 1.6 %collective-permute-start.6 = (bf16[512,128]{1,0:T(8,128)(2,1)S(1)}, bf16[512,128]{1,0:T(8,128)(2,1)S(1)}, u32[]{:S(2)}, u32[]{:S(2)}) collective-permute-start(bf16[512,128]{1,0:T(8,128)(2,1)S(1)} %get-tuple-element.56), channel_id=1, source_target_pairs={{0,3},{1,2},{2,1},{3,0},{4,7},{5,6},{6,5},{7,4},{8,11},{9,10},{10,... | collective-permute-start | bytes 393224 | tf_op jit(solution)/shard_map/ppermute | solution.py:357
  25.2 3.0 %collective-permute-done.4.refs_5_.refs_10_ = bf16[512,128]{1,0:T(8,128)(2,1)S(1)} collective-permute-done((bf16[512,128]{1,0:T(8,128)(2,1)S(1)}, bf16[512,128]{1,0:T(8,128)(2,1)S(1)}, u32[]{:S(2)}, u32[]{:S(2)}) %collective-permute-start.4) | collective-permute-done | bytes 131104 | tf_op jit(solution)/shard_map/ppermute | solution.py:357
  28.7 1.2 %collective-permute-done.6.refs_7_.refs_12_ = bf16[512,128]{1,0:T(8,128)(2,1)S(1)} collective-permute-done((bf16[512,128]{1,0:T(8,128)(2,1)S(1)}, bf16[512,128]{1,0:T(8,128)(2,1)S(1)}, u32[]{:S(2)}, u32[]{:S(2)}) %collective-permute-start.6) | collective-permute-done | bytes 131104 | tf_op jit(solution)/shard_map/ppermute | solution.py:357
  29.8 1.0 %shard_map.97 = (f32[128,512]{1,0:T(8,128)S(1)}, f32[128,128]{1,0:T(8,128)S(1)}, bf16[128,2048]{1,0:T(8,128)(2,1)S(1)}, bf16[544,128]{1,0:T(8,128)(2,1)S(1)}, bf...) custom-call(bf16[128,2048]{1,0:T(8,128)(2,1)S(1)} %bitcast.26, ...), custom_call_target="tpu_custom_call" | custom-call | flops 134217728 | bytes 4825088 | tf_op jit(solution)/shard_map/pallas_call | solution.py:328
  30.8 2.2 %collective-permute-start.7 = (bf16[544,128]{1,0:T(8,128)(2,1)S(1)}, bf16[544,128]{1,0:T(8,128)(2,1)S(1)}, u32[]{:S(2)}, u32[]{:S(2)}) collective-permute-start(bf16[544,128]{1,0:T(8,128)(2,1)S(1)} %get-tuple-element.65), channel_id=1, source_target_pairs={{0,3},{1,2},{2,1},{3,0},{4,7},{5,6},{6,5},{7,4},{8,11},{9,10},{10,... | collective-permute-start | bytes 417800 | tf_op jit(solution)/shard_map/ppermute | solution.py:357
  33.0 0.5 collective-permute-start.8
  33.5 0.9 %collective-permute-start.9 = (bf16[544,128]{1,0:T(8,128)(2,1)S(1)}, bf16[544,128]{1,0:T(8,128)(2,1)S(1)}, u32[]{:S(2)}, u32[]{:S(2)}) collective-permute-start(bf16[544,128]{1,0:T(8,128)(2,1)S(1)} %get-tuple-element.67), channel_id=1, source_target_pairs={{0,2},{1,3},{2,0},{3,1},{4,6},{5,7},{6,4},{7,5},{8,10},{9,11},{10,... | collective-permute-start | bytes 417800 | tf_op jit(solution)/shard_map/ppermute | solution.py:357
  34.4 3.4 %collective-permute-done.7.refs_1_.refs_2_ = bf16[544,128]{1,0:T(8,128)(2,1)S(1)} collective-permute-done((bf16[544,128]{1,0:T(8,128)(2,1)S(1)}, bf16[544,128]{1,0:T(8,128)(2,1)S(1)}, u32[]{:S(2)}, u32[]{:S(2)}) %collective-permute-start.7) | collective-permute-done | bytes 139296 | tf_op jit(solution)/shard_map/ppermute | solution.py:357
  37.8 1.2 %collective-permute-done.8.refs_2_.refs_3_ = bf16[544,128]{1,0:T(8,128)(2,1)S(1)} collective-permute-done((bf16[544,128]{1,0:T(8,128)(2,1)S(1)}, bf16[544,128]{1,0:T(8,128)(2,1)S(1)}, u32[]{:S(2)}, u32[]{:S(2)}) %collective-permute-start.8) | collective-permute-done | bytes 139296 | tf_op jit(solution)/shard_map/ppermute | solution.py:357
  39.0 2.6 %collective-permute-start.10 = (bf16[544,128]{1,0:T(8,128)(2,1)S(1)}, bf16[544,128]{1,0:T(8,128)(2,1)S(1)}, u32[]{:S(2)}, u32[]{:S(2)}) collective-permute-start(bf16[544,128]{1,0:T(8,128)(2,1)S(1)} %shard_map.99.refs_5_), channel_id=1, source_target_pairs={{0,4},{1,5},{2,6},{3,7},{4,0},{5,1},{6,2},{7,3},{8,12},{9,13},{10,... | collective-permute-start | bytes 417800 | tf_op jit(solution)/shard_map/ppermute | solution.py:374
  41.7 3.5 %shard_map.98 = (bf16[128,2048]{1,0:T(8,128)(2,1)}, bf16[128,2048]{1,0:T(8,128)(2,1)}, f32[128,2048]{1,0:T(8,128)S(1)}, f32[128,2048]{1,0:T(8,128)S(1)}, f32[8,128]{1,0:T(8,128)S(1)}) custom-call(bf16[128,2048]{1,0:T(8,128)(2,1)S(1)} %bitcast.27, bf16[128,2048]{1,0:T(8,128)(2,1)S(1)} %bitcast.12, bf16[128,2048]{1,0:T(8,128)(2,1)S(1)} %bitcast.19, ...), custom_call_target="tpu_custom_call" | custom-call | flops 335544320 | bytes 7680000 | tf_op jit(solution)/shard_map/pallas_call | solution.py:328
  45.1 0.9 %collective-permute-done.10.refs_0_ = bf16[544,128]{1,0:T(8,128)(2,1)S(1)} collective-permute-done((bf16[544,128]{1,0:T(8,128)(2,1)S(1)}, bf16[544,128]{1,0:T(8,128)(2,1)S(1)}, u32[]{:S(2)}, u32[]{:S(2)}) %collective-permute-start.10) | collective-permute-done | bytes 139296 | tf_op jit(solution)/shard_map/ppermute | solution.py:374
  46.4 1.0 %collective-permute-start.13 = (bf16[512,128]{1,0:T(8,128)(2,1)S(1)}, bf16[512,128]{1,0:T(8,128)(2,1)S(1)}, u32[]{:S(2)}, u32[]{:S(2)}) collective-permute-start(bf16[512,128]{1,0:T(8,128)(2,1)S(1)} %get-tuple-element.71), channel_id=1, source_target_pairs={{0,3},{1,2},{2,1},{3,0},{4,7},{5,6},{6,5},{7,4},{8,11},{9,10},{10,... | collective-permute-start | bytes 393224 | tf_op jit(solution)/shard_map/ppermute | solution.py:357
  47.4 2.0 %collective-permute-start.12 = (bf16[512,128]{1,0:T(8,128)(2,1)S(1)}, bf16[512,128]{1,0:T(8,128)(2,1)S(1)}, u32[]{:S(2)}, u32[]{:S(2)}) collective-permute-start(bf16[512,128]{1,0:T(8,128)(2,1)S(1)} %get-tuple-element.70), channel_id=1, source_target_pairs={{0,1},{1,0},{2,3},{3,2},{4,5},{5,4},{6,7},{7,6},{8,9},{9,8},{10,11... | collective-permute-start | bytes 393224 | tf_op jit(solution)/shard_map/ppermute | solution.py:357
  49.4 0.5 collective-permute-start.11
  49.9 1.4 %collective-permute-start.15 = (f32[16,128]{1,0:T(8,128)S(1)}, f32[16,128]{1,0:T(8,128)S(1)}, u32[]{:S(2)}, u32[]{:S(2)}) collective-permute-start(f32[16,128]{1,0:T(8,128)S(1)} %get-tuple-element.79.refs_7_), channel_id=1, source_target_pairs={{0,16},{8,24},{16,0},{24,8},{1,17},{9,25},{17,1},{25,9},{2,18},{10... | collective-permute-start | bytes 24584 | tf_op jit(solution)/shard_map/ppermute | solution.py:346
  51.4 1.0 %shard_map.101 = (bf16[128,2048]{1,0:T(8,128)(2,1)}, bf16[128,2048]{1,0:T(8,128)(2,1)}) custom-call(bf16[128,2048]{1,0:T(8,128)(2,1)S(1)} %bitcast.13, bf16[128,2048]{1,0:T(8,128)(2,1)S(1)} %bitcast.20, f32[128,2048]{1,0:T(8,128)S(1)} %get-tuple-element.62.refs_2_, f32[128,2048]{1,0:T(8,128)S(1)} %get-tuple-element.63.refs_3_, ...), custom_call_target="tpu_custom_call" | custom-call | flops 67108864 | bytes 4325376 | tf_op jit(solution)/shard_map/pallas_call | solution.py:328
  52.8 1.0 %shard_map.102 = (bf16[128,2048]{1,0:T(8,128)(2,1)}, bf16[128,2048]{1,0:T(8,128)(2,1)}) custom-call(bf16[128,2048]{1,0:T(8,128)(2,1)S(1)} %bitcast.14, bf16[128,2048]{1,0:T(8,128)(2,1)S(1)} %bitcast.21, f32[128,2048]{1,0:T(8,128)S(1)} %get-tuple-element.62.refs_2_, ...), custom_call_target="tpu_custom_call", output_to_operand_aliasing={{0}: (5, {}), {1}: (6, {})} | custom-call | flops 67108864 | bytes 5373952 | tf_op jit(solution)/shard_map/pallas_call | solution.py:328
  53.8 1.0 %shard_map.103 = (bf16[128,2048]{1,0:T(8,128)(2,1)}, bf16[128,2048]{1,0:T(8,128)(2,1)}) custom-call(bf16[128,2048]{1,0:T(8,128)(2,1)S(1)} %bitcast.15, bf16[128,2048]{1,0:T(8,128)(2,1)S(1)} %bitcast.22, f32[128,2048]{1,0:T(8,128)S(1)} %get-tuple-element.62.refs_2_, ...), custom_call_target="tpu_custom_call", output_to_operand_aliasing={{0}: (5, {}), {1}: (6, {})} | custom-call | flops 67108864 | bytes 5373952 | tf_op jit(solution)/shard_map/pallas_call | solution.py:328
  54.8 0.7 %collective-permute-done.16.refs_10_ = f32[16,128]{1,0:T(8,128)S(1)} collective-permute-done((f32[16,128]{1,0:T(8,128)S(1)}, f32[16,128]{1,0:T(8,128)S(1)}, u32[]{:S(2)}, u32[]{:S(2)}) %collective-permute-start.16) | collective-permute-done | bytes 8224 | tf_op jit(solution)/shard_map/ppermute | solution.py:346
  55.5 1.0 %shard_map.104 = (bf16[128,2048]{1,0:T(8,128)(2,1)}, bf16[128,2048]{1,0:T(8,128)(2,1)}, f32[16,128]{1,0:T(8,128)}) custom-call(bf16[128,2048]{1,0:T(8,128)(2,1)S(1)} %bitcast.16, bf16[128,2048]{1,0:T(8,128)(2,1)S(1)} %bitcast.23, f32[128,2048]{1,0:T(8,128)S(1)} %get-tuple-element.62.refs_2_, ...), custom_call_target="tpu_custom_call", output_to_operand_aliasing={{0}: (5, {}), {1}: (6, {})} | custom-call | flops 67108864 | bytes 5414912 | tf_op jit(solution)/shard_map/pallas_call | solution.py:328
  (25 shorter events, 1.7 us)
Async XLA Ops:
  0.6 15.3 %copy-start.1 = (bf16[1,128,2048]{2,1,0:T(8,128)(2,1)S(1)}, bf16[1,128,2048]{2,1,0:T(8,128)(2,1)}, u32[]{:S(2)}) copy-start(bf16[1,128,2048]{2,1,0:T(8,128)(2,1)} %param.7) | copy-start | bytes 1572868
  0.6 15.3 %copy-start.2 = (bf16[1,128,2048]{2,1,0:T(8,128)(2,1)S(1)}, bf16[1,128,2048]{2,1,0:T(8,128)(2,1)}, u32[]{:S(2)}) copy-start(bf16[1,128,2048]{2,1,0:T(8,128)(2,1)} %param.5) | copy-start | bytes 1572868
  2.5 13.5 %copy-start = (bf16[1,128,2048]{2,1,0:T(8,128)(2,1)S(1)}, bf16[1,128,2048]{2,1,0:T(8,128)(2,1)}, u32[]{:S(2)}) copy-start(bf16[1,128,2048]{2,1,0:T(8,128)(2,1)} %param.6) | copy-start | bytes 1572868
  2.5 7.7 %collective-permute-start = (bf16[512,128]{1,0:T(8,128)(2,1)S(1)}, bf16[512,128]{1,0:T(8,128)(2,1)S(1)}, u32[]{:S(2)}, u32[]{:S(2)}) collective-permute-start(bf16[512,128]{1,0:T(8,128)(2,1)S(1)} %get-tuple-element.47), channel_id=1, source_target_pairs={{0,1},{1,0},{2,3},{3,2},{4,5},{5,4},{6,7},{7,6},{8,10},{9,11},{10,... | collective-permute-start | bytes 393224 | tf_op jit(solution)/shard_map/ppermute | solution.py:357
  5.5 6.2 %collective-permute-start.1 = (bf16[512,128]{1,0:T(8,128)(2,1)S(1)}, bf16[512,128]{1,0:T(8,128)(2,1)S(1)}, u32[]{:S(2)}, u32[]{:S(2)}) collective-permute-start(bf16[512,128]{1,0:T(8,128)(2,1)S(1)} %get-tuple-element.48), channel_id=1, source_target_pairs={{0,2},{1,3},{2,0},{3,1},{4,6},{5,7},{6,4},{7,5},{8,9},{9,8},{10,11... | collective-permute-start | bytes 393224 | tf_op jit(solution)/shard_map/ppermute | solution.py:357
  7.1 5.9 %collective-permute-start.2 = (bf16[512,128]{1,0:T(8,128)(2,1)S(1)}, bf16[512,128]{1,0:T(8,128)(2,1)S(1)}, u32[]{:S(2)}, u32[]{:S(2)}) collective-permute-start(bf16[512,128]{1,0:T(8,128)(2,1)S(1)} %get-tuple-element.49), channel_id=1, source_target_pairs={{0,3},{1,2},{2,1},{3,0},{4,7},{5,6},{6,5},{7,4},{8,11},{9,10},{10,... | collective-permute-start | bytes 393224 | tf_op jit(solution)/shard_map/ppermute | solution.py:357
  13.0 8.3 %collective-permute-start.3 = (bf16[512,128]{1,0:T(8,128)(2,1)S(1)}, bf16[512,128]{1,0:T(8,128)(2,1)S(1)}, u32[]{:S(2)}, u32[]{:S(2)}) collective-permute-start(bf16[512,128]{1,0:T(8,128)(2,1)S(1)} %shard_map.94), channel_id=1, source_target_pairs={{0,4},{1,5},{2,6},{3,7},{4,0},{5,1},{6,2},{7,3},{8,12},{9,13},{10,... | collective-permute-start | bytes 393224 | tf_op jit(solution)/shard_map/ppermute | solution.py:374
  21.4 6.9 %copy-start.3 = (bf16[1,128,2048]{2,1,0:T(8,128)(2,1)S(1)}, bf16[1,128,2048]{2,1,0:T(8,128)(2,1)}, u32[]{:S(2)}) copy-start(bf16[1,128,2048]{2,1,0:T(8,128)(2,1)} %param.9) | copy-start | bytes 1572868
  21.7 6.6 %copy-start.4 = (f32[2048]{0:T(1024)S(1)}, f32[2048]{0:T(1024)}, u32[]{:S(2)}) copy-start(f32[2048]{0:T(1024)} %param.8) | copy-start | bytes 24580
  21.7 6.6 %collective-permute-start.4 = (bf16[512,128]{1,0:T(8,128)(2,1)S(1)}, bf16[512,128]{1,0:T(8,128)(2,1)S(1)}, u32[]{:S(2)}, u32[]{:S(2)}) collective-permute-start(bf16[512,128]{1,0:T(8,128)(2,1)S(1)} %get-tuple-element.51), channel_id=1, source_target_pairs={{0,1},{1,0},{2,3},{3,2},{4,5},{5,4},{6,7},{7,6},{8,10},{9,11},{10,... | collective-permute-start | bytes 393224 | tf_op jit(solution)/shard_map/ppermute | solution.py:357
  22.9 5.3 %collective-permute-start.5 = (bf16[512,128]{1,0:T(8,128)(2,1)S(1)}, bf16[512,128]{1,0:T(8,128)(2,1)S(1)}, u32[]{:S(2)}, u32[]{:S(2)}) collective-permute-start(bf16[512,128]{1,0:T(8,128)(2,1)S(1)} %get-tuple-element.52), channel_id=1, source_target_pairs={{0,2},{1,3},{2,0},{3,1},{4,6},{5,7},{6,4},{7,5},{8,9},{9,8},{10,11... | collective-permute-start | bytes 393224 | tf_op jit(solution)/shard_map/ppermute | solution.py:357
  23.6 6.2 %collective-permute-start.6 = (bf16[512,128]{1,0:T(8,128)(2,1)S(1)}, bf16[512,128]{1,0:T(8,128)(2,1)S(1)}, u32[]{:S(2)}, u32[]{:S(2)}) collective-permute-start(bf16[512,128]{1,0:T(8,128)(2,1)S(1)} %get-tuple-element.56), channel_id=1, source_target_pairs={{0,3},{1,2},{2,1},{3,0},{4,7},{5,6},{6,5},{7,4},{8,11},{9,10},{10,... | collective-permute-start | bytes 393224 | tf_op jit(solution)/shard_map/ppermute | solution.py:357
  30.8 6.9 %collective-permute-start.7 = (bf16[544,128]{1,0:T(8,128)(2,1)S(1)}, bf16[544,128]{1,0:T(8,128)(2,1)S(1)}, u32[]{:S(2)}, u32[]{:S(2)}) collective-permute-start(bf16[544,128]{1,0:T(8,128)(2,1)S(1)} %get-tuple-element.65), channel_id=1, source_target_pairs={{0,3},{1,2},{2,1},{3,0},{4,7},{5,6},{6,5},{7,4},{8,11},{9,10},{10,... | collective-permute-start | bytes 417800 | tf_op jit(solution)/shard_map/ppermute | solution.py:357
  33.0 5.9 %collective-permute-start.8 = (bf16[544,128]{1,0:T(8,128)(2,1)S(1)}, bf16[544,128]{1,0:T(8,128)(2,1)S(1)}, u32[]{:S(2)}, u32[]{:S(2)}) collective-permute-start(bf16[544,128]{1,0:T(8,128)(2,1)S(1)} %get-tuple-element.66), channel_id=1, source_target_pairs={{0,1},{1,0},{2,3},{3,2},{4,5},{5,4},{6,7},{7,6},{8,9},{9,8},{10,11... | collective-permute-start | bytes 417800 | tf_op jit(solution)/shard_map/ppermute | solution.py:357
  33.5 5.4 %collective-permute-start.9 = (bf16[544,128]{1,0:T(8,128)(2,1)S(1)}, bf16[544,128]{1,0:T(8,128)(2,1)S(1)}, u32[]{:S(2)}, u32[]{:S(2)}) collective-permute-start(bf16[544,128]{1,0:T(8,128)(2,1)S(1)} %get-tuple-element.67), channel_id=1, source_target_pairs={{0,2},{1,3},{2,0},{3,1},{4,6},{5,7},{6,4},{7,5},{8,10},{9,11},{10,... | collective-permute-start | bytes 417800 | tf_op jit(solution)/shard_map/ppermute | solution.py:357
  39.0 7.0 %collective-permute-start.10 = (bf16[544,128]{1,0:T(8,128)(2,1)S(1)}, bf16[544,128]{1,0:T(8,128)(2,1)S(1)}, u32[]{:S(2)}, u32[]{:S(2)}) collective-permute-start(bf16[544,128]{1,0:T(8,128)(2,1)S(1)} %shard_map.99.refs_5_), channel_id=1, source_target_pairs={{0,4},{1,5},{2,6},{3,7},{4,0},{5,1},{6,2},{7,3},{8,12},{9,13},{10,... | collective-permute-start | bytes 417800 | tf_op jit(solution)/shard_map/ppermute | solution.py:374
  46.4 6.0 %collective-permute-start.13 = (bf16[512,128]{1,0:T(8,128)(2,1)S(1)}, bf16[512,128]{1,0:T(8,128)(2,1)S(1)}, u32[]{:S(2)}, u32[]{:S(2)}) collective-permute-start(bf16[512,128]{1,0:T(8,128)(2,1)S(1)} %get-tuple-element.71), channel_id=1, source_target_pairs={{0,3},{1,2},{2,1},{3,0},{4,7},{5,6},{6,5},{7,4},{8,11},{9,10},{10,... | collective-permute-start | bytes 393224 | tf_op jit(solution)/shard_map/ppermute | solution.py:357
  47.4 6.5 %collective-permute-start.12 = (bf16[512,128]{1,0:T(8,128)(2,1)S(1)}, bf16[512,128]{1,0:T(8,128)(2,1)S(1)}, u32[]{:S(2)}, u32[]{:S(2)}) collective-permute-start(bf16[512,128]{1,0:T(8,128)(2,1)S(1)} %get-tuple-element.70), channel_id=1, source_target_pairs={{0,1},{1,0},{2,3},{3,2},{4,5},{5,4},{6,7},{7,6},{8,9},{9,8},{10,11... | collective-permute-start | bytes 393224 | tf_op jit(solution)/shard_map/ppermute | solution.py:357
  49.4 6.1 %collective-permute-start.11 = (bf16[512,128]{1,0:T(8,128)(2,1)S(1)}, bf16[512,128]{1,0:T(8,128)(2,1)S(1)}, u32[]{:S(2)}, u32[]{:S(2)}) collective-permute-start(bf16[512,128]{1,0:T(8,128)(2,1)S(1)} %get-tuple-element.69), channel_id=1, source_target_pairs={{0,2},{1,3},{2,0},{3,1},{4,6},{5,7},{6,4},{7,5},{8,10},{9,11},{10,... | collective-permute-start | bytes 393224 | tf_op jit(solution)/shard_map/ppermute | solution.py:357
  49.9 4.9 %collective-permute-start.14 = (f32[16,128]{1,0:T(8,128)S(1)}, f32[16,128]{1,0:T(8,128)S(1)}, u32[]{:S(2)}, u32[]{:S(2)}) collective-permute-start(f32[16,128]{1,0:T(8,128)S(1)} %get-tuple-element.79.refs_7_), channel_id=1, source_target_pairs={{0,8},{8,0},{16,24},{24,16},{1,9},{9,1},{17,25},{25,17},{2,10},{10... | collective-permute-start | bytes 24584 | tf_op jit(solution)/shard_map/ppermute | solution.py:346
  49.9 4.9 %collective-permute-start.15 = (f32[16,128]{1,0:T(8,128)S(1)}, f32[16,128]{1,0:T(8,128)S(1)}, u32[]{:S(2)}, u32[]{:S(2)}) collective-permute-start(f32[16,128]{1,0:T(8,128)S(1)} %get-tuple-element.79.refs_7_), channel_id=1, source_target_pairs={{0,16},{8,24},{16,0},{24,8},{1,17},{9,25},{17,1},{25,9},{2,18},{10... | collective-permute-start | bytes 24584 | tf_op jit(solution)/shard_map/ppermute | solution.py:346
  52.4 3.1 %collective-permute-start.16 = (f32[16,128]{1,0:T(8,128)S(1)}, f32[16,128]{1,0:T(8,128)S(1)}, u32[]{:S(2)}, u32[]{:S(2)}) collective-permute-start(f32[16,128]{1,0:T(8,128)S(1)} %get-tuple-element.79.refs_7_), channel_id=1, source_target_pairs={{0,24},{8,16},{16,8},{24,0},{1,25},{9,17},{17,9},{25,1},{2,26},{10... | collective-permute-start | bytes 24584 | tf_op jit(solution)/shard_map/ppermute | solution.py:346

commit v7 on v6

--- a/solution.py
+++ b/solution.py
@@ -33,6 +33,10 @@
 
 CROSSED = ((0, 1, 2, 3), (0, 2, 1, 3))
 DIAGONAL_FIRST = ((0, 3, 1, 2), (0, 3, 1, 2))
+X_FIRST = ((0, 1, 2, 3), (0, 1, 2, 3))
+STATE_ORDERS = (CROSSED, X_FIRST)
+GRAD_ORDERS = (DIAGONAL_FIRST, DIAGONAL_FIRST)
+NORM_ORDERS = (STATE_ORDERS[1], GRAD_ORDERS[0])
 
 
 def partner_of(order, slot):
@@ -64,22 +68,18 @@
 def state_kernel(head, group, k_ref, v_ref, *refs):
     piece_refs = refs[:group]
     whole_ref, k_buffer, v_buffer, arrived = refs[group:]
-    step = k_buffer.shape[0] // arrived.shape[1]
-    copies = []
-    for i in range(arrived.shape[1]):
-        part = columns(i * step, step)
-        for n, (ref, buffer) in enumerate(((k_ref, k_buffer), (v_ref, v_buffer))):
-            copy = pltpu.make_async_copy(
-                ref.at[part, :], buffer.at[part, :], arrived.at[n, i]
-            )
-            copy.start()
-            copies.append(copy)
+    copies = [
+        pltpu.make_async_copy(k_ref, k_buffer, arrived.at[0]),
+        pltpu.make_async_copy(v_ref, v_buffer, arrived.at[1]),
+    ]
+    for copy in copies:
+        copy.start()
     for copy in copies:
         copy.wait()
     for h in range(HEADS):
         part = columns(h * head, head)
         whole_ref[part, :] = dot(k_buffer[:, part], v_buffer[:, part], 0, 0).astype(HALF)
-    scattered(CROSSED, whole_ref, piece_refs[0].shape[0], piece_refs)
+    scattered(STATE_ORDERS[0], whole_ref, piece_refs[0].shape[0], piece_refs)
 
 
 def local_kernel(head, q_ref, k_ref, v_ref, scores_ref, intra_ref):
@@ -188,12 +188,12 @@
     rows = q_ref.shape[0]
     mask = causal(rows)
     scaling = head ** (-0.5)
-    gathered(CROSSED, prefix_refs, prefix_refs[0].shape[0], whole_ref)
+    gathered(STATE_ORDERS[1], prefix_refs, prefix_refs[0].shape[0], whole_ref)
     inverse = inverse_ref[...]
     width = late_ref.shape[1]
     for slot in range(group):
         for i in range(width // head):
-            part = features_at(CROSSED, slot, i, width, head)
+            part = features_at(STATE_ORDERS[1], slot, i, width, head)
             if slot == group - 1:
                 attended = late_ref[:, columns(i * head, head)]
             else:
@@ -215,36 +215,37 @@
     token_ref[...] = jnp.zeros_like(token_ref)
 
 
-def final_kernel(head, slot, last, *refs):
-    k_ref, v_ref, key_part_ref, value_part_ref, suffix_ref = refs[:5]
+def final_kernel(head, slots, last, *refs):
+    k_ref, v_ref, key_part_ref, value_part_ref = refs[:4]
+    suffix_refs = refs[4 : 4 + len(slots)]
+    refs = refs[4 + len(slots) :]
     copies = []
     if last:
         gain_grad_ref, total_ref, gain_written = refs[-6], refs[-2], refs[-1]
-        total_ref[...] = tree_sum([ref[...] for ref in refs[7:-8]])
+        total_ref[...] = tree_sum([ref[...] for ref in refs[2:-8]])
         copies.append(pltpu.make_async_copy(total_ref, gain_grad_ref, gain_written))
         copies[0].start()
         out_refs, refs = refs[-8:-6], refs[-5:-2]
     else:
-        out_refs, refs = refs[-5:-3], refs[-3:]
-    buffers, written = refs[:2], refs[2]
-    rows, width = buffers[0].shape
-    for i in range(width // head):
-        part = features_at(DIAGONAL_FIRST, slot, i, width, head)
-        local = columns(i * head, head)
-        suffix = suffix_ref[local, :]
-        buffers[0][:, local] = (
-            key_part_ref[:, part] + dot(v_ref[:, part], suffix, 1, 1)
-        ).astype(HALF)
-        buffers[1][:, local] = (
-            value_part_ref[:, part] + dot(k_ref[:, part], suffix, 1, 0)
-        ).astype(HALF)
-    block = block_at(partner_of(DIAGONAL_FIRST, slot), width)
-    step = rows // written.shape[1]
-    for n in range(written.shape[1]):
-        part = columns(n * step, step)
-        for i in range(2):
+        out_refs, refs = refs[:2], refs[2:]
+    key_buffer, value_buffer, written = refs
+    width = key_buffer.shape[2]
+    for n, slot in enumerate(slots):
+        for i in range(width // head):
+            part = features_at(GRAD_ORDERS[1], slot, i, width, head)
+            local = columns(i * head, head)
+            suffix = suffix_refs[n][local, :]
+            key_buffer[n, :, local] = (
+                key_part_ref[:, part] + dot(v_ref[:, part], suffix, 1, 1)
+            ).astype(HALF)
+            value_buffer[n, :, local] = (
+                value_part_ref[:, part] + dot(k_ref[:, part], suffix, 1, 0)
+            ).astype(HALF)
+        for i, buffer in enumerate((key_buffer, value_buffer)):
             copy = pltpu.make_async_copy(
-                buffers[i].at[part, :], out_refs[i].at[part, block], written.at[i, n]
+                buffer.at[n],
+                out_refs[i].at[:, block_at(partner_of(GRAD_ORDERS[1], slot), width)],
+                written.at[i, n],
             )
             copy.start()
             copies.append(copy)
@@ -271,14 +272,16 @@
     ref[columns(start + rows, rows), :] = (value - high.astype(F32)).astype(HALF)
 
 
-def total_kernel(size, *refs):
-    out_ref = refs[-1]
+def total_kernel(size, count, *refs):
+    refs, out_refs = refs[:count], refs[count + 1 :]
     total = refs[0][0:size, :].astype(F32)
-    for ref in refs[1:-1]:
+    for ref in refs[1:]:
         total += ref[0:size, :].astype(F32)
-    out_ref[0:size, :] = total.astype(HALF)
-    if out_ref.shape[0] > size:
-        put_wide_rows(out_ref, size, tree_sum([wide_rows(ref, size) for ref in refs[:-1]]))
+    out_refs[0][0:size, :] = total.astype(HALF)
+    if len(out_refs) > 1:
+        gain = tree_sum([wide_rows(ref, size) for ref in refs])
+        put_wide_rows(out_refs[0], size, gain)
+        out_refs[1][...] = wide_rows(out_refs[0], size)
 
 
 def group_flag(group, reverse, distance):
@@ -296,8 +299,9 @@
     out_ref[...] = (own + moved).astype(HALF)
 
 
-def scan_kernel(group, order, reverse, masked, size, riding, *refs):
-    members = [partner_of(order, j) for j in range(group)]
+def scan_kernel(group, orders, reverse, masked, size, riding, *refs):
+    sources = [partner_of(orders[0], j) for j in range(group)]
+    targets = [partner_of(orders[1], j) for j in range(group)]
     carry = refs[0][0:size, :].astype(F32)
     if masked:
         carry = carry * group_flag(group, reverse, 1)
@@ -306,13 +310,12 @@
     for j in range(group):
         total = carry
         for i in range(group):
-            if i != j:
-                earlier = members[i] < members[j]
-                keep = jnp.where(earlier != reverse, 1.0, 0.0)
-                total += keep * blocks[i]
+            earlier = sources[i] < targets[j]
+            later = sources[i] > targets[j]
+            total += jnp.where(later if reverse else earlier, 1.0, 0.0) * blocks[i]
         out_refs[j][...] = total.astype(HALF)
     if riding:
-        refs[-1][...] = wide_rows(refs[0], size) + wide_rows(refs[1 + group], size)
+        refs[-1][...] = refs[1 + group][...] + wide_rows(refs[0], size)
 
 
 VMEM = pl.BlockSpec(memory_space=pltpu.VMEM)
@@ -358,9 +361,9 @@
     return results
 
 
-def exclusive_scan(pieces, order, size, reverse, token):
+def exclusive_scan(pieces, orders, size, reverse, token):
     group = len(pieces)
-    count = lax.axis_size("seq")
+    count, rows = lax.axis_size("seq"), lax.axis_size("dp")
     groups = count // group
     part = functools.partial
     lanes = pieces[0].shape[1]
@@ -373,20 +376,28 @@
         pairs = [(i, (i + step) % count) for i in range(count)]
         return lax.ppermute(array, "seq", pairs)
 
-    received = own_and_swapped(pieces, order)
-    (total,) = call(
-        part(total_kernel, size),
-        [jax.ShapeDtypeStruct(pieces[0].shape, HALF)],
-        received,
+    received = own_and_swapped(pieces, orders[0])
+    totals = call(
+        part(total_kernel, size, group),
+        [jax.ShapeDtypeStruct(pieces[0].shape, HALF)] + [gain_shape] * (extra > 0),
+        received + [token],
         0,
-    )
-    riding = int(extra > 0 and groups == 2)
-    gain = None
-    if extra and not riding:
-        gain = total[size : size + extra // 2].astype(F32) + total[size + extra // 2 :]
-        gain = tree_sum(summed_over("seq", group, gain))
-        total = total[:size]
-    carry = shifted(total, group)
+        ins={group: ANY},
+    )
+    total, gains = totals[0], list(totals[1:])
+    riding = int(extra > 0 and groups == 2 and rows == 4)
+    carry = shifted(total if riding else total[:size], group)
+    if riding:
+        for offset in (0, group):
+            pairs = [
+                (row * count + i, (row ^ 2) * count + (i ^ offset))
+                for row in range(rows)
+                for i in range(count)
+            ]
+            gains.append(lax.ppermute(gains[0], ("dp", "seq"), pairs))
+    elif extra:
+        gains = [tree_sum(summed_over("seq", group, gains[0]))]
+        gains = [tree_sum(summed_over("dp", 2, gains[0]))]
     distance = 1
     while distance < groups - 1:
         moved = shifted(carry, distance * group)
@@ -395,16 +406,16 @@
         )
         (carry,) = call(kernel, [piece], [carry, moved], 0)
         distance *= 2
-    inputs = [carry] + received + ([total] if riding else []) + [token]
     sums = call(
-        part(scan_kernel, group, order, reverse, groups <= 2, size, riding),
+        part(scan_kernel, group, orders, reverse, groups <= 2, size, riding),
         [piece] * group + [gain_shape] * riding,
-        inputs,
+        [carry] + received + (gains[:1] if riding else []),
         0,
-        ins={len(inputs) - 1: ANY},
-    )
-    results = own_and_swapped(sums[:group], order)
-    return results, (sums[-1] if riding else gain)
+    )
+    results = own_and_swapped(sums[:group], orders[1])
+    if riding:
+        gains = [sums[-1] + (gains[1] + gains[2])]
+    return results, (gains[0] if gains else None)
 
 
 def summed_over(axis, stride, array):
@@ -444,21 +455,21 @@
         1,
         [whole]
         + [pltpu.VMEM((rows, features), HALF)] * 2
-        + [pltpu.SemaphoreType.DMA((2, 4))],
+        + [pltpu.SemaphoreType.DMA((2,))],
         ins={0: HBM, 1: HBM},
     )
     scores, intra = call(part(local_kernel, head), [scores_shape, wide], [q, k, v], 2)
-    prefix, _ = exclusive_scan(pieces, CROSSED, width, False, intra)
+    prefix, _ = exclusive_scan(pieces, STATE_ORDERS, width, False, intra)
     message = jax.ShapeDtypeStruct((width + 2 * HEADS, head), HALF)
     sources = [q, intra, gain_row, cot]
     early, squares, inner = call(
-        part(early_norm_kernel, head, CROSSED),
+        part(early_norm_kernel, head, STATE_ORDERS[1]),
         [wide, square, square],
         sources + prefix[:-1],
         1,
     )
     late, inverse, grad, *pieces = call(
-        part(norm_kernel, head, group, (CROSSED, DIAGONAL_FIRST), lax.axis_size("dp")),
+        part(norm_kernel, head, group, NORM_ORDERS, lax.axis_size("dp")),
         [jax.ShapeDtypeStruct((rows, width), F32), square, half] + [message] * group,
         sources + [early, squares, inner, prefix[-1]],
         2,
@@ -471,27 +482,27 @@
         5,
         [whole],
     )
-    suffix, gain_grad = exclusive_scan(pieces, DIAGONAL_FIRST, width, True, token)
-    gains = summed_over("dp", 1, gain_grad)
+    suffix, gain_grad = exclusive_scan(pieces, GRAD_ORDERS, width, True, token)
+    gains = [gain_grad, swap(gain_grad, "dp", 1)]
     inputs = [k, v, key_part, value_part]
     outs = []
-    for slot in range(group):
-        last = slot == group - 1
-        args = inputs + [suffix[slot]] + outs + (gains if last else [])
-        at = len(inputs) + 1
-        *outs, gain_grad = call(
-            part(final_kernel, head, slot, last),
+    for slots in ((0, 1, 2), (3,)):
+        last = group - 1 in slots
+        at = len(inputs) + len(slots)
+        results = call(
+            part(final_kernel, head, slots, last),
             [half, half] + [gain_shape] * last,
-            args,
+            inputs + [suffix[slot] for slot in slots] + outs + (gains if last else []),
             1,
-            [pltpu.VMEM((rows, width), HALF)] * 2
-            + [pltpu.SemaphoreType.DMA((2, 2))]
+            [pltpu.VMEM((len(slots), rows, width), HALF)] * 2
+            + [pltpu.SemaphoreType.DMA((2, len(slots)))]
             + [pltpu.VMEM((HEADS, head), F32), pltpu.SemaphoreType.DMA(())] * last,
             ins={at + i: HBM for i in range(len(outs))},
             out_specs={0: HBM, 1: HBM, 2: HBM},
             aliases={at + i: i for i in range(len(outs))},
-        ) + (() if last else (None,))
-    grad_key, grad_value = outs
+        )
+        outs = list(results[:2])
+    grad_key, grad_value, gain_grad = results
     return (
         output[None],
         grad_query[None],

time: 56.6 us -> 58.5 us (1.034)
  waiting for transfers between devices: 19 us -> 21.1 us
  Pallas kernels: 14 us -> 12.3 us
  local copies, waits for them, and re-layouts: 0.02 us -> 1.06 us
    ppermute x2, waiting for transfers between devices: 3.7 us -> 7.59 us  [shifted(): return lax.ppermute(array, 'seq', pairs)]
    ppermute x0 -> x2, starting transfers between devices: none -> 2.4 us  [exclusive_scan(): gains.append(lax.ppermute(gains[0], ('dp', 'seq'), pairs))]
    ppermute x3 -> x1, starting transfers between devices: 1.89 us -> 0.07 us  [swap(): return lax.ppermute(array, axis, [(i, i ^ offset) for i in range(count)])]
    pallas_call x13 -> x11, Pallas kernels: 14 us -> 12.3 us  [call(): pl.pallas_call(kernel, out_shape=tuple(outs), in_specs=[ins.get(i, VMEM)...]
    ppermute x12, waiting for transfers between devices: 14.7 us -> 13.5 us  [own_and_swapped(): results.append(lax.ppermute(pieces[slot], ('dp', 'seq'), pairs))]
    unnamed x10 -> x12, local copies, waits for them, and re-layouts: 0.02 us -> 1.06 us
    ppermute x3 -> x1, waiting for transfers between devices: 0.67 us -> 0.01 us  [swap(): return lax.ppermute(array, axis, [(i, i ^ offset) for i in range(count)])]
    ppermute x2, starting transfers between devices: 5.56 us -> 4.97 us  [shifted(): return lax.ppermute(array, 'seq', pairs)]
  transfers between devices with their start and end apart: 17 -> 17, of which waited for: 11 -> 10; matrix products, arithmetic and copies ran while one was open for 0% -> 0% of each run, Pallas kernels for 17% -> 14%
where the time goes in v7:
time: 58.5 us; the launch traced here: 58.3 us
  starting transfers between devices  23.1 us (39%)
  waiting for transfers between devices  21.1 us (36%)
  Pallas kernels  12.3 us (21%)
  local copies, waits for them, and re-layouts  1.06 us (2%)
  between operations  0.76 us (1%)
    ppermute x12, starting transfers between devices, own_and_swapped(): results.append(lax.ppermute(pieces[slot], ('dp', 'seq'), pairs))  15.6 us
    ppermute x12, waiting for transfers between devices, own_and_swapped(): results.append(lax.ppermute(pieces[slot], ('dp', 'seq'), pairs))  13.5 us
    pallas_call x11, Pallas kernels, call(): pl.pallas_call(kernel, out_shape=tuple(outs), in_specs=[ins.get(i, VMEM)...  12.3 us
    ppermute x2, waiting for transfers between devices, shifted(): return lax.ppermute(array, 'seq', pairs)  7.59 us
    ppermute x2, starting transfers between devices, shifted(): return lax.ppermute(array, 'seq', pairs)  4.97 us
    ppermute x2, starting transfers between devices, exclusive_scan(): gains.append(lax.ppermute(gains[0], ('dp', 'seq'), pairs))  2.4 us
  transfers between devices with their start and end apart: 17, of which 10 were waited for; matrix products, arithmetic and copies ran while one was open for 0% of the time, Pallas kernels for 14%

profile of v7, /device:TPU:0, one launch (start us, length us, event | category | flops | bytes accessed | tf_op | source)
XLA Modules:
  0.0 58.3 jit_solution(14739601102715543103)
XLA Ops:
  0.7 1.7 %shard_map.93 = (bf16[512,128]{1,0:T(8,128)(2,1)S(1)}, bf16[512,128]{1,0:T(8,128)(2,1)S(1)}, bf16[512,128]{1,0:T(8,128)(2,1)S(1)}, bf16[512,128]{1,0:T(8,128)(2,1)S(1)}) custom-call(bf16[128,2048]{1,0:T(8,128)(2,1)} %bitcast.10, bf16[128,2048]{1,0:T(8,128)(2,1)} %bitcast.15), custom_call_target="tpu_custom_call" | custom-call | flops 67108864 | bytes 1572864 | tf_op jit(solution)/shard_map/pallas_call | solution.py:331
  2.3 3.0 %collective-permute-start = (bf16[512,128]{1,0:T(8,128)(2,1)S(1)}, bf16[512,128]{1,0:T(8,128)(2,1)S(1)}, u32[]{:S(2)}, u32[]{:S(2)}) collective-permute-start(bf16[512,128]{1,0:T(8,128)(2,1)S(1)} %get-tuple-element.45), channel_id=1, source_target_pairs={{0,1},{1,0},{2,3},{3,2},{4,5},{5,4},{6,7},{7,6},{8,10},{9,11},{10,... | collective-permute-start | bytes 393224 | tf_op jit(solution)/shard_map/ppermute | solution.py:360
  5.4 1.6 %collective-permute-start.1 = (bf16[512,128]{1,0:T(8,128)(2,1)S(1)}, bf16[512,128]{1,0:T(8,128)(2,1)S(1)}, u32[]{:S(2)}, u32[]{:S(2)}) collective-permute-start(bf16[512,128]{1,0:T(8,128)(2,1)S(1)} %get-tuple-element.46), channel_id=1, source_target_pairs={{0,2},{1,3},{2,0},{3,1},{4,6},{5,7},{6,4},{7,5},{8,9},{9,8},{10,11... | collective-permute-start | bytes 393224 | tf_op jit(solution)/shard_map/ppermute | solution.py:360
  7.0 1.0 %copy-done.2 = bf16[1,128,2048]{2,1,0:T(8,128)(2,1)S(1)} copy-done((bf16[1,128,2048]{2,1,0:T(8,128)(2,1)S(1)}, bf16[1,128,2048]{2,1,0:T(8,128)(2,1)}, u32[]{:S(2)}) %copy-start.2) | copy-done | bytes 524312
  8.0 2.6 %shard_map.92 = (bf16[2048,128]{1,0:T(8,128)(2,1)S(1)}, f32[128,2048]{1,0:T(8,128)S(1)}) custom-call(bf16[128,2048]{1,0:T(8,128)(2,1)S(1)} %bitcast.20, bf16[128,2048]{1,0:T(8,128)(2,1)S(1)} %bitcast.11, bf16[128,2048]{1,0:T(8,128)(2,1)S(1)} %bitcast.16), custom_call_target="tpu_custom_call" | custom-call | flops 134217728 | bytes 3145728 | tf_op jit(solution)/shard_map/pallas_call | solution.py:331
  10.6 1.0 %collective-permute-done.1.refs_2_.refs_3_ = bf16[512,128]{1,0:T(8,128)(2,1)S(1)} collective-permute-done((bf16[512,128]{1,0:T(8,128)(2,1)S(1)}, bf16[512,128]{1,0:T(8,128)(2,1)S(1)}, u32[]{:S(2)}, u32[]{:S(2)}) %collective-permute-start.1) | collective-permute-done | bytes 131104 | tf_op jit(solution)/shard_map/ppermute | solution.py:360
  11.6 1.3 %collective-permute-done.2.refs_3_.refs_4_ = bf16[512,128]{1,0:T(8,128)(2,1)S(1)} collective-permute-done((bf16[512,128]{1,0:T(8,128)(2,1)S(1)}, bf16[512,128]{1,0:T(8,128)(2,1)S(1)}, u32[]{:S(2)}, u32[]{:S(2)}) %collective-permute-start.2) | collective-permute-done | bytes 131104 | tf_op jit(solution)/shard_map/ppermute | solution.py:360
  12.9 2.9 %collective-permute-start.3 = (bf16[512,128]{1,0:T(8,128)(2,1)S(1)}, bf16[512,128]{1,0:T(8,128)(2,1)S(1)}, u32[]{:S(2)}, u32[]{:S(2)}) collective-permute-start(bf16[512,128]{1,0:T(8,128)(2,1)S(1)} %shard_map.94), channel_id=1, source_target_pairs={{0,4},{1,5},{2,6},{3,7},{4,0},{5,1},{6,2},{7,3},{8,12},{9,13},{10,... | collective-permute-start | bytes 393224 | tf_op jit(solution)/shard_map/ppermute | solution.py:377
  15.8 5.4 %collective-permute-done.3.refs_0_ = bf16[512,128]{1,0:T(8,128)(2,1)S(1)} collective-permute-done((bf16[512,128]{1,0:T(8,128)(2,1)S(1)}, bf16[512,128]{1,0:T(8,128)(2,1)S(1)}, u32[]{:S(2)}, u32[]{:S(2)}) %collective-permute-start.3) | collective-permute-done | bytes 131104 | tf_op jit(solution)/shard_map/ppermute | solution.py:377
  21.6 1.3 %collective-permute-start.4 = (bf16[512,128]{1,0:T(8,128)(2,1)S(1)}, bf16[512,128]{1,0:T(8,128)(2,1)S(1)}, u32[]{:S(2)}, u32[]{:S(2)}) collective-permute-start(bf16[512,128]{1,0:T(8,128)(2,1)S(1)} %get-tuple-element.49), channel_id=1, source_target_pairs={{0,1},{1,0},{2,3},{3,2},{4,5},{5,4},{6,7},{7,6},{8,9},{9,8},{10,11... | collective-permute-start | bytes 393224 | tf_op jit(solution)/shard_map/ppermute | solution.py:360
  22.9 0.7 %collective-permute-start.5 = (bf16[512,128]{1,0:T(8,128)(2,1)S(1)}, bf16[512,128]{1,0:T(8,128)(2,1)S(1)}, u32[]{:S(2)}, u32[]{:S(2)}) collective-permute-start(bf16[512,128]{1,0:T(8,128)(2,1)S(1)} %get-tuple-element.50), channel_id=1, source_target_pairs={{0,2},{1,3},{2,0},{3,1},{4,6},{5,7},{6,4},{7,5},{8,10},{9,11},{10,... | collective-permute-start | bytes 393224 | tf_op jit(solution)/shard_map/ppermute | solution.py:360
  23.5 1.6 %collective-permute-start.6 = (bf16[512,128]{1,0:T(8,128)(2,1)S(1)}, bf16[512,128]{1,0:T(8,128)(2,1)S(1)}, u32[]{:S(2)}, u32[]{:S(2)}) collective-permute-start(bf16[512,128]{1,0:T(8,128)(2,1)S(1)} %get-tuple-element.54), channel_id=1, source_target_pairs={{0,3},{1,2},{2,1},{3,0},{4,7},{5,6},{6,5},{7,4},{8,11},{9,10},{10,... | collective-permute-start | bytes 393224 | tf_op jit(solution)/shard_map/ppermute | solution.py:360
  25.2 2.0 %collective-permute-done.4.refs_5_.refs_10_ = bf16[512,128]{1,0:T(8,128)(2,1)S(1)} collective-permute-done((bf16[512,128]{1,0:T(8,128)(2,1)S(1)}, bf16[512,128]{1,0:T(8,128)(2,1)S(1)}, u32[]{:S(2)}, u32[]{:S(2)}) %collective-permute-start.4) | collective-permute-done | bytes 131104 | tf_op jit(solution)/shard_map/ppermute | solution.py:360
  27.2 1.4 %collective-permute-done.5.refs_6_.refs_11_ = bf16[512,128]{1,0:T(8,128)(2,1)S(1)} collective-permute-done((bf16[512,128]{1,0:T(8,128)(2,1)S(1)}, bf16[512,128]{1,0:T(8,128)(2,1)S(1)}, u32[]{:S(2)}, u32[]{:S(2)}) %collective-permute-start.5) | collective-permute-done | bytes 131104 | tf_op jit(solution)/shard_map/ppermute | solution.py:360
  29.0 1.6 %collective-permute-done.6.refs_7_.refs_12_ = bf16[512,128]{1,0:T(8,128)(2,1)S(1)} collective-permute-done((bf16[512,128]{1,0:T(8,128)(2,1)S(1)}, bf16[512,128]{1,0:T(8,128)(2,1)S(1)}, u32[]{:S(2)}, u32[]{:S(2)}) %collective-permute-start.6) | collective-permute-done | bytes 131104 | tf_op jit(solution)/shard_map/ppermute | solution.py:360
  30.7 1.0 %shard_map.97 = (f32[128,512]{1,0:T(8,128)S(1)}, f32[128,128]{1,0:T(8,128)S(1)}, bf16[128,2048]{1,0:T(8,128)(2,1)S(1)}, bf16[544,128]{1,0:T(8,128)(2,1)S(1)}, bf...) custom-call(bf16[128,2048]{1,0:T(8,128)(2,1)S(1)} %bitcast.22, ...), custom_call_target="tpu_custom_call" | custom-call | flops 134217728 | bytes 4825088 | tf_op jit(solution)/shard_map/pallas_call | solution.py:331
  31.7 1.3 %collective-permute-start.7 = (bf16[544,128]{1,0:T(8,128)(2,1)S(1)}, bf16[544,128]{1,0:T(8,128)(2,1)S(1)}, u32[]{:S(2)}, u32[]{:S(2)}) collective-permute-start(bf16[544,128]{1,0:T(8,128)(2,1)S(1)} %get-tuple-element.63), channel_id=1, source_target_pairs={{0,3},{1,2},{2,1},{3,0},{4,7},{5,6},{6,5},{7,4},{8,11},{9,10},{10,... | collective-permute-start | bytes 417800 | tf_op jit(solution)/shard_map/ppermute | solution.py:360
  33.0 0.5 collective-permute-start.8
  33.5 1.7 %collective-permute-start.9 = (bf16[544,128]{1,0:T(8,128)(2,1)S(1)}, bf16[544,128]{1,0:T(8,128)(2,1)S(1)}, u32[]{:S(2)}, u32[]{:S(2)}) collective-permute-start(bf16[544,128]{1,0:T(8,128)(2,1)S(1)} %get-tuple-element.65), channel_id=1, source_target_pairs={{0,2},{1,3},{2,0},{3,1},{4,6},{5,7},{6,4},{7,5},{8,10},{9,11},{10,... | collective-permute-start | bytes 417800 | tf_op jit(solution)/shard_map/ppermute | solution.py:360
  35.2 3.5 %shard_map.98 = (bf16[128,2048]{1,0:T(8,128)(2,1)}, bf16[128,2048]{1,0:T(8,128)(2,1)}, f32[128,2048]{1,0:T(8,128)S(1)}, f32[128,2048]{1,0:T(8,128)S(1)}, f32[8,128]{1,0:T(8,128)S(1)}) custom-call(bf16[128,2048]{1,0:T(8,128)(2,1)S(1)} %bitcast.23, bf16[128,2048]{1,0:T(8,128)(2,1)S(1)} %bitcast.12, bf16[128,2048]{1,0:T(8,128)(2,1)S(1)} %bitcast.17, ...), custom_call_target="tpu_custom_call" | custom-call | flops 335544320 | bytes 7680000 | tf_op jit(solution)/shard_map/pallas_call | solution.py:331
  38.7 0.6 %collective-permute-done.8.refs_2_.refs_3_ = bf16[544,128]{1,0:T(8,128)(2,1)S(1)} collective-permute-done((bf16[544,128]{1,0:T(8,128)(2,1)S(1)}, bf16[544,128]{1,0:T(8,128)(2,1)S(1)}, u32[]{:S(2)}, u32[]{:S(2)}) %collective-permute-start.8) | collective-permute-done | bytes 139296 | tf_op jit(solution)/shard_map/ppermute | solution.py:360
  39.4 2.0 %collective-permute-start.10 = (bf16[544,128]{1,0:T(8,128)(2,1)S(1)}, bf16[544,128]{1,0:T(8,128)(2,1)S(1)}, u32[]{:S(2)}, u32[]{:S(2)}) collective-permute-start(bf16[544,128]{1,0:T(8,128)(2,1)S(1)} %get-tuple-element.67), channel_id=1, source_target_pairs={{0,4},{1,5},{2,6},{3,7},{4,0},{5,1},{6,2},{7,3},{8,12},{9,13},{10,... | collective-permute-start | bytes 417800 | tf_op jit(solution)/shard_map/ppermute | solution.py:377
  41.5 1.5 %collective-permute-start.15 = (f32[16,128]{1,0:T(8,128)S(1)}, f32[16,128]{1,0:T(8,128)S(1)}, u32[]{:S(2)}, u32[]{:S(2)}) collective-permute-start(f32[16,128]{1,0:T(8,128)S(1)} %get-tuple-element.68.refs_5_), channel_id=1, source_target_pairs={{0,20},{1,21},{2,22},{3,23},{4,16},{5,17},{6,18},{7,19},{8,28},{9,... | collective-permute-start | bytes 24584 | tf_op jit(solution)/shard_map/ppermute | solution.py:397
  43.0 0.9 %collective-permute-start.14 = (f32[16,128]{1,0:T(8,128)S(1)}, f32[16,128]{1,0:T(8,128)S(1)}, u32[]{:S(2)}, u32[]{:S(2)}) collective-permute-start(f32[16,128]{1,0:T(8,128)S(1)} %get-tuple-element.68.refs_5_), channel_id=1, source_target_pairs={{0,16},{1,17},{2,18},{3,19},{4,20},{5,21},{6,22},{7,23},{8,24},{9,... | collective-permute-start | bytes 24584 | tf_op jit(solution)/shard_map/ppermute | solution.py:397
  43.9 2.2 %collective-permute-done.10.refs_0_ = bf16[544,128]{1,0:T(8,128)(2,1)S(1)} collective-permute-done((bf16[544,128]{1,0:T(8,128)(2,1)S(1)}, bf16[544,128]{1,0:T(8,128)(2,1)S(1)}, u32[]{:S(2)}, u32[]{:S(2)}) %collective-permute-start.10) | collective-permute-done | bytes 139296 | tf_op jit(solution)/shard_map/ppermute | solution.py:377
  46.4 2.3 %collective-permute-start.11 = (bf16[512,128]{1,0:T(8,128)(2,1)S(1)}, bf16[512,128]{1,0:T(8,128)(2,1)S(1)}, u32[]{:S(2)}, u32[]{:S(2)}) collective-permute-start(bf16[512,128]{1,0:T(8,128)(2,1)S(1)} %get-tuple-element.69), channel_id=1, source_target_pairs={{0,2},{1,3},{2,0},{3,1},{4,6},{5,7},{6,4},{7,5},{8,10},{9,11},{10,... | collective-permute-start | bytes 393224 | tf_op jit(solution)/shard_map/ppermute | solution.py:360
  48.8 1.1 %collective-permute-start.12 = (bf16[512,128]{1,0:T(8,128)(2,1)S(1)}, bf16[512,128]{1,0:T(8,128)(2,1)S(1)}, u32[]{:S(2)}, u32[]{:S(2)}) collective-permute-start(bf16[512,128]{1,0:T(8,128)(2,1)S(1)} %get-tuple-element.71), channel_id=1, source_target_pairs={{0,3},{1,2},{2,1},{3,0},{4,7},{5,6},{6,5},{7,4},{8,11},{9,10},{10,... | collective-permute-start | bytes 393224 | tf_op jit(solution)/shard_map/ppermute | solution.py:360
  49.9 0.5 collective-permute-start.13
  50.4 4.3 %collective-permute-done.12.refs_5_ = bf16[512,128]{1,0:T(8,128)(2,1)S(1)} collective-permute-done((bf16[512,128]{1,0:T(8,128)(2,1)S(1)}, bf16[512,128]{1,0:T(8,128)(2,1)S(1)}, u32[]{:S(2)}, u32[]{:S(2)}) %collective-permute-start.12) | collective-permute-done | bytes 131104 | tf_op jit(solution)/shard_map/ppermute | solution.py:360
  54.8 1.3 %collective-permute-done.13.refs_6_ = bf16[512,128]{1,0:T(8,128)(2,1)S(1)} collective-permute-done((bf16[512,128]{1,0:T(8,128)(2,1)S(1)}, bf16[512,128]{1,0:T(8,128)(2,1)S(1)}, u32[]{:S(2)}, u32[]{:S(2)}) %collective-permute-start.13) | collective-permute-done | bytes 131104 | tf_op jit(solution)/shard_map/ppermute | solution.py:360
  56.1 1.3 %shard_map.101 = (bf16[128,2048]{1,0:T(8,128)(2,1)}, bf16[128,2048]{1,0:T(8,128)(2,1)}) custom-call(bf16[128,2048]{1,0:T(8,128)(2,1)S(1)} %bitcast.13, bf16[128,2048]{1,0:T(8,128)(2,1)S(1)} %bitcast.18, f32[128,2048]{1,0:T(8,128)S(1)} %get-tuple-element.60.refs_2_, f32[128,2048]{1,0:T(8,128)S(1)} %get-tuple-element.61.refs_3_, ...), custom_call_target="tpu_custom_call" | custom-call | flops 67108864 | bytes 4587520 | tf_op jit(solution)/shard_map/pallas_call | solution.py:331
  57.3 1.0 %shard_map.102 = (bf16[128,2048]{1,0:T(8,128)(2,1)}, bf16[128,2048]{1,0:T(8,128)(2,1)}, f32[16,128]{1,0:T(8,128)}) custom-call(bf16[128,2048]{1,0:T(8,128)(2,1)S(1)} %bitcast.14, bf16[128,2048]{1,0:T(8,128)(2,1)S(1)} %bitcast.19, f32[128,2048]{1,0:T(8,128)S(1)} %get-tuple-element.60.refs_2_, ...), custom_call_target="tpu_custom_call", output_to_operand_aliasing={{0}: (5, {}), {1}: (6, {})} | custom-call | flops 67108864 | bytes 5398528 | tf_op jit(solution)/shard_map/pallas_call | solution.py:331
  (26 shorter events, 1.4 us)
Async XLA Ops:
  0.6 6.3 %copy-start = (bf16[1,128,2048]{2,1,0:T(8,128)(2,1)S(1)}, bf16[1,128,2048]{2,1,0:T(8,128)(2,1)}, u32[]{:S(2)}) copy-start(bf16[1,128,2048]{2,1,0:T(8,128)(2,1)} %param.6) | copy-start | bytes 1572868
  0.6 6.3 %copy-start.1 = (bf16[1,128,2048]{2,1,0:T(8,128)(2,1)S(1)}, bf16[1,128,2048]{2,1,0:T(8,128)(2,1)}, u32[]{:S(2)}) copy-start(bf16[1,128,2048]{2,1,0:T(8,128)(2,1)} %param.7) | copy-start | bytes 1572868
  2.3 8.3 %collective-permute-start = (bf16[512,128]{1,0:T(8,128)(2,1)S(1)}, bf16[512,128]{1,0:T(8,128)(2,1)S(1)}, u32[]{:S(2)}, u32[]{:S(2)}) collective-permute-start(bf16[512,128]{1,0:T(8,128)(2,1)S(1)} %get-tuple-element.45), channel_id=1, source_target_pairs={{0,1},{1,0},{2,3},{3,2},{4,5},{5,4},{6,7},{7,6},{8,10},{9,11},{10,... | collective-permute-start | bytes 393224 | tf_op jit(solution)/shard_map/ppermute | solution.py:360
  5.4 6.2 %collective-permute-start.1 = (bf16[512,128]{1,0:T(8,128)(2,1)S(1)}, bf16[512,128]{1,0:T(8,128)(2,1)S(1)}, u32[]{:S(2)}, u32[]{:S(2)}) collective-permute-start(bf16[512,128]{1,0:T(8,128)(2,1)S(1)} %get-tuple-element.46), channel_id=1, source_target_pairs={{0,2},{1,3},{2,0},{3,1},{4,6},{5,7},{6,4},{7,5},{8,9},{9,8},{10,11... | collective-permute-start | bytes 393224 | tf_op jit(solution)/shard_map/ppermute | solution.py:360
  7.0 5.9 %collective-permute-start.2 = (bf16[512,128]{1,0:T(8,128)(2,1)S(1)}, bf16[512,128]{1,0:T(8,128)(2,1)S(1)}, u32[]{:S(2)}, u32[]{:S(2)}) collective-permute-start(bf16[512,128]{1,0:T(8,128)(2,1)S(1)} %get-tuple-element.47), channel_id=1, source_target_pairs={{0,3},{1,2},{2,1},{3,0},{4,7},{5,6},{6,5},{7,4},{8,11},{9,10},{10,... | collective-permute-start | bytes 393224 | tf_op jit(solution)/shard_map/ppermute | solution.py:360
  7.0 1.0 %copy-start.2 = (bf16[1,128,2048]{2,1,0:T(8,128)(2,1)S(1)}, bf16[1,128,2048]{2,1,0:T(8,128)(2,1)}, u32[]{:S(2)}) copy-start(bf16[1,128,2048]{2,1,0:T(8,128)(2,1)} %param.5) | copy-start | bytes 1572868
  12.9 15.7 %copy-start.4 = (bf16[1,128,2048]{2,1,0:T(8,128)(2,1)S(1)}, bf16[1,128,2048]{2,1,0:T(8,128)(2,1)}, u32[]{:S(2)}) copy-start(bf16[1,128,2048]{2,1,0:T(8,128)(2,1)} %param.9) | copy-start | bytes 1572868
  12.9 8.3 %collective-permute-start.3 = (bf16[512,128]{1,0:T(8,128)(2,1)S(1)}, bf16[512,128]{1,0:T(8,128)(2,1)S(1)}, u32[]{:S(2)}, u32[]{:S(2)}) collective-permute-start(bf16[512,128]{1,0:T(8,128)(2,1)S(1)} %shard_map.94), channel_id=1, source_target_pairs={{0,4},{1,5},{2,6},{3,7},{4,0},{5,1},{6,2},{7,3},{8,12},{9,13},{10,... | collective-permute-start | bytes 393224 | tf_op jit(solution)/shard_map/ppermute | solution.py:377
  21.6 7.0 %copy-start.5 = (f32[2048]{0:T(1024)S(1)}, f32[2048]{0:T(1024)}, u32[]{:S(2)}) copy-start(f32[2048]{0:T(1024)} %param.8) | copy-start | bytes 24580
  21.6 5.6 %collective-permute-start.4 = (bf16[512,128]{1,0:T(8,128)(2,1)S(1)}, bf16[512,128]{1,0:T(8,128)(2,1)S(1)}, u32[]{:S(2)}, u32[]{:S(2)}) collective-permute-start(bf16[512,128]{1,0:T(8,128)(2,1)S(1)} %get-tuple-element.49), channel_id=1, source_target_pairs={{0,1},{1,0},{2,3},{3,2},{4,5},{5,4},{6,7},{7,6},{8,9},{9,8},{10,11... | collective-permute-start | bytes 393224 | tf_op jit(solution)/shard_map/ppermute | solution.py:360
  22.9 5.7 %collective-permute-start.5 = (bf16[512,128]{1,0:T(8,128)(2,1)S(1)}, bf16[512,128]{1,0:T(8,128)(2,1)S(1)}, u32[]{:S(2)}, u32[]{:S(2)}) collective-permute-start(bf16[512,128]{1,0:T(8,128)(2,1)S(1)} %get-tuple-element.50), channel_id=1, source_target_pairs={{0,2},{1,3},{2,0},{3,1},{4,6},{5,7},{6,4},{7,5},{8,10},{9,11},{10,... | collective-permute-start | bytes 393224 | tf_op jit(solution)/shard_map/ppermute | solution.py:360
  23.5 7.1 %collective-permute-start.6 = (bf16[512,128]{1,0:T(8,128)(2,1)S(1)}, bf16[512,128]{1,0:T(8,128)(2,1)S(1)}, u32[]{:S(2)}, u32[]{:S(2)}) collective-permute-start(bf16[512,128]{1,0:T(8,128)(2,1)S(1)} %get-tuple-element.54), channel_id=1, source_target_pairs={{0,3},{1,2},{2,1},{3,0},{4,7},{5,6},{6,5},{7,4},{8,11},{9,10},{10,... | collective-permute-start | bytes 393224 | tf_op jit(solution)/shard_map/ppermute | solution.py:360
  30.7 4.6 %copy-start.3 = (bf16[1,128,2048]{2,1,0:T(8,128)(2,1)S(1)}, bf16[1,128,2048]{2,1,0:T(8,128)(2,1)}, u32[]{:S(2)}) copy-start(bf16[1,128,2048]{2,1,0:T(8,128)(2,1)} %param.5) | copy-start | bytes 1572868
  31.7 7.0 %collective-permute-start.7 = (bf16[544,128]{1,0:T(8,128)(2,1)S(1)}, bf16[544,128]{1,0:T(8,128)(2,1)S(1)}, u32[]{:S(2)}, u32[]{:S(2)}) collective-permute-start(bf16[544,128]{1,0:T(8,128)(2,1)S(1)} %get-tuple-element.63), channel_id=1, source_target_pairs={{0,3},{1,2},{2,1},{3,0},{4,7},{5,6},{6,5},{7,4},{8,11},{9,10},{10,... | collective-permute-start | bytes 417800 | tf_op jit(solution)/shard_map/ppermute | solution.py:360
  33.0 6.3 %collective-permute-start.8 = (bf16[544,128]{1,0:T(8,128)(2,1)S(1)}, bf16[544,128]{1,0:T(8,128)(2,1)S(1)}, u32[]{:S(2)}, u32[]{:S(2)}) collective-permute-start(bf16[544,128]{1,0:T(8,128)(2,1)S(1)} %get-tuple-element.64), channel_id=1, source_target_pairs={{0,1},{1,0},{2,3},{3,2},{4,5},{5,4},{6,7},{7,6},{8,9},{9,8},{10,11... | collective-permute-start | bytes 417800 | tf_op jit(solution)/shard_map/ppermute | solution.py:360
  33.5 5.8 %collective-permute-start.9 = (bf16[544,128]{1,0:T(8,128)(2,1)S(1)}, bf16[544,128]{1,0:T(8,128)(2,1)S(1)}, u32[]{:S(2)}, u32[]{:S(2)}) collective-permute-start(bf16[544,128]{1,0:T(8,128)(2,1)S(1)} %get-tuple-element.65), channel_id=1, source_target_pairs={{0,2},{1,3},{2,0},{3,1},{4,6},{5,7},{6,4},{7,5},{8,10},{9,11},{10,... | collective-permute-start | bytes 417800 | tf_op jit(solution)/shard_map/ppermute | solution.py:360
  39.4 6.7 %collective-permute-start.10 = (bf16[544,128]{1,0:T(8,128)(2,1)S(1)}, bf16[544,128]{1,0:T(8,128)(2,1)S(1)}, u32[]{:S(2)}, u32[]{:S(2)}) collective-permute-start(bf16[544,128]{1,0:T(8,128)(2,1)S(1)} %get-tuple-element.67), channel_id=1, source_target_pairs={{0,4},{1,5},{2,6},{3,7},{4,0},{5,1},{6,2},{7,3},{8,12},{9,13},{10,... | collective-permute-start | bytes 417800 | tf_op jit(solution)/shard_map/ppermute | solution.py:377
  41.5 8.9 %collective-permute-start.15 = (f32[16,128]{1,0:T(8,128)S(1)}, f32[16,128]{1,0:T(8,128)S(1)}, u32[]{:S(2)}, u32[]{:S(2)}) collective-permute-start(f32[16,128]{1,0:T(8,128)S(1)} %get-tuple-element.68.refs_5_), channel_id=1, source_target_pairs={{0,20},{1,21},{2,22},{3,23},{4,16},{5,17},{6,18},{7,19},{8,28},{9,... | collective-permute-start | bytes 24584 | tf_op jit(solution)/shard_map/ppermute | solution.py:397
  43.0 7.4 %collective-permute-start.14 = (f32[16,128]{1,0:T(8,128)S(1)}, f32[16,128]{1,0:T(8,128)S(1)}, u32[]{:S(2)}, u32[]{:S(2)}) collective-permute-start(f32[16,128]{1,0:T(8,128)S(1)} %get-tuple-element.68.refs_5_), channel_id=1, source_target_pairs={{0,16},{1,17},{2,18},{3,19},{4,20},{5,21},{6,22},{7,23},{8,24},{9,... | collective-permute-start | bytes 24584 | tf_op jit(solution)/shard_map/ppermute | solution.py:397
  46.4 10.9 %collective-permute-start.11 = (bf16[512,128]{1,0:T(8,128)(2,1)S(1)}, bf16[512,128]{1,0:T(8,128)(2,1)S(1)}, u32[]{:S(2)}, u32[]{:S(2)}) collective-permute-start(bf16[512,128]{1,0:T(8,128)(2,1)S(1)} %get-tuple-element.69), channel_id=1, source_target_pairs={{0,2},{1,3},{2,0},{3,1},{4,6},{5,7},{6,4},{7,5},{8,10},{9,11},{10,... | collective-permute-start | bytes 393224 | tf_op jit(solution)/shard_map/ppermute | solution.py:360
  48.8 6.0 %collective-permute-start.12 = (bf16[512,128]{1,0:T(8,128)(2,1)S(1)}, bf16[512,128]{1,0:T(8,128)(2,1)S(1)}, u32[]{:S(2)}, u32[]{:S(2)}) collective-permute-start(bf16[512,128]{1,0:T(8,128)(2,1)S(1)} %get-tuple-element.71), channel_id=1, source_target_pairs={{0,3},{1,2},{2,1},{3,0},{4,7},{5,6},{6,5},{7,4},{8,11},{9,10},{10,... | collective-permute-start | bytes 393224 | tf_op jit(solution)/shard_map/ppermute | solution.py:360
  49.9 6.2 %collective-permute-start.13 = (bf16[512,128]{1,0:T(8,128)(2,1)S(1)}, bf16[512,128]{1,0:T(8,128)(2,1)S(1)}, u32[]{:S(2)}, u32[]{:S(2)}) collective-permute-start(bf16[512,128]{1,0:T(8,128)(2,1)S(1)} %get-tuple-element.72), channel_id=1, source_target_pairs={{0,1},{1,0},{2,3},{3,2},{4,5},{5,4},{6,7},{7,6},{8,9},{9,8},{10,11... | collective-permute-start | bytes 393224 | tf_op jit(solution)/shard_map/ppermute | solution.py:360
  50.4 7.0 %collective-permute-start.16 = (f32[16,128]{1,0:T(8,128)S(1)}, f32[16,128]{1,0:T(8,128)S(1)}, u32[]{:S(2)}, u32[]{:S(2)}) collective-permute-start(f32[16,128]{1,0:T(8,128)S(1)} %add_add_fusion.refs_7_), channel_id=1, source_target_pairs={{0,8},{8,0},{16,24},{24,16},{1,9},{9,1},{17,25},{25,17},{2,10},{10... | collective-permute-start | bytes 24584 | tf_op jit(solution)/shard_map/ppermute | solution.py:349

commit v8 on v7

--- a/solution.py
+++ b/solution.py
@@ -299,21 +299,20 @@
     out_ref[...] = (own + moved).astype(HALF)
 
 
-def scan_kernel(group, orders, reverse, masked, size, riding, *refs):
+def scan_kernel(group, orders, slots, reverse, masked, size, riding, *refs):
     sources = [partner_of(orders[0], j) for j in range(group)]
-    targets = [partner_of(orders[1], j) for j in range(group)]
     carry = refs[0][0:size, :].astype(F32)
     if masked:
         carry = carry * group_flag(group, reverse, 1)
     blocks = [ref[0:size, :].astype(F32) for ref in refs[1 : 1 + group]]
-    out_refs = refs[-group - riding :][:group]
-    for j in range(group):
+    out_refs = refs[-len(slots) - riding :][: len(slots)]
+    for slot, out_ref in zip(slots, out_refs):
+        target = partner_of(orders[1], slot)
         total = carry
         for i in range(group):
-            earlier = sources[i] < targets[j]
-            later = sources[i] > targets[j]
-            total += jnp.where(later if reverse else earlier, 1.0, 0.0) * blocks[i]
-        out_refs[j][...] = total.astype(HALF)
+            known = sources[i] > target if reverse else sources[i] < target
+            total += jnp.where(known, 1.0, 0.0) * blocks[i]
+        out_ref[...] = total.astype(HALF)
     if riding:
         refs[-1][...] = refs[1 + group][...] + wide_rows(refs[0], size)
 
@@ -406,13 +405,20 @@
         )
         (carry,) = call(kernel, [piece], [carry, moved], 0)
         distance *= 2
-    sums = call(
-        part(scan_kernel, group, orders, reverse, groups <= 2, size, riding),
-        [piece] * group + [gain_shape] * riding,
-        [carry] + received + (gains[:1] if riding else []),
-        0,
-    )
-    results = own_and_swapped(sums[:group], orders[1])
+    pieces, after = {}, []
+    for slots in ((1,), (2,), (3, 0)):
+        adding = riding if 0 in slots else 0
+        inputs = [carry] + received + gains[:adding] + after
+        sums = call(
+            part(scan_kernel, group, orders, slots, reverse, groups <= 2, size, adding),
+            [piece] * len(slots) + [gain_shape] * adding,
+            inputs,
+            0,
+            ins={len(inputs) - 1: ANY} if after else {},
+        )
+        pieces.update(zip(slots, sums))
+        after = [sums[0]]
+    results = own_and_swapped([pieces[slot] for slot in range(group)], orders[1])
     if riding:
         gains = [sums[-1] + (gains[1] + gains[2])]
     return results, (gains[0] if gains else None)

time: 58.5 us -> 57.3 us (0.979)
  waiting for transfers between devices: 21.1 us -> 18.4 us
  starting transfers between devices: 23.1 us -> 24.1 us
    ppermute x12, waiting for transfers between devices: 13.5 us -> 11.7 us  [own_and_swapped(): results.append(lax.ppermute(pieces[slot], ('dp', 'seq'), pairs))]
    ppermute x2, waiting for transfers between devices: 7.59 us -> 6.72 us  [shifted(): return lax.ppermute(array, 'seq', pairs)]
    ppermute x2, starting transfers between devices: 2.4 us -> 3.22 us  [exclusive_scan(): gains.append(lax.ppermute(gains[0], ('dp', 'seq'), pairs))]
    pallas_call x11 -> x15, Pallas kernels: 12.3 us -> 12.7 us  [call(): pl.pallas_call(kernel, out_shape=tuple(outs), in_specs=[ins.get(i, VMEM)...]
  transfers between devices with their start and end apart: 17 -> 17, of which waited for: 10 -> 10; matrix products, arithmetic and copies ran while one was open for 0% -> 0% of each run, Pallas kernels for 14% -> 15%
where the time goes in v8:
time: 57.3 us; the launch traced here: 57.1 us
  starting transfers between devices  24.1 us (42%)
  waiting for transfers between devices  18.4 us (32%)
  Pallas kernels  12.7 us (22%)
  local copies, waits for them, and re-layouts  1.06 us (2%)
  between operations  0.8 us (1%)
    ppermute x12, starting transfers between devices, own_and_swapped(): results.append(lax.ppermute(pieces[slot], ('dp', 'seq'), pairs))  16 us
    pallas_call x15, Pallas kernels, call(): pl.pallas_call(kernel, out_shape=tuple(outs), in_specs=[ins.get(i, VMEM)...  12.7 us
    ppermute x12, waiting for transfers between devices, own_and_swapped(): results.append(lax.ppermute(pieces[slot], ('dp', 'seq'), pairs))  11.7 us
    ppermute x2, waiting for transfers between devices, shifted(): return lax.ppermute(array, 'seq', pairs)  6.72 us
    ppermute x2, starting transfers between devices, shifted(): return lax.ppermute(array, 'seq', pairs)  4.89 us
    ppermute x2, starting transfers between devices, exclusive_scan(): gains.append(lax.ppermute(gains[0], ('dp', 'seq'), pairs))  3.22 us
  transfers between devices with their start and end apart: 17, of which 10 were waited for; matrix products, arithmetic and copies ran while one was open for 0% of the time, Pallas kernels for 15%

profile of v8, /device:TPU:0, one launch (start us, length us, event | category | flops | bytes accessed | tf_op | source)
XLA Modules:
  0.0 57.1 jit_solution(10496793649734387461)
XLA Ops:
  0.7 1.7 %shard_map.93 = (bf16[512,128]{1,0:T(8,128)(2,1)S(1)}, bf16[512,128]{1,0:T(8,128)(2,1)S(1)}, bf16[512,128]{1,0:T(8,128)(2,1)S(1)}, bf16[512,128]{1,0:T(8,128)(2,1)S(1)}) custom-call(bf16[128,2048]{1,0:T(8,128)(2,1)} %bitcast.10, bf16[128,2048]{1,0:T(8,128)(2,1)} %bitcast.15), custom_call_target="tpu_custom_call" | custom-call | flops 67108864 | bytes 1572864 | tf_op jit(solution)/shard_map/pallas_call | solution.py:330
  2.3 3.0 %collective-permute-start = (bf16[512,128]{1,0:T(8,128)(2,1)S(1)}, bf16[512,128]{1,0:T(8,128)(2,1)S(1)}, u32[]{:S(2)}, u32[]{:S(2)}) collective-permute-start(bf16[512,128]{1,0:T(8,128)(2,1)S(1)} %get-tuple-element.41), channel_id=1, source_target_pairs={{0,1},{1,0},{2,3},{3,2},{4,5},{5,4},{6,7},{7,6},{8,10},{9,11},{10,... | collective-permute-start | bytes 393224 | tf_op jit(solution)/shard_map/ppermute | solution.py:359
  5.4 1.6 %collective-permute-start.1 = (bf16[512,128]{1,0:T(8,128)(2,1)S(1)}, bf16[512,128]{1,0:T(8,128)(2,1)S(1)}, u32[]{:S(2)}, u32[]{:S(2)}) collective-permute-start(bf16[512,128]{1,0:T(8,128)(2,1)S(1)} %get-tuple-element.42), channel_id=1, source_target_pairs={{0,2},{1,3},{2,0},{3,1},{4,6},{5,7},{6,4},{7,5},{8,9},{9,8},{10,11... | collective-permute-start | bytes 393224 | tf_op jit(solution)/shard_map/ppermute | solution.py:359
  7.0 1.0 %copy-done.2 = bf16[1,128,2048]{2,1,0:T(8,128)(2,1)S(1)} copy-done((bf16[1,128,2048]{2,1,0:T(8,128)(2,1)S(1)}, bf16[1,128,2048]{2,1,0:T(8,128)(2,1)}, u32[]{:S(2)}) %copy-start.2) | copy-done | bytes 524312
  8.0 2.6 %shard_map.92 = (bf16[2048,128]{1,0:T(8,128)(2,1)S(1)}, f32[128,2048]{1,0:T(8,128)S(1)}) custom-call(bf16[128,2048]{1,0:T(8,128)(2,1)S(1)} %bitcast.20, bf16[128,2048]{1,0:T(8,128)(2,1)S(1)} %bitcast.11, bf16[128,2048]{1,0:T(8,128)(2,1)S(1)} %bitcast.16), custom_call_target="tpu_custom_call" | custom-call | flops 134217728 | bytes 3145728 | tf_op jit(solution)/shard_map/pallas_call | solution.py:330
  10.6 1.0 %collective-permute-done.1.refs_2_.refs_3_ = bf16[512,128]{1,0:T(8,128)(2,1)S(1)} collective-permute-done((bf16[512,128]{1,0:T(8,128)(2,1)S(1)}, bf16[512,128]{1,0:T(8,128)(2,1)S(1)}, u32[]{:S(2)}, u32[]{:S(2)}) %collective-permute-start.1) | collective-permute-done | bytes 131104 | tf_op jit(solution)/shard_map/ppermute | solution.py:359
  11.6 1.3 %collective-permute-done.2.refs_3_.refs_4_ = bf16[512,128]{1,0:T(8,128)(2,1)S(1)} collective-permute-done((bf16[512,128]{1,0:T(8,128)(2,1)S(1)}, bf16[512,128]{1,0:T(8,128)(2,1)S(1)}, u32[]{:S(2)}, u32[]{:S(2)}) %collective-permute-start.2) | collective-permute-done | bytes 131104 | tf_op jit(solution)/shard_map/ppermute | solution.py:359
  12.9 2.9 %collective-permute-start.3 = (bf16[512,128]{1,0:T(8,128)(2,1)S(1)}, bf16[512,128]{1,0:T(8,128)(2,1)S(1)}, u32[]{:S(2)}, u32[]{:S(2)}) collective-permute-start(bf16[512,128]{1,0:T(8,128)(2,1)S(1)} %shard_map.94), channel_id=1, source_target_pairs={{0,4},{1,5},{2,6},{3,7},{4,0},{5,1},{6,2},{7,3},{8,12},{9,13},{10,... | collective-permute-start | bytes 393224 | tf_op jit(solution)/shard_map/ppermute | solution.py:376
  15.8 5.4 %collective-permute-done.3.refs_0_ = bf16[512,128]{1,0:T(8,128)(2,1)S(1)} collective-permute-done((bf16[512,128]{1,0:T(8,128)(2,1)S(1)}, bf16[512,128]{1,0:T(8,128)(2,1)S(1)}, u32[]{:S(2)}, u32[]{:S(2)}) %collective-permute-start.3) | collective-permute-done | bytes 131104 | tf_op jit(solution)/shard_map/ppermute | solution.py:376
  21.2 0.1 shard_map.95.refs_5_
  21.4 0.1 shard_map.96.refs_5_
  21.6 1.8 %collective-permute-start.4 = (bf16[512,128]{1,0:T(8,128)(2,1)S(1)}, bf16[512,128]{1,0:T(8,128)(2,1)S(1)}, u32[]{:S(2)}, u32[]{:S(2)}) collective-permute-start(bf16[512,128]{1,0:T(8,128)(2,1)S(1)} %shard_map.95.refs_5_), channel_id=1, source_target_pairs={{0,1},{1,0},{2,3},{3,2},{4,5},{5,4},{6,7},{7,6},{8,9},{9,8},{10,11... | collective-permute-start | bytes 393224 | tf_op jit(solution)/shard_map/ppermute | solution.py:359
  23.5 0.2 shard_map.97
  23.7 1.7 %collective-permute-start.6 = (bf16[512,128]{1,0:T(8,128)(2,1)S(1)}, bf16[512,128]{1,0:T(8,128)(2,1)S(1)}, u32[]{:S(2)}, u32[]{:S(2)}) collective-permute-start(bf16[512,128]{1,0:T(8,128)(2,1)S(1)} %get-tuple-element.48), channel_id=1, source_target_pairs={{0,3},{1,2},{2,1},{3,0},{4,7},{5,6},{6,5},{7,4},{8,11},{9,10},{10,... | collective-permute-start | bytes 393224 | tf_op jit(solution)/shard_map/ppermute | solution.py:359
  25.4 2.4 %collective-permute-done.5.refs_6_.refs_11_ = bf16[512,128]{1,0:T(8,128)(2,1)S(1)} collective-permute-done((bf16[512,128]{1,0:T(8,128)(2,1)S(1)}, bf16[512,128]{1,0:T(8,128)(2,1)S(1)}, u32[]{:S(2)}, u32[]{:S(2)}) %collective-permute-start.5) | collective-permute-done | bytes 131104 | tf_op jit(solution)/shard_map/ppermute | solution.py:359
  28.0 0.4 shard_map.98
  28.4 1.5 %collective-permute-done.6.refs_7_.refs_12_ = bf16[512,128]{1,0:T(8,128)(2,1)S(1)} collective-permute-done((bf16[512,128]{1,0:T(8,128)(2,1)S(1)}, bf16[512,128]{1,0:T(8,128)(2,1)S(1)}, u32[]{:S(2)}, u32[]{:S(2)}) %collective-permute-start.6) | collective-permute-done | bytes 131104 | tf_op jit(solution)/shard_map/ppermute | solution.py:359
  29.8 1.0 %shard_map.99 = (f32[128,512]{1,0:T(8,128)S(1)}, f32[128,128]{1,0:T(8,128)S(1)}, bf16[128,2048]{1,0:T(8,128)(2,1)S(1)}, bf16[544,128]{1,0:T(8,128)(2,1)S(1)}, bf...) custom-call(bf16[128,2048]{1,0:T(8,128)(2,1)S(1)} %bitcast.22, ...), custom_call_target="tpu_custom_call" | custom-call | flops 134217728 | bytes 4825088 | tf_op jit(solution)/shard_map/pallas_call | solution.py:330
  30.8 2.7 %collective-permute-start.7 = (bf16[544,128]{1,0:T(8,128)(2,1)S(1)}, bf16[544,128]{1,0:T(8,128)(2,1)S(1)}, u32[]{:S(2)}, u32[]{:S(2)}) collective-permute-start(bf16[544,128]{1,0:T(8,128)(2,1)S(1)} %get-tuple-element.57), channel_id=1, source_target_pairs={{0,3},{1,2},{2,1},{3,0},{4,7},{5,6},{6,5},{7,4},{8,11},{9,10},{10,... | collective-permute-start | bytes 417800 | tf_op jit(solution)/shard_map/ppermute | solution.py:359
  33.5 0.8 %collective-permute-start.8 = (bf16[544,128]{1,0:T(8,128)(2,1)S(1)}, bf16[544,128]{1,0:T(8,128)(2,1)S(1)}, u32[]{:S(2)}, u32[]{:S(2)}) collective-permute-start(bf16[544,128]{1,0:T(8,128)(2,1)S(1)} %get-tuple-element.58), channel_id=1, source_target_pairs={{0,1},{1,0},{2,3},{3,2},{4,5},{5,4},{6,7},{7,6},{8,9},{9,8},{10,11... | collective-permute-start | bytes 417800 | tf_op jit(solution)/shard_map/ppermute | solution.py:359
  34.4 3.5 %shard_map.100 = (bf16[128,2048]{1,0:T(8,128)(2,1)}, bf16[128,2048]{1,0:T(8,128)(2,1)}, f32[128,2048]{1,0:T(8,128)S(1)}, f32[128,2048]{1,0:T(8,128)S(1)}, f32[8,128]{1,0:T(8,128)S(1)}) custom-call(bf16[128,2048]{1,0:T(8,128)(2,1)S(1)} %bitcast.23, bf16[128,2048]{1,0:T(8,128)(2,1)S(1)} %bitcast.12, bf16[128,2048]{1,0:T(8,128)(2,1)S(1)} %bitcast.17, ...), custom_call_target="tpu_custom_call" | custom-call | flops 335544320 | bytes 7680000 | tf_op jit(solution)/shard_map/pallas_call | solution.py:330
  37.9 0.7 %collective-permute-done.8.refs_2_.refs_3_ = bf16[544,128]{1,0:T(8,128)(2,1)S(1)} collective-permute-done((bf16[544,128]{1,0:T(8,128)(2,1)S(1)}, bf16[544,128]{1,0:T(8,128)(2,1)S(1)}, u32[]{:S(2)}, u32[]{:S(2)}) %collective-permute-start.8) | collective-permute-done | bytes 139296 | tf_op jit(solution)/shard_map/ppermute | solution.py:359
  38.6 0.8 %collective-permute-done.9.refs_3_.refs_4_ = bf16[544,128]{1,0:T(8,128)(2,1)S(1)} collective-permute-done((bf16[544,128]{1,0:T(8,128)(2,1)S(1)}, bf16[544,128]{1,0:T(8,128)(2,1)S(1)}, u32[]{:S(2)}, u32[]{:S(2)}) %collective-permute-start.9) | collective-permute-done | bytes 139296 | tf_op jit(solution)/shard_map/ppermute | solution.py:359
  39.5 2.0 %collective-permute-start.10 = (bf16[544,128]{1,0:T(8,128)(2,1)S(1)}, bf16[544,128]{1,0:T(8,128)(2,1)S(1)}, u32[]{:S(2)}, u32[]{:S(2)}) collective-permute-start(bf16[544,128]{1,0:T(8,128)(2,1)S(1)} %get-tuple-element.61), channel_id=1, source_target_pairs={{0,4},{1,5},{2,6},{3,7},{4,0},{5,1},{6,2},{7,3},{8,12},{9,13},{10,... | collective-permute-start | bytes 417800 | tf_op jit(solution)/shard_map/ppermute | solution.py:376
  41.5 3.2 %collective-permute-start.15 = (f32[16,128]{1,0:T(8,128)S(1)}, f32[16,128]{1,0:T(8,128)S(1)}, u32[]{:S(2)}, u32[]{:S(2)}) collective-permute-start(f32[16,128]{1,0:T(8,128)S(1)} %get-tuple-element.62.refs_5_), channel_id=1, source_target_pairs={{0,20},{1,21},{2,22},{3,23},{4,16},{5,17},{6,18},{7,19},{8,28},{9,... | collective-permute-start | bytes 24584 | tf_op jit(solution)/shard_map/ppermute | solution.py:396
  44.7 1.3 %collective-permute-done.10.refs_0_ = bf16[544,128]{1,0:T(8,128)(2,1)S(1)} collective-permute-done((bf16[544,128]{1,0:T(8,128)(2,1)S(1)}, bf16[544,128]{1,0:T(8,128)(2,1)S(1)}, u32[]{:S(2)}, u32[]{:S(2)}) %collective-permute-start.10) | collective-permute-done | bytes 139296 | tf_op jit(solution)/shard_map/ppermute | solution.py:376
  46.2 3.4 %collective-permute-start.12 = (bf16[512,128]{1,0:T(8,128)(2,1)S(1)}, bf16[512,128]{1,0:T(8,128)(2,1)S(1)}, u32[]{:S(2)}, u32[]{:S(2)}) collective-permute-start(bf16[512,128]{1,0:T(8,128)(2,1)S(1)} %shard_map.102.refs_5_), channel_id=1, source_target_pairs={{0,3},{1,2},{2,1},{3,0},{4,7},{5,6},{6,5},{7,4},{8,11},{9,10},{10,... | collective-permute-start | bytes 393224 | tf_op jit(solution)/shard_map/ppermute | solution.py:359
  49.8 0.7 %collective-permute-start.13 = (bf16[512,128]{1,0:T(8,128)(2,1)S(1)}, bf16[512,128]{1,0:T(8,128)(2,1)S(1)}, u32[]{:S(2)}, u32[]{:S(2)}) collective-permute-start(bf16[512,128]{1,0:T(8,128)(2,1)S(1)} %shard_map.103.refs_6_), channel_id=1, source_target_pairs={{0,1},{1,0},{2,3},{3,2},{4,5},{5,4},{6,7},{7,6},{8,9},{9,8},{10,11... | collective-permute-start | bytes 393224 | tf_op jit(solution)/shard_map/ppermute | solution.py:359
  50.5 0.2 shard_map.104
  50.9 3.9 %collective-permute-done.13.refs_6_ = bf16[512,128]{1,0:T(8,128)(2,1)S(1)} collective-permute-done((bf16[512,128]{1,0:T(8,128)(2,1)S(1)}, bf16[512,128]{1,0:T(8,128)(2,1)S(1)}, u32[]{:S(2)}, u32[]{:S(2)}) %collective-permute-start.13) | collective-permute-done | bytes 131104 | tf_op jit(solution)/shard_map/ppermute | solution.py:359
  54.8 1.3 %shard_map.105 = (bf16[128,2048]{1,0:T(8,128)(2,1)}, bf16[128,2048]{1,0:T(8,128)(2,1)}) custom-call(bf16[128,2048]{1,0:T(8,128)(2,1)S(1)} %bitcast.13, bf16[128,2048]{1,0:T(8,128)(2,1)S(1)} %bitcast.18, f32[128,2048]{1,0:T(8,128)S(1)} %get-tuple-element.54.refs_2_, f32[128,2048]{1,0:T(8,128)S(1)} %get-tuple-element.55.refs_3_, ...), custom_call_target="tpu_custom_call" | custom-call | flops 67108864 | bytes 4587520 | tf_op jit(solution)/shard_map/pallas_call | solution.py:330
  56.1 1.0 %shard_map.106 = (bf16[128,2048]{1,0:T(8,128)(2,1)}, bf16[128,2048]{1,0:T(8,128)(2,1)}, f32[16,128]{1,0:T(8,128)}) custom-call(bf16[128,2048]{1,0:T(8,128)(2,1)S(1)} %bitcast.14, bf16[128,2048]{1,0:T(8,128)(2,1)S(1)} %bitcast.19, f32[128,2048]{1,0:T(8,128)S(1)} %get-tuple-element.54.refs_2_, ...), custom_call_target="tpu_custom_call", output_to_operand_aliasing={{0}: (5, {}), {1}: (6, {})} | custom-call | flops 67108864 | bytes 5398528 | tf_op jit(solution)/shard_map/pallas_call | solution.py:330
  (30 shorter events, 0.8 us)
Async XLA Ops:
  0.6 6.3 %copy-start = (bf16[1,128,2048]{2,1,0:T(8,128)(2,1)S(1)}, bf16[1,128,2048]{2,1,0:T(8,128)(2,1)}, u32[]{:S(2)}) copy-start(bf16[1,128,2048]{2,1,0:T(8,128)(2,1)} %param.6) | copy-start | bytes 1572868
  0.6 6.3 %copy-start.1 = (bf16[1,128,2048]{2,1,0:T(8,128)(2,1)S(1)}, bf16[1,128,2048]{2,1,0:T(8,128)(2,1)}, u32[]{:S(2)}) copy-start(bf16[1,128,2048]{2,1,0:T(8,128)(2,1)} %param.7) | copy-start | bytes 1572868
  2.3 8.3 %collective-permute-start = (bf16[512,128]{1,0:T(8,128)(2,1)S(1)}, bf16[512,128]{1,0:T(8,128)(2,1)S(1)}, u32[]{:S(2)}, u32[]{:S(2)}) collective-permute-start(bf16[512,128]{1,0:T(8,128)(2,1)S(1)} %get-tuple-element.41), channel_id=1, source_target_pairs={{0,1},{1,0},{2,3},{3,2},{4,5},{5,4},{6,7},{7,6},{8,10},{9,11},{10,... | collective-permute-start | bytes 393224 | tf_op jit(solution)/shard_map/ppermute | solution.py:359
  5.4 6.2 %collective-permute-start.1 = (bf16[512,128]{1,0:T(8,128)(2,1)S(1)}, bf16[512,128]{1,0:T(8,128)(2,1)S(1)}, u32[]{:S(2)}, u32[]{:S(2)}) collective-permute-start(bf16[512,128]{1,0:T(8,128)(2,1)S(1)} %get-tuple-element.42), channel_id=1, source_target_pairs={{0,2},{1,3},{2,0},{3,1},{4,6},{5,7},{6,4},{7,5},{8,9},{9,8},{10,11... | collective-permute-start | bytes 393224 | tf_op jit(solution)/shard_map/ppermute | solution.py:359
  7.0 5.9 %collective-permute-start.2 = (bf16[512,128]{1,0:T(8,128)(2,1)S(1)}, bf16[512,128]{1,0:T(8,128)(2,1)S(1)}, u32[]{:S(2)}, u32[]{:S(2)}) collective-permute-start(bf16[512,128]{1,0:T(8,128)(2,1)S(1)} %get-tuple-element.43), channel_id=1, source_target_pairs={{0,3},{1,2},{2,1},{3,0},{4,7},{5,6},{6,5},{7,4},{8,11},{9,10},{10,... | collective-permute-start | bytes 393224 | tf_op jit(solution)/shard_map/ppermute | solution.py:359
  7.0 1.0 %copy-start.2 = (bf16[1,128,2048]{2,1,0:T(8,128)(2,1)S(1)}, bf16[1,128,2048]{2,1,0:T(8,128)(2,1)}, u32[]{:S(2)}) copy-start(bf16[1,128,2048]{2,1,0:T(8,128)(2,1)} %param.5) | copy-start | bytes 1572868
  12.9 8.3 %collective-permute-start.3 = (bf16[512,128]{1,0:T(8,128)(2,1)S(1)}, bf16[512,128]{1,0:T(8,128)(2,1)S(1)}, u32[]{:S(2)}, u32[]{:S(2)}) collective-permute-start(bf16[512,128]{1,0:T(8,128)(2,1)S(1)} %shard_map.94), channel_id=1, source_target_pairs={{0,4},{1,5},{2,6},{3,7},{4,0},{5,1},{6,2},{7,3},{8,12},{9,13},{10,... | collective-permute-start | bytes 393224 | tf_op jit(solution)/shard_map/ppermute | solution.py:376
  21.5 6.4 %copy-start.4 = (bf16[1,128,2048]{2,1,0:T(8,128)(2,1)S(1)}, bf16[1,128,2048]{2,1,0:T(8,128)(2,1)}, u32[]{:S(2)}) copy-start(bf16[1,128,2048]{2,1,0:T(8,128)(2,1)} %param.9) | copy-start | bytes 1572868
  21.5 6.3 %collective-permute-start.5 = (bf16[512,128]{1,0:T(8,128)(2,1)S(1)}, bf16[512,128]{1,0:T(8,128)(2,1)S(1)}, u32[]{:S(2)}, u32[]{:S(2)}) collective-permute-start(bf16[512,128]{1,0:T(8,128)(2,1)S(1)} %shard_map.96.refs_5_), channel_id=1, source_target_pairs={{0,2},{1,3},{2,0},{3,1},{4,6},{5,7},{6,4},{7,5},{8,10},{9,11},{10,... | collective-permute-start | bytes 393224 | tf_op jit(solution)/shard_map/ppermute | solution.py:359
  21.6 6.3 %collective-permute-start.4 = (bf16[512,128]{1,0:T(8,128)(2,1)S(1)}, bf16[512,128]{1,0:T(8,128)(2,1)S(1)}, u32[]{:S(2)}, u32[]{:S(2)}) collective-permute-start(bf16[512,128]{1,0:T(8,128)(2,1)S(1)} %shard_map.95.refs_5_), channel_id=1, source_target_pairs={{0,1},{1,0},{2,3},{3,2},{4,5},{5,4},{6,7},{7,6},{8,9},{9,8},{10,11... | collective-permute-start | bytes 393224 | tf_op jit(solution)/shard_map/ppermute | solution.py:359
  23.5 4.5 %copy-start.5 = (f32[2048]{0:T(1024)S(1)}, f32[2048]{0:T(1024)}, u32[]{:S(2)}) copy-start(f32[2048]{0:T(1024)} %param.8) | copy-start | bytes 24580
  23.7 6.1 %collective-permute-start.6 = (bf16[512,128]{1,0:T(8,128)(2,1)S(1)}, bf16[512,128]{1,0:T(8,128)(2,1)S(1)}, u32[]{:S(2)}, u32[]{:S(2)}) collective-permute-start(bf16[512,128]{1,0:T(8,128)(2,1)S(1)} %get-tuple-element.48), channel_id=1, source_target_pairs={{0,3},{1,2},{2,1},{3,0},{4,7},{5,6},{6,5},{7,4},{8,11},{9,10},{10,... | collective-permute-start | bytes 393224 | tf_op jit(solution)/shard_map/ppermute | solution.py:359
  29.8 4.6 %copy-start.3 = (bf16[1,128,2048]{2,1,0:T(8,128)(2,1)S(1)}, bf16[1,128,2048]{2,1,0:T(8,128)(2,1)}, u32[]{:S(2)}) copy-start(bf16[1,128,2048]{2,1,0:T(8,128)(2,1)} %param.5) | copy-start | bytes 1572868
  30.8 7.0 %collective-permute-start.7 = (bf16[544,128]{1,0:T(8,128)(2,1)S(1)}, bf16[544,128]{1,0:T(8,128)(2,1)S(1)}, u32[]{:S(2)}, u32[]{:S(2)}) collective-permute-start(bf16[544,128]{1,0:T(8,128)(2,1)S(1)} %get-tuple-element.57), channel_id=1, source_target_pairs={{0,3},{1,2},{2,1},{3,0},{4,7},{5,6},{6,5},{7,4},{8,11},{9,10},{10,... | collective-permute-start | bytes 417800 | tf_op jit(solution)/shard_map/ppermute | solution.py:359
  33.5 5.1 %collective-permute-start.8 = (bf16[544,128]{1,0:T(8,128)(2,1)S(1)}, bf16[544,128]{1,0:T(8,128)(2,1)S(1)}, u32[]{:S(2)}, u32[]{:S(2)}) collective-permute-start(bf16[544,128]{1,0:T(8,128)(2,1)S(1)} %get-tuple-element.58), channel_id=1, source_target_pairs={{0,1},{1,0},{2,3},{3,2},{4,5},{5,4},{6,7},{7,6},{8,9},{9,8},{10,11... | collective-permute-start | bytes 417800 | tf_op jit(solution)/shard_map/ppermute | solution.py:359
  34.4 5.1 %collective-permute-start.9 = (bf16[544,128]{1,0:T(8,128)(2,1)S(1)}, bf16[544,128]{1,0:T(8,128)(2,1)S(1)}, u32[]{:S(2)}, u32[]{:S(2)}) collective-permute-start(bf16[544,128]{1,0:T(8,128)(2,1)S(1)} %get-tuple-element.59), channel_id=1, source_target_pairs={{0,2},{1,3},{2,0},{3,1},{4,6},{5,7},{6,4},{7,5},{8,10},{9,11},{10,... | collective-permute-start | bytes 417800 | tf_op jit(solution)/shard_map/ppermute | solution.py:359
  39.5 6.5 %collective-permute-start.10 = (bf16[544,128]{1,0:T(8,128)(2,1)S(1)}, bf16[544,128]{1,0:T(8,128)(2,1)S(1)}, u32[]{:S(2)}, u32[]{:S(2)}) collective-permute-start(bf16[544,128]{1,0:T(8,128)(2,1)S(1)} %get-tuple-element.61), channel_id=1, source_target_pairs={{0,4},{1,5},{2,6},{3,7},{4,0},{5,1},{6,2},{7,3},{8,12},{9,13},{10,... | collective-permute-start | bytes 417800 | tf_op jit(solution)/shard_map/ppermute | solution.py:376
  41.5 9.3 %collective-permute-start.15 = (f32[16,128]{1,0:T(8,128)S(1)}, f32[16,128]{1,0:T(8,128)S(1)}, u32[]{:S(2)}, u32[]{:S(2)}) collective-permute-start(f32[16,128]{1,0:T(8,128)S(1)} %get-tuple-element.62.refs_5_), channel_id=1, source_target_pairs={{0,20},{1,21},{2,22},{3,23},{4,16},{5,17},{6,18},{7,19},{8,28},{9,... | collective-permute-start | bytes 24584 | tf_op jit(solution)/shard_map/ppermute | solution.py:396
  44.7 6.1 %collective-permute-start.14 = (f32[16,128]{1,0:T(8,128)S(1)}, f32[16,128]{1,0:T(8,128)S(1)}, u32[]{:S(2)}, u32[]{:S(2)}) collective-permute-start(f32[16,128]{1,0:T(8,128)S(1)} %get-tuple-element.62.refs_5_), channel_id=1, source_target_pairs={{0,16},{1,17},{2,18},{3,19},{4,20},{5,21},{6,22},{7,23},{8,24},{9,... | collective-permute-start | bytes 24584 | tf_op jit(solution)/shard_map/ppermute | solution.py:396
  46.2 8.6 %collective-permute-start.12 = (bf16[512,128]{1,0:T(8,128)(2,1)S(1)}, bf16[512,128]{1,0:T(8,128)(2,1)S(1)}, u32[]{:S(2)}, u32[]{:S(2)}) collective-permute-start(bf16[512,128]{1,0:T(8,128)(2,1)S(1)} %shard_map.102.refs_5_), channel_id=1, source_target_pairs={{0,3},{1,2},{2,1},{3,0},{4,7},{5,6},{6,5},{7,4},{8,11},{9,10},{10,... | collective-permute-start | bytes 393224 | tf_op jit(solution)/shard_map/ppermute | solution.py:359
  49.8 5.0 %collective-permute-start.13 = (bf16[512,128]{1,0:T(8,128)(2,1)S(1)}, bf16[512,128]{1,0:T(8,128)(2,1)S(1)}, u32[]{:S(2)}, u32[]{:S(2)}) collective-permute-start(bf16[512,128]{1,0:T(8,128)(2,1)S(1)} %shard_map.103.refs_6_), channel_id=1, source_target_pairs={{0,1},{1,0},{2,3},{3,2},{4,5},{5,4},{6,7},{7,6},{8,9},{9,8},{10,11... | collective-permute-start | bytes 393224 | tf_op jit(solution)/shard_map/ppermute | solution.py:359
  50.7 5.4 %collective-permute-start.11 = (bf16[512,128]{1,0:T(8,128)(2,1)S(1)}, bf16[512,128]{1,0:T(8,128)(2,1)S(1)}, u32[]{:S(2)}, u32[]{:S(2)}) collective-permute-start(bf16[512,128]{1,0:T(8,128)(2,1)S(1)} %get-tuple-element.63), channel_id=1, source_target_pairs={{0,2},{1,3},{2,0},{3,1},{4,6},{5,7},{6,4},{7,5},{8,10},{9,11},{10,... | collective-permute-start | bytes 393224 | tf_op jit(solution)/shard_map/ppermute | solution.py:359
  50.8 5.3 %collective-permute-start.16 = (f32[16,128]{1,0:T(8,128)S(1)}, f32[16,128]{1,0:T(8,128)S(1)}, u32[]{:S(2)}, u32[]{:S(2)}) collective-permute-start(f32[16,128]{1,0:T(8,128)S(1)} %add_add_fusion.refs_7_), channel_id=1, source_target_pairs={{0,8},{8,0},{16,24},{24,16},{1,9},{9,1},{17,25},{25,17},{2,10},{10... | collective-permute-start | bytes 24584 | tf_op jit(solution)/shard_map/ppermute | solution.py:348

commit v9 on v8

--- a/solution.py
+++ b/solution.py
@@ -31,11 +31,8 @@
     return lax.rem(lax.axis_index("seq"), group)
 
 
-CROSSED = ((0, 1, 2, 3), (0, 2, 1, 3))
-DIAGONAL_FIRST = ((0, 3, 1, 2), (0, 3, 1, 2))
-X_FIRST = ((0, 1, 2, 3), (0, 1, 2, 3))
-STATE_ORDERS = (CROSSED, X_FIRST)
-GRAD_ORDERS = (DIAGONAL_FIRST, DIAGONAL_FIRST)
+STATE_ORDERS = (((0, 1, 2, 3), (0, 2, 1, 3)), ((0, 1, 2, 3), (0, 1, 2, 3)))
+GRAD_ORDERS = (((0, 2, 3, 1), (0, 3, 1, 2)), ((0, 3, 1, 2), (0, 1, 3, 2)))
 NORM_ORDERS = (STATE_ORDERS[1], GRAD_ORDERS[0])
 
 
@@ -135,6 +132,7 @@
     features = q_ref.shape[1]
     width = features // group
     last = orders[0][0][group - 1]
+    odd = lax.rem(lax.axis_index("dp"), 2) == 1
     squares, inner = attend(
         head,
         orders[0],
@@ -156,10 +154,11 @@
         for i in range(width // head):
             part = features_at(orders[1], slot, i, width, head)
             local = columns(i * head, head)
-            if orders[1][0][slot] == last:
-                attended = late_ref[:, local]
-            else:
-                attended = early_ref[:, part]
+            late = [order[slot] == last for order in orders[1]]
+            attended = late_ref[:, local] if late[0] else early_ref[:, part]
+            if late[0] != late[1]:
+                other = late_ref[:, local] if late[1] else early_ref[:, part]
+                attended = jnp.where(odd, other, attended)
             normalized = attended * inverse
             upstream = cot_ref[:, part].astype(F32)
             gain_grad_ref[:, part] = jnp.sum(

time: 57.3 us -> 57.7 us (level)
  waiting for transfers between devices: 18.4 us -> 20 us
  starting transfers between devices: 24.1 us -> 23 us
    ppermute x2, waiting for transfers between devices: 6.72 us -> 8.21 us  [shifted(): return lax.ppermute(array, 'seq', pairs)]
    ppermute x2, starting transfers between devices: 3.22 us -> 2.5 us  [exclusive_scan(): gains.append(lax.ppermute(gains[0], ('dp', 'seq'), pairs))]
where the time goes in v9:
time: 57.7 us; the launch traced here: 57.5 us
  starting transfers between devices  23 us (40%)
  waiting for transfers between devices  20 us (35%)
  Pallas kernels  12.7 us (22%)
  local copies, waits for them, and re-layouts  1.06 us (2%)
  between operations  0.78 us (1%)
    ppermute x12, starting transfers between devices, own_and_swapped(): results.append(lax.ppermute(pieces[slot], ('dp', 'seq'), pairs))  15.5 us
    pallas_call x15, Pallas kernels, call(): pl.pallas_call(kernel, out_shape=tuple(outs), in_specs=[ins.get(i, VMEM)...  12.7 us
    ppermute x12, waiting for transfers between devices, own_and_swapped(): results.append(lax.ppermute(pieces[slot], ('dp', 'seq'), pairs))  11.8 us
    ppermute x2, waiting for transfers between devices, shifted(): return lax.ppermute(array, 'seq', pairs)  8.21 us
    ppermute x2, starting transfers between devices, shifted(): return lax.ppermute(array, 'seq', pairs)  4.87 us
    ppermute x2, starting transfers between devices, exclusive_scan(): gains.append(lax.ppermute(gains[0], ('dp', 'seq'), pairs))  2.5 us
  transfers between devices with their start and end apart: 17, of which 10 were waited for; matrix products, arithmetic and copies ran while one was open for 0% of the time, Pallas kernels for 15%

profile of v9, /device:TPU:0, one launch (start us, length us, event | category | flops | bytes accessed | tf_op | source)
XLA Modules:
  0.0 57.5 jit_solution(16579884532205631397)
XLA Ops:
  0.7 1.7 %shard_map.93 = (bf16[512,128]{1,0:T(8,128)(2,1)S(1)}, bf16[512,128]{1,0:T(8,128)(2,1)S(1)}, bf16[512,128]{1,0:T(8,128)(2,1)S(1)}, bf16[512,128]{1,0:T(8,128)(2,1)S(1)}) custom-call(bf16[128,2048]{1,0:T(8,128)(2,1)} %bitcast.10, bf16[128,2048]{1,0:T(8,128)(2,1)} %bitcast.15), custom_call_target="tpu_custom_call" | custom-call | flops 67108864 | bytes 1572864 | tf_op jit(solution)/shard_map/pallas_call | solution.py:329
  2.3 3.0 %collective-permute-start = (bf16[512,128]{1,0:T(8,128)(2,1)S(1)}, bf16[512,128]{1,0:T(8,128)(2,1)S(1)}, u32[]{:S(2)}, u32[]{:S(2)}) collective-permute-start(bf16[512,128]{1,0:T(8,128)(2,1)S(1)} %get-tuple-element.41), channel_id=1, source_target_pairs={{0,1},{1,0},{2,3},{3,2},{4,5},{5,4},{6,7},{7,6},{8,10},{9,11},{10,... | collective-permute-start | bytes 393224 | tf_op jit(solution)/shard_map/ppermute | solution.py:358
  5.4 1.6 %collective-permute-start.1 = (bf16[512,128]{1,0:T(8,128)(2,1)S(1)}, bf16[512,128]{1,0:T(8,128)(2,1)S(1)}, u32[]{:S(2)}, u32[]{:S(2)}) collective-permute-start(bf16[512,128]{1,0:T(8,128)(2,1)S(1)} %get-tuple-element.42), channel_id=1, source_target_pairs={{0,2},{1,3},{2,0},{3,1},{4,6},{5,7},{6,4},{7,5},{8,9},{9,8},{10,11... | collective-permute-start | bytes 393224 | tf_op jit(solution)/shard_map/ppermute | solution.py:358
  7.0 1.0 %copy-done.2 = bf16[1,128,2048]{2,1,0:T(8,128)(2,1)S(1)} copy-done((bf16[1,128,2048]{2,1,0:T(8,128)(2,1)S(1)}, bf16[1,128,2048]{2,1,0:T(8,128)(2,1)}, u32[]{:S(2)}) %copy-start.2) | copy-done | bytes 524312
  8.0 2.6 %shard_map.92 = (bf16[2048,128]{1,0:T(8,128)(2,1)S(1)}, f32[128,2048]{1,0:T(8,128)S(1)}) custom-call(bf16[128,2048]{1,0:T(8,128)(2,1)S(1)} %bitcast.20, bf16[128,2048]{1,0:T(8,128)(2,1)S(1)} %bitcast.11, bf16[128,2048]{1,0:T(8,128)(2,1)S(1)} %bitcast.16), custom_call_target="tpu_custom_call" | custom-call | flops 134217728 | bytes 3145728 | tf_op jit(solution)/shard_map/pallas_call | solution.py:329
  10.6 1.0 %collective-permute-done.1.refs_2_.refs_3_ = bf16[512,128]{1,0:T(8,128)(2,1)S(1)} collective-permute-done((bf16[512,128]{1,0:T(8,128)(2,1)S(1)}, bf16[512,128]{1,0:T(8,128)(2,1)S(1)}, u32[]{:S(2)}, u32[]{:S(2)}) %collective-permute-start.1) | collective-permute-done | bytes 131104 | tf_op jit(solution)/shard_map/ppermute | solution.py:358
  11.6 1.3 %collective-permute-done.2.refs_3_.refs_4_ = bf16[512,128]{1,0:T(8,128)(2,1)S(1)} collective-permute-done((bf16[512,128]{1,0:T(8,128)(2,1)S(1)}, bf16[512,128]{1,0:T(8,128)(2,1)S(1)}, u32[]{:S(2)}, u32[]{:S(2)}) %collective-permute-start.2) | collective-permute-done | bytes 131104 | tf_op jit(solution)/shard_map/ppermute | solution.py:358
  12.9 2.9 %collective-permute-start.3 = (bf16[512,128]{1,0:T(8,128)(2,1)S(1)}, bf16[512,128]{1,0:T(8,128)(2,1)S(1)}, u32[]{:S(2)}, u32[]{:S(2)}) collective-permute-start(bf16[512,128]{1,0:T(8,128)(2,1)S(1)} %shard_map.94), channel_id=1, source_target_pairs={{0,4},{1,5},{2,6},{3,7},{4,0},{5,1},{6,2},{7,3},{8,12},{9,13},{10,... | collective-permute-start | bytes 393224 | tf_op jit(solution)/shard_map/ppermute | solution.py:375
  15.8 5.4 %collective-permute-done.3.refs_0_ = bf16[512,128]{1,0:T(8,128)(2,1)S(1)} collective-permute-done((bf16[512,128]{1,0:T(8,128)(2,1)S(1)}, bf16[512,128]{1,0:T(8,128)(2,1)S(1)}, u32[]{:S(2)}, u32[]{:S(2)}) %collective-permute-start.3) | collective-permute-done | bytes 131104 | tf_op jit(solution)/shard_map/ppermute | solution.py:375
  21.6 1.8 %collective-permute-start.4 = (bf16[512,128]{1,0:T(8,128)(2,1)S(1)}, bf16[512,128]{1,0:T(8,128)(2,1)S(1)}, u32[]{:S(2)}, u32[]{:S(2)}) collective-permute-start(bf16[512,128]{1,0:T(8,128)(2,1)S(1)} %shard_map.95.refs_5_), channel_id=1, source_target_pairs={{0,1},{1,0},{2,3},{3,2},{4,5},{5,4},{6,7},{7,6},{8,9},{9,8},{10,11... | collective-permute-start | bytes 393224 | tf_op jit(solution)/shard_map/ppermute | solution.py:358
  23.7 1.7 %collective-permute-start.6 = (bf16[512,128]{1,0:T(8,128)(2,1)S(1)}, bf16[512,128]{1,0:T(8,128)(2,1)S(1)}, u32[]{:S(2)}, u32[]{:S(2)}) collective-permute-start(bf16[512,128]{1,0:T(8,128)(2,1)S(1)} %get-tuple-element.48), channel_id=1, source_target_pairs={{0,3},{1,2},{2,1},{3,0},{4,7},{5,6},{6,5},{7,4},{8,11},{9,10},{10,... | collective-permute-start | bytes 393224 | tf_op jit(solution)/shard_map/ppermute | solution.py:358
  25.4 2.4 %collective-permute-done.5.refs_6_.refs_11_ = bf16[512,128]{1,0:T(8,128)(2,1)S(1)} collective-permute-done((bf16[512,128]{1,0:T(8,128)(2,1)S(1)}, bf16[512,128]{1,0:T(8,128)(2,1)S(1)}, u32[]{:S(2)}, u32[]{:S(2)}) %collective-permute-start.5) | collective-permute-done | bytes 131104 | tf_op jit(solution)/shard_map/ppermute | solution.py:358
  28.0 0.4 shard_map.98
  28.4 1.5 %collective-permute-done.6.refs_7_.refs_12_ = bf16[512,128]{1,0:T(8,128)(2,1)S(1)} collective-permute-done((bf16[512,128]{1,0:T(8,128)(2,1)S(1)}, bf16[512,128]{1,0:T(8,128)(2,1)S(1)}, u32[]{:S(2)}, u32[]{:S(2)}) %collective-permute-start.6) | collective-permute-done | bytes 131104 | tf_op jit(solution)/shard_map/ppermute | solution.py:358
  29.8 1.1 %shard_map.99 = (f32[128,512]{1,0:T(8,128)S(1)}, f32[128,128]{1,0:T(8,128)S(1)}, bf16[128,2048]{1,0:T(8,128)(2,1)S(1)}, bf16[544,128]{1,0:T(8,128)(2,1)S(1)}, bf...) custom-call(bf16[128,2048]{1,0:T(8,128)(2,1)S(1)} %bitcast.22, ...), custom_call_target="tpu_custom_call" | custom-call | flops 134217728 | bytes 4825088 | tf_op jit(solution)/shard_map/pallas_call | solution.py:329
  30.9 2.1 %collective-permute-start.7 = (bf16[544,128]{1,0:T(8,128)(2,1)S(1)}, bf16[544,128]{1,0:T(8,128)(2,1)S(1)}, u32[]{:S(2)}, u32[]{:S(2)}) collective-permute-start(bf16[544,128]{1,0:T(8,128)(2,1)S(1)} %get-tuple-element.57), channel_id=1, source_target_pairs={{0,2},{1,3},{2,0},{3,1},{4,6},{5,7},{6,4},{7,5},{8,11},{9,10},{10,... | collective-permute-start | bytes 417800 | tf_op jit(solution)/shard_map/ppermute | solution.py:358
  33.0 1.2 %collective-permute-start.8 = (bf16[544,128]{1,0:T(8,128)(2,1)S(1)}, bf16[544,128]{1,0:T(8,128)(2,1)S(1)}, u32[]{:S(2)}, u32[]{:S(2)}) collective-permute-start(bf16[544,128]{1,0:T(8,128)(2,1)S(1)} %get-tuple-element.58), channel_id=1, source_target_pairs={{0,3},{1,2},{2,1},{3,0},{4,7},{5,6},{6,5},{7,4},{8,9},{9,8},{10,11... | collective-permute-start | bytes 417800 | tf_op jit(solution)/shard_map/ppermute | solution.py:358
  34.2 0.3 collective-permute-start.9
  34.5 3.5 %shard_map.100 = (bf16[128,2048]{1,0:T(8,128)(2,1)}, bf16[128,2048]{1,0:T(8,128)(2,1)}, f32[128,2048]{1,0:T(8,128)S(1)}, f32[128,2048]{1,0:T(8,128)S(1)}, f32[8,128]{1,0:T(8,128)S(1)}) custom-call(bf16[128,2048]{1,0:T(8,128)(2,1)S(1)} %bitcast.23, bf16[128,2048]{1,0:T(8,128)(2,1)S(1)} %bitcast.12, bf16[128,2048]{1,0:T(8,128)(2,1)S(1)} %bitcast.17, ...), custom_call_target="tpu_custom_call" | custom-call | flops 335544320 | bytes 7680000 | tf_op jit(solution)/shard_map/pallas_call | solution.py:329
  38.0 1.0 %collective-permute-done.8.refs_2_.refs_3_ = bf16[544,128]{1,0:T(8,128)(2,1)S(1)} collective-permute-done((bf16[544,128]{1,0:T(8,128)(2,1)S(1)}, bf16[544,128]{1,0:T(8,128)(2,1)S(1)}, u32[]{:S(2)}, u32[]{:S(2)}) %collective-permute-start.8) | collective-permute-done | bytes 139296 | tf_op jit(solution)/shard_map/ppermute | solution.py:358
  39.0 1.4 %collective-permute-done.9.refs_3_.refs_4_ = bf16[544,128]{1,0:T(8,128)(2,1)S(1)} collective-permute-done((bf16[544,128]{1,0:T(8,128)(2,1)S(1)}, bf16[544,128]{1,0:T(8,128)(2,1)S(1)}, u32[]{:S(2)}, u32[]{:S(2)}) %collective-permute-start.9) | collective-permute-done | bytes 139296 | tf_op jit(solution)/shard_map/ppermute | solution.py:358
  40.5 1.9 %collective-permute-start.10 = (bf16[544,128]{1,0:T(8,128)(2,1)S(1)}, bf16[544,128]{1,0:T(8,128)(2,1)S(1)}, u32[]{:S(2)}, u32[]{:S(2)}) collective-permute-start(bf16[544,128]{1,0:T(8,128)(2,1)S(1)} %get-tuple-element.61), channel_id=1, source_target_pairs={{0,4},{1,5},{2,6},{3,7},{4,0},{5,1},{6,2},{7,3},{8,12},{9,13},{10,... | collective-permute-start | bytes 417800 | tf_op jit(solution)/shard_map/ppermute | solution.py:375
  42.5 2.0 %collective-permute-start.15 = (f32[16,128]{1,0:T(8,128)S(1)}, f32[16,128]{1,0:T(8,128)S(1)}, u32[]{:S(2)}, u32[]{:S(2)}) collective-permute-start(f32[16,128]{1,0:T(8,128)S(1)} %get-tuple-element.62.refs_5_), channel_id=1, source_target_pairs={{0,20},{1,21},{2,22},{3,23},{4,16},{5,17},{6,18},{7,19},{8,28},{9,... | collective-permute-start | bytes 24584 | tf_op jit(solution)/shard_map/ppermute | solution.py:395
  44.5 0.5 collective-permute-start.14
  45.0 2.8 %collective-permute-done.10.refs_0_ = bf16[544,128]{1,0:T(8,128)(2,1)S(1)} collective-permute-done((bf16[544,128]{1,0:T(8,128)(2,1)S(1)}, bf16[544,128]{1,0:T(8,128)(2,1)S(1)}, u32[]{:S(2)}, u32[]{:S(2)}) %collective-permute-start.10) | collective-permute-done | bytes 139296 | tf_op jit(solution)/shard_map/ppermute | solution.py:375
  47.9 1.2 %collective-permute-start.12 = (bf16[512,128]{1,0:T(8,128)(2,1)S(1)}, bf16[512,128]{1,0:T(8,128)(2,1)S(1)}, u32[]{:S(2)}, u32[]{:S(2)}) collective-permute-start(bf16[512,128]{1,0:T(8,128)(2,1)S(1)} %shard_map.102.refs_5_), channel_id=1, source_target_pairs={{0,3},{1,2},{2,1},{3,0},{4,7},{5,6},{6,5},{7,4},{8,9},{9,8},{10,11... | collective-permute-start | bytes 393224 | tf_op jit(solution)/shard_map/ppermute | solution.py:358
  49.3 1.4 %collective-permute-start.13 = (bf16[512,128]{1,0:T(8,128)(2,1)S(1)}, bf16[512,128]{1,0:T(8,128)(2,1)S(1)}, u32[]{:S(2)}, u32[]{:S(2)}) collective-permute-start(bf16[512,128]{1,0:T(8,128)(2,1)S(1)} %shard_map.103.refs_6_), channel_id=1, source_target_pairs={{0,1},{1,0},{2,3},{3,2},{4,5},{5,4},{6,7},{7,6},{8,11},{9,10},{10,... | collective-permute-start | bytes 393224 | tf_op jit(solution)/shard_map/ppermute | solution.py:358
  50.7 0.3 shard_map.104
  51.0 1.0 %collective-permute-start.11 = (bf16[512,128]{1,0:T(8,128)(2,1)S(1)}, bf16[512,128]{1,0:T(8,128)(2,1)S(1)}, u32[]{:S(2)}, u32[]{:S(2)}) collective-permute-start(bf16[512,128]{1,0:T(8,128)(2,1)S(1)} %get-tuple-element.63), channel_id=1, source_target_pairs={{0,2},{1,3},{2,0},{3,1},{4,6},{5,7},{6,4},{7,5},{8,10},{9,11},{10,... | collective-permute-start | bytes 393224 | tf_op jit(solution)/shard_map/ppermute | solution.py:358
  52.1 3.2 %collective-permute-done.13.refs_6_ = bf16[512,128]{1,0:T(8,128)(2,1)S(1)} collective-permute-done((bf16[512,128]{1,0:T(8,128)(2,1)S(1)}, bf16[512,128]{1,0:T(8,128)(2,1)S(1)}, u32[]{:S(2)}, u32[]{:S(2)}) %collective-permute-start.13) | collective-permute-done | bytes 131104 | tf_op jit(solution)/shard_map/ppermute | solution.py:358
  55.3 1.3 %shard_map.105 = (bf16[128,2048]{1,0:T(8,128)(2,1)}, bf16[128,2048]{1,0:T(8,128)(2,1)}) custom-call(bf16[128,2048]{1,0:T(8,128)(2,1)S(1)} %bitcast.13, bf16[128,2048]{1,0:T(8,128)(2,1)S(1)} %bitcast.18, f32[128,2048]{1,0:T(8,128)S(1)} %get-tuple-element.54.refs_2_, f32[128,2048]{1,0:T(8,128)S(1)} %get-tuple-element.55.refs_3_, ...), custom_call_target="tpu_custom_call" | custom-call | flops 67108864 | bytes 4587520 | tf_op jit(solution)/shard_map/pallas_call | solution.py:329
  56.6 1.0 %shard_map.106 = (bf16[128,2048]{1,0:T(8,128)(2,1)}, bf16[128,2048]{1,0:T(8,128)(2,1)}, f32[16,128]{1,0:T(8,128)}) custom-call(bf16[128,2048]{1,0:T(8,128)(2,1)S(1)} %bitcast.14, bf16[128,2048]{1,0:T(8,128)(2,1)S(1)} %bitcast.19, f32[128,2048]{1,0:T(8,128)S(1)} %get-tuple-element.54.refs_2_, ...), custom_call_target="tpu_custom_call", output_to_operand_aliasing={{0}: (5, {}), {1}: (6, {})} | custom-call | flops 67108864 | bytes 5398528 | tf_op jit(solution)/shard_map/pallas_call | solution.py:329
  (30 shorter events, 1.3 us)
Async XLA Ops:
  0.6 6.3 %copy-start = (bf16[1,128,2048]{2,1,0:T(8,128)(2,1)S(1)}, bf16[1,128,2048]{2,1,0:T(8,128)(2,1)}, u32[]{:S(2)}) copy-start(bf16[1,128,2048]{2,1,0:T(8,128)(2,1)} %param.6) | copy-start | bytes 1572868
  0.6 6.3 %copy-start.1 = (bf16[1,128,2048]{2,1,0:T(8,128)(2,1)S(1)}, bf16[1,128,2048]{2,1,0:T(8,128)(2,1)}, u32[]{:S(2)}) copy-start(bf16[1,128,2048]{2,1,0:T(8,128)(2,1)} %param.7) | copy-start | bytes 1572868
  2.3 8.3 %collective-permute-start = (bf16[512,128]{1,0:T(8,128)(2,1)S(1)}, bf16[512,128]{1,0:T(8,128)(2,1)S(1)}, u32[]{:S(2)}, u32[]{:S(2)}) collective-permute-start(bf16[512,128]{1,0:T(8,128)(2,1)S(1)} %get-tuple-element.41), channel_id=1, source_target_pairs={{0,1},{1,0},{2,3},{3,2},{4,5},{5,4},{6,7},{7,6},{8,10},{9,11},{10,... | collective-permute-start | bytes 393224 | tf_op jit(solution)/shard_map/ppermute | solution.py:358
  5.4 6.2 %collective-permute-start.1 = (bf16[512,128]{1,0:T(8,128)(2,1)S(1)}, bf16[512,128]{1,0:T(8,128)(2,1)S(1)}, u32[]{:S(2)}, u32[]{:S(2)}) collective-permute-start(bf16[512,128]{1,0:T(8,128)(2,1)S(1)} %get-tuple-element.42), channel_id=1, source_target_pairs={{0,2},{1,3},{2,0},{3,1},{4,6},{5,7},{6,4},{7,5},{8,9},{9,8},{10,11... | collective-permute-start | bytes 393224 | tf_op jit(solution)/shard_map/ppermute | solution.py:358
  7.0 5.9 %collective-permute-start.2 = (bf16[512,128]{1,0:T(8,128)(2,1)S(1)}, bf16[512,128]{1,0:T(8,128)(2,1)S(1)}, u32[]{:S(2)}, u32[]{:S(2)}) collective-permute-start(bf16[512,128]{1,0:T(8,128)(2,1)S(1)} %get-tuple-element.43), channel_id=1, source_target_pairs={{0,3},{1,2},{2,1},{3,0},{4,7},{5,6},{6,5},{7,4},{8,11},{9,10},{10,... | collective-permute-start | bytes 393224 | tf_op jit(solution)/shard_map/ppermute | solution.py:358
  7.0 1.0 %copy-start.2 = (bf16[1,128,2048]{2,1,0:T(8,128)(2,1)S(1)}, bf16[1,128,2048]{2,1,0:T(8,128)(2,1)}, u32[]{:S(2)}) copy-start(bf16[1,128,2048]{2,1,0:T(8,128)(2,1)} %param.5) | copy-start | bytes 1572868
  12.9 8.3 %collective-permute-start.3 = (bf16[512,128]{1,0:T(8,128)(2,1)S(1)}, bf16[512,128]{1,0:T(8,128)(2,1)S(1)}, u32[]{:S(2)}, u32[]{:S(2)}) collective-permute-start(bf16[512,128]{1,0:T(8,128)(2,1)S(1)} %shard_map.94), channel_id=1, source_target_pairs={{0,4},{1,5},{2,6},{3,7},{4,0},{5,1},{6,2},{7,3},{8,12},{9,13},{10,... | collective-permute-start | bytes 393224 | tf_op jit(solution)/shard_map/ppermute | solution.py:375
  21.5 6.4 %copy-start.4 = (bf16[1,128,2048]{2,1,0:T(8,128)(2,1)S(1)}, bf16[1,128,2048]{2,1,0:T(8,128)(2,1)}, u32[]{:S(2)}) copy-start(bf16[1,128,2048]{2,1,0:T(8,128)(2,1)} %param.9) | copy-start | bytes 1572868
  21.5 6.3 %collective-permute-start.5 = (bf16[512,128]{1,0:T(8,128)(2,1)S(1)}, bf16[512,128]{1,0:T(8,128)(2,1)S(1)}, u32[]{:S(2)}, u32[]{:S(2)}) collective-permute-start(bf16[512,128]{1,0:T(8,128)(2,1)S(1)} %shard_map.96.refs_5_), channel_id=1, source_target_pairs={{0,2},{1,3},{2,0},{3,1},{4,6},{5,7},{6,4},{7,5},{8,10},{9,11},{10,... | collective-permute-start | bytes 393224 | tf_op jit(solution)/shard_map/ppermute | solution.py:358
  21.6 6.3 %collective-permute-start.4 = (bf16[512,128]{1,0:T(8,128)(2,1)S(1)}, bf16[512,128]{1,0:T(8,128)(2,1)S(1)}, u32[]{:S(2)}, u32[]{:S(2)}) collective-permute-start(bf16[512,128]{1,0:T(8,128)(2,1)S(1)} %shard_map.95.refs_5_), channel_id=1, source_target_pairs={{0,1},{1,0},{2,3},{3,2},{4,5},{5,4},{6,7},{7,6},{8,9},{9,8},{10,11... | collective-permute-start | bytes 393224 | tf_op jit(solution)/shard_map/ppermute | solution.py:358
  23.5 4.5 %copy-start.5 = (f32[2048]{0:T(1024)S(1)}, f32[2048]{0:T(1024)}, u32[]{:S(2)}) copy-start(f32[2048]{0:T(1024)} %param.8) | copy-start | bytes 24580
  23.7 6.1 %collective-permute-start.6 = (bf16[512,128]{1,0:T(8,128)(2,1)S(1)}, bf16[512,128]{1,0:T(8,128)(2,1)S(1)}, u32[]{:S(2)}, u32[]{:S(2)}) collective-permute-start(bf16[512,128]{1,0:T(8,128)(2,1)S(1)} %get-tuple-element.48), channel_id=1, source_target_pairs={{0,3},{1,2},{2,1},{3,0},{4,7},{5,6},{6,5},{7,4},{8,11},{9,10},{10,... | collective-permute-start | bytes 393224 | tf_op jit(solution)/shard_map/ppermute | solution.py:358
  29.8 4.7 %copy-start.3 = (bf16[1,128,2048]{2,1,0:T(8,128)(2,1)S(1)}, bf16[1,128,2048]{2,1,0:T(8,128)(2,1)}, u32[]{:S(2)}) copy-start(bf16[1,128,2048]{2,1,0:T(8,128)(2,1)} %param.5) | copy-start | bytes 1572868
  30.9 7.1 %collective-permute-start.7 = (bf16[544,128]{1,0:T(8,128)(2,1)S(1)}, bf16[544,128]{1,0:T(8,128)(2,1)S(1)}, u32[]{:S(2)}, u32[]{:S(2)}) collective-permute-start(bf16[544,128]{1,0:T(8,128)(2,1)S(1)} %get-tuple-element.57), channel_id=1, source_target_pairs={{0,2},{1,3},{2,0},{3,1},{4,6},{5,7},{6,4},{7,5},{8,11},{9,10},{10,... | collective-permute-start | bytes 417800 | tf_op jit(solution)/shard_map/ppermute | solution.py:358
  33.0 6.1 %collective-permute-start.8 = (bf16[544,128]{1,0:T(8,128)(2,1)S(1)}, bf16[544,128]{1,0:T(8,128)(2,1)S(1)}, u32[]{:S(2)}, u32[]{:S(2)}) collective-permute-start(bf16[544,128]{1,0:T(8,128)(2,1)S(1)} %get-tuple-element.58), channel_id=1, source_target_pairs={{0,3},{1,2},{2,1},{3,0},{4,7},{5,6},{6,5},{7,4},{8,9},{9,8},{10,11... | collective-permute-start | bytes 417800 | tf_op jit(solution)/shard_map/ppermute | solution.py:358
  34.2 6.2 %collective-permute-start.9 = (bf16[544,128]{1,0:T(8,128)(2,1)S(1)}, bf16[544,128]{1,0:T(8,128)(2,1)S(1)}, u32[]{:S(2)}, u32[]{:S(2)}) collective-permute-start(bf16[544,128]{1,0:T(8,128)(2,1)S(1)} %get-tuple-element.59), channel_id=1, source_target_pairs={{0,1},{1,0},{2,3},{3,2},{4,5},{5,4},{6,7},{7,6},{8,10},{9,11},{10,... | collective-permute-start | bytes 417800 | tf_op jit(solution)/shard_map/ppermute | solution.py:358
  40.5 7.3 %collective-permute-start.10 = (bf16[544,128]{1,0:T(8,128)(2,1)S(1)}, bf16[544,128]{1,0:T(8,128)(2,1)S(1)}, u32[]{:S(2)}, u32[]{:S(2)}) collective-permute-start(bf16[544,128]{1,0:T(8,128)(2,1)S(1)} %get-tuple-element.61), channel_id=1, source_target_pairs={{0,4},{1,5},{2,6},{3,7},{4,0},{5,1},{6,2},{7,3},{8,12},{9,13},{10,... | collective-permute-start | bytes 417800 | tf_op jit(solution)/shard_map/ppermute | solution.py:375
  42.5 9.6 %collective-permute-start.15 = (f32[16,128]{1,0:T(8,128)S(1)}, f32[16,128]{1,0:T(8,128)S(1)}, u32[]{:S(2)}, u32[]{:S(2)}) collective-permute-start(f32[16,128]{1,0:T(8,128)S(1)} %get-tuple-element.62.refs_5_), channel_id=1, source_target_pairs={{0,20},{1,21},{2,22},{3,23},{4,16},{5,17},{6,18},{7,19},{8,28},{9,... | collective-permute-start | bytes 24584 | tf_op jit(solution)/shard_map/ppermute | solution.py:395
  44.5 7.6 %collective-permute-start.14 = (f32[16,128]{1,0:T(8,128)S(1)}, f32[16,128]{1,0:T(8,128)S(1)}, u32[]{:S(2)}, u32[]{:S(2)}) collective-permute-start(f32[16,128]{1,0:T(8,128)S(1)} %get-tuple-element.62.refs_5_), channel_id=1, source_target_pairs={{0,16},{1,17},{2,18},{3,19},{4,20},{5,21},{6,22},{7,23},{8,24},{9,... | collective-permute-start | bytes 24584 | tf_op jit(solution)/shard_map/ppermute | solution.py:395
  47.9 7.3 %collective-permute-start.12 = (bf16[512,128]{1,0:T(8,128)(2,1)S(1)}, bf16[512,128]{1,0:T(8,128)(2,1)S(1)}, u32[]{:S(2)}, u32[]{:S(2)}) collective-permute-start(bf16[512,128]{1,0:T(8,128)(2,1)S(1)} %shard_map.102.refs_5_), channel_id=1, source_target_pairs={{0,3},{1,2},{2,1},{3,0},{4,7},{5,6},{6,5},{7,4},{8,9},{9,8},{10,11... | collective-permute-start | bytes 393224 | tf_op jit(solution)/shard_map/ppermute | solution.py:358
  49.3 6.0 %collective-permute-start.13 = (bf16[512,128]{1,0:T(8,128)(2,1)S(1)}, bf16[512,128]{1,0:T(8,128)(2,1)S(1)}, u32[]{:S(2)}, u32[]{:S(2)}) collective-permute-start(bf16[512,128]{1,0:T(8,128)(2,1)S(1)} %shard_map.103.refs_6_), channel_id=1, source_target_pairs={{0,1},{1,0},{2,3},{3,2},{4,5},{5,4},{6,7},{7,6},{8,11},{9,10},{10,... | collective-permute-start | bytes 393224 | tf_op jit(solution)/shard_map/ppermute | solution.py:358
  51.0 5.6 %collective-permute-start.11 = (bf16[512,128]{1,0:T(8,128)(2,1)S(1)}, bf16[512,128]{1,0:T(8,128)(2,1)S(1)}, u32[]{:S(2)}, u32[]{:S(2)}) collective-permute-start(bf16[512,128]{1,0:T(8,128)(2,1)S(1)} %get-tuple-element.63), channel_id=1, source_target_pairs={{0,2},{1,3},{2,0},{3,1},{4,6},{5,7},{6,4},{7,5},{8,10},{9,11},{10,... | collective-permute-start | bytes 393224 | tf_op jit(solution)/shard_map/ppermute | solution.py:358
  52.0 4.5 %collective-permute-start.16 = (f32[16,128]{1,0:T(8,128)S(1)}, f32[16,128]{1,0:T(8,128)S(1)}, u32[]{:S(2)}, u32[]{:S(2)}) collective-permute-start(f32[16,128]{1,0:T(8,128)S(1)} %add_add_fusion.refs_7_), channel_id=1, source_target_pairs={{0,8},{8,0},{16,24},{24,16},{1,9},{9,1},{17,25},{25,17},{2,10},{10... | collective-permute-start | bytes 24584 | tf_op jit(solution)/shard_map/ppermute | solution.py:347

commit v10 on v9

--- a/solution.py
+++ b/solution.py
@@ -31,8 +31,8 @@
     return lax.rem(lax.axis_index("seq"), group)
 
 
-STATE_ORDERS = (((0, 1, 2, 3), (0, 2, 1, 3)), ((0, 1, 2, 3), (0, 1, 2, 3)))
-GRAD_ORDERS = (((0, 2, 3, 1), (0, 3, 1, 2)), ((0, 3, 1, 2), (0, 1, 3, 2)))
+STATE_ORDERS = (((0, 1, 2, 3), (0, 2, 1, 3)), ((0, 2, 1, 3), (0, 1, 2, 3)))
+GRAD_ORDERS = (((0, 3, 1, 2), (0, 3, 1, 2)), ((0, 1, 2, 3), (0, 2, 1, 3)))
 NORM_ORDERS = (STATE_ORDERS[1], GRAD_ORDERS[0])
 
 
@@ -53,30 +53,35 @@
         whole_ref[block_at(partner_of(order, j), size), :] = ref[0:size, :]
 
 
-def scattered(order, whole_ref, size, piece_refs):
-    for j, ref in enumerate(piece_refs):
-        ref[0:size, :] = whole_ref[block_at(partner_of(order, j), size), :]
-
-
 def columns(first, count):
     return slice(first, first + count)
 
 
-def state_kernel(head, group, k_ref, v_ref, *refs):
-    piece_refs = refs[:group]
-    whole_ref, k_buffer, v_buffer, arrived = refs[group:]
+def first_state_kernel(head, slot, k_ref, v_ref, piece_ref, k_buffer, v_buffer, arrived):
+    width = piece_ref.shape[0]
+    source = block_at(partner_of(STATE_ORDERS[0], slot), width)
     copies = [
-        pltpu.make_async_copy(k_ref, k_buffer, arrived.at[0]),
-        pltpu.make_async_copy(v_ref, v_buffer, arrived.at[1]),
+        pltpu.make_async_copy(k_ref.at[:, source], k_buffer, arrived.at[0]),
+        pltpu.make_async_copy(v_ref.at[:, source], v_buffer, arrived.at[1]),
     ]
     for copy in copies:
         copy.start()
     for copy in copies:
         copy.wait()
-    for h in range(HEADS):
-        part = columns(h * head, head)
-        whole_ref[part, :] = dot(k_buffer[:, part], v_buffer[:, part], 0, 0).astype(HALF)
-    scattered(STATE_ORDERS[0], whole_ref, piece_refs[0].shape[0], piece_refs)
+    for i in range(width // head):
+        part = columns(i * head, head)
+        piece_ref[part, :] = dot(k_buffer[:, part], v_buffer[:, part], 0, 0).astype(HALF)
+
+
+def state_kernel(head, slots, k_ref, v_ref, token_ref, *piece_refs):
+    del token_ref
+    for slot, piece_ref in zip(slots, piece_refs):
+        width = piece_ref.shape[0]
+        for i in range(width // head):
+            part = features_at(STATE_ORDERS[0], slot, i, width, head)
+            piece_ref[columns(i * head, head), :] = dot(
+                k_ref[:, part], v_ref[:, part], 0, 0
+            ).astype(HALF)
 
 
 def local_kernel(head, q_ref, k_ref, v_ref, scores_ref, intra_ref):
@@ -453,16 +458,21 @@
     whole = pltpu.VMEM((features, head), HALF)
     gain_row = gain.reshape(1, features)
 
-    pieces = call(
-        part(state_kernel, head, group),
-        [piece] * group,
+    (first,) = call(
+        part(first_state_kernel, head, 1),
+        [piece],
         [pltpu.with_memory_space_constraint(a, pltpu.HBM) for a in (k, v)],
         1,
-        [whole]
-        + [pltpu.VMEM((rows, features), HALF)] * 2
-        + [pltpu.SemaphoreType.DMA((2,))],
+        [pltpu.VMEM((rows, width), HALF)] * 2 + [pltpu.SemaphoreType.DMA((2,))],
         ins={0: HBM, 1: HBM},
     )
+    slots = (2, 3, 0)
+    rest = call(
+        part(state_kernel, head, slots), [piece] * 3, [k, v, first], 1, ins={2: ANY}
+    )
+    pieces = dict(zip(slots, rest))
+    pieces[1] = first
+    pieces = [pieces[slot] for slot in range(group)]
     scores, intra = call(part(local_kernel, head), [scores_shape, wide], [q, k, v], 2)
     prefix, _ = exclusive_scan(pieces, STATE_ORDERS, width, False, intra)
     message = jax.ShapeDtypeStruct((width + 2 * HEADS, head), HALF)

time: 57.7 us -> 56.9 us (0.986)
  local copies, waits for them, and re-layouts: 1.06 us -> 0.02 us
    unnamed x12 -> x10, local copies, waits for them, and re-layouts: 1.06 us -> 0.02 us
    pallas_call x15 -> x16, Pallas kernels: 12.7 us -> 12.6 us  [call(): pl.pallas_call(kernel, out_shape=tuple(outs), in_specs=[ins.get(i, VMEM)...]
  transfers between devices with their start and end apart: 17 -> 17, of which waited for: 10 -> 11; matrix products, arithmetic and copies ran while one was open for 0% -> 0% of each run, Pallas kernels for 15% -> 16%
where the time goes in v10:
time: 56.9 us; the launch traced here: 56.8 us
  starting transfers between devices  23 us (40%)
  waiting for transfers between devices  20.3 us (36%)
  Pallas kernels  12.6 us (22%)
  between operations  0.78 us (1%)
    ppermute x12, starting transfers between devices, own_and_swapped(): results.append(lax.ppermute(pieces[slot], ('dp', 'seq'), pairs))  15.5 us
    pallas_call x16, Pallas kernels, call(): pl.pallas_call(kernel, out_shape=tuple(outs), in_specs=[ins.get(i, VMEM)...  12.6 us
    ppermute x12, waiting for transfers between devices, own_and_swapped(): results.append(lax.ppermute(pieces[slot], ('dp', 'seq'), pairs))  11.9 us
    ppermute x2, waiting for transfers between devices, shifted(): return lax.ppermute(array, 'seq', pairs)  8.43 us
    ppermute x2, starting transfers between devices, shifted(): return lax.ppermute(array, 'seq', pairs)  4.74 us
    ppermute x2, starting transfers between devices, exclusive_scan(): gains.append(lax.ppermute(gains[0], ('dp', 'seq'), pairs))  2.66 us
  transfers between devices with their start and end apart: 17, of which 11 were waited for; matrix products, arithmetic and copies ran while one was open for 0% of the time, Pallas kernels for 16%

profile of v10, /device:TPU:0, one launch (start us, length us, event | category | flops | bytes accessed | tf_op | source)
XLA Modules:
  0.0 56.8 jit_solution(3099157971224156503)
XLA Ops:
  0.7 1.3 %shard_map.93.token_ref = bf16[512,128]{1,0:T(8,128)(2,1)S(1)} custom-call(bf16[128,2048]{1,0:T(8,128)(2,1)} %bitcast.10, bf16[128,2048]{1,0:T(8,128)(2,1)} %bitcast.16), custom_call_target="tpu_custom_call" | custom-call | flops 67108864 | bytes 1179648 | tf_op jit(solution)/shard_map/pallas_call | solution.py:334
  2.0 3.0 %collective-permute-start = (bf16[512,128]{1,0:T(8,128)(2,1)S(1)}, bf16[512,128]{1,0:T(8,128)(2,1)S(1)}, u32[]{:S(2)}, u32[]{:S(2)}) collective-permute-start(bf16[512,128]{1,0:T(8,128)(2,1)S(1)} %shard_map.93.token_ref), channel_id=1, source_target_pairs={{0,1},{1,0},{2,3},{3,2},{4,5},{5,4},{6,7},{7,6},{8,10},{9,11},{10,... | collective-permute-start | bytes 393224 | tf_op jit(solution)/shard_map/ppermute | solution.py:363
  5.0 0.4 shard_map.94
  5.4 1.6 %collective-permute-start.1 = (bf16[512,128]{1,0:T(8,128)(2,1)S(1)}, bf16[512,128]{1,0:T(8,128)(2,1)S(1)}, u32[]{:S(2)}, u32[]{:S(2)}) collective-permute-start(bf16[512,128]{1,0:T(8,128)(2,1)S(1)} %get-tuple-element.40), channel_id=1, source_target_pairs={{0,2},{1,3},{2,0},{3,1},{4,6},{5,7},{6,4},{7,5},{8,9},{9,8},{10,11... | collective-permute-start | bytes 393224 | tf_op jit(solution)/shard_map/ppermute | solution.py:363
  7.1 2.6 %shard_map.92 = (bf16[2048,128]{1,0:T(8,128)(2,1)S(1)}, f32[128,2048]{1,0:T(8,128)S(1)}) custom-call(bf16[128,2048]{1,0:T(8,128)(2,1)S(1)} %bitcast.22, bf16[128,2048]{1,0:T(8,128)(2,1)S(1)} %bitcast.12, bf16[128,2048]{1,0:T(8,128)(2,1)S(1)} %bitcast.18), custom_call_target="tpu_custom_call" | custom-call | flops 134217728 | bytes 3145728 | tf_op jit(solution)/shard_map/pallas_call | solution.py:334
  9.7 2.0 %collective-permute-done.1.refs_2_.refs_3_ = bf16[512,128]{1,0:T(8,128)(2,1)S(1)} collective-permute-done((bf16[512,128]{1,0:T(8,128)(2,1)S(1)}, bf16[512,128]{1,0:T(8,128)(2,1)S(1)}, u32[]{:S(2)}, u32[]{:S(2)}) %collective-permute-start.1) | collective-permute-done | bytes 131104 | tf_op jit(solution)/shard_map/ppermute | solution.py:363
  11.7 1.2 %collective-permute-done.2.refs_3_.refs_4_ = bf16[512,128]{1,0:T(8,128)(2,1)S(1)} collective-permute-done((bf16[512,128]{1,0:T(8,128)(2,1)S(1)}, bf16[512,128]{1,0:T(8,128)(2,1)S(1)}, u32[]{:S(2)}, u32[]{:S(2)}) %collective-permute-start.2) | collective-permute-done | bytes 131104 | tf_op jit(solution)/shard_map/ppermute | solution.py:363
  12.9 3.0 %collective-permute-start.3 = (bf16[512,128]{1,0:T(8,128)(2,1)S(1)}, bf16[512,128]{1,0:T(8,128)(2,1)S(1)}, u32[]{:S(2)}, u32[]{:S(2)}) collective-permute-start(bf16[512,128]{1,0:T(8,128)(2,1)S(1)} %shard_map.95), channel_id=1, source_target_pairs={{0,4},{1,5},{2,6},{3,7},{4,0},{5,1},{6,2},{7,3},{8,12},{9,13},{10,... | collective-permute-start | bytes 393224 | tf_op jit(solution)/shard_map/ppermute | solution.py:380
  15.9 5.3 %collective-permute-done.3.refs_0_ = bf16[512,128]{1,0:T(8,128)(2,1)S(1)} collective-permute-done((bf16[512,128]{1,0:T(8,128)(2,1)S(1)}, bf16[512,128]{1,0:T(8,128)(2,1)S(1)}, u32[]{:S(2)}, u32[]{:S(2)}) %collective-permute-start.3) | collective-permute-done | bytes 131104 | tf_op jit(solution)/shard_map/ppermute | solution.py:380
  21.5 0.9 %collective-permute-start.5 = (bf16[512,128]{1,0:T(8,128)(2,1)S(1)}, bf16[512,128]{1,0:T(8,128)(2,1)S(1)}, u32[]{:S(2)}, u32[]{:S(2)}) collective-permute-start(bf16[512,128]{1,0:T(8,128)(2,1)S(1)} %shard_map.97.refs_5_), channel_id=1, source_target_pairs={{0,1},{1,0},{2,3},{3,2},{4,5},{5,4},{6,7},{7,6},{8,10},{9,11},{10,... | collective-permute-start | bytes 393224 | tf_op jit(solution)/shard_map/ppermute | solution.py:363
  22.4 0.2 shard_map.98
  22.7 2.7 %collective-permute-start.6 = (bf16[512,128]{1,0:T(8,128)(2,1)S(1)}, bf16[512,128]{1,0:T(8,128)(2,1)S(1)}, u32[]{:S(2)}, u32[]{:S(2)}) collective-permute-start(bf16[512,128]{1,0:T(8,128)(2,1)S(1)} %get-tuple-element.46), channel_id=1, source_target_pairs={{0,3},{1,2},{2,1},{3,0},{4,7},{5,6},{6,5},{7,4},{8,11},{9,10},{10,... | collective-permute-start | bytes 393224 | tf_op jit(solution)/shard_map/ppermute | solution.py:363
  25.4 2.7 %collective-permute-done.5.refs_6_.refs_11_ = bf16[512,128]{1,0:T(8,128)(2,1)S(1)} collective-permute-done((bf16[512,128]{1,0:T(8,128)(2,1)S(1)}, bf16[512,128]{1,0:T(8,128)(2,1)S(1)}, u32[]{:S(2)}, u32[]{:S(2)}) %collective-permute-start.5) | collective-permute-done | bytes 131104 | tf_op jit(solution)/shard_map/ppermute | solution.py:363
  28.1 0.4 shard_map.99
  28.6 0.9 %collective-permute-done.6.refs_7_.refs_12_ = bf16[512,128]{1,0:T(8,128)(2,1)S(1)} collective-permute-done((bf16[512,128]{1,0:T(8,128)(2,1)S(1)}, bf16[512,128]{1,0:T(8,128)(2,1)S(1)}, u32[]{:S(2)}, u32[]{:S(2)}) %collective-permute-start.6) | collective-permute-done | bytes 131104 | tf_op jit(solution)/shard_map/ppermute | solution.py:363
  29.5 1.0 %shard_map.100 = (f32[128,512]{1,0:T(8,128)S(1)}, f32[128,128]{1,0:T(8,128)S(1)}, bf16[128,2048]{1,0:T(8,128)(2,1)S(1)}, bf16[544,128]{1,0:T(8,128)(2,1)S(1)}, b...) custom-call(bf16[128,2048]{1,0:T(8,128)(2,1)S(1)} %bitcast.24, ...), custom_call_target="tpu_custom_call" | custom-call | flops 134217728 | bytes 4825088 | tf_op jit(solution)/shard_map/pallas_call | solution.py:334
  30.5 1.8 %collective-permute-start.7 = (bf16[544,128]{1,0:T(8,128)(2,1)S(1)}, bf16[544,128]{1,0:T(8,128)(2,1)S(1)}, u32[]{:S(2)}, u32[]{:S(2)}) collective-permute-start(bf16[544,128]{1,0:T(8,128)(2,1)S(1)} %get-tuple-element.55), channel_id=1, source_target_pairs={{0,3},{1,2},{2,1},{3,0},{4,7},{5,6},{6,5},{7,4},{8,11},{9,10},{10,... | collective-permute-start | bytes 417800 | tf_op jit(solution)/shard_map/ppermute | solution.py:363
  32.3 1.0 %collective-permute-start.8 = (bf16[544,128]{1,0:T(8,128)(2,1)S(1)}, bf16[544,128]{1,0:T(8,128)(2,1)S(1)}, u32[]{:S(2)}, u32[]{:S(2)}) collective-permute-start(bf16[544,128]{1,0:T(8,128)(2,1)S(1)} %get-tuple-element.56), channel_id=1, source_target_pairs={{0,1},{1,0},{2,3},{3,2},{4,5},{5,4},{6,7},{7,6},{8,9},{9,8},{10,11... | collective-permute-start | bytes 417800 | tf_op jit(solution)/shard_map/ppermute | solution.py:363
  33.3 0.7 %collective-permute-start.9 = (bf16[544,128]{1,0:T(8,128)(2,1)S(1)}, bf16[544,128]{1,0:T(8,128)(2,1)S(1)}, u32[]{:S(2)}, u32[]{:S(2)}) collective-permute-start(bf16[544,128]{1,0:T(8,128)(2,1)S(1)} %get-tuple-element.57), channel_id=1, source_target_pairs={{0,2},{1,3},{2,0},{3,1},{4,6},{5,7},{6,4},{7,5},{8,10},{9,11},{10,... | collective-permute-start | bytes 417800 | tf_op jit(solution)/shard_map/ppermute | solution.py:363
  34.1 3.5 %shard_map.101 = (bf16[128,2048]{1,0:T(8,128)(2,1)}, bf16[128,2048]{1,0:T(8,128)(2,1)}, f32[128,2048]{1,0:T(8,128)S(1)}, f32[128,2048]{1,0:T(8,128)S(1)}, f32[8,128]{1,0:T(8,128)S(1)}) custom-call(bf16[128,2048]{1,0:T(8,128)(2,1)S(1)} %bitcast.25, bf16[128,2048]{1,0:T(8,128)(2,1)S(1)} %bitcast.13, bf16[128,2048]{1,0:T(8,128)(2,1)S(1)} %bitcast.19, ...), custom_call_target="tpu_custom_call" | custom-call | flops 335544320 | bytes 7680000 | tf_op jit(solution)/shard_map/pallas_call | solution.py:334
  37.6 0.9 %collective-permute-done.8.refs_2_.refs_3_ = bf16[544,128]{1,0:T(8,128)(2,1)S(1)} collective-permute-done((bf16[544,128]{1,0:T(8,128)(2,1)S(1)}, bf16[544,128]{1,0:T(8,128)(2,1)S(1)}, u32[]{:S(2)}, u32[]{:S(2)}) %collective-permute-start.8) | collective-permute-done | bytes 139296 | tf_op jit(solution)/shard_map/ppermute | solution.py:363
  38.8 1.8 %collective-permute-start.10 = (bf16[544,128]{1,0:T(8,128)(2,1)S(1)}, bf16[544,128]{1,0:T(8,128)(2,1)S(1)}, u32[]{:S(2)}, u32[]{:S(2)}) collective-permute-start(bf16[544,128]{1,0:T(8,128)(2,1)S(1)} %get-tuple-element.59), channel_id=1, source_target_pairs={{0,4},{1,5},{2,6},{3,7},{4,0},{5,1},{6,2},{7,3},{8,12},{9,13},{10,... | collective-permute-start | bytes 417800 | tf_op jit(solution)/shard_map/ppermute | solution.py:380
  40.6 2.0 %collective-permute-start.15 = (f32[16,128]{1,0:T(8,128)S(1)}, f32[16,128]{1,0:T(8,128)S(1)}, u32[]{:S(2)}, u32[]{:S(2)}) collective-permute-start(f32[16,128]{1,0:T(8,128)S(1)} %get-tuple-element.60.refs_5_), channel_id=1, source_target_pairs={{0,20},{1,21},{2,22},{3,23},{4,16},{5,17},{6,18},{7,19},{8,28},{9,... | collective-permute-start | bytes 24584 | tf_op jit(solution)/shard_map/ppermute | solution.py:400
  42.6 0.7 %collective-permute-start.14 = (f32[16,128]{1,0:T(8,128)S(1)}, f32[16,128]{1,0:T(8,128)S(1)}, u32[]{:S(2)}, u32[]{:S(2)}) collective-permute-start(f32[16,128]{1,0:T(8,128)S(1)} %get-tuple-element.60.refs_5_), channel_id=1, source_target_pairs={{0,16},{1,17},{2,18},{3,19},{4,20},{5,21},{6,22},{7,23},{8,24},{9,... | collective-permute-start | bytes 24584 | tf_op jit(solution)/shard_map/ppermute | solution.py:400
  43.2 3.1 %collective-permute-done.10.refs_0_ = bf16[544,128]{1,0:T(8,128)(2,1)S(1)} collective-permute-done((bf16[544,128]{1,0:T(8,128)(2,1)S(1)}, bf16[544,128]{1,0:T(8,128)(2,1)S(1)}, u32[]{:S(2)}, u32[]{:S(2)}) %collective-permute-start.10) | collective-permute-done | bytes 139296 | tf_op jit(solution)/shard_map/ppermute | solution.py:380
  46.7 2.9 %collective-permute-start.13 = (bf16[512,128]{1,0:T(8,128)(2,1)S(1)}, bf16[512,128]{1,0:T(8,128)(2,1)S(1)}, u32[]{:S(2)}, u32[]{:S(2)}) collective-permute-start(bf16[512,128]{1,0:T(8,128)(2,1)S(1)} %shard_map.104.refs_6_), channel_id=1, source_target_pairs={{0,2},{1,3},{2,0},{3,1},{4,6},{5,7},{6,4},{7,5},{8,9},{9,8},{10,11... | collective-permute-start | bytes 393224 | tf_op jit(solution)/shard_map/ppermute | solution.py:363
  49.6 0.2 shard_map.105
  49.9 0.7 %collective-permute-start.11 = (bf16[512,128]{1,0:T(8,128)(2,1)S(1)}, bf16[512,128]{1,0:T(8,128)(2,1)S(1)}, u32[]{:S(2)}, u32[]{:S(2)}) collective-permute-start(bf16[512,128]{1,0:T(8,128)(2,1)S(1)} %get-tuple-element.61), channel_id=1, source_target_pairs={{0,3},{1,2},{2,1},{3,0},{4,7},{5,6},{6,5},{7,4},{8,11},{9,10},{10,... | collective-permute-start | bytes 393224 | tf_op jit(solution)/shard_map/ppermute | solution.py:363
  50.6 1.9 %collective-permute-done.13.refs_6_ = bf16[512,128]{1,0:T(8,128)(2,1)S(1)} collective-permute-done((bf16[512,128]{1,0:T(8,128)(2,1)S(1)}, bf16[512,128]{1,0:T(8,128)(2,1)S(1)}, u32[]{:S(2)}, u32[]{:S(2)}) %collective-permute-start.13) | collective-permute-done | bytes 131104 | tf_op jit(solution)/shard_map/ppermute | solution.py:363
  52.6 1.3 %shard_map.106 = (bf16[128,2048]{1,0:T(8,128)(2,1)}, bf16[128,2048]{1,0:T(8,128)(2,1)}) custom-call(bf16[128,2048]{1,0:T(8,128)(2,1)S(1)} %bitcast.14, bf16[128,2048]{1,0:T(8,128)(2,1)S(1)} %bitcast.20, f32[128,2048]{1,0:T(8,128)S(1)} %get-tuple-element.52.refs_2_, f32[128,2048]{1,0:T(8,128)S(1)} %get-tuple-element.53.refs_3_, ...), custom_call_target="tpu_custom_call" | custom-call | flops 67108864 | bytes 4587520 | tf_op jit(solution)/shard_map/pallas_call | solution.py:334
  53.8 1.9 %collective-permute-done.11.refs_4_ = bf16[512,128]{1,0:T(8,128)(2,1)S(1)} collective-permute-done((bf16[512,128]{1,0:T(8,128)(2,1)S(1)}, bf16[512,128]{1,0:T(8,128)(2,1)S(1)}, u32[]{:S(2)}, u32[]{:S(2)}) %collective-permute-start.11) | collective-permute-done | bytes 131104 | tf_op jit(solution)/shard_map/ppermute | solution.py:363
  55.8 1.0 %shard_map.107 = (bf16[128,2048]{1,0:T(8,128)(2,1)}, bf16[128,2048]{1,0:T(8,128)(2,1)}, f32[16,128]{1,0:T(8,128)}) custom-call(bf16[128,2048]{1,0:T(8,128)(2,1)S(1)} %bitcast.15, bf16[128,2048]{1,0:T(8,128)(2,1)S(1)} %bitcast.21, f32[128,2048]{1,0:T(8,128)S(1)} %get-tuple-element.52.refs_2_, ...), custom_call_target="tpu_custom_call", output_to_operand_aliasing={{0}: (5, {}), {1}: (6, {})} | custom-call | flops 67108864 | bytes 5398528 | tf_op jit(solution)/shard_map/pallas_call | solution.py:334
  (29 shorter events, 1.3 us)
Async XLA Ops:
  0.6 4.3 %copy-start = (bf16[1,128,2048]{2,1,0:T(8,128)(2,1)S(1)}, bf16[1,128,2048]{2,1,0:T(8,128)(2,1)}, u32[]{:S(2)}) copy-start(bf16[1,128,2048]{2,1,0:T(8,128)(2,1)} %param.6) | copy-start | bytes 1572868
  0.6 4.3 %copy-start.1 = (bf16[1,128,2048]{2,1,0:T(8,128)(2,1)S(1)}, bf16[1,128,2048]{2,1,0:T(8,128)(2,1)}, u32[]{:S(2)}) copy-start(bf16[1,128,2048]{2,1,0:T(8,128)(2,1)} %param.7) | copy-start | bytes 1572868
  2.0 5.1 %copy-start.2 = (bf16[1,128,2048]{2,1,0:T(8,128)(2,1)S(1)}, bf16[1,128,2048]{2,1,0:T(8,128)(2,1)}, u32[]{:S(2)}) copy-start(bf16[1,128,2048]{2,1,0:T(8,128)(2,1)} %param.5) | copy-start | bytes 1572868
  2.0 7.7 %collective-permute-start = (bf16[512,128]{1,0:T(8,128)(2,1)S(1)}, bf16[512,128]{1,0:T(8,128)(2,1)S(1)}, u32[]{:S(2)}, u32[]{:S(2)}) collective-permute-start(bf16[512,128]{1,0:T(8,128)(2,1)S(1)} %shard_map.93.token_ref), channel_id=1, source_target_pairs={{0,1},{1,0},{2,3},{3,2},{4,5},{5,4},{6,7},{7,6},{8,10},{9,11},{10,... | collective-permute-start | bytes 393224 | tf_op jit(solution)/shard_map/ppermute | solution.py:363
  5.4 6.3 %collective-permute-start.1 = (bf16[512,128]{1,0:T(8,128)(2,1)S(1)}, bf16[512,128]{1,0:T(8,128)(2,1)S(1)}, u32[]{:S(2)}, u32[]{:S(2)}) collective-permute-start(bf16[512,128]{1,0:T(8,128)(2,1)S(1)} %get-tuple-element.40), channel_id=1, source_target_pairs={{0,2},{1,3},{2,0},{3,1},{4,6},{5,7},{6,4},{7,5},{8,9},{9,8},{10,11... | collective-permute-start | bytes 393224 | tf_op jit(solution)/shard_map/ppermute | solution.py:363
  7.0 5.9 %collective-permute-start.2 = (bf16[512,128]{1,0:T(8,128)(2,1)S(1)}, bf16[512,128]{1,0:T(8,128)(2,1)S(1)}, u32[]{:S(2)}, u32[]{:S(2)}) collective-permute-start(bf16[512,128]{1,0:T(8,128)(2,1)S(1)} %get-tuple-element.41), channel_id=1, source_target_pairs={{0,3},{1,2},{2,1},{3,0},{4,7},{5,6},{6,5},{7,4},{8,11},{9,10},{10,... | collective-permute-start | bytes 393224 | tf_op jit(solution)/shard_map/ppermute | solution.py:363
  12.9 8.3 %collective-permute-start.3 = (bf16[512,128]{1,0:T(8,128)(2,1)S(1)}, bf16[512,128]{1,0:T(8,128)(2,1)S(1)}, u32[]{:S(2)}, u32[]{:S(2)}) collective-permute-start(bf16[512,128]{1,0:T(8,128)(2,1)S(1)} %shard_map.95), channel_id=1, source_target_pairs={{0,4},{1,5},{2,6},{3,7},{4,0},{5,1},{6,2},{7,3},{8,12},{9,13},{10,... | collective-permute-start | bytes 393224 | tf_op jit(solution)/shard_map/ppermute | solution.py:380
  21.5 6.6 %copy-start.3 = (bf16[1,128,2048]{2,1,0:T(8,128)(2,1)S(1)}, bf16[1,128,2048]{2,1,0:T(8,128)(2,1)}, u32[]{:S(2)}) copy-start(bf16[1,128,2048]{2,1,0:T(8,128)(2,1)} %param.9) | copy-start | bytes 1572868
  21.5 6.5 %collective-permute-start.5 = (bf16[512,128]{1,0:T(8,128)(2,1)S(1)}, bf16[512,128]{1,0:T(8,128)(2,1)S(1)}, u32[]{:S(2)}, u32[]{:S(2)}) collective-permute-start(bf16[512,128]{1,0:T(8,128)(2,1)S(1)} %shard_map.97.refs_5_), channel_id=1, source_target_pairs={{0,1},{1,0},{2,3},{3,2},{4,5},{5,4},{6,7},{7,6},{8,10},{9,11},{10,... | collective-permute-start | bytes 393224 | tf_op jit(solution)/shard_map/ppermute | solution.py:363
  22.4 5.7 %collective-permute-start.4 = (bf16[512,128]{1,0:T(8,128)(2,1)S(1)}, bf16[512,128]{1,0:T(8,128)(2,1)S(1)}, u32[]{:S(2)}, u32[]{:S(2)}) collective-permute-start(bf16[512,128]{1,0:T(8,128)(2,1)S(1)} %shard_map.96.refs_5_), channel_id=1, source_target_pairs={{0,2},{1,3},{2,0},{3,1},{4,6},{5,7},{6,4},{7,5},{8,9},{9,8},{10,11... | collective-permute-start | bytes 393224 | tf_op jit(solution)/shard_map/ppermute | solution.py:363
  22.4 5.7 %copy-start.4 = (f32[2048]{0:T(1024)S(1)}, f32[2048]{0:T(1024)}, u32[]{:S(2)}) copy-start(f32[2048]{0:T(1024)} %param.8) | copy-start | bytes 24580
  22.7 6.9 %collective-permute-start.6 = (bf16[512,128]{1,0:T(8,128)(2,1)S(1)}, bf16[512,128]{1,0:T(8,128)(2,1)S(1)}, u32[]{:S(2)}, u32[]{:S(2)}) collective-permute-start(bf16[512,128]{1,0:T(8,128)(2,1)S(1)} %get-tuple-element.46), channel_id=1, source_target_pairs={{0,3},{1,2},{2,1},{3,0},{4,7},{5,6},{6,5},{7,4},{8,11},{9,10},{10,... | collective-permute-start | bytes 393224 | tf_op jit(solution)/shard_map/ppermute | solution.py:363
  30.5 7.0 %collective-permute-start.7 = (bf16[544,128]{1,0:T(8,128)(2,1)S(1)}, bf16[544,128]{1,0:T(8,128)(2,1)S(1)}, u32[]{:S(2)}, u32[]{:S(2)}) collective-permute-start(bf16[544,128]{1,0:T(8,128)(2,1)S(1)} %get-tuple-element.55), channel_id=1, source_target_pairs={{0,3},{1,2},{2,1},{3,0},{4,7},{5,6},{6,5},{7,4},{8,11},{9,10},{10,... | collective-permute-start | bytes 417800 | tf_op jit(solution)/shard_map/ppermute | solution.py:363
  32.3 6.1 %collective-permute-start.8 = (bf16[544,128]{1,0:T(8,128)(2,1)S(1)}, bf16[544,128]{1,0:T(8,128)(2,1)S(1)}, u32[]{:S(2)}, u32[]{:S(2)}) collective-permute-start(bf16[544,128]{1,0:T(8,128)(2,1)S(1)} %get-tuple-element.56), channel_id=1, source_target_pairs={{0,1},{1,0},{2,3},{3,2},{4,5},{5,4},{6,7},{7,6},{8,9},{9,8},{10,11... | collective-permute-start | bytes 417800 | tf_op jit(solution)/shard_map/ppermute | solution.py:363
  33.3 5.3 %collective-permute-start.9 = (bf16[544,128]{1,0:T(8,128)(2,1)S(1)}, bf16[544,128]{1,0:T(8,128)(2,1)S(1)}, u32[]{:S(2)}, u32[]{:S(2)}) collective-permute-start(bf16[544,128]{1,0:T(8,128)(2,1)S(1)} %get-tuple-element.57), channel_id=1, source_target_pairs={{0,2},{1,3},{2,0},{3,1},{4,6},{5,7},{6,4},{7,5},{8,10},{9,11},{10,... | collective-permute-start | bytes 417800 | tf_op jit(solution)/shard_map/ppermute | solution.py:363
  38.8 7.6 %collective-permute-start.10 = (bf16[544,128]{1,0:T(8,128)(2,1)S(1)}, bf16[544,128]{1,0:T(8,128)(2,1)S(1)}, u32[]{:S(2)}, u32[]{:S(2)}) collective-permute-start(bf16[544,128]{1,0:T(8,128)(2,1)S(1)} %get-tuple-element.59), channel_id=1, source_target_pairs={{0,4},{1,5},{2,6},{3,7},{4,0},{5,1},{6,2},{7,3},{8,12},{9,13},{10,... | collective-permute-start | bytes 417800 | tf_op jit(solution)/shard_map/ppermute | solution.py:380
  40.6 10.0 %collective-permute-start.15 = (f32[16,128]{1,0:T(8,128)S(1)}, f32[16,128]{1,0:T(8,128)S(1)}, u32[]{:S(2)}, u32[]{:S(2)}) collective-permute-start(f32[16,128]{1,0:T(8,128)S(1)} %get-tuple-element.60.refs_5_), channel_id=1, source_target_pairs={{0,20},{1,21},{2,22},{3,23},{4,16},{5,17},{6,18},{7,19},{8,28},{9,... | collective-permute-start | bytes 24584 | tf_op jit(solution)/shard_map/ppermute | solution.py:400
  42.6 8.0 %collective-permute-start.14 = (f32[16,128]{1,0:T(8,128)S(1)}, f32[16,128]{1,0:T(8,128)S(1)}, u32[]{:S(2)}, u32[]{:S(2)}) collective-permute-start(f32[16,128]{1,0:T(8,128)S(1)} %get-tuple-element.60.refs_5_), channel_id=1, source_target_pairs={{0,16},{1,17},{2,18},{3,19},{4,20},{5,21},{6,22},{7,23},{8,24},{9,... | collective-permute-start | bytes 24584 | tf_op jit(solution)/shard_map/ppermute | solution.py:400
  46.5 6.1 %collective-permute-start.12 = (bf16[512,128]{1,0:T(8,128)(2,1)S(1)}, bf16[512,128]{1,0:T(8,128)(2,1)S(1)}, u32[]{:S(2)}, u32[]{:S(2)}) collective-permute-start(bf16[512,128]{1,0:T(8,128)(2,1)S(1)} %shard_map.103.refs_5_), channel_id=1, source_target_pairs={{0,1},{1,0},{2,3},{3,2},{4,5},{5,4},{6,7},{7,6},{8,10},{9,11},{10,... | collective-permute-start | bytes 393224 | tf_op jit(solution)/shard_map/ppermute | solution.py:363
  46.7 5.9 %collective-permute-start.13 = (bf16[512,128]{1,0:T(8,128)(2,1)S(1)}, bf16[512,128]{1,0:T(8,128)(2,1)S(1)}, u32[]{:S(2)}, u32[]{:S(2)}) collective-permute-start(bf16[512,128]{1,0:T(8,128)(2,1)S(1)} %shard_map.104.refs_6_), channel_id=1, source_target_pairs={{0,2},{1,3},{2,0},{3,1},{4,6},{5,7},{6,4},{7,5},{8,9},{9,8},{10,11... | collective-permute-start | bytes 393224 | tf_op jit(solution)/shard_map/ppermute | solution.py:363
  49.9 5.9 %collective-permute-start.11 = (bf16[512,128]{1,0:T(8,128)(2,1)S(1)}, bf16[512,128]{1,0:T(8,128)(2,1)S(1)}, u32[]{:S(2)}, u32[]{:S(2)}) collective-permute-start(bf16[512,128]{1,0:T(8,128)(2,1)S(1)} %get-tuple-element.61), channel_id=1, source_target_pairs={{0,3},{1,2},{2,1},{3,0},{4,7},{5,6},{6,5},{7,4},{8,11},{9,10},{10,... | collective-permute-start | bytes 393224 | tf_op jit(solution)/shard_map/ppermute | solution.py:363
  50.6 3.3 %collective-permute-start.16 = (f32[16,128]{1,0:T(8,128)S(1)}, f32[16,128]{1,0:T(8,128)S(1)}, u32[]{:S(2)}, u32[]{:S(2)}) collective-permute-start(f32[16,128]{1,0:T(8,128)S(1)} %add_add_fusion.refs_7_), channel_id=1, source_target_pairs={{0,8},{8,0},{16,24},{24,16},{1,9},{9,1},{17,25},{25,17},{2,10},{10... | collective-permute-start | bytes 24584 | tf_op jit(solution)/shard_map/ppermute | solution.py:352

commit v11 on v10

--- a/solution.py
+++ b/solution.py
@@ -32,7 +32,7 @@
 
 
 STATE_ORDERS = (((0, 1, 2, 3), (0, 2, 1, 3)), ((0, 2, 1, 3), (0, 1, 2, 3)))
-GRAD_ORDERS = (((0, 3, 1, 2), (0, 3, 1, 2)), ((0, 1, 2, 3), (0, 2, 1, 3)))
+GRAD_ORDERS = (((0, 3, 1, 2), (0, 3, 1, 2)), ((0, 3, 1, 2), (0, 1, 2, 3)))
 NORM_ORDERS = (STATE_ORDERS[1], GRAD_ORDERS[0])
 
 

time: 56.9 us -> 56.2 us (0.988)
  waiting for transfers between devices: 20.3 us -> 19.6 us
    ppermute x12, waiting for transfers between devices: 11.9 us -> 11.2 us  [own_and_swapped(): results.append(lax.ppermute(pieces[slot], ('dp', 'seq'), pairs))]
  transfers between devices with their start and end apart: 17 -> 17, of which waited for: 11 -> 10; matrix products, arithmetic and copies ran while one was open for 0% -> 0% of each run, Pallas kernels for 16% -> 16%
where the time goes in v11:
time: 56.2 us; the launch traced here: 56.1 us
  starting transfers between devices  23 us (41%)
  waiting for transfers between devices  19.6 us (35%)
  Pallas kernels  12.7 us (23%)
  between operations  0.77 us (1%)
    ppermute x12, starting transfers between devices, own_and_swapped(): results.append(lax.ppermute(pieces[slot], ('dp', 'seq'), pairs))  15.5 us
    pallas_call x16, Pallas kernels, call(): pl.pallas_call(kernel, out_shape=tuple(outs), in_specs=[ins.get(i, VMEM)...  12.7 us
    ppermute x12, waiting for transfers between devices, own_and_swapped(): results.append(lax.ppermute(pieces[slot], ('dp', 'seq'), pairs))  11.2 us
    ppermute x2, waiting for transfers between devices, shifted(): return lax.ppermute(array, 'seq', pairs)  8.4 us
    ppermute x2, starting transfers between devices, shifted(): return lax.ppermute(array, 'seq', pairs)  4.74 us
    ppermute x2, starting transfers between devices, exclusive_scan(): gains.append(lax.ppermute(gains[0], ('dp', 'seq'), pairs))  2.66 us
  transfers between devices with their start and end apart: 17, of which 10 were waited for; matrix products, arithmetic and copies ran while one was open for 0% of the time, Pallas kernels for 16%

profile of v11, /device:TPU:0, one launch (start us, length us, event | category | flops | bytes accessed | tf_op | source)
XLA Modules:
  0.0 56.1 jit_solution(7007062742714449463)
XLA Ops:
  0.7 1.3 %shard_map.93.token_ref = bf16[512,128]{1,0:T(8,128)(2,1)S(1)} custom-call(bf16[128,2048]{1,0:T(8,128)(2,1)} %bitcast.10, bf16[128,2048]{1,0:T(8,128)(2,1)} %bitcast.16), custom_call_target="tpu_custom_call" | custom-call | flops 67108864 | bytes 1179648 | tf_op jit(solution)/shard_map/pallas_call | solution.py:334
  2.0 3.0 %collective-permute-start = (bf16[512,128]{1,0:T(8,128)(2,1)S(1)}, bf16[512,128]{1,0:T(8,128)(2,1)S(1)}, u32[]{:S(2)}, u32[]{:S(2)}) collective-permute-start(bf16[512,128]{1,0:T(8,128)(2,1)S(1)} %shard_map.93.token_ref), channel_id=1, source_target_pairs={{0,1},{1,0},{2,3},{3,2},{4,5},{5,4},{6,7},{7,6},{8,10},{9,11},{10,... | collective-permute-start | bytes 393224 | tf_op jit(solution)/shard_map/ppermute | solution.py:363
  5.0 0.4 shard_map.94
  5.4 1.6 %collective-permute-start.1 = (bf16[512,128]{1,0:T(8,128)(2,1)S(1)}, bf16[512,128]{1,0:T(8,128)(2,1)S(1)}, u32[]{:S(2)}, u32[]{:S(2)}) collective-permute-start(bf16[512,128]{1,0:T(8,128)(2,1)S(1)} %get-tuple-element.40), channel_id=1, source_target_pairs={{0,2},{1,3},{2,0},{3,1},{4,6},{5,7},{6,4},{7,5},{8,9},{9,8},{10,11... | collective-permute-start | bytes 393224 | tf_op jit(solution)/shard_map/ppermute | solution.py:363
  7.1 2.6 %shard_map.92 = (bf16[2048,128]{1,0:T(8,128)(2,1)S(1)}, f32[128,2048]{1,0:T(8,128)S(1)}) custom-call(bf16[128,2048]{1,0:T(8,128)(2,1)S(1)} %bitcast.22, bf16[128,2048]{1,0:T(8,128)(2,1)S(1)} %bitcast.12, bf16[128,2048]{1,0:T(8,128)(2,1)S(1)} %bitcast.18), custom_call_target="tpu_custom_call" | custom-call | flops 134217728 | bytes 3145728 | tf_op jit(solution)/shard_map/pallas_call | solution.py:334
  9.7 2.0 %collective-permute-done.1.refs_2_.refs_3_ = bf16[512,128]{1,0:T(8,128)(2,1)S(1)} collective-permute-done((bf16[512,128]{1,0:T(8,128)(2,1)S(1)}, bf16[512,128]{1,0:T(8,128)(2,1)S(1)}, u32[]{:S(2)}, u32[]{:S(2)}) %collective-permute-start.1) | collective-permute-done | bytes 131104 | tf_op jit(solution)/shard_map/ppermute | solution.py:363
  11.7 1.2 %collective-permute-done.2.refs_3_.refs_4_ = bf16[512,128]{1,0:T(8,128)(2,1)S(1)} collective-permute-done((bf16[512,128]{1,0:T(8,128)(2,1)S(1)}, bf16[512,128]{1,0:T(8,128)(2,1)S(1)}, u32[]{:S(2)}, u32[]{:S(2)}) %collective-permute-start.2) | collective-permute-done | bytes 131104 | tf_op jit(solution)/shard_map/ppermute | solution.py:363
  12.9 3.0 %collective-permute-start.3 = (bf16[512,128]{1,0:T(8,128)(2,1)S(1)}, bf16[512,128]{1,0:T(8,128)(2,1)S(1)}, u32[]{:S(2)}, u32[]{:S(2)}) collective-permute-start(bf16[512,128]{1,0:T(8,128)(2,1)S(1)} %shard_map.95), channel_id=1, source_target_pairs={{0,4},{1,5},{2,6},{3,7},{4,0},{5,1},{6,2},{7,3},{8,12},{9,13},{10,... | collective-permute-start | bytes 393224 | tf_op jit(solution)/shard_map/ppermute | solution.py:380
  15.9 5.3 %collective-permute-done.3.refs_0_ = bf16[512,128]{1,0:T(8,128)(2,1)S(1)} collective-permute-done((bf16[512,128]{1,0:T(8,128)(2,1)S(1)}, bf16[512,128]{1,0:T(8,128)(2,1)S(1)}, u32[]{:S(2)}, u32[]{:S(2)}) %collective-permute-start.3) | collective-permute-done | bytes 131104 | tf_op jit(solution)/shard_map/ppermute | solution.py:380
  21.5 0.9 %collective-permute-start.5 = (bf16[512,128]{1,0:T(8,128)(2,1)S(1)}, bf16[512,128]{1,0:T(8,128)(2,1)S(1)}, u32[]{:S(2)}, u32[]{:S(2)}) collective-permute-start(bf16[512,128]{1,0:T(8,128)(2,1)S(1)} %shard_map.97.refs_5_), channel_id=1, source_target_pairs={{0,1},{1,0},{2,3},{3,2},{4,5},{5,4},{6,7},{7,6},{8,10},{9,11},{10,... | collective-permute-start | bytes 393224 | tf_op jit(solution)/shard_map/ppermute | solution.py:363
  22.4 0.2 shard_map.98
  22.7 2.7 %collective-permute-start.6 = (bf16[512,128]{1,0:T(8,128)(2,1)S(1)}, bf16[512,128]{1,0:T(8,128)(2,1)S(1)}, u32[]{:S(2)}, u32[]{:S(2)}) collective-permute-start(bf16[512,128]{1,0:T(8,128)(2,1)S(1)} %get-tuple-element.46), channel_id=1, source_target_pairs={{0,3},{1,2},{2,1},{3,0},{4,7},{5,6},{6,5},{7,4},{8,11},{9,10},{10,... | collective-permute-start | bytes 393224 | tf_op jit(solution)/shard_map/ppermute | solution.py:363
  25.4 2.7 %collective-permute-done.5.refs_6_.refs_11_ = bf16[512,128]{1,0:T(8,128)(2,1)S(1)} collective-permute-done((bf16[512,128]{1,0:T(8,128)(2,1)S(1)}, bf16[512,128]{1,0:T(8,128)(2,1)S(1)}, u32[]{:S(2)}, u32[]{:S(2)}) %collective-permute-start.5) | collective-permute-done | bytes 131104 | tf_op jit(solution)/shard_map/ppermute | solution.py:363
  28.1 0.4 shard_map.99
  28.6 0.9 %collective-permute-done.6.refs_7_.refs_12_ = bf16[512,128]{1,0:T(8,128)(2,1)S(1)} collective-permute-done((bf16[512,128]{1,0:T(8,128)(2,1)S(1)}, bf16[512,128]{1,0:T(8,128)(2,1)S(1)}, u32[]{:S(2)}, u32[]{:S(2)}) %collective-permute-start.6) | collective-permute-done | bytes 131104 | tf_op jit(solution)/shard_map/ppermute | solution.py:363
  29.5 1.0 %shard_map.100 = (f32[128,512]{1,0:T(8,128)S(1)}, f32[128,128]{1,0:T(8,128)S(1)}, bf16[128,2048]{1,0:T(8,128)(2,1)S(1)}, bf16[544,128]{1,0:T(8,128)(2,1)S(1)}, b...) custom-call(bf16[128,2048]{1,0:T(8,128)(2,1)S(1)} %bitcast.24, ...), custom_call_target="tpu_custom_call" | custom-call | flops 134217728 | bytes 4825088 | tf_op jit(solution)/shard_map/pallas_call | solution.py:334
  30.5 1.8 %collective-permute-start.7 = (bf16[544,128]{1,0:T(8,128)(2,1)S(1)}, bf16[544,128]{1,0:T(8,128)(2,1)S(1)}, u32[]{:S(2)}, u32[]{:S(2)}) collective-permute-start(bf16[544,128]{1,0:T(8,128)(2,1)S(1)} %get-tuple-element.55), channel_id=1, source_target_pairs={{0,3},{1,2},{2,1},{3,0},{4,7},{5,6},{6,5},{7,4},{8,11},{9,10},{10,... | collective-permute-start | bytes 417800 | tf_op jit(solution)/shard_map/ppermute | solution.py:363
  32.3 1.0 %collective-permute-start.8 = (bf16[544,128]{1,0:T(8,128)(2,1)S(1)}, bf16[544,128]{1,0:T(8,128)(2,1)S(1)}, u32[]{:S(2)}, u32[]{:S(2)}) collective-permute-start(bf16[544,128]{1,0:T(8,128)(2,1)S(1)} %get-tuple-element.56), channel_id=1, source_target_pairs={{0,1},{1,0},{2,3},{3,2},{4,5},{5,4},{6,7},{7,6},{8,9},{9,8},{10,11... | collective-permute-start | bytes 417800 | tf_op jit(solution)/shard_map/ppermute | solution.py:363
  33.3 0.7 %collective-permute-start.9 = (bf16[544,128]{1,0:T(8,128)(2,1)S(1)}, bf16[544,128]{1,0:T(8,128)(2,1)S(1)}, u32[]{:S(2)}, u32[]{:S(2)}) collective-permute-start(bf16[544,128]{1,0:T(8,128)(2,1)S(1)} %get-tuple-element.57), channel_id=1, source_target_pairs={{0,2},{1,3},{2,0},{3,1},{4,6},{5,7},{6,4},{7,5},{8,10},{9,11},{10,... | collective-permute-start | bytes 417800 | tf_op jit(solution)/shard_map/ppermute | solution.py:363
  34.1 3.5 %shard_map.101 = (bf16[128,2048]{1,0:T(8,128)(2,1)}, bf16[128,2048]{1,0:T(8,128)(2,1)}, f32[128,2048]{1,0:T(8,128)S(1)}, f32[128,2048]{1,0:T(8,128)S(1)}, f32[8,128]{1,0:T(8,128)S(1)}) custom-call(bf16[128,2048]{1,0:T(8,128)(2,1)S(1)} %bitcast.25, bf16[128,2048]{1,0:T(8,128)(2,1)S(1)} %bitcast.13, bf16[128,2048]{1,0:T(8,128)(2,1)S(1)} %bitcast.19, ...), custom_call_target="tpu_custom_call" | custom-call | flops 335544320 | bytes 7680000 | tf_op jit(solution)/shard_map/pallas_call | solution.py:334
  37.6 0.9 %collective-permute-done.8.refs_2_.refs_3_ = bf16[544,128]{1,0:T(8,128)(2,1)S(1)} collective-permute-done((bf16[544,128]{1,0:T(8,128)(2,1)S(1)}, bf16[544,128]{1,0:T(8,128)(2,1)S(1)}, u32[]{:S(2)}, u32[]{:S(2)}) %collective-permute-start.8) | collective-permute-done | bytes 139296 | tf_op jit(solution)/shard_map/ppermute | solution.py:363
  38.8 1.8 %collective-permute-start.10 = (bf16[544,128]{1,0:T(8,128)(2,1)S(1)}, bf16[544,128]{1,0:T(8,128)(2,1)S(1)}, u32[]{:S(2)}, u32[]{:S(2)}) collective-permute-start(bf16[544,128]{1,0:T(8,128)(2,1)S(1)} %get-tuple-element.59), channel_id=1, source_target_pairs={{0,4},{1,5},{2,6},{3,7},{4,0},{5,1},{6,2},{7,3},{8,12},{9,13},{10,... | collective-permute-start | bytes 417800 | tf_op jit(solution)/shard_map/ppermute | solution.py:380
  40.6 2.0 %collective-permute-start.15 = (f32[16,128]{1,0:T(8,128)S(1)}, f32[16,128]{1,0:T(8,128)S(1)}, u32[]{:S(2)}, u32[]{:S(2)}) collective-permute-start(f32[16,128]{1,0:T(8,128)S(1)} %get-tuple-element.60.refs_5_), channel_id=1, source_target_pairs={{0,20},{1,21},{2,22},{3,23},{4,16},{5,17},{6,18},{7,19},{8,28},{9,... | collective-permute-start | bytes 24584 | tf_op jit(solution)/shard_map/ppermute | solution.py:400
  42.6 0.7 %collective-permute-start.14 = (f32[16,128]{1,0:T(8,128)S(1)}, f32[16,128]{1,0:T(8,128)S(1)}, u32[]{:S(2)}, u32[]{:S(2)}) collective-permute-start(f32[16,128]{1,0:T(8,128)S(1)} %get-tuple-element.60.refs_5_), channel_id=1, source_target_pairs={{0,16},{1,17},{2,18},{3,19},{4,20},{5,21},{6,22},{7,23},{8,24},{9,... | collective-permute-start | bytes 24584 | tf_op jit(solution)/shard_map/ppermute | solution.py:400
  43.2 3.1 %collective-permute-done.10.refs_0_ = bf16[544,128]{1,0:T(8,128)(2,1)S(1)} collective-permute-done((bf16[544,128]{1,0:T(8,128)(2,1)S(1)}, bf16[544,128]{1,0:T(8,128)(2,1)S(1)}, u32[]{:S(2)}, u32[]{:S(2)}) %collective-permute-start.10) | collective-permute-done | bytes 139296 | tf_op jit(solution)/shard_map/ppermute | solution.py:380
  46.5 1.2 %collective-permute-start.12 = (bf16[512,128]{1,0:T(8,128)(2,1)S(1)}, bf16[512,128]{1,0:T(8,128)(2,1)S(1)}, u32[]{:S(2)}, u32[]{:S(2)}) collective-permute-start(bf16[512,128]{1,0:T(8,128)(2,1)S(1)} %shard_map.103.refs_5_), channel_id=1, source_target_pairs={{0,3},{1,2},{2,1},{3,0},{4,7},{5,6},{6,5},{7,4},{8,9},{9,8},{10,11... | collective-permute-start | bytes 393224 | tf_op jit(solution)/shard_map/ppermute | solution.py:363
  47.8 0.3 collective-permute-start.13
  48.1 0.3 shard_map.105
  48.3 2.2 %collective-permute-start.11 = (bf16[512,128]{1,0:T(8,128)(2,1)S(1)}, bf16[512,128]{1,0:T(8,128)(2,1)S(1)}, u32[]{:S(2)}, u32[]{:S(2)}) collective-permute-start(bf16[512,128]{1,0:T(8,128)(2,1)S(1)} %get-tuple-element.61), channel_id=1, source_target_pairs={{0,2},{1,3},{2,0},{3,1},{4,6},{5,7},{6,4},{7,5},{8,11},{9,10},{10,... | collective-permute-start | bytes 393224 | tf_op jit(solution)/shard_map/ppermute | solution.py:363
  50.6 3.2 %collective-permute-done.13.refs_6_ = bf16[512,128]{1,0:T(8,128)(2,1)S(1)} collective-permute-done((bf16[512,128]{1,0:T(8,128)(2,1)S(1)}, bf16[512,128]{1,0:T(8,128)(2,1)S(1)}, u32[]{:S(2)}, u32[]{:S(2)}) %collective-permute-start.13) | collective-permute-done | bytes 131104 | tf_op jit(solution)/shard_map/ppermute | solution.py:363
  53.8 1.3 %shard_map.106 = (bf16[128,2048]{1,0:T(8,128)(2,1)}, bf16[128,2048]{1,0:T(8,128)(2,1)}) custom-call(bf16[128,2048]{1,0:T(8,128)(2,1)S(1)} %bitcast.14, bf16[128,2048]{1,0:T(8,128)(2,1)S(1)} %bitcast.20, f32[128,2048]{1,0:T(8,128)S(1)} %get-tuple-element.52.refs_2_, f32[128,2048]{1,0:T(8,128)S(1)} %get-tuple-element.53.refs_3_, ...), custom_call_target="tpu_custom_call" | custom-call | flops 67108864 | bytes 4587520 | tf_op jit(solution)/shard_map/pallas_call | solution.py:334
  55.1 1.0 %shard_map.107 = (bf16[128,2048]{1,0:T(8,128)(2,1)}, bf16[128,2048]{1,0:T(8,128)(2,1)}, f32[16,128]{1,0:T(8,128)}) custom-call(bf16[128,2048]{1,0:T(8,128)(2,1)S(1)} %bitcast.15, bf16[128,2048]{1,0:T(8,128)(2,1)S(1)} %bitcast.21, f32[128,2048]{1,0:T(8,128)S(1)} %get-tuple-element.52.refs_2_, ...), custom_call_target="tpu_custom_call", output_to_operand_aliasing={{0}: (5, {}), {1}: (6, {})} | custom-call | flops 67108864 | bytes 5398528 | tf_op jit(solution)/shard_map/pallas_call | solution.py:334
  (29 shorter events, 1.2 us)
Async XLA Ops:
  0.6 4.3 %copy-start = (bf16[1,128,2048]{2,1,0:T(8,128)(2,1)S(1)}, bf16[1,128,2048]{2,1,0:T(8,128)(2,1)}, u32[]{:S(2)}) copy-start(bf16[1,128,2048]{2,1,0:T(8,128)(2,1)} %param.6) | copy-start | bytes 1572868
  0.6 4.3 %copy-start.1 = (bf16[1,128,2048]{2,1,0:T(8,128)(2,1)S(1)}, bf16[1,128,2048]{2,1,0:T(8,128)(2,1)}, u32[]{:S(2)}) copy-start(bf16[1,128,2048]{2,1,0:T(8,128)(2,1)} %param.7) | copy-start | bytes 1572868
  2.0 5.1 %copy-start.2 = (bf16[1,128,2048]{2,1,0:T(8,128)(2,1)S(1)}, bf16[1,128,2048]{2,1,0:T(8,128)(2,1)}, u32[]{:S(2)}) copy-start(bf16[1,128,2048]{2,1,0:T(8,128)(2,1)} %param.5) | copy-start | bytes 1572868
  2.0 7.7 %collective-permute-start = (bf16[512,128]{1,0:T(8,128)(2,1)S(1)}, bf16[512,128]{1,0:T(8,128)(2,1)S(1)}, u32[]{:S(2)}, u32[]{:S(2)}) collective-permute-start(bf16[512,128]{1,0:T(8,128)(2,1)S(1)} %shard_map.93.token_ref), channel_id=1, source_target_pairs={{0,1},{1,0},{2,3},{3,2},{4,5},{5,4},{6,7},{7,6},{8,10},{9,11},{10,... | collective-permute-start | bytes 393224 | tf_op jit(solution)/shard_map/ppermute | solution.py:363
  5.4 6.3 %collective-permute-start.1 = (bf16[512,128]{1,0:T(8,128)(2,1)S(1)}, bf16[512,128]{1,0:T(8,128)(2,1)S(1)}, u32[]{:S(2)}, u32[]{:S(2)}) collective-permute-start(bf16[512,128]{1,0:T(8,128)(2,1)S(1)} %get-tuple-element.40), channel_id=1, source_target_pairs={{0,2},{1,3},{2,0},{3,1},{4,6},{5,7},{6,4},{7,5},{8,9},{9,8},{10,11... | collective-permute-start | bytes 393224 | tf_op jit(solution)/shard_map/ppermute | solution.py:363
  7.0 5.9 %collective-permute-start.2 = (bf16[512,128]{1,0:T(8,128)(2,1)S(1)}, bf16[512,128]{1,0:T(8,128)(2,1)S(1)}, u32[]{:S(2)}, u32[]{:S(2)}) collective-permute-start(bf16[512,128]{1,0:T(8,128)(2,1)S(1)} %get-tuple-element.41), channel_id=1, source_target_pairs={{0,3},{1,2},{2,1},{3,0},{4,7},{5,6},{6,5},{7,4},{8,11},{9,10},{10,... | collective-permute-start | bytes 393224 | tf_op jit(solution)/shard_map/ppermute | solution.py:363
  12.9 8.3 %collective-permute-start.3 = (bf16[512,128]{1,0:T(8,128)(2,1)S(1)}, bf16[512,128]{1,0:T(8,128)(2,1)S(1)}, u32[]{:S(2)}, u32[]{:S(2)}) collective-permute-start(bf16[512,128]{1,0:T(8,128)(2,1)S(1)} %shard_map.95), channel_id=1, source_target_pairs={{0,4},{1,5},{2,6},{3,7},{4,0},{5,1},{6,2},{7,3},{8,12},{9,13},{10,... | collective-permute-start | bytes 393224 | tf_op jit(solution)/shard_map/ppermute | solution.py:380
  21.5 6.6 %copy-start.3 = (bf16[1,128,2048]{2,1,0:T(8,128)(2,1)S(1)}, bf16[1,128,2048]{2,1,0:T(8,128)(2,1)}, u32[]{:S(2)}) copy-start(bf16[1,128,2048]{2,1,0:T(8,128)(2,1)} %param.9) | copy-start | bytes 1572868
  21.5 6.5 %collective-permute-start.5 = (bf16[512,128]{1,0:T(8,128)(2,1)S(1)}, bf16[512,128]{1,0:T(8,128)(2,1)S(1)}, u32[]{:S(2)}, u32[]{:S(2)}) collective-permute-start(bf16[512,128]{1,0:T(8,128)(2,1)S(1)} %shard_map.97.refs_5_), channel_id=1, source_target_pairs={{0,1},{1,0},{2,3},{3,2},{4,5},{5,4},{6,7},{7,6},{8,10},{9,11},{10,... | collective-permute-start | bytes 393224 | tf_op jit(solution)/shard_map/ppermute | solution.py:363
  22.4 5.7 %collective-permute-start.4 = (bf16[512,128]{1,0:T(8,128)(2,1)S(1)}, bf16[512,128]{1,0:T(8,128)(2,1)S(1)}, u32[]{:S(2)}, u32[]{:S(2)}) collective-permute-start(bf16[512,128]{1,0:T(8,128)(2,1)S(1)} %shard_map.96.refs_5_), channel_id=1, source_target_pairs={{0,2},{1,3},{2,0},{3,1},{4,6},{5,7},{6,4},{7,5},{8,9},{9,8},{10,11... | collective-permute-start | bytes 393224 | tf_op jit(solution)/shard_map/ppermute | solution.py:363
  22.4 5.7 %copy-start.4 = (f32[2048]{0:T(1024)S(1)}, f32[2048]{0:T(1024)}, u32[]{:S(2)}) copy-start(f32[2048]{0:T(1024)} %param.8) | copy-start | bytes 24580
  22.7 6.9 %collective-permute-start.6 = (bf16[512,128]{1,0:T(8,128)(2,1)S(1)}, bf16[512,128]{1,0:T(8,128)(2,1)S(1)}, u32[]{:S(2)}, u32[]{:S(2)}) collective-permute-start(bf16[512,128]{1,0:T(8,128)(2,1)S(1)} %get-tuple-element.46), channel_id=1, source_target_pairs={{0,3},{1,2},{2,1},{3,0},{4,7},{5,6},{6,5},{7,4},{8,11},{9,10},{10,... | collective-permute-start | bytes 393224 | tf_op jit(solution)/shard_map/ppermute | solution.py:363
  30.5 7.0 %collective-permute-start.7 = (bf16[544,128]{1,0:T(8,128)(2,1)S(1)}, bf16[544,128]{1,0:T(8,128)(2,1)S(1)}, u32[]{:S(2)}, u32[]{:S(2)}) collective-permute-start(bf16[544,128]{1,0:T(8,128)(2,1)S(1)} %get-tuple-element.55), channel_id=1, source_target_pairs={{0,3},{1,2},{2,1},{3,0},{4,7},{5,6},{6,5},{7,4},{8,11},{9,10},{10,... | collective-permute-start | bytes 417800 | tf_op jit(solution)/shard_map/ppermute | solution.py:363
  32.3 6.1 %collective-permute-start.8 = (bf16[544,128]{1,0:T(8,128)(2,1)S(1)}, bf16[544,128]{1,0:T(8,128)(2,1)S(1)}, u32[]{:S(2)}, u32[]{:S(2)}) collective-permute-start(bf16[544,128]{1,0:T(8,128)(2,1)S(1)} %get-tuple-element.56), channel_id=1, source_target_pairs={{0,1},{1,0},{2,3},{3,2},{4,5},{5,4},{6,7},{7,6},{8,9},{9,8},{10,11... | collective-permute-start | bytes 417800 | tf_op jit(solution)/shard_map/ppermute | solution.py:363
  33.3 5.3 %collective-permute-start.9 = (bf16[544,128]{1,0:T(8,128)(2,1)S(1)}, bf16[544,128]{1,0:T(8,128)(2,1)S(1)}, u32[]{:S(2)}, u32[]{:S(2)}) collective-permute-start(bf16[544,128]{1,0:T(8,128)(2,1)S(1)} %get-tuple-element.57), channel_id=1, source_target_pairs={{0,2},{1,3},{2,0},{3,1},{4,6},{5,7},{6,4},{7,5},{8,10},{9,11},{10,... | collective-permute-start | bytes 417800 | tf_op jit(solution)/shard_map/ppermute | solution.py:363
  38.8 7.5 %collective-permute-start.10 = (bf16[544,128]{1,0:T(8,128)(2,1)S(1)}, bf16[544,128]{1,0:T(8,128)(2,1)S(1)}, u32[]{:S(2)}, u32[]{:S(2)}) collective-permute-start(bf16[544,128]{1,0:T(8,128)(2,1)S(1)} %get-tuple-element.59), channel_id=1, source_target_pairs={{0,4},{1,5},{2,6},{3,7},{4,0},{5,1},{6,2},{7,3},{8,12},{9,13},{10,... | collective-permute-start | bytes 417800 | tf_op jit(solution)/shard_map/ppermute | solution.py:380
  40.6 10.0 %collective-permute-start.15 = (f32[16,128]{1,0:T(8,128)S(1)}, f32[16,128]{1,0:T(8,128)S(1)}, u32[]{:S(2)}, u32[]{:S(2)}) collective-permute-start(f32[16,128]{1,0:T(8,128)S(1)} %get-tuple-element.60.refs_5_), channel_id=1, source_target_pairs={{0,20},{1,21},{2,22},{3,23},{4,16},{5,17},{6,18},{7,19},{8,28},{9,... | collective-permute-start | bytes 24584 | tf_op jit(solution)/shard_map/ppermute | solution.py:400
  42.6 8.0 %collective-permute-start.14 = (f32[16,128]{1,0:T(8,128)S(1)}, f32[16,128]{1,0:T(8,128)S(1)}, u32[]{:S(2)}, u32[]{:S(2)}) collective-permute-start(f32[16,128]{1,0:T(8,128)S(1)} %get-tuple-element.60.refs_5_), channel_id=1, source_target_pairs={{0,16},{1,17},{2,18},{3,19},{4,20},{5,21},{6,22},{7,23},{8,24},{9,... | collective-permute-start | bytes 24584 | tf_op jit(solution)/shard_map/ppermute | solution.py:400
  46.5 7.3 %collective-permute-start.12 = (bf16[512,128]{1,0:T(8,128)(2,1)S(1)}, bf16[512,128]{1,0:T(8,128)(2,1)S(1)}, u32[]{:S(2)}, u32[]{:S(2)}) collective-permute-start(bf16[512,128]{1,0:T(8,128)(2,1)S(1)} %shard_map.103.refs_5_), channel_id=1, source_target_pairs={{0,3},{1,2},{2,1},{3,0},{4,7},{5,6},{6,5},{7,4},{8,9},{9,8},{10,11... | collective-permute-start | bytes 393224 | tf_op jit(solution)/shard_map/ppermute | solution.py:363
  47.8 6.0 %collective-permute-start.13 = (bf16[512,128]{1,0:T(8,128)(2,1)S(1)}, bf16[512,128]{1,0:T(8,128)(2,1)S(1)}, u32[]{:S(2)}, u32[]{:S(2)}) collective-permute-start(bf16[512,128]{1,0:T(8,128)(2,1)S(1)} %shard_map.104.refs_6_), channel_id=1, source_target_pairs={{0,1},{1,0},{2,3},{3,2},{4,5},{5,4},{6,7},{7,6},{8,10},{9,11},{10,... | collective-permute-start | bytes 393224 | tf_op jit(solution)/shard_map/ppermute | solution.py:363
  48.3 6.8 %collective-permute-start.11 = (bf16[512,128]{1,0:T(8,128)(2,1)S(1)}, bf16[512,128]{1,0:T(8,128)(2,1)S(1)}, u32[]{:S(2)}, u32[]{:S(2)}) collective-permute-start(bf16[512,128]{1,0:T(8,128)(2,1)S(1)} %get-tuple-element.61), channel_id=1, source_target_pairs={{0,2},{1,3},{2,0},{3,1},{4,6},{5,7},{6,4},{7,5},{8,11},{9,10},{10,... | collective-permute-start | bytes 393224 | tf_op jit(solution)/shard_map/ppermute | solution.py:363
  50.6 4.5 %collective-permute-start.16 = (f32[16,128]{1,0:T(8,128)S(1)}, f32[16,128]{1,0:T(8,128)S(1)}, u32[]{:S(2)}, u32[]{:S(2)}) collective-permute-start(f32[16,128]{1,0:T(8,128)S(1)} %add_add_fusion.refs_7_), channel_id=1, source_target_pairs={{0,8},{8,0},{16,24},{24,16},{1,9},{9,1},{17,25},{25,17},{2,10},{10... | collective-permute-start | bytes 24584 | tf_op jit(solution)/shard_map/ppermute | solution.py:352
